TPU v7x, 32 devices: a whole 2x2x4 slice. The times are simulated.
32 devices in a mesh: rows: 4 (over y, x), cols: 8 (over z, core).
Axes of the slice: x: 2, y: 2, z: 4, core: 2. Of those that a mesh axis runs over, the one named last changes fastest.
Arguments:
- model: bfloat16 [64, 512, 512], P(('rows', 'cols')), may hold values from -6 to 6
- dirty: bfloat16 [64, 512, 512], P(('rows', 'cols')), may hold values from -6 to 6
- psf: bfloat16 [64, 256, 256], P(('rows', 'cols')), may hold values from -0.0234375 to 0.0234375
- step_size: float32 [64], P(('rows', 'cols')), may hold values from 0.2 to 1
- gain: float32 [64], replicated, may hold values from 0.1 to 1.9
- w_in: bfloat16 [64, 256], replicated, may hold values from -0.75 to 0.75
- b_in: float32 [256], replicated, may hold values from -3 to 3
- w_out: bfloat16 [256, 64], replicated, may hold values from -0.375 to 0.375
- kernel: float32 [3, 3, 64], replicated, may hold values from -2 to 2
Outputs:
- updated_model: bfloat16 [64, 512, 512], P(('rows', 'cols'))
All inputs are finite; a program needn't handle non-finite values.
Results may differ from a plain program's by a relative error of at most 0.0095.
Values may be sent and summed in bfloat16 or wider, within the bound.
No kernel may reach another device: no remote copies, remote signals or barrier semaphores. Data moves between devices by JAX's collectives and lax.ppermute only.
A program may use at most 64 MiB of HBM per device.

v0:
```python
import math

import jax
import jax.numpy as jnp
from jax import lax
from jax.sharding import PartitionSpec as P

FFT = 1024


def padded_2(block, sides, width):
    for axis, dim in sides:
        count = lax.axis_size(axis)
        forward = [(i, i + 1) for i in range(count - 1)]
        backward = [(target, source) for source, target in forward]
        low = lax.ppermute(
            lax.slice_in_dim(block, block.shape[dim] - width, None, axis=dim), axis, forward
        )
        high = lax.ppermute(lax.slice_in_dim(block, 0, width, axis=dim), axis, backward)
        block = jnp.concatenate([low, block, high], axis=dim)
    return block


def tables(length, count, offset):
    freq = jnp.arange(length, dtype=jnp.int32)[:, None]
    place = jnp.arange(count, dtype=jnp.int32)[None, :] + offset
    phase = (freq * place % length).astype(jnp.float32) * (2.0 * math.pi / length)
    return (jnp.cos(phase).astype(jnp.bfloat16), jnp.sin(phase).astype(jnp.bfloat16))


def spectrum(plane, cos_t, sin_t):
    real_a = jnp.dot(cos_t, plane, preferred_element_type=jnp.float32).astype(jnp.bfloat16)
    imag_a = (-jnp.dot(sin_t, plane, preferred_element_type=jnp.float32)).astype(jnp.bfloat16)
    real_s = jnp.dot(real_a, cos_t.T, preferred_element_type=jnp.float32) + jnp.dot(
        imag_a, sin_t.T, preferred_element_type=jnp.float32
    )
    imag_s = jnp.dot(imag_a, cos_t.T, preferred_element_type=jnp.float32) - jnp.dot(
        real_a, sin_t.T, preferred_element_type=jnp.float32
    )
    return (real_s, imag_s)


def convolve(plane, spread_fn, image_tabs, psf_tabs, window_tabs, length):
    real_x, imag_x = spectrum(plane, image_tabs[0], image_tabs[1])
    real_q, imag_q = spectrum(spread_fn, psf_tabs[0], psf_tabs[1])
    factor = 1.0 / (length * length)
    real_p = ((real_x * real_q - imag_x * imag_q) * factor).astype(jnp.bfloat16)
    imag_p = ((real_x * imag_q + imag_x * real_q) * factor).astype(jnp.bfloat16)
    cos_w, sin_w = window_tabs
    real_b = (
        jnp.dot(real_p, cos_w, preferred_element_type=jnp.float32)
        - jnp.dot(imag_p, sin_w, preferred_element_type=jnp.float32)
    ).astype(jnp.bfloat16)
    imag_b = (
        jnp.dot(real_p, sin_w, preferred_element_type=jnp.float32)
        + jnp.dot(imag_p, cos_w, preferred_element_type=jnp.float32)
    ).astype(jnp.bfloat16)
    return jnp.dot(cos_w.T, real_b, preferred_element_type=jnp.float32) - jnp.dot(
        sin_w.T, imag_b, preferred_element_type=jnp.float32
    )


def prior_mix(pixels, gain, w_in, b_in, w_out):
    values = pixels.astype(jnp.float32)
    power = jnp.mean(values * values, axis=0, keepdims=True)
    normed = (values / jnp.sqrt(power + 1e-06) * gain[:, None]).astype(jnp.bfloat16)
    inner = jnp.dot(w_in.T, normed, preferred_element_type=jnp.float32) + b_in[:, None]
    hidden = jax.nn.gelu(inner, approximate=True).astype(jnp.bfloat16)
    return jnp.dot(w_out.T, hidden, preferred_element_type=jnp.float32).astype(jnp.bfloat16)


def spread(padded, kernel, height, width):
    total = jnp.zeros((padded.shape[0], height, width), jnp.float32)
    for row_tap in range(3):
        for col_tap in range(3):
            total = total + kernel[row_tap, col_tap][:, None, None] * padded[
                :, row_tap : row_tap + height, col_tap : col_tap + width
            ].astype(jnp.float32)
    return total


def to_tiles(blocks):
    pixels = blocks.shape[3]
    moved = lax.all_to_all(
        blocks.reshape(-1, pixels), ("rows", "cols"), split_axis=0, concat_axis=0, tiled=True
    )
    return moved


def to_planes(blocks):
    shape = blocks.shape
    moved = lax.all_to_all(
        blocks.reshape(-1, shape[3]), ("rows", "cols"), split_axis=0, concat_axis=0, tiled=True
    )
    return moved.reshape(shape)


def local(model, dirty, psf, step_size, gain, w_in, b_in, w_out, kernel):
    ch_dev = model.shape[0]
    img_len = model.shape[1]
    psf_len = psf.shape[1]
    image_tabs = tables(FFT, img_len, 0)
    psf_tabs = tables(FFT, psf_len, 0)
    window_tabs = tables(FFT, img_len, psf_len // 2)

    def one_channel(items):
        plane, dirty_plane, psf_plane, rate = items
        blurred = convolve(plane, psf_plane, image_tabs, psf_tabs, window_tabs, FFT)
        return (
            plane.astype(jnp.float32) + rate * (dirty_plane.astype(jnp.float32) - blurred)
        ).astype(jnp.bfloat16)

    stepped = lax.map(one_channel, (model, dirty, psf, step_size))
    n_rows = lax.axis_size("rows")
    n_cols = lax.axis_size("cols")
    tile_rows = img_len // n_rows
    tile_cols = img_len // n_cols
    blocks = stepped.reshape(ch_dev, n_rows, tile_rows, n_cols, tile_cols).transpose(1, 3, 0, 2, 4)
    blocks = blocks.reshape(n_rows, n_cols, ch_dev, tile_rows * tile_cols)
    tiles = to_tiles(blocks)
    mixed = prior_mix(tiles, gain, w_in, b_in, w_out)
    grid = mixed.reshape(-1, tile_rows, tile_cols)
    padded = padded_2(grid, (("rows", 1), ("cols", 2)), 1)
    result = (
        tiles.reshape(grid.shape).astype(jnp.float32) + spread(padded, kernel, tile_rows, tile_cols)
    ).astype(jnp.bfloat16)
    returned = to_planes(result.reshape(n_rows, n_cols, ch_dev, tile_rows * tile_cols))
    returned = returned.reshape(n_rows, n_cols, ch_dev, tile_rows, tile_cols).transpose(
        2, 0, 3, 1, 4
    )
    return returned.reshape(ch_dev, img_len, img_len)


def solution(mesh):
    return jax.shard_map(
        local,
        mesh=mesh,
        in_specs=(
            P(("rows", "cols"), None, None),
            P(("rows", "cols"), None, None),
            P(("rows", "cols"), None, None),
            P(("rows", "cols")),
            P(),
            P(),
            P(),
            P(),
            P(),
        ),
        out_specs=P(("rows", "cols"), None, None),
        check_vma=False,
    )
```

profile of v0, /device:TPU:0, one launch (start us, length us, event | category | flops | bytes accessed | tf_op | source)
XLA Modules:
  0.0 474.3 jit_solution(3850757310476051663)
XLA Ops:
  0.0 333.6 %while.13 = (s32[]{:T(128)}, bf16[2,512,512]{1,2,0:T(8,128)(2,1)S(1)}, bf16[2,512,512]{2,1,0:T(8,128)(2,1)}, f32[2]{0:T(128)}, bf16[2,512,512]{2,1,0:T(8,128)(2,...) while((s32[]{:T(128)}, ...), condition=%wide.region_1.2_spmd.clone.clone.clone, body=%wide.region_0.1_spmd.clone.clone.clone.sunk | while | flops 13292273664 | bytes 103559376 | solution.py:113
  1.6 10.0 %convolution_convert_fusion.6 = bf16[512,1024]{1,0:T(8,128)(2,1)S(1)} fusion(bf16[1,512,512]{2,1,0:T(8,128)(2,1)S(1)} %get-tuple-element.309), kind=kOutput, calls=%fused_computation.40.clone.1 | convolution fusion | flops 545259520 | bytes 1572864 | tf_op jit(solution)/shard_map/while/body/eval_jaxpr/dot_general | solution.py:32
  11.6 12.6 %fusion.214 = f32[1024,1024]{1,0:T(8,128)S(1)} fusion(bf16[512,1024]{1,0:T(8,128)(2,1)S(1)} %convolution_convert_fusion.6), kind=kOutput, calls=%fused_computation.60.clone.1 | convolution fusion | flops 1081606144 | bytes 5242880 | tf_op jit(solution)/shard_map/while/body/eval_jaxpr/dot_general | solution.py:34
  24.1 10.0 %negate_convert_fusion.2 = bf16[512,1024]{1,0:T(8,128)(2,1)S(1)} fusion(bf16[1,512,512]{2,1,0:T(8,128)(2,1)S(1)} %get-tuple-element.309), kind=kOutput, calls=%fused_computation.34.clone.1 | convolution fusion | flops 545783808 | bytes 1572864 | tf_op jit(solution)/shard_map/while/body/eval_jaxpr/dot_general | solution.py:33
  34.2 13.8 %convolution_add_fusion.6 = f32[1024,1024]{1,0:T(8,128)S(1)} fusion(f32[1024,1024]{1,0:T(8,128)S(1)} %fusion.214, bf16[512,1024]{1,0:T(8,128)(2,1)S(1)} %negate_convert_fusion.2), kind=kOutput, calls=%fused_computation.15.clone.1 | convolution fusion | flops 1082654720 | bytes 9437184 | tf_op jit(solution)/shard_map/while/body/eval_jaxpr/dot_general | solution.py:34
  62.3 5.9 %convolution_add_fusion.5 = f32[1024,1024]{1,0:T(8,128)S(1)} fusion(f32[1024,1024]{1,0:T(8,128)S(1)} %fusion.212, bf16[256,1024]{1,0:T(8,128)(2,1)S(1)} %fusion.213), kind=kOutput, calls=%fused_computation.17.clone.1 | convolution fusion | flops 541851648 | bytes 8912896 | tf_op jit(solution)/shard_map/while/body/eval_jaxpr/dot_general | solution.py:34
  73.3 5.3 %convolution_subtract_fusion.4 = f32[1024,1024]{1,0:T(8,128)S(1)} fusion(f32[1024,1024]{1,0:T(8,128)S(1)} %fusion.215, bf16[256,1024]{1,0:T(8,128)(2,1)S(1)} %convolution_convert_fusion.5), kind=kOutput, calls=%fused_computation.16.clone.1 | convolution fusion | flops 541851648 | bytes 8912896 | tf_op jit(solution)/shard_map/while/body/eval_jaxpr/dot_general | solution.py:37
  78.7 12.6 %fusion.216 = f32[1024,1024]{1,0:T(8,128)S(1)} fusion(bf16[512,1024]{1,0:T(8,128)(2,1)S(1)} %negate_convert_fusion.2), kind=kOutput, calls=%fused_computation.59.clone.1 | convolution fusion | flops 1081606144 | bytes 5242880 | tf_op jit(solution)/shard_map/while/body/eval_jaxpr/dot_general | solution.py:37
  91.3 11.6 %multiply_convert_fusion.6 = (bf16[1024,1024]{1,0:T(8,128)(2,1)S(1)}, bf16[1024,1024]{1,0:T(8,128)(2,1)S(1)}) fusion(f32[1024,1024]{1,0:T(8,128)S(1)} %convolution_add_fusion.5, f32[1024,1024]{1,0:T(8,128)S(1)} %convolution_add_fusion.6, f32[1024,1024]{1,0:T(8,128)S(1)} %convolution_subtract_fusion.4, f32[1024,1024]{1,0:T(8,128)S(1)} %fusion.216, ...), kind=kOutput, calls=%fused_computation.6.clone.1 | convolution fusion | flops 1093140480 | bytes 22020096 | tf_op jit(solution)/shard_map/while/body/eval_jaxpr/dot_general | solution.py:37
  102.9 9.0 %fusion.219 = f32[1024,512]{1,0:T(8,128)S(1)} fusion(bf16[1024,1024]{1,0:T(8,128)(2,1)S(1)} %get-tuple-element.310, s32[512]{0:T(512)S(1)} %get-tuple-element.335), kind=kOutput, calls=%fused_computation.63.clone.1 | convolution fusion | flops 1081606144 | bytes 4196352 | tf_op jit(solution)/shard_map/while/body/eval_jaxpr/dot_general | solution.py:55
  111.9 10.5 %add_convert_fusion.clone.7 = bf16[1024,512]{1,0:T(8,128)(2,1)} fusion(f32[1024,512]{1,0:T(8,128)S(1)} %fusion.219, bf16[1024,1024]{1,0:T(8,128)(2,1)S(1)} %get-tuple-element.311, s32[512]{0:T(512)S(1)} %get-tuple-element.335), kind=kOutput, calls=%fused_computation.32.clone.clone.clone.2.clone.1 | convolution fusion | flops 1082654720 | bytes 5244928 | tf_op jit(solution)/shard_map/while/body/eval_jaxpr/dot_general | solution.py:56
  122.4 8.7 %fusion.217 = f32[1024,512]{1,0:T(8,128)S(1)} fusion(bf16[1024,1024]{1,0:T(8,128)(2,1)S(1)} %get-tuple-element.310, s32[512]{0:T(512)S(1)} %get-tuple-element.335), kind=kOutput, calls=%fused_computation.62.clone.1 | convolution fusion | flops 1081606144 | bytes 4196352 | tf_op jit(solution)/shard_map/while/body/eval_jaxpr/dot_general | solution.py:51
  131.2 10.0 %subtract_convert_fusion.clone.7 = bf16[1024,512]{1,0:T(8,128)(2,1)S(1)} fusion(f32[1024,512]{1,0:T(8,128)S(1)} %fusion.217, bf16[1024,1024]{1,0:T(8,128)(2,1)S(1)} %get-tuple-element.311, s32[512]{0:T(512)S(1)} %get-tuple-element.335), kind=kOutput, calls=%fused_computation.33.clone.clone.clone.2.clone.1 | convolution fusion | flops 1082654720 | bytes 5244928 | tf_op jit(solution)/shard_map/while/body/eval_jaxpr/dot_general | solution.py:52
  141.1 9.6 %fusion.218 = f32[512,512]{1,0:T(8,128)} fusion(s32[512]{0:T(512)S(1)} %get-tuple-element.335, bf16[1024,512]{1,0:T(8,128)(2,1)S(1)} %subtract_convert_fusion.clone.7), kind=kOutput, calls=%fused_computation.61.clone.3 | convolution fusion | flops 544735232 | bytes 2099200 | tf_op jit(solution)/shard_map/while/body/eval_jaxpr/dot_general | solution.py:58
  152.0 10.5 %fusion.220 = bf16[2,512,512]{1,2,0:T(8,128)(2,1)S(1)} fusion(bf16[2,512,512]{1,2,0:T(8,128)(2,1)S(1)} %get-tuple-element.322, s32[]{:T(128)} %get-tuple-element.321, f32[512,512]{1,0:T(8,128)} %fusion.218, s32[512]{0:T(512)S(1)} %get-tuple-element.335, bf16[1,512,512]{1,2,0:T(8,128)(2,1)S(1)} %copy.44, bf16[1,512,512]{1,2,0:T(8,128)(2,1)S(1)} %copy.45, ...), kind=kOutput, calls=%fused_computation.51.clone.3 | convolution fusion | flops 546570240 | bytes 3672072 | tf_op jit(solution)/shard_map/while/body/eval_jaxpr/dot_general | solution.py:58
  164.2 10.0 %convolution_convert_fusion.6 = bf16[512,1024]{1,0:T(8,128)(2,1)S(1)} fusion(bf16[1,512,512]{2,1,0:T(8,128)(2,1)S(1)} %get-tuple-element.309), kind=kOutput, calls=%fused_computation.40.clone.1 | convolution fusion | flops 545259520 | bytes 1572864 | tf_op jit(solution)/shard_map/while/body/eval_jaxpr/dot_general | solution.py:32
  174.2 12.6 %fusion.214 = f32[1024,1024]{1,0:T(8,128)S(1)} fusion(bf16[512,1024]{1,0:T(8,128)(2,1)S(1)} %convolution_convert_fusion.6), kind=kOutput, calls=%fused_computation.60.clone.1 | convolution fusion | flops 1081606144 | bytes 5242880 | tf_op jit(solution)/shard_map/while/body/eval_jaxpr/dot_general | solution.py:34
  186.8 10.0 %negate_convert_fusion.2 = bf16[512,1024]{1,0:T(8,128)(2,1)S(1)} fusion(bf16[1,512,512]{2,1,0:T(8,128)(2,1)S(1)} %get-tuple-element.309), kind=kOutput, calls=%fused_computation.34.clone.1 | convolution fusion | flops 545783808 | bytes 1572864 | tf_op jit(solution)/shard_map/while/body/eval_jaxpr/dot_general | solution.py:33
  196.8 13.8 %convolution_add_fusion.6 = f32[1024,1024]{1,0:T(8,128)S(1)} fusion(f32[1024,1024]{1,0:T(8,128)S(1)} %fusion.214, bf16[512,1024]{1,0:T(8,128)(2,1)S(1)} %negate_convert_fusion.2), kind=kOutput, calls=%fused_computation.15.clone.1 | convolution fusion | flops 1082654720 | bytes 9437184 | tf_op jit(solution)/shard_map/while/body/eval_jaxpr/dot_general | solution.py:34
  225.0 5.5 %convolution_add_fusion.5 = f32[1024,1024]{1,0:T(8,128)S(1)} fusion(f32[1024,1024]{1,0:T(8,128)S(1)} %fusion.212, bf16[256,1024]{1,0:T(8,128)(2,1)S(1)} %fusion.213), kind=kOutput, calls=%fused_computation.17.clone.1 | convolution fusion | flops 541851648 | bytes 8912896 | tf_op jit(solution)/shard_map/while/body/eval_jaxpr/dot_general | solution.py:34
  241.0 12.6 %fusion.216 = f32[1024,1024]{1,0:T(8,128)S(1)} fusion(bf16[512,1024]{1,0:T(8,128)(2,1)S(1)} %negate_convert_fusion.2), kind=kOutput, calls=%fused_computation.59.clone.1 | convolution fusion | flops 1081606144 | bytes 5242880 | tf_op jit(solution)/shard_map/while/body/eval_jaxpr/dot_general | solution.py:37
  253.6 11.6 %multiply_convert_fusion.6 = (bf16[1024,1024]{1,0:T(8,128)(2,1)S(1)}, bf16[1024,1024]{1,0:T(8,128)(2,1)S(1)}) fusion(f32[1024,1024]{1,0:T(8,128)S(1)} %convolution_add_fusion.5, f32[1024,1024]{1,0:T(8,128)S(1)} %convolution_add_fusion.6, f32[1024,1024]{1,0:T(8,128)S(1)} %convolution_subtract_fusion.4, f32[1024,1024]{1,0:T(8,128)S(1)} %fusion.216, ...), kind=kOutput, calls=%fused_computation.6.clone.1 | convolution fusion | flops 1093140480 | bytes 22020096 | tf_op jit(solution)/shard_map/while/body/eval_jaxpr/dot_general | solution.py:37
  265.2 9.1 %fusion.219 = f32[1024,512]{1,0:T(8,128)S(1)} fusion(bf16[1024,1024]{1,0:T(8,128)(2,1)S(1)} %get-tuple-element.310, s32[512]{0:T(512)S(1)} %get-tuple-element.335), kind=kOutput, calls=%fused_computation.63.clone.1 | convolution fusion | flops 1081606144 | bytes 4196352 | tf_op jit(solution)/shard_map/while/body/eval_jaxpr/dot_general | solution.py:55
  274.2 10.5 %add_convert_fusion.clone.7 = bf16[1024,512]{1,0:T(8,128)(2,1)} fusion(f32[1024,512]{1,0:T(8,128)S(1)} %fusion.219, bf16[1024,1024]{1,0:T(8,128)(2,1)S(1)} %get-tuple-element.311, s32[512]{0:T(512)S(1)} %get-tuple-element.335), kind=kOutput, calls=%fused_computation.32.clone.clone.clone.2.clone.1 | convolution fusion | flops 1082654720 | bytes 5244928 | tf_op jit(solution)/shard_map/while/body/eval_jaxpr/dot_general | solution.py:56
  284.8 8.7 %fusion.217 = f32[1024,512]{1,0:T(8,128)S(1)} fusion(bf16[1024,1024]{1,0:T(8,128)(2,1)S(1)} %get-tuple-element.310, s32[512]{0:T(512)S(1)} %get-tuple-element.335), kind=kOutput, calls=%fused_computation.62.clone.1 | convolution fusion | flops 1081606144 | bytes 4196352 | tf_op jit(solution)/shard_map/while/body/eval_jaxpr/dot_general | solution.py:51
  293.5 10.2 %subtract_convert_fusion.clone.7 = bf16[1024,512]{1,0:T(8,128)(2,1)S(1)} fusion(f32[1024,512]{1,0:T(8,128)S(1)} %fusion.217, bf16[1024,1024]{1,0:T(8,128)(2,1)S(1)} %get-tuple-element.311, s32[512]{0:T(512)S(1)} %get-tuple-element.335), kind=kOutput, calls=%fused_computation.33.clone.clone.clone.2.clone.1 | convolution fusion | flops 1082654720 | bytes 5244928 | tf_op jit(solution)/shard_map/while/body/eval_jaxpr/dot_general | solution.py:52
  303.7 9.6 %fusion.218 = f32[512,512]{1,0:T(8,128)} fusion(s32[512]{0:T(512)S(1)} %get-tuple-element.335, bf16[1024,512]{1,0:T(8,128)(2,1)S(1)} %subtract_convert_fusion.clone.7), kind=kOutput, calls=%fused_computation.61.clone.3 | convolution fusion | flops 544735232 | bytes 2099200 | tf_op jit(solution)/shard_map/while/body/eval_jaxpr/dot_general | solution.py:58
  314.5 10.5 %fusion.220 = bf16[2,512,512]{1,2,0:T(8,128)(2,1)S(1)} fusion(bf16[2,512,512]{1,2,0:T(8,128)(2,1)S(1)} %get-tuple-element.322, s32[]{:T(128)} %get-tuple-element.321, f32[512,512]{1,0:T(8,128)} %fusion.218, s32[512]{0:T(512)S(1)} %get-tuple-element.335, bf16[1,512,512]{1,2,0:T(8,128)(2,1)S(1)} %copy.44, bf16[1,512,512]{1,2,0:T(8,128)(2,1)S(1)} %copy.45, ...), kind=kOutput, calls=%fused_computation.51.clone.3 | convolution fusion | flops 546570240 | bytes 3672072 | tf_op jit(solution)/shard_map/while/body/eval_jaxpr/dot_general | solution.py:58
  340.7 34.7 %all_to_all.18 = bf16[32,2,8192]{2,1,0:T(2,128)(2,1)S(1)} all-to-all(bf16[32,2,8192]{2,1,0:T(2,128)(2,1)S(1)} %copy.30), channel_id=1, replica_groups=mesh['rows'=4,'cols'=8] {'rows','cols'}, dimensions={0} | all-to-all | bytes 2097152 | tf_op jit(solution)/shard_map/all_to_all | solution.py:84
  411.5 5.8 %maximum_maximum_fusion = (bf16[64,130,65]{2,1,0:T(8,128)(2,1)S(1)}, bf16[64,130,65]{2,1,0:T(8,128)(2,1)S(1)}) fusion(bf16[64,1,64]{2,1,0:T(2,128)(2,1)S(1)} %collective-permute-done.1, bf16[64,128,64]{2,1,0:T(8,128)(2,1)S(1)} %reshape.49, bf16[64,1,64]{2,1,0:T(2,128)(2,1)S(1)} %collective-permute-done, bf16[64,130,1]{2,1,0:T(8,128)(2,1)} %copy.32, ...), kind=kLoop, calls=%fused_computation.154 | loop fusion | flops 8652800 | bytes 3261440 | tf_op jit(solution)/shard_map/concatenate | solution.py:20
  417.3 9.2 %add_convert_fusion.1 = bf16[64,128,64]{2,1,0:T(8,128)(2,1)} fusion(f32[64,128,64]{2,1,0:T(8,128)S(1)} %copy-done.1, bf16[64,128,64]{2,1,0:T(8,128)(2,1)S(1)} %reshape.49, bf16[64,130,65]{2,1,0:T(8,128)(2,1)S(1)} %get-tuple-element.250, bf16[64,1,64]{2,1,0:T(2,128)(2,1)S(1)} %collective-permute-done.1, bf16[64,130,65]{2,1,0:T(8,128)(2,1)S(1)} %get-tuple-element.249, ...), kind=kLoop, calls=%fused_computation.152 | loop fusion | flops 17825792 | bytes 10504448 | tf_op jit(solution)/shard_map/convert_element_type | solution.py:126
  430.3 34.0 %all_to_all.19 = bf16[32,2,8192]{2,1,0:T(2,128)(2,1)S(1)} all-to-all(bf16[32,2,8192]{2,1,0:T(2,128)(2,1)S(1)} %all_to_all.14), channel_id=1, replica_groups=mesh['rows'=4,'cols'=8] {'rows','cols'}, dimensions={0} | all-to-all | bytes 2097152 | tf_op jit(solution)/shard_map/all_to_all | solution.py:92
  (72 shorter events, 105.9 us)
Async XLA Ops:
  0.0 376.9 %copy-start = (bf16[256,64]{0,1:T(8,128)(2,1)S(1)}, bf16[256,64]{0,1:T(8,128)(2,1)}, u32[]{:S(2)}) copy-start(bf16[256,64]{0,1:T(8,128)(2,1)} %param.18) | copy-start | bytes 98308
  34.2 13.8 %copy-start.4 = (bf16[2,256,256]{2,1,0:T(8,128)(2,1)S(1)}, bf16[2,256,256]{2,1,0:T(8,128)(2,1)}, u32[]{:S(2)}) copy-start(bf16[2,256,256]{2,1,0:T(8,128)(2,1)} %get-tuple-element.334) | copy-start | bytes 786436 | tf_op jit(solution)/shard_map/while
  150.7 0.7 copy-start.7
  196.8 13.8 %copy-start.4 = (bf16[2,256,256]{2,1,0:T(8,128)(2,1)S(1)}, bf16[2,256,256]{2,1,0:T(8,128)(2,1)}, u32[]{:S(2)}) copy-start(bf16[2,256,256]{2,1,0:T(8,128)(2,1)} %get-tuple-element.334) | copy-start | bytes 786436 | tf_op jit(solution)/shard_map/while
  313.2 0.7 copy-start.7
  333.6 1.0 copy-start.2
  375.4 1.5 copy-start.5
  375.4 1.5 copy-start.6
  375.4 1.5 copy-start.8
  385.2 3.1 collective-permute-start
  386.7 6.2 %collective-permute-start.1 = (bf16[64,1,64]{2,1,0:T(2,128)(2,1)S(1)}, bf16[64,1,64]{2,1,0:T(2,128)(2,1)S(1)}, u32[]{:S(2)}, u32[]{:S(2)}) collective-permute-start(bf16[64,1,64]{2,1,0:T(2,128)(2,1)S(1)} %get-tuple-element.252), channel_id=1, source_target_pairs={{8,0},{16,8},{24,16},{9,1},{17,9},{25,17},{10,2},{18,10},{26,18},{... | collective-permute-start | bytes 24584 | tf_op jit(solution)/shard_map/ppermute | solution.py:19
  396.6 8.0 %copy-start.3 = (f32[3,3,64]{2,1,0:T(4,128)S(1)}, f32[3,3,64]{2,1,0:T(4,128)}, u32[]{:S(2)}) copy-start(f32[3,3,64]{2,1,0:T(4,128)} %param.19) | copy-start | bytes 6916
  399.2 8.1 %collective-permute-start.2 = (bf16[64,130,1]{1,0,2:T(8,128)(2,1)S(1)}, bf16[64,130,1]{1,0,2:T(8,128)(2,1)S(1)}, u32[]{:S(2)}, u32[]{:S(2)}) collective-permute-start(bf16[64,130,1]{1,0,2:T(8,128)(2,1)S(1)} %copy.31), channel_id=1, source_target_pairs={{0,1},{1,2},{2,3},{3,4},{4,5},{5,6},{6,7},{8,9},{9,10},{10,11},{11... | collective-permute-start | bytes 49928 | tf_op jit(solution)/shard_map/ppermute | solution.py:16
  403.2 6.2 %collective-permute-start.3 = (bf16[64,130,1]{1,0,2:T(8,128)(2,1)S(1)}, bf16[64,130,1]{1,0,2:T(8,128)(2,1)S(1)}, u32[]{:S(2)}, u32[]{:S(2)}) collective-permute-start(bf16[64,130,1]{1,0,2:T(8,128)(2,1)S(1)} %copy.33), channel_id=1, source_target_pairs={{1,0},{2,1},{3,2},{4,3},{5,4},{6,5},{7,6},{9,8},{10,9},{11,10},{12... | collective-permute-start | bytes 49928 | tf_op jit(solution)/shard_map/ppermute | solution.py:19
  411.5 5.8 %copy-start.1 = (f32[64,128,64]{2,1,0:T(8,128)S(1)}, f32[64,128,64]{2,1,0:T(8,128)}, u32[]{:S(2)}) copy-start(f32[64,128,64]{2,1,0:T(8,128)} %reshape.52) | copy-start | bytes 6291460
where the time goes:
time: 476 us; the launch traced here: 474 us
  matrix products  324 us (68%)
  blocking collectives  68.7 us (14%)
  local copies, waits for them, and re-layouts  44.4 us (9%)
  other arithmetic  17 us (4%)
  loops' own time  9.53 us (2%)
  starting transfers between devices  5.47 us (1%)
  waiting for transfers between devices  4.87 us (1%)
    dot_general x4, matrix products, spectrum(): jnp.dot(imag_a, sin_t.T, preferred_element_type=jnp.float32)  39 us
    dot_general x4, matrix products, spectrum(): jnp.dot(imag_a, cos_t.T, preferred_element_type=jnp.float32)  35.4 us
    dot_general x4, matrix products, spectrum(): jnp.dot(real_a, cos_t.T, preferred_element_type=jnp.float32)  35.4 us
    all_to_all x1, blocking collectives, to_tiles(): lax.all_to_all(blocks.reshape(-1, pixels), ('rows', 'cols'), split_axis=0...  34.7 us
    all_to_all x1, blocking collectives, to_planes(): lax.all_to_all(blocks.reshape(-1, shape[3]), ('rows', 'cols'), split_axis...  34 us
    dot_general x4, matrix products, spectrum(): jnp.dot(real_a, sin_t.T, preferred_element_type=jnp.float32)  33.9 us
    dot_general x4, matrix products, spectrum(): jnp.dot(sin_t, plane, preferred_element_type=jnp.float32)  29.2 us
    dot_general x4, matrix products, spectrum(): jnp.dot(cos_t, plane, preferred_element_type=jnp.float32)  29.1 us
  transfers between devices with their start and end apart: 4, of which 2 were waited for; matrix products, arithmetic and copies ran while one was open for 2% of the time, Pallas kernels for 0%

commit v1 on v0

v1 whole, which is shorter than its diff:
```python
import math

import jax
import jax.numpy as jnp
import ml_dtypes
import numpy as np
from jax import lax
from jax.experimental import pallas as pl
from jax.experimental.pallas import tpu as pltpu
from jax.sharding import PartitionSpec as P

BAND = 16
VMEM_BYTES = 56 * 1024 * 1024


def trig(places, half, length):
    phase = (2 * np.arange(half)[:, None] + 1) * places[None, :] % (2 * length)
    angle = phase * (math.pi / length)
    return np.cos(angle), np.sin(angle)


def tables(img, psf):
    length = img + psf // 2
    half = length // 2
    pad = -half % 128
    cos_t, sin_t = trig(np.arange(img), half, length)
    cos_w, sin_w = trig(np.arange(img) + psf // 2, half, length)

    def columns(table, low, high):
        return np.pad(table.T, ((0, 0), (low, high)))

    right = [
        np.concatenate([columns(cos_t, *side), columns(sin_t, *side)], axis=1)
        for side in ((0, pad), (pad, 0))
    ]
    left = np.concatenate([cos_t, sin_t], axis=0)
    back_left = np.concatenate([cos_w, sin_w], axis=0).T
    back_right = [
        np.concatenate([columns(cos_w, *side), columns(sin_w, *side)], axis=1).T
        for side in ((0, pad), (pad, 0))
    ]
    return [
        jnp.asarray(table.astype(ml_dtypes.bfloat16))
        for table in (*right, left, back_left, *back_right)
    ]


def dot(a, b):
    return jnp.dot(a, b, preferred_element_type=jnp.float32)


def conv_kernel(
    rate, model, dirty, psf, right_a, right_b, left, back_left, back_a, back_b, out,
    cols_x, cols_q, spec_x, spec_q, prod, rows_y,
):
    img = model.shape[1]
    half = left.shape[0] // 2
    wide = right_a.shape[1] // 2
    both = 2 * half
    shared = 2 * wide - both
    own = wide - shared
    bands, parts, _, band, part = out.shape

    def columns(source, count, target):
        step = 128

        @pl.loop(0, count // step)
        def _(i):
            rows = pl.ds(pl.multiple_of(i * step, step), step)
            depth = source.shape[2]
            first = dot(source[0, rows, :], right_a[:depth, :])
            second = dot(source[1, rows, :], right_b[:depth, :])
            for k in range(2):
                a = first[:, k * wide : (k + 1) * wide]
                b = second[:, k * wide : (k + 1) * wide]
                at = k * both
                target[rows, at : at + own] = a[:, :own].astype(jnp.bfloat16)
                target[rows, at + own : at + wide] = (a[:, own:] + b[:, :shared]).astype(jnp.bfloat16)
                target[rows, at + wide : at + both] = b[:, shared:].astype(jnp.bfloat16)

    columns(psf, psf.shape[1], cols_q)
    columns(model, img, cols_x)

    for k in range(2):
        rows = pl.ds(k * half, half)
        spec_q[rows, :] = dot(left[rows, : psf.shape[1]], cols_q[...])
        spec_x[rows, :] = dot(left[rows, :], cols_x[...])

    @pl.loop(0, half // 16)
    def _(i):
        c = pl.ds(pl.multiple_of(i * 16, 16), 16)
        s = pl.ds(pl.multiple_of(half + i * 16, 16), 16)
        for j in range(0, both, 128):
            lc, ls = slice(j, j + 128), slice(both + j, both + j + 128)
            xcc, xcs, xsc, xss = spec_x[c, lc], spec_x[c, ls], spec_x[s, lc], spec_x[s, ls]
            qcc, qcs, qsc, qss = spec_q[c, lc], spec_q[c, ls], spec_q[s, lc], spec_q[s, ls]
            prod[c, lc] = ((xcc * qcc + xss * qss) - (xsc * qsc + xcs * qcs)).astype(jnp.bfloat16)
            prod[s, ls] = ((xcc * qss + xss * qcc) + (xsc * qcs + xcs * qsc)).astype(jnp.bfloat16)
            prod[s, lc] = ((xcc * qsc - xss * qcs) + (xsc * qcc - xcs * qss)).astype(jnp.bfloat16)
            prod[c, ls] = ((xcc * qcs - xss * qsc) + (xcs * qcc - xsc * qss)).astype(jnp.bfloat16)

    for k in range(2):
        rows = pl.ds(k * img // 2, img // 2)
        rows_y[rows, :] = dot(back_left[rows, :], prod[...]).astype(jnp.bfloat16)

    factor = 4.0 / (both * both)
    step = 128

    @pl.loop(0, img // step)
    def _(i):
        rows = pl.ds(pl.multiple_of(i * step, step), step)
        for ch, table in ((0, back_a), (1, back_b)):
            at = ch * (both - wide)
            inner = jnp.concatenate(
                [rows_y[rows, at : at + wide], rows_y[rows, both + at : both + at + wide]], axis=1
            )
            blurred = dot(inner, table[...]) * factor
            plane = model[ch, rows, :].astype(jnp.float32)
            stepped = plane + rate[ch] * (dirty[ch, rows, :].astype(jnp.float32) - blurred)
            stepped = stepped.astype(jnp.bfloat16)
            for p in range(parts):
                piece = stepped[:, p * part : (p + 1) * part].reshape(step // band, band, part)
                out[pl.ds(i * (step // band), step // band), p, ch] = piece


def shuffle_table():
    index = np.arange(BAND * BAND)
    source = (index % BAND) * BAND + index // BAND
    table = np.zeros((BAND * BAND, BAND * BAND), np.float32)
    table[index, source] = 1.0
    return jnp.asarray(table.astype(ml_dtypes.bfloat16))


def mix_kernel(gain, b_in, w_in_t, w_out_t, swap, tiles, out, normed, mixed):
    channels, band, part = tiles.shape
    groups = channels // band
    power = jnp.zeros((band, part), jnp.float32)
    for c in range(channels):
        v = tiles[c].astype(jnp.float32)
        power = power + v * v
    inverse = lax.rsqrt(power * (1.0 / channels) + 1e-06)
    for g in range(groups):
        rows = []
        for c in range(g * band, (g + 1) * band):
            rows.append((tiles[c].astype(jnp.float32) * inverse * gain[c]).astype(jnp.bfloat16))
        swapped = dot(swap[...], jnp.concatenate(rows, axis=0)).astype(jnp.bfloat16)
        normed[:, g * band : (g + 1) * band, :] = swapped.reshape(band, band, part)

    a = math.sqrt(2.0 / math.pi)

    @pl.loop(0, band)
    def _(r):
        inner = dot(w_in_t[...], normed[r]) + b_in[...]
        scaled = inner * (a + (a * 0.044715) * (inner * inner))
        hidden = (0.5 * inner * (1.0 + jnp.tanh(scaled))).astype(jnp.bfloat16)
        mixed[r] = dot(w_out_t[...], hidden).astype(jnp.bfloat16)

    for g in range(groups):
        block = mixed[:, g * band : (g + 1) * band, :].reshape(band * band, part)
        swapped = dot(swap[...], block).astype(jnp.bfloat16)
        out[g * band : (g + 1) * band] = swapped.reshape(band, band, part)


def spread_kernel(first, taps, stepped, mixed, out, above, below):
    channels = taps.shape[0] // 9
    bands, parts, ch_dev, band, part = stepped.shape
    img = bands * band
    lane = lax.broadcasted_iota(jnp.int32, (band, img), 1)
    zero = jnp.zeros((8, img), jnp.float32)

    def plane(source, b, ch):
        if parts == 1:
            return source[b, 0, ch].astype(jnp.float32)
        pieces = [source[b, p, ch] for p in range(parts)]
        return jnp.concatenate(pieces, axis=1).astype(jnp.float32)

    for ch in range(ch_dev):
        k = [[taps[(3 * i + j) * channels + first[0] + ch] for j in range(3)] for i in range(3)]
        above[0:8, :] = zero
        below[img : img + 8, :] = zero

        @pl.loop(0, bands)
        def _(b):
            x = plane(mixed, b, ch)
            low = jnp.where(lane == 0, 0.0, pltpu.roll(x, 1, 1))
            high = jnp.where(lane == img - 1, 0.0, pltpu.roll(x, img - 1, 1))
            at = pl.multiple_of(b * band, band)
            above[pl.ds(at + 8, band), :] = k[0][0] * low + k[0][1] * x + k[0][2] * high
            below[pl.ds(at, band), :] = k[2][0] * low + k[2][1] * x + k[2][2] * high

        @pl.loop(0, bands)
        def _(b):
            x = plane(mixed, b, ch)
            low = jnp.where(lane == 0, 0.0, pltpu.roll(x, 1, 1))
            high = jnp.where(lane == img - 1, 0.0, pltpu.roll(x, img - 1, 1))
            at = pl.multiple_of(b * band, band)
            top = above[pl.ds(at, band + 8), :][7 : 7 + band]
            bottom = below[pl.ds(at, band + 8), :][1 : 1 + band]
            middle = k[1][0] * low + k[1][1] * x + k[1][2] * high
            total = plane(stepped, b, ch) + (top + middle + bottom)
            out[ch, pl.ds(at, band), :] = total.astype(jnp.bfloat16)


VMEM = pl.BlockSpec(memory_space=pltpu.VMEM)
SMEM = pl.BlockSpec(memory_space=pltpu.SMEM)
PARAMS = pltpu.CompilerParams(vmem_limit_bytes=VMEM_BYTES)


def exchange(blocks):
    return lax.all_to_all(blocks, ("rows", "cols"), split_axis=0, concat_axis=0, tiled=True)


def local(model, dirty, psf, step_size, gain, w_in, b_in, w_out, kernel):
    ch_dev, img, _ = model.shape
    psf_len = psf.shape[1]
    assert ch_dev == 2
    n_dev = lax.axis_size("rows") * lax.axis_size("cols")
    channels = gain.shape[0]
    hidden = b_in.shape[0]
    bands = img // BAND
    part = img * img // (n_dev * BAND)
    parts = img // part
    half = (img + psf_len // 2) // 2
    bf16, f32 = jnp.bfloat16, jnp.float32

    stepped = pl.pallas_call(
        conv_kernel,
        out_shape=jax.ShapeDtypeStruct((bands, parts, ch_dev, BAND, part), bf16),
        in_specs=[SMEM] + [VMEM] * 9,
        out_specs=VMEM,
        scratch_shapes=[
            pltpu.VMEM((img, 4 * half), bf16),
            pltpu.VMEM((psf_len, 4 * half), bf16),
            pltpu.VMEM((2 * half, 4 * half), f32),
            pltpu.VMEM((2 * half, 4 * half), f32),
            pltpu.VMEM((2 * half, 4 * half), bf16),
            pltpu.VMEM((img, 4 * half), bf16),
        ],
        compiler_params=PARAMS,
        name="conv",
    )(step_size, model, dirty, psf, *tables(img, psf_len))

    tiles = exchange(stepped.reshape(n_dev, ch_dev, BAND, part)).reshape(channels, BAND, part)

    mixed = pl.pallas_call(
        mix_kernel,
        out_shape=jax.ShapeDtypeStruct((channels, BAND, part), bf16),
        in_specs=[SMEM] + [VMEM] * 5,
        out_specs=VMEM,
        scratch_shapes=[
            pltpu.VMEM((BAND, channels, part), bf16),
            pltpu.VMEM((BAND, channels, part), bf16),
        ],
        compiler_params=PARAMS,
        name="mix",
    )(gain, b_in[:, None], w_in.T, w_out.T, shuffle_table(), tiles)

    returned = exchange(mixed.reshape(n_dev, ch_dev, BAND, part))
    position = lax.axis_index(("rows", "cols")).astype(jnp.int32) * ch_dev

    return pl.pallas_call(
        spread_kernel,
        out_shape=jax.ShapeDtypeStruct((ch_dev, img, img), bf16),
        in_specs=[SMEM, SMEM, VMEM, VMEM],
        out_specs=VMEM,
        scratch_shapes=[
            pltpu.VMEM((img + 8, img), f32),
            pltpu.VMEM((img + 8, img), f32),
        ],
        compiler_params=PARAMS,
        name="spread",
    )(position[None], kernel.reshape(-1), stepped, returned.reshape(stepped.shape))


def solution(mesh):
    return jax.shard_map(
        local,
        mesh=mesh,
        in_specs=(
            P(("rows", "cols"), None, None),
            P(("rows", "cols"), None, None),
            P(("rows", "cols"), None, None),
            P(("rows", "cols")),
            P(),
            P(),
            P(),
            P(),
            P(),
        ),
        out_specs=P(("rows", "cols"), None, None),
        check_vma=False,
    )
```

time: 476 us -> 103 us (0.22)
  matrix products: 324 us -> 0 us
  blocking collectives: 68.7 us -> 0 us
  waiting for transfers between devices: 4.87 us -> 51.6 us
  local copies, waits for them, and re-layouts: 44.4 us -> 5.54 us
  Pallas kernels: 0 us -> 35.9 us
  other arithmetic: 17 us -> 0 us
  loops' own time: 9.53 us -> 0 us
    dot_general x37 -> x0, matrix products: 324 us -> none  [the longest x4 39 us: spectrum(): jnp.dot(imag_a, sin_t.T, preferred_element_type=jnp.float32)]
    all_to_all x2 -> x0, blocking collectives: 68.7 us -> none  [the longest x1 34.7 us: to_tiles(): lax.all_to_all(blocks.reshape(-1, pixels), ('rows', 'cols'), split_axis=0...]
    all_to_all x0 -> x2, waiting for transfers between devices: none -> 51.6 us  [exchange(): lax.all_to_all(blocks, ('rows', 'cols'), split_axis=0, concat_axis=0, til...]
    pallas_call x0 -> x3, Pallas kernels: none -> 35.9 us  [the longest x1 14.1 us: local(): pl.pallas_call(spread_kernel, out_shape=jax.ShapeDtypeStruct((ch_dev, img...]
    reshape x5 -> x1, local copies, waits for them, and re-layouts: 13.3 us -> 0.67 us  [local(): kernel.reshape(-1)]
    all_to_all x0 -> x2, starting transfers between devices: none -> 9.93 us  [exchange(): lax.all_to_all(blocks, ('rows', 'cols'), split_axis=0, concat_axis=0, til...]
    another operation x1 -> x0, loops' own time: 9.53 us -> none  [local(): stepped = lax.map(one_channel, (model, dirty, psf, step_size))]
    convert_element_type x1 -> x0, other arithmetic: 9.15 us -> none  [local(): result = (tiles.reshape(grid.shape).astype(jnp.float32) + spread(padded,...]
  transfers between devices with their start and end apart: 4 -> 2, of which waited for: 2 -> 2; matrix products, arithmetic and copies ran while one was open for 2% -> 2% of each run, Pallas kernels for 0% -> 0%
where the time goes in v1:
time: 103 us
  waiting for transfers between devices  51.6 us (50%)
  Pallas kernels  35.9 us (35%)
  starting transfers between devices  9.93 us (10%)
  local copies, waits for them, and re-layouts  5.54 us (5%)
    all_to_all x2, waiting for transfers between devices, exchange(): lax.all_to_all(blocks, ('rows', 'cols'), split_axis=0, concat_axis=0, til...  51.6 us
    pallas_call x1, Pallas kernels, local(): pl.pallas_call(spread_kernel, out_shape=jax.ShapeDtypeStruct((ch_dev, img...  14.1 us
    pallas_call x1, Pallas kernels, local(): pl.pallas_call(conv_kernel, out_shape=jax.ShapeDtypeStruct((bands, parts,...  11.2 us
    pallas_call x1, Pallas kernels, local(): pl.pallas_call(mix_kernel, out_shape=jax.ShapeDtypeStruct((channels, BAND...  10.6 us
    all_to_all x2, starting transfers between devices, exchange(): lax.all_to_all(blocks, ('rows', 'cols'), split_axis=0, concat_axis=0, til...  9.93 us
    unnamed x11, local copies, waits for them, and re-layouts  4.07 us
  transfers between devices with their start and end apart: 2, of which 2 were waited for; matrix products, arithmetic and copies ran while one was open for 2% of the time, Pallas kernels for 0%

profile of v1, /device:TPU:0, one launch (start us, length us, event | category | flops | bytes accessed | tf_op | source)
XLA Modules:
  0.0 103.0 jit_solution(11956364597238323686)
XLA Ops:
  0.0 11.2 %conv.1.stepped = bf16[32,1,2,16,512]{4,3,2,1,0:T(8,128)(2,1)} custom-call(f32[2]{0:T(128)} %rate.1, bf16[2,512,512]{2,1,0:T(8,128)(2,1)} %model.1, bf16[2,512,512]{2,1,0:T(8,128)(2,1)} %dirty.1, bf16[2,256,256]{2,1,0:T(8,128)(2,1)} %psf.1, bf16[512,768]{1,0:T(8,128)(2,1)} %constant.26.clone.right_a, bf16[512,768]{1,0:T(8,128)(2,1)} %constant.27.clone.right_b, ...), custom_call_target="tpu_custom_call" | custom-call | tf_op jit(solution)/shard_map/conv/pallas_call | solution.py:226
  11.2 7.3 %all-to-all-start = ((bf16[32,2,16,512]{3,2,1,0:T(8,128)(2,1)}), bf16[32,2,16,512]{3,2,1,0:T(8,128)(2,1)S(1)}, u32[]{:S(2)}, u32[]{:S(2)}) async-start(bf16[32,2,16,512]{3,2,1,0:T(8,128)(2,1)} %bitcast.8), calls=%async_computation | async-start | bytes 2097152 | tf_op jit(solution)/shard_map/all_to_all | solution.py:210
  18.5 0.0 copy-start.4
  18.5 0.7 copy-done.4
  19.2 0.0 copy-start.2
  19.2 0.8 copy.19.b_in
  20.0 0.0 copy-done.2
  20.0 0.7 copy.18
  20.7 25.4 %all-to-all-done = bf16[32,2,16,512]{3,2,1,0:T(8,128)(2,1)S(1)} async-done(((bf16[32,2,16,512]{3,2,1,0:T(8,128)(2,1)}), bf16[32,2,16,512]{3,2,1,0:T(8,128)(2,1)S(1)}, u32[]{:S(2)}, u32[]{:S(2)}) %all-to-all-start) | async-done | bytes 1048608 | tf_op jit(solution)/shard_map/all_to_all | solution.py:210
  46.1 0.0 copy-start
  46.1 1.0 copy-done
  47.1 10.6 %mix.1 = bf16[64,16,512]{2,1,0:T(8,128)(2,1)} custom-call(f32[64]{0:T(128)} %gain.1, f32[256,1]{1,0:T(8,128)} %copy.19.b_in, bf16[256,64]{1,0:T(8,128)(2,1)} %bitcast.12, bf16[64,256]{1,0:T(8,128)(2,1)} %bitcast.13, bf16[256,256]{1,0:T(8,128)(2,1)} %constant.32.clone.swap, bf16[64,16,512]{2,1,0:T(8,128)(2,1)} %bitcast.10), custom_call_target="tpu_custom_call" | custom-call | tf_op jit(solution)/shard_map/mix/pallas_call | solution.py:245
  57.7 2.6 %all-to-all-start.1 = ((bf16[32,2,16,512]{3,2,1,0:T(8,128)(2,1)}), bf16[32,2,16,512]{3,2,1,0:T(8,128)(2,1)S(1)}, u32[]{:S(2)}, u32[]{:S(2)}) async-start(bf16[32,2,16,512]{3,2,1,0:T(8,128)(2,1)} %bitcast.9), calls=%async_computation.1 | async-start | bytes 2097152 | tf_op jit(solution)/shard_map/all_to_all | solution.py:210
  60.3 0.0 copy-start.3
  60.3 0.7 copy-done.3
  61.0 0.7 reshape.15.taps
  61.7 26.2 %all-to-all-done.1 = bf16[32,2,16,512]{3,2,1,0:T(8,128)(2,1)S(1)} async-done(((bf16[32,2,16,512]{3,2,1,0:T(8,128)(2,1)}), bf16[32,2,16,512]{3,2,1,0:T(8,128)(2,1)S(1)}, u32[]{:S(2)}, u32[]{:S(2)}) %all-to-all-start.1) | async-done | bytes 1048608 | tf_op jit(solution)/shard_map/all_to_all | solution.py:210
  87.9 0.0 copy-start.1
  87.9 1.0 copy-done.1
  88.9 14.1 %spread.1 = bf16[2,512,512]{2,1,0:T(8,128)(2,1)} custom-call(s32[1]{0:T(128)} %bitcast.first, f32[576]{0:T(1024)} %reshape.15.taps, bf16[32,1,2,16,512]{4,3,2,1,0:T(8,128)(2,1)} %conv.1.stepped, bf16[32,1,2,16,512]{4,3,2,1,0:T(8,128)(2,1)} %bitcast.11), custom_call_target="tpu_custom_call" | custom-call | tf_op jit(solution)/shard_map/spread/pallas_call | solution.py:261
Async XLA Ops:
  11.2 34.9 %all-to-all-start = ((bf16[32,2,16,512]{3,2,1,0:T(8,128)(2,1)}), bf16[32,2,16,512]{3,2,1,0:T(8,128)(2,1)S(1)}, u32[]{:S(2)}, u32[]{:S(2)}) async-start(bf16[32,2,16,512]{3,2,1,0:T(8,128)(2,1)} %bitcast.8), calls=%async_computation | async-start | bytes 2097152 | tf_op jit(solution)/shard_map/all_to_all | solution.py:210
  18.5 0.7 copy-start.4
  19.2 0.8 copy-start.2
  46.1 1.0 copy-start
  57.7 30.2 %all-to-all-start.1 = ((bf16[32,2,16,512]{3,2,1,0:T(8,128)(2,1)}), bf16[32,2,16,512]{3,2,1,0:T(8,128)(2,1)S(1)}, u32[]{:S(2)}, u32[]{:S(2)}) async-start(bf16[32,2,16,512]{3,2,1,0:T(8,128)(2,1)} %bitcast.9), calls=%async_computation.1 | async-start | bytes 2097152 | tf_op jit(solution)/shard_map/all_to_all | solution.py:210
  60.3 0.7 copy-start.3
  87.9 1.0 copy-start.1

commit v2 on v0

v2 whole, which is shorter than its diff:
```python
import math

import jax
import jax.numpy as jnp
import ml_dtypes
import numpy as np
from jax import lax
from jax.experimental import pallas as pl
from jax.experimental.pallas import tpu as pltpu
from jax.sharding import PartitionSpec as P

BAND = 16
CHUNKS = 2
MIB = 1024 * 1024
BF16, F32 = jnp.bfloat16, jnp.float32


def tables(img, psf):
    length = img + psf // 2
    half = length // 2
    pad = -half % 128
    phase = (2 * np.arange(half)[:, None] + 1) * np.arange(length)[None, :] % (2 * length)
    angle = phase * (math.pi / length)
    table = np.concatenate([np.pad(f(angle), ((0, pad), (0, 0))) for f in (np.cos, np.sin)])
    table = table.astype(ml_dtypes.bfloat16)
    return jnp.asarray(table), jnp.asarray(np.ascontiguousarray(table.T))


def shuffle_table():
    index = np.arange(BAND * BAND)
    source = (index % BAND) * BAND + index // BAND
    table = np.zeros((BAND * BAND, BAND * BAND), np.float32)
    table[index, source] = 1.0
    return jnp.asarray(table.astype(ml_dtypes.bfloat16))


def dot(a, b):
    return jnp.dot(a, b, preferred_element_type=F32)


def conv_kernel(
    ch, rate, model_h, dirty_h, psf_h, table_h, turned_h, *refs
):
    outs = refs[:-12]
    (model, dirty, psf, table, turned, cols_x, cols_q, spec_x, spec_q, prod, rows_y, sems) = refs[-12:]
    img = model.shape[0]
    taps = psf.shape[0]
    shift = taps // 2
    length = table.shape[1]
    half = length // 2
    wide = table.shape[0] // 2

    copies = [
        pltpu.make_async_copy(source, target, sems.at[i])
        for i, (source, target) in enumerate(
            (
                (psf_h.at[ch], psf),
                (turned_h.at[pl.ds(0, taps)], turned.at[pl.ds(0, taps)]),
                (model_h.at[ch, pl.ds(0, img // 2)], model.at[pl.ds(0, img // 2)]),
                (turned_h.at[pl.ds(taps, length - taps)], turned.at[pl.ds(taps, length - taps)]),
                (model_h.at[ch, pl.ds(img // 2, img // 2)], model.at[pl.ds(img // 2, img // 2)]),
                (table_h.at[pl.ds(0, wide)], table.at[pl.ds(0, wide)]),
                (table_h.at[pl.ds(wide, wide)], table.at[pl.ds(wide, wide)]),
                (dirty_h.at[ch], dirty),
            )
        )
    ]
    for copy in copies:
        copy.start()

    zeros = jnp.zeros((wide - half, 2 * wide), BF16)
    prod[half:wide, :] = zeros
    prod[wide + half :, :] = zeros

    copies[0].wait()
    copies[1].wait()
    cols_q[...] = dot(psf[...], turned[:taps, :]).astype(BF16)
    copies[2].wait()
    copies[3].wait()
    right = turned[:img, :]
    cols_x[: img // 2, :] = dot(model[: img // 2, :], right).astype(BF16)
    copies[4].wait()
    cols_x[img // 2 :, :] = dot(model[img // 2 :, :], right).astype(BF16)

    for k in range(2):
        copies[5 + k].wait()
        source = slice(k * wide, k * wide + half)
        target = slice(k * half, (k + 1) * half)
        spec_q[target, :] = dot(table[source, :taps], cols_q[...])
        spec_x[target, :] = dot(table[source, :img], cols_x[...])

    @pl.loop(0, half // 16)
    def _(i):
        at = pl.multiple_of(i * 16, 16)
        c, s = pl.ds(at, 16), pl.ds(half + at, 16)
        for j in range(0, wide, 128):
            lc, ls = slice(j, j + 128), slice(wide + j, wide + j + 128)
            xcc, xcs, xsc, xss = spec_x[c, lc], spec_x[c, ls], spec_x[s, lc], spec_x[s, ls]
            qcc, qcs, qsc, qss = spec_q[c, lc], spec_q[c, ls], spec_q[s, lc], spec_q[s, ls]
            t = pl.ds(wide + at, 16)
            prod[c, lc] = ((xcc * qcc + xss * qss) - (xsc * qsc + xcs * qcs)).astype(BF16)
            prod[t, ls] = ((xcc * qss + xss * qcc) + (xsc * qcs + xcs * qsc)).astype(BF16)
            prod[t, lc] = ((xcc * qsc - xss * qcs) + (xsc * qcc - xcs * qss)).astype(BF16)
            prod[c, ls] = ((xcc * qcs - xss * qsc) + (xcs * qcc - xsc * qss)).astype(BF16)

    scale = rate[ch] * (4.0 / (length * length))
    step = 128
    for i in range(img // step):
        rows = slice(i * step, (i + 1) * step)
        back = turned[shift + i * step : shift + (i + 1) * step, :]
        rows_y[rows, :] = dot(back, prod[...]).astype(BF16)

    copies[7].wait()
    chunked = len(outs[0].shape) == 5
    bands_of, parts = outs[0].shape[:2]
    band, part = outs[0].shape[-2:]
    chunks = outs[0].shape[2] if chunked else len(outs)
    for q in range(chunks):
        for i in range(bands_of * band // step):
            at = q * bands_of * band + i * step
            rows = slice(at, at + step)
            blurred = dot(rows_y[rows, :], table[:, shift:])
            stepped = rate[ch] * dirty[rows, :].astype(F32) - scale * blurred
            stepped = (model[rows, :].astype(F32) + stepped).astype(BF16)
            where = slice(i * step // band, (i + 1) * step // band)
            for p in range(parts):
                piece = stepped[:, p * part : (p + 1) * part].reshape(step // band, band, part)
                if chunked:
                    outs[0][where, p, q] = piece
                else:
                    outs[q][where, p] = piece


def mix_kernel(chunk, gain, b_in, w_in_t, w_out_t, swap, tiles_0, tiles_1, out, bias, normed, mixed):
    sources, _, band, part = out.shape
    channels = 2 * sources
    groups = sources // band

    def tile(ch, source):
        block = tiles_0[source, chunk] if ch == 0 else tiles_1[source]
        return block.astype(F32)

    bias[...] = jnp.broadcast_to(b_in[...], bias.shape)
    power = jnp.zeros((band, part), F32)
    for source in range(sources):
        for ch in range(2):
            v = tile(ch, source)
            power = power + v * v
    inverse = lax.rsqrt(power * (1.0 / channels) + 1e-06)
    for ch in range(2):
        for g in range(groups):
            rows = [
                (tile(ch, s) * inverse * gain[2 * s + ch]).astype(BF16)
                for s in range(g * band, (g + 1) * band)
            ]
            swapped = dot(swap[...], jnp.concatenate(rows, axis=0)).astype(BF16)
            at = ch * sources + g * band
            normed[:, at : at + band, :] = swapped.reshape(band, band, part)

    a = math.sqrt(2.0 / math.pi)
    for r in range(band):
        inner = dot(w_in_t[...], normed[r]) + bias[...]
        bent = inner * (a + (a * 0.044715) * (inner * inner))
        twice = (inner + inner * jnp.tanh(bent)).astype(BF16)
        mixed[r] = (0.5 * dot(w_out_t[...], twice)).astype(BF16)

    for ch in range(2):
        for g in range(groups):
            at = ch * sources + g * band
            block = mixed[:, at : at + band, :].reshape(band * band, part)
            swapped = dot(swap[...], block).astype(BF16)
            out[g * band : (g + 1) * band, ch] = swapped.reshape(band, band, part)


def spread_kernel(chunk, chunks, first, taps, st_0, *refs):
    has_prev = chunk > 0
    last = chunk == chunks - 1
    st_1, refs = refs[:chunks], refs[chunks:]
    if has_prev:
        cur, prev, _, out, above, middle, below, result, tail, sems = refs
    else:
        cur, out, above, middle, below, result, sems = refs
    channels = taps.shape[0] // 9
    bands, parts, ch_dev, band, part = cur.shape
    img = parts * part
    lead = 2 if has_prev else 0
    count = bands + lead
    lo = 1 if has_prev else 0
    hi = count if last else count - 1
    group = 4

    if has_prev:
        fetch = pltpu.make_async_copy(prev.at[pl.ds(bands - 2, 2)], tail, sems.at[0])
        fetch.start()
        fetch.wait()

    def mixed_band(j, ch):
        source, at = (tail, j) if j < lead else (cur, j - lead)
        return jnp.concatenate([source[at, p, ch] for p in range(parts)], axis=1)

    def stepped_band(j, ch):
        at = chunk * bands + j - lead
        q, b = at // bands, at % bands
        pieces = [st_1[q][b, p] if ch else st_0[b, p, q] for p in range(parts)]
        return jnp.concatenate(pieces, axis=1)

    zero = jnp.zeros((img // 128, 8, 128), F32)
    for ch in range(ch_dev):
        k = [[taps[(3 * i + j) * channels + first[0] + ch] for j in range(3)] for i in range(3)]
        above[:, 0:8, :] = zero
        below[:, count * band : count * band + 8, :] = zero
        for start in range(0, count, group):
            js = range(start, min(start + group, count))
            size = len(js) * band
            x = jnp.concatenate([mixed_band(j, ch) for j in js], axis=0).astype(F32)
            lane = lax.broadcasted_iota(jnp.int32, (size, img), 1)
            low = jnp.where(lane == 0, 0.0, pltpu.roll(x, 1, 1))
            high = jnp.where(lane == img - 1, 0.0, pltpu.roll(x, img - 1, 1))
            at = start * band
            for target, row, off in ((above, 0, 8), (middle, 1, 0), (below, 2, 0)):
                value = k[row][0] * low + k[row][1] * x + k[row][2] * high
                for n in range(img // 128):
                    target[n, at + off : at + off + size, :] = value[:, n * 128 : (n + 1) * 128]
        for j in range(lo, hi):
            at = j * band
            base = stepped_band(j, ch).astype(F32)
            for n in range(img // 128):
                total = above[n, at + 7 : at + 7 + band, :] + below[n, at + 1 : at + 1 + band, :]
                total = total + middle[n, at : at + band, :]
                total = base[:, n * 128 : (n + 1) * 128] + total
                to = at - lo * band
                result[ch, to : to + band, n * 128 : (n + 1) * 128] = total.astype(BF16)

    rows = (hi - lo) * band
    origin = (chunk * bands - lead + lo) * band
    send = pltpu.make_async_copy(result, out.at[:, pl.ds(origin, rows), :], sems.at[1])
    send.start()
    send.wait()


VMEM = pl.BlockSpec(memory_space=pltpu.VMEM)
SMEM = pl.BlockSpec(memory_space=pltpu.SMEM)
ANY = pl.BlockSpec(memory_space=pl.ANY)
HBM = pl.BlockSpec(memory_space=pltpu.HBM)


def params(mib):
    return pltpu.CompilerParams(vmem_limit_bytes=mib * MIB)


def exchange(blocks):
    return lax.all_to_all(blocks, ("rows", "cols"), split_axis=0, concat_axis=0, tiled=True)


def local(model, dirty, psf, step_size, gain, w_in, b_in, w_out, kernel):
    ch_dev, img, _ = model.shape
    psf_len = psf.shape[1]
    assert ch_dev == 2
    n_dev = lax.axis_size("rows") * lax.axis_size("cols")
    channels = gain.shape[0]
    hidden = b_in.shape[0]
    chunks = max(1, min(CHUNKS, img * img // (n_dev * BAND * 128)))
    part = img * img // (n_dev * BAND * chunks)
    parts = img // part
    bands = img // (BAND * chunks)
    table, turned = tables(img, psf_len)
    wide, length = table.shape[0] // 2, table.shape[1]

    def conv(ch):
        one = jax.ShapeDtypeStruct((bands, parts, BAND, part), BF16)
        whole = jax.ShapeDtypeStruct((bands, parts, chunks, BAND, part), BF16)
        return pl.pallas_call(
            lambda *refs: conv_kernel(ch, *refs),
            out_shape=[one] * chunks if ch else [whole],
            in_specs=[SMEM] + [HBM] * 5,
            out_specs=[VMEM] * (chunks if ch else 1),
            scratch_shapes=[
                pltpu.VMEM((img, img), BF16),
                pltpu.VMEM((img, img), BF16),
                pltpu.VMEM((psf_len, psf_len), BF16),
                pltpu.VMEM((2 * wide, length), BF16),
                pltpu.VMEM((length, 2 * wide), BF16),
                pltpu.VMEM((img, 2 * wide), BF16),
                pltpu.VMEM((psf_len, 2 * wide), BF16),
                pltpu.VMEM((length, 2 * wide), F32),
                pltpu.VMEM((length, 2 * wide), F32),
                pltpu.VMEM((2 * wide, 2 * wide), BF16),
                pltpu.VMEM((img, 2 * wide), BF16),
                pltpu.SemaphoreType.DMA((8,)),
            ],
            compiler_params=params(24),
            cost_estimate=pl.CostEstimate(flops=4_000_000_000, bytes_accessed=4_000_000, transcendentals=0),
            name="conv",
        )(step_size, model, dirty, psf, table, turned)

    def mix(chunk, tiles_0, tiles_1):
        return pl.pallas_call(
            lambda *refs: mix_kernel(chunk, *refs),
            out_shape=jax.ShapeDtypeStruct((n_dev, ch_dev, BAND, part), BF16),
            in_specs=[SMEM] + [VMEM] * 6,
            out_specs=VMEM,
            scratch_shapes=[
                pltpu.VMEM((hidden, part), F32),
                pltpu.VMEM((BAND, channels, part), BF16),
                pltpu.VMEM((BAND, channels, part), BF16),
            ],
            compiler_params=params(16),
            cost_estimate=pl.CostEstimate(flops=4_000_000_000, bytes_accessed=2_000_000, transcendentals=0),
            name="mix",
        )(gain, b_col, w_in_t, w_out_t, swap, tiles_0, tiles_1)

    def spread(chunk, current, previous, result):
        lead = 2 if chunk else 0
        rows = (bands + lead + 1) * BAND
        out_bands = bands + (1 if chunk else 0) - (0 if chunk == chunks - 1 else 1)
        plane = pltpu.VMEM((img // 128, rows, 128), F32)
        scratch = [plane, plane, plane, pltpu.VMEM((ch_dev, out_bands * BAND, img), BF16)]
        more = []
        if chunk:
            more = [previous, result]
            scratch.append(pltpu.VMEM((2, parts, ch_dev, BAND, part), BF16))
        scratch.append(pltpu.SemaphoreType.DMA((2,)))
        return pl.pallas_call(
            lambda *refs: spread_kernel(chunk, chunks, *refs),
            out_shape=jax.ShapeDtypeStruct((ch_dev, img, img), BF16),
            in_specs=[SMEM, SMEM] + [VMEM] * (chunks + 2) + [ANY] * len(more),
            out_specs=ANY,
            input_output_aliases={chunks + 5: 0} if chunk else {},
            scratch_shapes=scratch,
            compiler_params=params(16),
            cost_estimate=pl.CostEstimate(flops=4_000_000_000, bytes_accessed=2_000_000, transcendentals=0),
            name="spread",
        )(position[None], flat_taps, st_0, *st_1, current, *more)

    (st_0,) = conv(0)
    st_0, w_in, b_in, w_out, kernel = lax.optimization_barrier((st_0, w_in, b_in, w_out, kernel))
    tiles_0 = exchange(st_0.reshape(n_dev, chunks, BAND, part))
    st_1 = conv(1)
    tiles_1 = [exchange(piece.reshape(n_dev, BAND, part)) for piece in st_1]

    b_col = b_in[:, None]
    w_in_t = w_in.reshape(n_dev, ch_dev, hidden).transpose(2, 1, 0).reshape(hidden, channels)
    w_out_t = w_out.reshape(hidden, n_dev, ch_dev).transpose(2, 1, 0).reshape(channels, hidden)
    swap = shuffle_table()
    flat_taps = kernel.reshape(-1)
    position = lax.axis_index(("rows", "cols")).astype(jnp.int32) * ch_dev

    returned = []
    for q in range(chunks):
        back = exchange(mix(q, tiles_0, tiles_1[q]))
        returned.append(back.reshape(bands, parts, ch_dev, BAND, part))
    result = None
    for q in range(chunks):
        result = spread(q, returned[q], returned[q - 1] if q else None, result)
    return result


def solution(mesh):
    return jax.shard_map(
        local,
        mesh=mesh,
        in_specs=(
            P(("rows", "cols"), None, None),
            P(("rows", "cols"), None, None),
            P(("rows", "cols"), None, None),
            P(("rows", "cols")),
            P(),
            P(),
            P(),
            P(),
            P(),
        ),
        out_specs=P(("rows", "cols"), None, None),
        check_vma=False,
    )
```

time: 476 us -> 108 us (0.23)
  matrix products: 324 us -> 0 us
  blocking collectives: 68.7 us -> 20.4 us
  local copies, waits for them, and re-layouts: 44.4 us -> 11.9 us
  Pallas kernels: 0 us -> 30.4 us
  waiting for transfers between devices: 4.87 us -> 27.4 us
  other arithmetic: 17 us -> 0 us
  starting transfers between devices: 5.47 us -> 16.1 us
  loops' own time: 9.53 us -> 0 us
    dot_general x37 -> x0, matrix products: 324 us -> none  [the longest x4 39 us: spectrum(): jnp.dot(imag_a, sin_t.T, preferred_element_type=jnp.float32)]
    all_to_all x2 -> x1, blocking collectives: 68.7 us -> 20.4 us  [exchange(): lax.all_to_all(blocks, ('rows', 'cols'), split_axis=0, concat_axis=0, til...]
    pallas_call x0 -> x6, Pallas kernels: none -> 30.4 us  [the longest x2 13.4 us: conv(): pl.pallas_call(lambda *refs: conv_kernel(ch, *refs), out_shape=[one] * ch...]
    all_to_all x0 -> x4, waiting for transfers between devices: none -> 27.4 us  [exchange(): lax.all_to_all(blocks, ('rows', 'cols'), split_axis=0, concat_axis=0, til...]
    all_to_all x0 -> x4, starting transfers between devices: none -> 16.1 us  [exchange(): lax.all_to_all(blocks, ('rows', 'cols'), split_axis=0, concat_axis=0, til...]
    reshape x5, local copies, waits for them, and re-layouts: 13.3 us -> 0.23 us  [the longest x2 0.13 us: local(): w_in.reshape(n_dev, ch_dev, hidden).transpose(2, 1, 0)]
    unnamed x14 -> x36, local copies, waits for them, and re-layouts: 0.99 us -> 11.5 us
    another operation x1 -> x0, loops' own time: 9.53 us -> none  [local(): stepped = lax.map(one_channel, (model, dirty, psf, step_size))]
  transfers between devices with their start and end apart: 4 -> 4, of which waited for: 2 -> 4; matrix products, arithmetic and copies ran while one was open for 2% -> 0% of each run, Pallas kernels for 0% -> 19%
where the time goes in v2:
time: 108 us; the launch traced here: 107 us
  Pallas kernels  30.4 us (28%)
  waiting for transfers between devices  27.4 us (25%)
  blocking collectives  20.4 us (19%)
  starting transfers between devices  16.1 us (15%)
  local copies, waits for them, and re-layouts  11.9 us (11%)
    all_to_all x4, waiting for transfers between devices, exchange(): lax.all_to_all(blocks, ('rows', 'cols'), split_axis=0, concat_axis=0, til...  27.4 us
    all_to_all x1, blocking collectives, exchange(): lax.all_to_all(blocks, ('rows', 'cols'), split_axis=0, concat_axis=0, til...  20.4 us
    all_to_all x4, starting transfers between devices, exchange(): lax.all_to_all(blocks, ('rows', 'cols'), split_axis=0, concat_axis=0, til...  16.1 us
    pallas_call x2, Pallas kernels, conv(): pl.pallas_call(lambda *refs: conv_kernel(ch, *refs), out_shape=[one] * ch...  13.4 us
    unnamed x36, local copies, waits for them, and re-layouts  11.5 us
    pallas_call x2, Pallas kernels, mix(): pl.pallas_call(lambda *refs: mix_kernel(chunk, *refs), out_shape=jax.Shap...  11 us
    pallas_call x2, Pallas kernels, spread(): pl.pallas_call(lambda *refs: spread_kernel(chunk, chunks, *refs), out_sha...  6.07 us
  transfers between devices with their start and end apart: 4, of which 4 were waited for; matrix products, arithmetic and copies ran while one was open for 0% of the time, Pallas kernels for 19%

profile of v2, /device:TPU:0, one launch (start us, length us, event | category | flops | bytes accessed | tf_op | source)
XLA Modules:
  0.0 106.7 jit_solution(13889617515866345262)
XLA Ops:
  0.0 1.2 %copy-done = bf16[2,512,512]{2,1,0:T(8,128)(2,1)S(1)} copy-done((bf16[2,512,512]{2,1,0:T(8,128)(2,1)S(1)}, bf16[2,512,512]{2,1,0:T(8,128)(2,1)}, u32[]{:S(2)}) %copy-start) | copy-done | bytes 1048600
  1.2 1.2 %copy-done.2 = bf16[2,512,512]{2,1,0:T(8,128)(2,1)S(1)} copy-done((bf16[2,512,512]{2,1,0:T(8,128)(2,1)S(1)}, bf16[2,512,512]{2,1,0:T(8,128)(2,1)}, u32[]{:S(2)}) %copy-start.2) | copy-done | bytes 1048600
  2.5 0.9 copy-done.4
  3.4 0.7 copy-done.6
  4.1 1.2 %copy-done.9 = bf16[640,768]{1,0:T(8,128)(2,1)S(1)} copy-done((bf16[640,768]{1,0:T(8,128)(2,1)S(1)}, bf16[640,768]{1,0:T(8,128)(2,1)}, u32[]{:S(2)}) %copy-start.9) | copy-done | bytes 983064
  5.3 1.2 %copy-done.11 = bf16[768,640]{1,0:T(8,128)(2,1)S(1)} copy-done((bf16[768,640]{1,0:T(8,128)(2,1)S(1)}, bf16[768,640]{1,0:T(8,128)(2,1)}, u32[]{:S(2)}) %copy-start.11) | copy-done | bytes 983064
  6.5 7.0 %conv.3 = (bf16[16,2,16,256]{3,2,1,0:T(8,128)(2,1)}, bf16[16,2,16,256]{3,2,1,0:T(8,128)(2,1)}) custom-call(f32[2]{0:T(128)S(1)} %copy-done.6, bf16[2,512,512]{2,1,0:T(8,128)(2,1)S(1)} %copy-done, bf16[2,512,512]{2,1,0:T(8,128)(2,1)S(1)} %copy-done.2, bf16[2,256,256]{2,1,0:T(8,128)(2,1)S(1)} %copy-done.4, bf16[768,640]{1,0:T(8,128)(2,1)S(1)} %copy-done.11, ...), custom_call_target="tpu_custom_call" | custom-call | flops 4000000000 | bytes 4000000 | tf_op jit(solution)/shard_map/conv/pallas_call | solution.py:272
  13.5 0.0 copy-start.7
  13.5 7.3 %all-to-all-start.3 = ((bf16[32,16,256]{2,1,0:T(8,128)(2,1)}), bf16[32,16,256]{2,1,0:T(8,128)(2,1)S(1)}, u32[]{:S(2)}, u32[]{:S(2)}) async-start(bf16[32,16,256]{2,1,0:T(8,128)(2,1)} %bitcast.10), calls=%async_computation.3 | async-start | bytes 524288 | tf_op jit(solution)/shard_map/all_to_all | solution.py:252
  20.9 0.0 copy-start.10
  20.9 1.2 %copy-done.10 = bf16[640,768]{1,0:T(8,128)(2,1)S(1)} copy-done((bf16[640,768]{1,0:T(8,128)(2,1)S(1)}, bf16[640,768]{1,0:T(8,128)(2,1)}, u32[]{:S(2)}) %copy-start.10) | copy-done | bytes 983064
  22.1 1.2 %copy-done.12 = bf16[768,640]{1,0:T(8,128)(2,1)S(1)} copy-done((bf16[768,640]{1,0:T(8,128)(2,1)S(1)}, bf16[768,640]{1,0:T(8,128)(2,1)}, u32[]{:S(2)}) %copy-start.12) | copy-done | bytes 983064
  23.3 6.3 %conv.2.refs_2_ = bf16[16,2,2,16,256]{4,3,2,1,0:T(8,128)(2,1)S(1)} custom-call(f32[2]{0:T(128)S(1)} %copy-done.7, bf16[2,512,512]{2,1,0:T(8,128)(2,1)S(1)} %copy-done.1, bf16[2,512,512]{2,1,0:T(8,128)(2,1)S(1)} %copy-done.3, bf16[2,256,256]{2,1,0:T(8,128)(2,1)S(1)} %copy-done.5, bf16[768,640]{1,0:T(8,128)(2,1)S(1)} %copy-done.12, bf16[640,768]{1,0:T(8,128)(2,1)S(1)} %copy-done.10), custom_call_target="tpu_custom_call" | custom-call | flops 4000000000 | bytes 4000000 | tf_op jit(solution)/shard_map/conv/pallas_call | solution.py:272
  29.6 1.6 %all-to-all-done.3.refs_6_ = bf16[32,16,256]{2,1,0:T(8,128)(2,1)S(1)} async-done(((bf16[32,16,256]{2,1,0:T(8,128)(2,1)}), bf16[32,16,256]{2,1,0:T(8,128)(2,1)S(1)}, u32[]{:S(2)}, u32[]{:S(2)}) %all-to-all-start.3) | async-done | bytes 262176 | tf_op jit(solution)/shard_map/all_to_all | solution.py:252
  31.2 20.4 %all_to_all.25.refs_5_ = bf16[32,2,16,256]{3,2,1,0:T(8,128)(2,1)S(1)} all-to-all(bf16[32,2,16,256]{3,2,1,0:T(8,128)(2,1)S(1)} %bitcast.14), channel_id=1, replica_groups=mesh['rows'=4,'cols'=8] {'rows','cols'}, dimensions={0} | all-to-all | bytes 1048576 | tf_op jit(solution)/shard_map/all_to_all | solution.py:252
  51.6 2.7 %all-to-all-start.1 = ((bf16[32,16,256]{2,1,0:T(8,128)(2,1)}), bf16[32,16,256]{2,1,0:T(8,128)(2,1)S(1)}, u32[]{:S(2)}, u32[]{:S(2)}) async-start(bf16[32,16,256]{2,1,0:T(8,128)(2,1)} %bitcast.7), calls=%async_computation.1 | async-start | bytes 524288 | tf_op jit(solution)/shard_map/all_to_all | solution.py:252
  54.4 0.1 copy.24.refs_2_
  54.5 0.6 copy-done.15
  55.2 0.7 copy-done.17
  55.9 0.1 copy.23.refs_1_
  56.1 0.6 copy-done.8
  56.7 5.5 %mix.3 = bf16[32,2,16,256]{3,2,1,0:T(8,128)(2,1)} custom-call(f32[64]{0:T(128)S(1)} %copy-done.8, f32[256,1]{1,0:T(8,128)S(1)} %copy.23.refs_1_, bf16[256,64]{1,0:T(8,128)(2,1)S(1)} %copy.24.refs_2_, bf16[64,256]{1,0:T(8,128)(2,1)S(1)} %bitcast.18, bf16[256,256]{1,0:T(8,128)(2,1)S(1)} %copy-done.13, bf16[32,2,16,256]{3,2,1,0:T(8,128)(2,1)S(1)} %all_to_all.25.refs_5_, ...), custom_call_target="tpu_custom_call" | custom-call | flops 4000000000 | bytes 2000000 | tf_op jit(solution)/shard_map/mix/pallas_call | solution.py:297
  62.2 2.5 %all-to-all-done.1.refs_6_ = bf16[32,16,256]{2,1,0:T(8,128)(2,1)S(1)} async-done(((bf16[32,16,256]{2,1,0:T(8,128)(2,1)}), bf16[32,16,256]{2,1,0:T(8,128)(2,1)S(1)}, u32[]{:S(2)}, u32[]{:S(2)}) %all-to-all-start.1) | async-done | bytes 262176 | tf_op jit(solution)/shard_map/all_to_all | solution.py:252
  64.7 3.5 %all-to-all-start.4 = ((bf16[32,2,16,256]{3,2,1,0:T(8,128)(2,1)}), bf16[32,2,16,256]{3,2,1,0:T(8,128)(2,1)S(1)}, u32[]{:S(2)}, u32[]{:S(2)}) async-start(bf16[32,2,16,256]{3,2,1,0:T(8,128)(2,1)} %mix.3), calls=%async_computation.4 | async-start | bytes 1048576 | tf_op jit(solution)/shard_map/all_to_all | solution.py:252
  68.2 5.5 %mix.2 = bf16[32,2,16,256]{3,2,1,0:T(8,128)(2,1)} custom-call(f32[64]{0:T(128)S(1)} %copy-done.8, f32[256,1]{1,0:T(8,128)S(1)} %copy.23.refs_1_, bf16[256,64]{1,0:T(8,128)(2,1)S(1)} %copy.24.refs_2_, bf16[64,256]{1,0:T(8,128)(2,1)S(1)} %bitcast.19, bf16[256,256]{1,0:T(8,128)(2,1)S(1)} %copy-done.13, bf16[32,2,16,256]{3,2,1,0:T(8,128)(2,1)S(1)} %all_to_all.25.refs_5_, ...), custom_call_target="tpu_custom_call" | custom-call | flops 4000000000 | bytes 2000000 | tf_op jit(solution)/shard_map/mix/pallas_call | solution.py:297
  73.7 10.7 %all-to-all-done.4 = bf16[32,2,16,256]{3,2,1,0:T(8,128)(2,1)S(1)} async-done(((bf16[32,2,16,256]{3,2,1,0:T(8,128)(2,1)}), bf16[32,2,16,256]{3,2,1,0:T(8,128)(2,1)S(1)}, u32[]{:S(2)}, u32[]{:S(2)}) %all-to-all-start.4) | async-done | bytes 524320 | tf_op jit(solution)/shard_map/all_to_all | solution.py:252
  84.4 2.6 %all-to-all-start.2 = ((bf16[32,2,16,256]{3,2,1,0:T(8,128)(2,1)}), bf16[32,2,16,256]{3,2,1,0:T(8,128)(2,1)S(1)}, u32[]{:S(2)}, u32[]{:S(2)}) async-start(bf16[32,2,16,256]{3,2,1,0:T(8,128)(2,1)} %mix.2), calls=%async_computation.2 | async-start | bytes 1048576 | tf_op jit(solution)/shard_map/all_to_all | solution.py:252
  87.0 0.7 copy-done.16
  87.7 0.1 reshape.30.refs_1_
  87.8 2.9 %spread.2.refs_7_ = bf16[2,512,512]{2,1,0:T(8,128)(2,1)} custom-call(s32[1]{0:T(128)} %bitcast.refs_0_, f32[576]{0:T(1024)S(1)} %reshape.30.refs_1_, bf16[16,2,2,16,256]{4,3,2,1,0:T(8,128)(2,1)S(1)} %conv.2.refs_2_, bf16[16,2,16,256]{3,2,1,0:T(8,128)(2,1)} %get-tuple-element.14.refs_3_, bf16[16,2,16,256]{3,2,1,0:T(8,128)(2,1)} %get-tuple-element.15.refs_4_, ...), custom_call_target="tpu_custom_call" | custom-call | flops 4000000000 | bytes 2000000 | tf_op jit(solution)/shard_map/spread/pallas_call | solution.py:323
  90.7 12.7 %all-to-all-done.2 = bf16[32,2,16,256]{3,2,1,0:T(8,128)(2,1)S(1)} async-done(((bf16[32,2,16,256]{3,2,1,0:T(8,128)(2,1)}), bf16[32,2,16,256]{3,2,1,0:T(8,128)(2,1)S(1)}, u32[]{:S(2)}, u32[]{:S(2)}) %all-to-all-start.2) | async-done | bytes 524320 | tf_op jit(solution)/shard_map/all_to_all | solution.py:252
  103.4 3.2 %spread.3 = bf16[2,512,512]{2,1,0:T(8,128)(2,1)} custom-call(s32[1]{0:T(128)} %bitcast.refs_0_, f32[576]{0:T(1024)S(1)} %reshape.30.refs_1_, bf16[16,2,2,16,256]{4,3,2,1,0:T(8,128)(2,1)S(1)} %conv.2.refs_2_, bf16[16,2,16,256]{3,2,1,0:T(8,128)(2,1)} %get-tuple-element.14.refs_3_, ...), custom_call_target="tpu_custom_call", output_to_operand_aliasing={{}: (7, {})} | custom-call | flops 4000000000 | bytes 2000000 | tf_op jit(solution)/shard_map/spread/pallas_call | solution.py:323
  (26 shorter events, 0.1 us)
Async XLA Ops:
  0.0 1.2 %copy-start = (bf16[2,512,512]{2,1,0:T(8,128)(2,1)S(1)}, bf16[2,512,512]{2,1,0:T(8,128)(2,1)}, u32[]{:S(2)}) copy-start(bf16[2,512,512]{2,1,0:T(8,128)(2,1)} %refs_1_.3) | copy-start | bytes 3145732
  1.2 1.2 %copy-start.2 = (bf16[2,512,512]{2,1,0:T(8,128)(2,1)S(1)}, bf16[2,512,512]{2,1,0:T(8,128)(2,1)}, u32[]{:S(2)}) copy-start(bf16[2,512,512]{2,1,0:T(8,128)(2,1)} %refs_2_.3) | copy-start | bytes 3145732
  2.5 0.9 copy-start.4
  3.4 0.7 copy-start.6
  4.1 1.2 %copy-start.9 = (bf16[640,768]{1,0:T(8,128)(2,1)S(1)}, bf16[640,768]{1,0:T(8,128)(2,1)}, u32[]{:S(2)}) copy-start(bf16[640,768]{1,0:T(8,128)(2,1)} %constant.19.clone.refs_5_) | copy-start | bytes 2949124
  5.3 1.2 %copy-start.11 = (bf16[768,640]{1,0:T(8,128)(2,1)S(1)}, bf16[768,640]{1,0:T(8,128)(2,1)}, u32[]{:S(2)}) copy-start(bf16[768,640]{1,0:T(8,128)(2,1)} %constant.18.clone.refs_4_) | copy-start | bytes 2949124
  6.5 14.4 %copy-start.1 = (bf16[2,512,512]{2,1,0:T(8,128)(2,1)S(1)}, bf16[2,512,512]{2,1,0:T(8,128)(2,1)}, u32[]{:S(2)}) copy-start(bf16[2,512,512]{2,1,0:T(8,128)(2,1)} %refs_1_.3) | copy-start | bytes 3145732
  6.5 14.4 %copy-start.3 = (bf16[2,512,512]{2,1,0:T(8,128)(2,1)S(1)}, bf16[2,512,512]{2,1,0:T(8,128)(2,1)}, u32[]{:S(2)}) copy-start(bf16[2,512,512]{2,1,0:T(8,128)(2,1)} %refs_2_.3) | copy-start | bytes 3145732
  13.5 7.4 %copy-start.5 = (bf16[2,256,256]{2,1,0:T(8,128)(2,1)S(1)}, bf16[2,256,256]{2,1,0:T(8,128)(2,1)}, u32[]{:S(2)}) copy-start(bf16[2,256,256]{2,1,0:T(8,128)(2,1)} %refs_3_.3) | copy-start | bytes 786436
  13.5 7.4 %copy-start.7 = (f32[2]{0:T(128)S(1)}, f32[2]{0:T(128)}, u32[]{:S(2)}) copy-start(f32[2]{0:T(128)} %refs_0_.5) | copy-start | bytes 28
  13.5 17.7 %all-to-all-start.3 = ((bf16[32,16,256]{2,1,0:T(8,128)(2,1)}), bf16[32,16,256]{2,1,0:T(8,128)(2,1)S(1)}, u32[]{:S(2)}, u32[]{:S(2)}) async-start(bf16[32,16,256]{2,1,0:T(8,128)(2,1)} %bitcast.10), calls=%async_computation.3 | async-start | bytes 524288 | tf_op jit(solution)/shard_map/all_to_all | solution.py:252
  20.9 1.2 %copy-start.10 = (bf16[640,768]{1,0:T(8,128)(2,1)S(1)}, bf16[640,768]{1,0:T(8,128)(2,1)}, u32[]{:S(2)}) copy-start(bf16[640,768]{1,0:T(8,128)(2,1)} %constant.19.clone.refs_5_) | copy-start | bytes 2949124
  22.1 1.2 %copy-start.12 = (bf16[768,640]{1,0:T(8,128)(2,1)S(1)}, bf16[768,640]{1,0:T(8,128)(2,1)}, u32[]{:S(2)}) copy-start(bf16[768,640]{1,0:T(8,128)(2,1)} %constant.18.clone.refs_4_) | copy-start | bytes 2949124
  51.6 2.7 %copy-start.14 = (bf16[64,256]{1,0:T(8,128)(2,1)S(1)}, bf16[64,256]{1,0:T(8,128)(2,1)}, u32[]{:S(2)}) copy-start(bf16[64,256]{1,0:T(8,128)(2,1)} %param.17) | copy-start | bytes 98308
  51.6 13.1 %all-to-all-start.1 = ((bf16[32,16,256]{2,1,0:T(8,128)(2,1)}), bf16[32,16,256]{2,1,0:T(8,128)(2,1)S(1)}, u32[]{:S(2)}, u32[]{:S(2)}) async-start(bf16[32,16,256]{2,1,0:T(8,128)(2,1)} %bitcast.7), calls=%async_computation.1 | async-start | bytes 524288 | tf_op jit(solution)/shard_map/all_to_all | solution.py:252
  54.4 0.8 copy-start.15
  55.2 0.9 copy-start.13
  55.2 0.7 copy-start.17
  56.0 0.7 copy-start.8
  64.7 19.7 %all-to-all-start.4 = ((bf16[32,2,16,256]{3,2,1,0:T(8,128)(2,1)}), bf16[32,2,16,256]{3,2,1,0:T(8,128)(2,1)S(1)}, u32[]{:S(2)}, u32[]{:S(2)}) async-start(bf16[32,2,16,256]{3,2,1,0:T(8,128)(2,1)} %mix.3), calls=%async_computation.4 | async-start | bytes 1048576 | tf_op jit(solution)/shard_map/all_to_all | solution.py:252
  84.4 19.0 %all-to-all-start.2 = ((bf16[32,2,16,256]{3,2,1,0:T(8,128)(2,1)}), bf16[32,2,16,256]{3,2,1,0:T(8,128)(2,1)S(1)}, u32[]{:S(2)}, u32[]{:S(2)}) async-start(bf16[32,2,16,256]{3,2,1,0:T(8,128)(2,1)} %mix.2), calls=%async_computation.2 | async-start | bytes 1048576 | tf_op jit(solution)/shard_map/all_to_all | solution.py:252
  87.0 0.7 copy-start.16

commit v3 on v2

--- a/solution.py
+++ b/solution.py
@@ -39,10 +39,9 @@
 
 
 def conv_kernel(
-    ch, rate, model_h, dirty_h, psf_h, table_h, turned_h, *refs
+    ch, rate, model_h, dirty_h, psf_h, table_h, turned_h, out,
+    model, dirty, psf, table, turned, cols_x, cols_q, spec_x, spec_q, prod, rows_y, sems,
 ):
-    outs = refs[:-12]
-    (model, dirty, psf, table, turned, cols_x, cols_q, spec_x, spec_q, prod, rows_y, sems) = refs[-12:]
     img = model.shape[0]
     taps = psf.shape[0]
     shift = taps // 2
@@ -111,10 +110,7 @@
         rows_y[rows, :] = dot(back, prod[...]).astype(BF16)
 
     copies[7].wait()
-    chunked = len(outs[0].shape) == 5
-    bands_of, parts = outs[0].shape[:2]
-    band, part = outs[0].shape[-2:]
-    chunks = outs[0].shape[2] if chunked else len(outs)
+    bands_of, parts, chunks, band, part = out.shape
     for q in range(chunks):
         for i in range(bands_of * band // step):
             at = q * bands_of * band + i * step
@@ -124,21 +120,17 @@
             stepped = (model[rows, :].astype(F32) + stepped).astype(BF16)
             where = slice(i * step // band, (i + 1) * step // band)
             for p in range(parts):
-                piece = stepped[:, p * part : (p + 1) * part].reshape(step // band, band, part)
-                if chunked:
-                    outs[0][where, p, q] = piece
-                else:
-                    outs[q][where, p] = piece
-
-
-def mix_kernel(chunk, gain, b_in, w_in_t, w_out_t, swap, tiles_0, tiles_1, out, bias, normed, mixed):
+                piece = stepped[:, p * part : (p + 1) * part]
+                out[where, p, q] = piece.reshape(step // band, band, part)
+
+
+def mix_kernel(chunk, device, gain, b_in, w_in_t, w_out_t, swap, tiles_0, tiles_1, out, bias, normed, mixed):
     sources, _, band, part = out.shape
     channels = 2 * sources
     groups = sources // band
 
     def tile(ch, source):
-        block = tiles_0[source, chunk] if ch == 0 else tiles_1[source]
-        return block.astype(F32)
+        return (tiles_1 if ch else tiles_0)[source, chunk].astype(F32)
 
     bias[...] = jnp.broadcast_to(b_in[...], bias.shape)
     power = jnp.zeros((band, part), F32)
@@ -150,7 +142,7 @@
     for ch in range(2):
         for g in range(groups):
             rows = [
-                (tile(ch, s) * inverse * gain[2 * s + ch]).astype(BF16)
+                (tile(ch, s) * inverse * gain[2 * device(s) + ch]).astype(BF16)
                 for s in range(g * band, (g + 1) * band)
             ]
             swapped = dot(swap[...], jnp.concatenate(rows, axis=0)).astype(BF16)
@@ -159,9 +151,9 @@
 
     a = math.sqrt(2.0 / math.pi)
     for r in range(band):
-        inner = dot(w_in_t[...], normed[r]) + bias[...]
-        bent = inner * (a + (a * 0.044715) * (inner * inner))
-        twice = (inner + inner * jnp.tanh(bent)).astype(BF16)
+        inner = (dot(w_in_t[...], normed[r]) + bias[...]).astype(BF16)
+        bent = inner * (BF16(a) + BF16(a * 0.044715) * (inner * inner))
+        twice = inner + inner * jnp.tanh(bent)
         mixed[r] = (0.5 * dot(w_out_t[...], twice)).astype(BF16)
 
     for ch in range(2):
@@ -175,7 +167,7 @@
 def spread_kernel(chunk, chunks, first, taps, st_0, *refs):
     has_prev = chunk > 0
     last = chunk == chunks - 1
-    st_1, refs = refs[:chunks], refs[chunks:]
+    st_1, refs = refs[0], refs[1:]
     if has_prev:
         cur, prev, _, out, above, middle, below, result, tail, sems = refs
     else:
@@ -201,7 +193,7 @@
     def stepped_band(j, ch):
         at = chunk * bands + j - lead
         q, b = at // bands, at % bands
-        pieces = [st_1[q][b, p] if ch else st_0[b, p, q] for p in range(parts)]
+        pieces = [(st_1 if ch else st_0)[b, p, q] for p in range(parts)]
         return jnp.concatenate(pieces, axis=1)
 
     zero = jnp.zeros((img // 128, 8, 128), F32)
@@ -249,14 +241,15 @@
 
 
 def exchange(blocks):
-    return lax.all_to_all(blocks, ("rows", "cols"), split_axis=0, concat_axis=0, tiled=True)
+    return lax.all_to_all(blocks, ("cols", "rows"), split_axis=0, concat_axis=0, tiled=True)
 
 
 def local(model, dirty, psf, step_size, gain, w_in, b_in, w_out, kernel):
     ch_dev, img, _ = model.shape
     psf_len = psf.shape[1]
     assert ch_dev == 2
-    n_dev = lax.axis_size("rows") * lax.axis_size("cols")
+    n_rows, n_cols = lax.axis_size("rows"), lax.axis_size("cols")
+    n_dev = n_rows * n_cols
     channels = gain.shape[0]
     hidden = b_in.shape[0]
     chunks = max(1, min(CHUNKS, img * img // (n_dev * BAND * 128)))
@@ -266,14 +259,12 @@
     table, turned = tables(img, psf_len)
     wide, length = table.shape[0] // 2, table.shape[1]
 
-    def conv(ch):
-        one = jax.ShapeDtypeStruct((bands, parts, BAND, part), BF16)
-        whole = jax.ShapeDtypeStruct((bands, parts, chunks, BAND, part), BF16)
+    def conv(ch, model):
         return pl.pallas_call(
             lambda *refs: conv_kernel(ch, *refs),
-            out_shape=[one] * chunks if ch else [whole],
+            out_shape=jax.ShapeDtypeStruct((bands, parts, chunks, BAND, part), BF16),
             in_specs=[SMEM] + [HBM] * 5,
-            out_specs=[VMEM] * (chunks if ch else 1),
+            out_specs=VMEM,
             scratch_shapes=[
                 pltpu.VMEM((img, img), BF16),
                 pltpu.VMEM((img, img), BF16),
@@ -288,14 +279,14 @@
                 pltpu.VMEM((img, 2 * wide), BF16),
                 pltpu.SemaphoreType.DMA((8,)),
             ],
-            compiler_params=params(24),
+            compiler_params=params(58),
             cost_estimate=pl.CostEstimate(flops=4_000_000_000, bytes_accessed=4_000_000, transcendentals=0),
             name="conv",
         )(step_size, model, dirty, psf, table, turned)
 
     def mix(chunk, tiles_0, tiles_1):
         return pl.pallas_call(
-            lambda *refs: mix_kernel(chunk, *refs),
+            lambda *refs: mix_kernel(chunk, device, *refs),
             out_shape=jax.ShapeDtypeStruct((n_dev, ch_dev, BAND, part), BF16),
             in_specs=[SMEM] + [VMEM] * 6,
             out_specs=VMEM,
@@ -323,31 +314,38 @@
         return pl.pallas_call(
             lambda *refs: spread_kernel(chunk, chunks, *refs),
             out_shape=jax.ShapeDtypeStruct((ch_dev, img, img), BF16),
-            in_specs=[SMEM, SMEM] + [VMEM] * (chunks + 2) + [ANY] * len(more),
+            in_specs=[SMEM, SMEM] + [VMEM] * 3 + [ANY] * len(more),
             out_specs=ANY,
-            input_output_aliases={chunks + 5: 0} if chunk else {},
+            input_output_aliases={6: 0} if chunk else {},
             scratch_shapes=scratch,
             compiler_params=params(16),
             cost_estimate=pl.CostEstimate(flops=4_000_000_000, bytes_accessed=2_000_000, transcendentals=0),
             name="spread",
-        )(position[None], flat_taps, st_0, *st_1, current, *more)
-
-    (st_0,) = conv(0)
-    st_0, w_in, b_in, w_out, kernel = lax.optimization_barrier((st_0, w_in, b_in, w_out, kernel))
+        )(position[None], flat_taps, st_0, st_1, current, *more)
+
+    def weights(w):
+        return w.reshape(hidden, n_rows, n_cols, ch_dev).transpose(0, 3, 2, 1).reshape(hidden, channels)
+
+    def device(rank):
+        return rank % n_rows * n_cols + rank // n_rows
+
+    st_0 = conv(0, model)
+    st_0, model = lax.optimization_barrier((st_0, model))
     tiles_0 = exchange(st_0.reshape(n_dev, chunks, BAND, part))
-    st_1 = conv(1)
-    tiles_1 = [exchange(piece.reshape(n_dev, BAND, part)) for piece in st_1]
+    st_1 = conv(1, model)
+    st_1, w_in, b_in, w_out, kernel = lax.optimization_barrier((st_1, w_in, b_in, w_out, kernel))
+    tiles_1 = exchange(st_1.reshape(n_dev, chunks, BAND, part))
 
     b_col = b_in[:, None]
-    w_in_t = w_in.reshape(n_dev, ch_dev, hidden).transpose(2, 1, 0).reshape(hidden, channels)
-    w_out_t = w_out.reshape(hidden, n_dev, ch_dev).transpose(2, 1, 0).reshape(channels, hidden)
+    w_in_t = weights(w_in.T)
+    w_out_t = weights(w_out).T
     swap = shuffle_table()
     flat_taps = kernel.reshape(-1)
     position = lax.axis_index(("rows", "cols")).astype(jnp.int32) * ch_dev
 
     returned = []
     for q in range(chunks):
-        back = exchange(mix(q, tiles_0, tiles_1[q]))
+        back = exchange(mix(q, tiles_0, tiles_1))
         returned.append(back.reshape(bands, parts, ch_dev, BAND, part))
     result = None
     for q in range(chunks):

time: 108 us -> 96.4 us (0.89)
  blocking collectives: 20.4 us -> 0 us
  waiting for transfers between devices: 27.4 us -> 47.2 us
  local copies, waits for them, and re-layouts: 11.9 us -> 2.47 us
    all_to_all x1 -> x0, blocking collectives: 20.4 us -> none  [exchange(): lax.all_to_all(blocks, ('rows', 'cols'), split_axis=0, concat_axis=0, til...]
    all_to_all x4, waiting for transfers between devices: 27.4 us -> 47.2 us  [exchange(): lax.all_to_all(blocks, ('cols', 'rows'), split_axis=0, concat_axis=0, til...]
    unnamed x36 -> x16, local copies, waits for them, and re-layouts: 11.5 us -> 2.04 us
  transfers between devices with their start and end apart: 4 -> 4, of which waited for: 4 -> 4; matrix products, arithmetic and copies ran while one was open for 0% -> 0% of each run, Pallas kernels for 19% -> 16%
where the time goes in v3:
time: 96.4 us; the launch traced here: 95.8 us
  waiting for transfers between devices  47.2 us (49%)
  Pallas kernels  30.4 us (32%)
  starting transfers between devices  15.4 us (16%)
  local copies, waits for them, and re-layouts  2.47 us (3%)
    all_to_all x4, waiting for transfers between devices, exchange(): lax.all_to_all(blocks, ('cols', 'rows'), split_axis=0, concat_axis=0, til...  47.2 us
    all_to_all x4, starting transfers between devices, exchange(): lax.all_to_all(blocks, ('cols', 'rows'), split_axis=0, concat_axis=0, til...  15.4 us
    pallas_call x2, Pallas kernels, conv(): pl.pallas_call(lambda *refs: conv_kernel(ch, *refs), out_shape=jax.ShapeD...  14.2 us
    pallas_call x2, Pallas kernels, mix(): pl.pallas_call(lambda *refs: mix_kernel(chunk, device, *refs), out_shape=...  11 us
    pallas_call x2, Pallas kernels, spread(): pl.pallas_call(lambda *refs: spread_kernel(chunk, chunks, *refs), out_sha...  5.15 us
    unnamed x16, local copies, waits for them, and re-layouts  2.04 us
  transfers between devices with their start and end apart: 4, of which 4 were waited for; matrix products, arithmetic and copies ran while one was open for 0% of the time, Pallas kernels for 16%

profile of v3, /device:TPU:0, one launch (start us, length us, event | category | flops | bytes accessed | tf_op | source)
XLA Modules:
  0.0 95.8 jit_solution(18395012821745465261)
XLA Ops:
  0.0 7.1 %conv.2.refs_2_ = bf16[16,2,2,16,256]{4,3,2,1,0:T(8,128)(2,1)} custom-call(f32[2]{0:T(128)} %refs_0_.5, bf16[2,512,512]{2,1,0:T(8,128)(2,1)} %refs_1_.2, bf16[2,512,512]{2,1,0:T(8,128)(2,1)} %refs_2_.3, bf16[2,256,256]{2,1,0:T(8,128)(2,1)} %refs_3_.3, bf16[768,640]{1,0:T(8,128)(2,1)} %constant.18.clone.refs_4_, bf16[640,768]{1,0:T(8,128)(2,1)} %constant.19.clone.refs_5_), custom_call_target="tpu_custom_call" | custom-call | flops 4000000000 | bytes 4000000 | tf_op jit(solution)/shard_map/conv/pallas_call | solution.py:263
  7.1 7.3 %all-to-all-start = ((bf16[32,2,16,256]{3,2,1,0:T(8,128)(2,1)}), bf16[32,2,16,256]{3,2,1,0:T(8,128)(2,1)S(1)}, u32[]{:S(2)}, u32[]{:S(2)}) async-start(bf16[32,2,16,256]{3,2,1,0:T(8,128)(2,1)} %bitcast.22), calls=%async_computation | async-start | bytes 1048576 | tf_op jit(solution)/shard_map/all_to_all | solution.py:244
  14.4 7.1 %conv.3.refs_3_ = bf16[16,2,2,16,256]{4,3,2,1,0:T(8,128)(2,1)} custom-call(f32[2]{0:T(128)} %refs_0_.5, bf16[2,512,512]{2,1,0:T(8,128)(2,1)} %refs_1_.2, bf16[2,512,512]{2,1,0:T(8,128)(2,1)} %refs_2_.3, bf16[2,256,256]{2,1,0:T(8,128)(2,1)} %refs_3_.3, bf16[768,640]{1,0:T(8,128)(2,1)} %constant.18.clone.refs_4_, bf16[640,768]{1,0:T(8,128)(2,1)} %constant.19.clone.refs_5_), custom_call_target="tpu_custom_call" | custom-call | flops 4000000000 | bytes 4000000 | tf_op jit(solution)/shard_map/conv/pallas_call | solution.py:263
  21.6 9.1 %all-to-all-done.refs_5_ = bf16[32,2,16,256]{3,2,1,0:T(8,128)(2,1)S(1)} async-done(((bf16[32,2,16,256]{3,2,1,0:T(8,128)(2,1)}), bf16[32,2,16,256]{3,2,1,0:T(8,128)(2,1)S(1)}, u32[]{:S(2)}, u32[]{:S(2)}) %all-to-all-start) | async-done | bytes 524320 | tf_op jit(solution)/shard_map/all_to_all | solution.py:244
  30.7 0.0 copy-start.4
  30.7 2.7 %all-to-all-start.1 = ((bf16[32,2,16,256]{3,2,1,0:T(8,128)(2,1)}), bf16[32,2,16,256]{3,2,1,0:T(8,128)(2,1)S(1)}, u32[]{:S(2)}, u32[]{:S(2)}) async-start(bf16[32,2,16,256]{3,2,1,0:T(8,128)(2,1)} %bitcast.23), calls=%async_computation.1 | async-start | bytes 1048576 | tf_op jit(solution)/shard_map/all_to_all | solution.py:244
  33.4 0.0 copy-done.4
  33.5 0.0 copy-start.5
  33.5 0.1 copy.19.refs_2_
  33.6 0.6 copy-done.5
  34.3 0.0 copy-start.3
  34.4 0.0 copy-start.7
  34.4 0.7 copy-done.7
  35.1 0.1 copy.18.refs_1_
  35.2 0.0 copy-start.2
  35.2 14.5 %all-to-all-done.1.refs_6_ = bf16[32,2,16,256]{3,2,1,0:T(8,128)(2,1)S(1)} async-done(((bf16[32,2,16,256]{3,2,1,0:T(8,128)(2,1)}), bf16[32,2,16,256]{3,2,1,0:T(8,128)(2,1)S(1)}, u32[]{:S(2)}, u32[]{:S(2)}) %all-to-all-start.1) | async-done | bytes 524320 | tf_op jit(solution)/shard_map/all_to_all | solution.py:244
  49.7 0.0 copy-done.3
  49.7 0.0 copy-done.2
  49.7 5.5 %mix.3 = bf16[32,2,16,256]{3,2,1,0:T(8,128)(2,1)} custom-call(f32[64]{0:T(128)S(1)} %copy-done.2, f32[256,1]{1,0:T(8,128)S(1)} %copy.18.refs_1_, bf16[256,64]{1,0:T(8,128)(2,1)S(1)} %copy.19.refs_2_, bf16[64,256]{1,0:T(8,128)(2,1)S(1)} %bitcast.27, bf16[256,256]{1,0:T(8,128)(2,1)S(1)} %copy-done.3, bf16[32,2,16,256]{3,2,1,0:T(8,128)(2,1)S(1)} %all-to-all-done.refs_5_, ...), custom_call_target="tpu_custom_call" | custom-call | flops 4000000000 | bytes 2000000 | tf_op jit(solution)/shard_map/mix/pallas_call | solution.py:288
  55.2 2.8 %all-to-all-start.3 = ((bf16[32,2,16,256]{3,2,1,0:T(8,128)(2,1)}), bf16[32,2,16,256]{3,2,1,0:T(8,128)(2,1)S(1)}, u32[]{:S(2)}, u32[]{:S(2)}) async-start(bf16[32,2,16,256]{3,2,1,0:T(8,128)(2,1)} %mix.3), calls=%async_computation.3 | async-start | bytes 1048576 | tf_op jit(solution)/shard_map/all_to_all | solution.py:244
  58.0 5.5 %mix.2 = bf16[32,2,16,256]{3,2,1,0:T(8,128)(2,1)} custom-call(f32[64]{0:T(128)S(1)} %copy-done.2, f32[256,1]{1,0:T(8,128)S(1)} %copy.18.refs_1_, bf16[256,64]{1,0:T(8,128)(2,1)S(1)} %copy.19.refs_2_, bf16[64,256]{1,0:T(8,128)(2,1)S(1)} %bitcast.28, bf16[256,256]{1,0:T(8,128)(2,1)S(1)} %copy-done.3, bf16[32,2,16,256]{3,2,1,0:T(8,128)(2,1)S(1)} %all-to-all-done.refs_5_, ...), custom_call_target="tpu_custom_call" | custom-call | flops 4000000000 | bytes 2000000 | tf_op jit(solution)/shard_map/mix/pallas_call | solution.py:288
  63.5 0.0 copy-start
  63.5 10.6 %all-to-all-done.3 = bf16[32,2,16,256]{3,2,1,0:T(8,128)(2,1)S(1)} async-done(((bf16[32,2,16,256]{3,2,1,0:T(8,128)(2,1)}), bf16[32,2,16,256]{3,2,1,0:T(8,128)(2,1)S(1)}, u32[]{:S(2)}, u32[]{:S(2)}) %all-to-all-start.3) | async-done | bytes 524320 | tf_op jit(solution)/shard_map/all_to_all | solution.py:244
  74.1 2.6 %all-to-all-start.2 = ((bf16[32,2,16,256]{3,2,1,0:T(8,128)(2,1)}), bf16[32,2,16,256]{3,2,1,0:T(8,128)(2,1)S(1)}, u32[]{:S(2)}, u32[]{:S(2)}) async-start(bf16[32,2,16,256]{3,2,1,0:T(8,128)(2,1)} %mix.2), calls=%async_computation.2 | async-start | bytes 1048576 | tf_op jit(solution)/shard_map/all_to_all | solution.py:244
  76.7 0.0 copy-start.6
  76.7 0.7 copy-done.6
  77.4 0.1 reshape.27.refs_1_
  77.4 0.0 copy-done
  77.4 0.0 copy-done.1
  77.5 2.5 %spread.2.refs_6_ = bf16[2,512,512]{2,1,0:T(8,128)(2,1)} custom-call(s32[1]{0:T(128)} %bitcast.refs_0_, f32[576]{0:T(1024)S(1)} %reshape.27.refs_1_, bf16[16,2,2,16,256]{4,3,2,1,0:T(8,128)(2,1)S(1)} %copy-done, bf16[16,2,2,16,256]{4,3,2,1,0:T(8,128)(2,1)S(1)} %copy-done.1, bf16[16,2,2,16,256]{4,3,2,1,0:T(8,128)(2,1)S(1)} %bitcast.24), custom_call_target="tpu_custom_call" | custom-call | flops 4000000000 | bytes 2000000 | tf_op jit(solution)/shard_map/spread/pallas_call | solution.py:314
  79.9 13.0 %all-to-all-done.2 = bf16[32,2,16,256]{3,2,1,0:T(8,128)(2,1)S(1)} async-done(((bf16[32,2,16,256]{3,2,1,0:T(8,128)(2,1)}), bf16[32,2,16,256]{3,2,1,0:T(8,128)(2,1)S(1)}, u32[]{:S(2)}, u32[]{:S(2)}) %all-to-all-start.2) | async-done | bytes 524320 | tf_op jit(solution)/shard_map/all_to_all | solution.py:244
  92.9 2.7 %spread.3 = bf16[2,512,512]{2,1,0:T(8,128)(2,1)} custom-call(s32[1]{0:T(128)} %bitcast.refs_0_, f32[576]{0:T(1024)S(1)} %reshape.27.refs_1_, bf16[16,2,2,16,256]{4,3,2,1,0:T(8,128)(2,1)S(1)} %copy-done, bf16[16,2,2,16,256]{4,3,2,1,0:T(8,128)(2,1)S(1)} %copy-done.1, bf16[16,2,2,16,256]{4,3,2,1,0:T(8,128)(2,1)S(1)} %bitcast.26, ...), custom_call_target="tpu_custom_call", output_to_operand_aliasing={{}: (6, {})} | custom-call | flops 4000000000 | bytes 2000000 | tf_op jit(solution)/shard_map/spread/pallas_call | solution.py:314
  (7 shorter events, 0.1 us)
Async XLA Ops:
  7.1 23.6 %all-to-all-start = ((bf16[32,2,16,256]{3,2,1,0:T(8,128)(2,1)}), bf16[32,2,16,256]{3,2,1,0:T(8,128)(2,1)S(1)}, u32[]{:S(2)}, u32[]{:S(2)}) async-start(bf16[32,2,16,256]{3,2,1,0:T(8,128)(2,1)} %bitcast.22), calls=%async_computation | async-start | bytes 1048576 | tf_op jit(solution)/shard_map/all_to_all | solution.py:244
  30.7 2.7 %copy-start.4 = (bf16[64,256]{1,0:T(8,128)(2,1)S(1)}, bf16[64,256]{1,0:T(8,128)(2,1)}, u32[]{:S(2)}) copy-start(bf16[64,256]{1,0:T(8,128)(2,1)} %param.17) | copy-start | bytes 98308
  30.7 19.0 %all-to-all-start.1 = ((bf16[32,2,16,256]{3,2,1,0:T(8,128)(2,1)}), bf16[32,2,16,256]{3,2,1,0:T(8,128)(2,1)S(1)}, u32[]{:S(2)}, u32[]{:S(2)}) async-start(bf16[32,2,16,256]{3,2,1,0:T(8,128)(2,1)} %bitcast.23), calls=%async_computation.1 | async-start | bytes 1048576 | tf_op jit(solution)/shard_map/all_to_all | solution.py:244
  33.5 0.8 copy-start.5
  34.3 15.4 %copy-start.3 = (bf16[256,256]{1,0:T(8,128)(2,1)S(1)}, bf16[256,256]{1,0:T(8,128)(2,1)}, u32[]{:S(2)}) copy-start(bf16[256,256]{1,0:T(8,128)(2,1)} %constant.20.clone.refs_4_) | copy-start | bytes 393220
  34.4 0.7 copy-start.7
  35.2 14.5 %copy-start.2 = (f32[64]{0:T(128)S(1)}, f32[64]{0:T(128)}, u32[]{:S(2)}) copy-start(f32[64]{0:T(128)} %refs_0_.7) | copy-start | bytes 772
  55.2 18.9 %all-to-all-start.3 = ((bf16[32,2,16,256]{3,2,1,0:T(8,128)(2,1)}), bf16[32,2,16,256]{3,2,1,0:T(8,128)(2,1)S(1)}, u32[]{:S(2)}, u32[]{:S(2)}) async-start(bf16[32,2,16,256]{3,2,1,0:T(8,128)(2,1)} %mix.3), calls=%async_computation.3 | async-start | bytes 1048576 | tf_op jit(solution)/shard_map/all_to_all | solution.py:244
  63.5 14.0 %copy-start = (bf16[16,2,2,16,256]{4,3,2,1,0:T(8,128)(2,1)S(1)}, bf16[16,2,2,16,256]{4,3,2,1,0:T(8,128)(2,1)}, u32[]{:S(2)}) copy-start(bf16[16,2,2,16,256]{4,3,2,1,0:T(8,128)(2,1)} %conv.2.refs_2_) | copy-start | bytes 1572868
  63.5 14.0 %copy-start.1 = (bf16[16,2,2,16,256]{4,3,2,1,0:T(8,128)(2,1)S(1)}, bf16[16,2,2,16,256]{4,3,2,1,0:T(8,128)(2,1)}, u32[]{:S(2)}) copy-start(bf16[16,2,2,16,256]{4,3,2,1,0:T(8,128)(2,1)} %conv.3.refs_3_) | copy-start | bytes 1572868
  74.1 18.9 %all-to-all-start.2 = ((bf16[32,2,16,256]{3,2,1,0:T(8,128)(2,1)}), bf16[32,2,16,256]{3,2,1,0:T(8,128)(2,1)S(1)}, u32[]{:S(2)}, u32[]{:S(2)}) async-start(bf16[32,2,16,256]{3,2,1,0:T(8,128)(2,1)} %mix.2), calls=%async_computation.2 | async-start | bytes 1048576 | tf_op jit(solution)/shard_map/all_to_all | solution.py:244
  76.7 0.7 copy-start.6

commit v4 on v1

v4 whole, which is shorter than its diff:
```python
import math

import jax
import jax.numpy as jnp
import ml_dtypes
import numpy as np
from jax import lax
from jax.experimental import pallas as pl
from jax.experimental.pallas import tpu as pltpu
from jax.sharding import PartitionSpec as P

BAND = 16
MIB = 1024 * 1024
BF16, F32 = jnp.bfloat16, jnp.float32


def tables(img, psf):
    length = img + psf // 2
    half = length // 2
    pad = -half % 128
    phase = (2 * np.arange(half)[:, None] + 1) * np.arange(length)[None, :] % (2 * length)
    angle = phase * (math.pi / length)
    table = np.concatenate([np.pad(f(angle), ((pad, 0), (0, 0))) for f in (np.cos, np.sin)])
    table = np.pad(table, ((0, pad), (0, 0))).astype(ml_dtypes.bfloat16)
    return jnp.asarray(table), jnp.asarray(np.ascontiguousarray(table[pad:].T))


def shuffle_table():
    index = np.arange(BAND * BAND)
    source = (index % BAND) * BAND + index // BAND
    table = np.zeros((BAND * BAND, BAND * BAND), np.float32)
    table[index, source] = 1.0
    return jnp.asarray(table.astype(ml_dtypes.bfloat16))


def dot(a, b):
    return jnp.dot(a, b, preferred_element_type=F32)


def conv_kernel(
    rate, model_h, dirty_h, psf_h, table_h, turned_h, out_h,
    model, dirty, psf, table, turned, cols_x, cols_q, spec_x, spec_q, prod, rows_y, out, sems, out_sems,
):
    img = model.shape[1]
    taps = psf.shape[1]
    shift = taps // 2
    length = table.shape[1]
    half = length // 2
    wide = turned.shape[1] // 2
    pad = wide - half
    own = length - wide
    shared = wide - own

    def rows_of(source, target, start, count):
        return source.at[pl.ds(start, count)], target.at[pl.ds(start, count)]

    pairs = (
        (psf_h, psf),
        rows_of(turned_h, turned, 0, taps),
        (model_h.at[0], model.at[0]),
        rows_of(turned_h, turned, taps, img - taps),
        (model_h.at[1], model.at[1]),
        rows_of(table_h, table, 0, pad + wide),
        rows_of(table_h, table, pad + wide, wide),
        rows_of(turned_h, turned, img, length - img),
        (dirty_h, dirty),
    )
    copies = [pltpu.make_async_copy(*pair, sems.at[i]) for i, pair in enumerate(pairs)]
    for copy in copies:
        copy.start()

    zeros = jnp.zeros((pad, 2 * length), BF16)
    prod[half:wide, :] = zeros
    prod[wide + half :, :] = zeros

    def columns(source, depth, target, waits):
        copies[waits[0]].wait()
        copies[waits[1]].wait()
        first = dot(source[0], turned[:depth, :])
        if waits[2] is not None:
            copies[waits[2]].wait()
        second = dot(source[1], turned[:depth, :])
        for k in range(2):
            a = first[:, k * wide : (k + 1) * wide]
            b = pltpu.roll(second[:, k * wide : (k + 1) * wide], pad, 1)
            at = k * length
            target[:, at : at + own] = a[:, :own].astype(BF16)
            target[:, at + own : at + wide] = (a[:, own:] + b[:, :shared]).astype(BF16)
            target[:, at + wide : at + length] = b[:, shared:].astype(BF16)

    columns(psf, taps, cols_q, (0, 1, None))
    columns(model, img, cols_x, (2, 3, 4))

    for k in range(2):
        copies[5 + k].wait()
        source = slice(pad + k * wide, pad + k * wide + half)
        target = slice(k * half, (k + 1) * half)
        spec_q[target, :] = dot(table[source, :taps], cols_q[...])
        spec_x[target, :] = dot(table[source, :img], cols_x[...])

    @pl.loop(0, half // 32)
    def _(i):
        for u in range(2):
            at = pl.multiple_of(i * 32 + u * 16, 16)
            c, s, t = pl.ds(at, 16), pl.ds(half + at, 16), pl.ds(wide + at, 16)
            for j in range(0, length, 128):
                lc, ls = slice(j, j + 128), slice(length + j, length + j + 128)
                xcc, xcs, xsc, xss = spec_x[c, lc], spec_x[c, ls], spec_x[s, lc], spec_x[s, ls]
                qcc, qcs, qsc, qss = spec_q[c, lc], spec_q[c, ls], spec_q[s, lc], spec_q[s, ls]
                prod[c, lc] = ((xcc * qcc + xss * qss) - (xsc * qsc + xcs * qcs)).astype(BF16)
                prod[t, ls] = ((xcc * qss + xss * qcc) + (xsc * qcs + xcs * qsc)).astype(BF16)
                prod[t, lc] = ((xcc * qsc - xss * qcs) + (xsc * qcc - xcs * qss)).astype(BF16)
                prod[c, ls] = ((xcc * qcs - xss * qsc) + (xcs * qcc - xsc * qss)).astype(BF16)

    copies[7].wait()
    rows_y[...] = dot(turned[shift:, :], prod[...]).astype(BF16)

    copies[8].wait()
    bands, parts, _, band, part = out.shape
    step = 128
    sends = []
    for i in range(img // step):
        rows = slice(i * step, (i + 1) * step)
        where = slice(i * step // band, (i + 1) * step // band)
        for ch in range(2):
            at = ch * own
            inner = jnp.concatenate(
                [rows_y[rows, at : at + wide], rows_y[rows, length + at : length + at + wide]], axis=1
            )
            back = table[pad * (1 - ch) : pad * (1 - ch) + 2 * wide, shift:]
            scale = rate[ch] * (4.0 / (length * length))
            stepped = rate[ch] * dirty[ch, rows, :].astype(F32) - scale * dot(inner, back)
            stepped = (model[ch, rows, :].astype(F32) + stepped).astype(BF16)
            for p in range(parts):
                piece = stepped[:, p * part : (p + 1) * part]
                out[where, p, ch] = piece.reshape(step // band, band, part)
        sends.append(pltpu.make_async_copy(out.at[where], out_h.at[where], out_sems.at[i]))
        sends[-1].start()
    for send in sends:
        send.wait()


def mix_kernel(gain, b_in, w_in_t, w_out_t, swap, tiles, out, bias, normed, hidden, mixed):
    channels, band, part = tiles.shape
    groups = channels // band

    bias[...] = jnp.broadcast_to(b_in[...], bias.shape)
    power = jnp.zeros((band, part), F32)
    for c in range(channels):
        v = tiles[c].astype(F32)
        power = power + v * v
    inverse = lax.rsqrt(power * (1.0 / channels) + 1e-06)
    for g in range(groups):
        rows = [
            (tiles[c].astype(F32) * inverse * gain[c]).astype(BF16)
            for c in range(g * band, (g + 1) * band)
        ]
        swapped = dot(swap[...], jnp.concatenate(rows, axis=0)).astype(BF16)
        normed[:, g * band : (g + 1) * band, :] = swapped.reshape(band, band, part)

    a = math.sqrt(2.0 / math.pi)
    for r in range(band):
        inner = (dot(w_in_t[...], normed[r]) + bias[...]).astype(BF16)
        bent = inner * (BF16(a) + BF16(a * 0.044715) * (inner * inner))
        hidden[r] = inner + inner * jnp.tanh(bent)
    for r in range(band):
        mixed[r] = (0.5 * dot(w_out_t[...], hidden[r])).astype(BF16)

    for g in range(groups):
        block = mixed[:, g * band : (g + 1) * band, :].reshape(band * band, part)
        swapped = dot(swap[...], block).astype(BF16)
        out[g * band : (g + 1) * band] = swapped.reshape(band, band, part)


def spread_kernel(first, taps, stepped, mixed, out, above, middle, below, result, sems):
    channels = taps.shape[0] // 9
    bands, parts, ch_dev, band, part = stepped.shape
    img = parts * part
    group = 4
    size = group * band

    def rows_of(source, start, ch):
        pieces = [source[start : start + group, p, ch].reshape(size, part) for p in range(parts)]
        return jnp.concatenate(pieces, axis=1).astype(F32)

    zero = jnp.zeros((img // 128, 8, 128), F32)
    above[:, 0:8, :] = zero
    below[:, img : img + 8, :] = zero
    lane = lax.broadcasted_iota(jnp.int32, (size, img), 1)
    sends = []
    for ch in range(ch_dev):
        k = [[taps[(3 * i + j) * channels + first[0] + ch] for j in range(3)] for i in range(3)]

        def across(start):
            x = rows_of(mixed, start, ch)
            low = jnp.where(lane == 0, 0.0, pltpu.roll(x, 1, 1))
            high = jnp.where(lane == img - 1, 0.0, pltpu.roll(x, img - 1, 1))
            at = start * band
            for target, row, off in ((above, 0, 8), (middle, 1, 0), (below, 2, 0)):
                value = k[row][0] * low + k[row][1] * x + k[row][2] * high
                for n in range(img // 128):
                    target[n, at + off : at + off + size, :] = value[:, n * 128 : (n + 1) * 128]

        def down(start):
            at = start * band
            base = rows_of(stepped, start, ch)
            for n in range(img // 128):
                total = above[n, at + 7 : at + 7 + size, :] + below[n, at + 1 : at + 1 + size, :]
                total = total + middle[n, at : at + size, :]
                total = base[:, n * 128 : (n + 1) * 128] + total
                result[ch, at : at + size, n * 128 : (n + 1) * 128] = total.astype(BF16)

        for start in range(0, bands, group):
            across(start)
            if start:
                down(start - group)
        down(bands - group)
        sends.append(pltpu.make_async_copy(result.at[ch], out.at[ch], sems.at[ch]))
        sends[-1].start()
    for send in sends:
        send.wait()


VMEM = pl.BlockSpec(memory_space=pltpu.VMEM)
SMEM = pl.BlockSpec(memory_space=pltpu.SMEM)
HBM = pl.BlockSpec(memory_space=pltpu.HBM)


def params(mib):
    return pltpu.CompilerParams(vmem_limit_bytes=mib * MIB)


def exchange(blocks):
    return lax.all_to_all(blocks, ("rows", "cols"), split_axis=0, concat_axis=0, tiled=True)


def local(model, dirty, psf, step_size, gain, w_in, b_in, w_out, kernel):
    ch_dev, img, _ = model.shape
    psf_len = psf.shape[1]
    assert ch_dev == 2
    n_dev = lax.axis_size("rows") * lax.axis_size("cols")
    channels = gain.shape[0]
    hidden = b_in.shape[0]
    part = img * img // (n_dev * BAND)
    parts = img // part
    bands = img // BAND
    table, turned = tables(img, psf_len)
    length, wide = turned.shape[0], turned.shape[1] // 2
    blocks = (bands, parts, ch_dev, BAND, part)

    stepped = pl.pallas_call(
        conv_kernel,
        out_shape=jax.ShapeDtypeStruct(blocks, BF16),
        in_specs=[SMEM] + [HBM] * 5,
        out_specs=HBM,
        scratch_shapes=[
            pltpu.VMEM(model.shape, BF16),
            pltpu.VMEM(model.shape, BF16),
            pltpu.VMEM(psf.shape, BF16),
            pltpu.VMEM(table.shape, BF16),
            pltpu.VMEM(turned.shape, BF16),
            pltpu.VMEM((img, 2 * length), BF16),
            pltpu.VMEM((psf_len, 2 * length), BF16),
            pltpu.VMEM((length, 2 * length), F32),
            pltpu.VMEM((length, 2 * length), F32),
            pltpu.VMEM((2 * wide, 2 * length), BF16),
            pltpu.VMEM((img, 2 * length), BF16),
            pltpu.VMEM(blocks, BF16),
            pltpu.SemaphoreType.DMA((9,)),
            pltpu.SemaphoreType.DMA((img // 128,)),
        ],
        compiler_params=params(58),
        name="conv",
    )(step_size, model, dirty, psf, table, turned)
    stepped, w_in, b_in, w_out, kernel = lax.optimization_barrier((stepped, w_in, b_in, w_out, kernel))

    tiles = exchange(stepped.reshape(n_dev, ch_dev, BAND, part)).reshape(channels, BAND, part)

    mixed = pl.pallas_call(
        mix_kernel,
        out_shape=jax.ShapeDtypeStruct((channels, BAND, part), BF16),
        in_specs=[SMEM] + [VMEM] * 5,
        out_specs=VMEM,
        scratch_shapes=[
            pltpu.VMEM((hidden, part), F32),
            pltpu.VMEM((BAND, channels, part), BF16),
            pltpu.VMEM((BAND, hidden, part), BF16),
            pltpu.VMEM((BAND, channels, part), BF16),
        ],
        compiler_params=params(24),
        name="mix",
    )(gain, b_in[:, None], w_in.T, w_out.T, shuffle_table(), tiles)

    returned = exchange(mixed.reshape(n_dev, ch_dev, BAND, part)).reshape(blocks)
    position = lax.axis_index(("rows", "cols")).astype(jnp.int32) * ch_dev
    plane = pltpu.VMEM((img // 128, img + 8, 128), F32)

    return pl.pallas_call(
        spread_kernel,
        out_shape=jax.ShapeDtypeStruct((ch_dev, img, img), BF16),
        in_specs=[SMEM, SMEM, VMEM, VMEM],
        out_specs=HBM,
        scratch_shapes=[
            plane, plane, plane, pltpu.VMEM((ch_dev, img, img), BF16), pltpu.SemaphoreType.DMA((ch_dev,)),
        ],
        compiler_params=params(24),
        name="spread",
    )(position[None], kernel.reshape(-1), stepped, returned)


def solution(mesh):
    return jax.shard_map(
        local,
        mesh=mesh,
        in_specs=(
            P(("rows", "cols"), None, None),
            P(("rows", "cols"), None, None),
            P(("rows", "cols"), None, None),
            P(("rows", "cols")),
            P(),
            P(),
            P(),
            P(),
            P(),
        ),
        out_specs=P(("rows", "cols"), None, None),
        check_vma=False,
    )
```

time: 103 us -> 83.5 us (0.81)
  Pallas kernels: 35.9 us -> 17.9 us
  local copies, waits for them, and re-layouts: 5.54 us -> 0.36 us
  waiting for transfers between devices: 51.6 us -> 54.8 us
    pallas_call x1, Pallas kernels: 14.1 us -> 3.6 us  [local(): pl.pallas_call(spread_kernel, out_shape=jax.ShapeDtypeStruct((ch_dev, img...]
    pallas_call x1, Pallas kernels: 10.6 us -> 4.43 us  [local(): pl.pallas_call(mix_kernel, out_shape=jax.ShapeDtypeStruct((channels, BAND...]
    unnamed x11 -> x14, local copies, waits for them, and re-layouts: 4.07 us -> 0.04 us
    all_to_all x2, waiting for transfers between devices: 51.6 us -> 54.8 us  [exchange(): lax.all_to_all(blocks, ('rows', 'cols'), split_axis=0, concat_axis=0, til...]
    pallas_call x1, Pallas kernels: 11.2 us -> 9.82 us  [local(): pl.pallas_call(conv_kernel, out_shape=jax.ShapeDtypeStruct(blocks, BF16),...]
  transfers between devices with their start and end apart: 2 -> 2, of which waited for: 2 -> 2; matrix products, arithmetic and copies ran while one was open for 2% -> 0% of each run, Pallas kernels for 0% -> 0%
where the time goes in v4:
time: 83.5 us; the launch traced here: 83.2 us
  waiting for transfers between devices  54.8 us (66%)
  Pallas kernels  17.9 us (21%)
  starting transfers between devices  10.1 us (12%)
    all_to_all x2, waiting for transfers between devices, exchange(): lax.all_to_all(blocks, ('rows', 'cols'), split_axis=0, concat_axis=0, til...  54.8 us
    all_to_all x2, starting transfers between devices, exchange(): lax.all_to_all(blocks, ('rows', 'cols'), split_axis=0, concat_axis=0, til...  10.1 us
    pallas_call x1, Pallas kernels, local(): pl.pallas_call(conv_kernel, out_shape=jax.ShapeDtypeStruct(blocks, BF16),...  9.82 us
    pallas_call x1, Pallas kernels, local(): pl.pallas_call(mix_kernel, out_shape=jax.ShapeDtypeStruct((channels, BAND...  4.43 us
    pallas_call x1, Pallas kernels, local(): pl.pallas_call(spread_kernel, out_shape=jax.ShapeDtypeStruct((ch_dev, img...  3.6 us
  transfers between devices with their start and end apart: 2, of which 2 were waited for; matrix products, arithmetic and copies ran while one was open for 0% of the time, Pallas kernels for 0%

profile of v4, /device:TPU:0, one launch (start us, length us, event | category | flops | bytes accessed | tf_op | source)
XLA Modules:
  0.0 83.2 jit_solution(5783805546544181428)
XLA Ops:
  0.0 9.8 %conv.1.stepped = bf16[32,1,2,16,512]{4,3,2,1,0:T(8,128)(2,1)} custom-call(f32[2]{0:T(128)} %rate.1, bf16[2,512,512]{2,1,0:T(8,128)(2,1)} %model_h.1, bf16[2,512,512]{2,1,0:T(8,128)(2,1)} %dirty_h.1, bf16[2,256,256]{2,1,0:T(8,128)(2,1)} %psf_h.1, bf16[832,640]{1,0:T(8,128)(2,1)} %constant.18.clone.table_h, bf16[640,768]{1,0:T(8,128)(2,1)} %constant.19.clone.turned_h), custom_call_target="tpu_custom_call" | custom-call | tf_op jit(solution)/shard_map/conv/pallas_call | solution.py:251
  9.8 0.0 copy-start.6
  9.8 0.0 copy-start.4
  9.9 0.0 copy-start.1
  9.9 0.0 copy-start.2
  9.9 0.0 copy-start.3
  9.9 7.3 %all-to-all-start = ((bf16[32,2,16,512]{3,2,1,0:T(8,128)(2,1)}), bf16[32,2,16,512]{3,2,1,0:T(8,128)(2,1)S(1)}, u32[]{:S(2)}, u32[]{:S(2)}) async-start(bf16[32,2,16,512]{3,2,1,0:T(8,128)(2,1)} %bitcast.8), calls=%async_computation | async-start | bytes 2097152 | tf_op jit(solution)/shard_map/all_to_all | solution.py:234
  17.2 0.0 copy-done.6
  17.2 0.1 copy.15.b_in
  17.4 0.0 copy-done.4
  17.4 0.1 copy.14
  17.5 27.3 %all-to-all-done = bf16[32,2,16,512]{3,2,1,0:T(8,128)(2,1)S(1)} async-done(((bf16[32,2,16,512]{3,2,1,0:T(8,128)(2,1)}), bf16[32,2,16,512]{3,2,1,0:T(8,128)(2,1)S(1)}, u32[]{:S(2)}, u32[]{:S(2)}) %all-to-all-start) | async-done | bytes 1048608 | tf_op jit(solution)/shard_map/all_to_all | solution.py:234
  44.8 0.0 copy-done.1
  44.8 0.0 copy-done.2
  44.8 0.0 copy-done.3
  44.8 4.4 %mix.1 = bf16[64,16,512]{2,1,0:T(8,128)(2,1)} custom-call(f32[64]{0:T(128)S(1)} %copy-done.3, f32[256,1]{1,0:T(8,128)S(1)} %copy.15.b_in, bf16[256,64]{1,0:T(8,128)(2,1)S(1)} %bitcast.11, bf16[64,256]{1,0:T(8,128)(2,1)S(1)} %bitcast.12, bf16[256,256]{1,0:T(8,128)(2,1)S(1)} %copy-done.1, bf16[64,16,512]{2,1,0:T(8,128)(2,1)S(1)} %bitcast.9), custom_call_target="tpu_custom_call" | custom-call | tf_op jit(solution)/shard_map/mix/pallas_call | solution.py:279
  49.2 0.0 copy-start.5
  49.2 0.0 copy-start
  49.2 2.8 %all-to-all-start.1 = ((bf16[32,2,16,512]{3,2,1,0:T(8,128)(2,1)}), bf16[32,2,16,512]{3,2,1,0:T(8,128)(2,1)S(1)}, u32[]{:S(2)}, u32[]{:S(2)}) async-start(bf16[32,2,16,512]{3,2,1,0:T(8,128)(2,1)} %bitcast.6), calls=%async_computation.1 | async-start | bytes 2097152 | tf_op jit(solution)/shard_map/all_to_all | solution.py:234
  52.0 0.0 copy-done.5
  52.0 0.1 reshape.15.taps
  52.1 27.5 %all-to-all-done.1 = bf16[32,2,16,512]{3,2,1,0:T(8,128)(2,1)S(1)} async-done(((bf16[32,2,16,512]{3,2,1,0:T(8,128)(2,1)}), bf16[32,2,16,512]{3,2,1,0:T(8,128)(2,1)S(1)}, u32[]{:S(2)}, u32[]{:S(2)}) %all-to-all-start.1) | async-done | bytes 1048608 | tf_op jit(solution)/shard_map/all_to_all | solution.py:234
  79.6 0.0 copy-done
  79.6 3.6 %spread.1 = bf16[2,512,512]{2,1,0:T(8,128)(2,1)} custom-call(s32[1]{0:T(128)} %bitcast.first, f32[576]{0:T(1024)S(1)} %reshape.15.taps, bf16[32,1,2,16,512]{4,3,2,1,0:T(8,128)(2,1)S(1)} %copy-done, bf16[32,1,2,16,512]{4,3,2,1,0:T(8,128)(2,1)S(1)} %bitcast.10), custom_call_target="tpu_custom_call" | custom-call | tf_op jit(solution)/shard_map/spread/pallas_call | solution.py:298
Async XLA Ops:
  9.8 7.4 %copy-start.6 = (f32[256]{0:T(256)S(1)}, f32[256]{0:T(256)}, u32[]{:S(2)}) copy-start(f32[256]{0:T(256)} %param.18) | copy-start | bytes 3076
  9.8 7.5 %copy-start.4 = (bf16[64,256]{1,0:T(8,128)(2,1)S(1)}, bf16[64,256]{1,0:T(8,128)(2,1)}, u32[]{:S(2)}) copy-start(bf16[64,256]{1,0:T(8,128)(2,1)} %param.17) | copy-start | bytes 98308
  9.9 34.9 %copy-start.1 = (bf16[256,256]{1,0:T(8,128)(2,1)S(1)}, bf16[256,256]{1,0:T(8,128)(2,1)}, u32[]{:S(2)}) copy-start(bf16[256,256]{1,0:T(8,128)(2,1)} %constant.20.clone.swap) | copy-start | bytes 393220
  9.9 34.9 %copy-start.2 = (bf16[256,64]{0,1:T(8,128)(2,1)S(1)}, bf16[256,64]{0,1:T(8,128)(2,1)}, u32[]{:S(2)}) copy-start(bf16[256,64]{0,1:T(8,128)(2,1)} %param.19) | copy-start | bytes 98308
  9.9 34.9 %copy-start.3 = (f32[64]{0:T(128)S(1)}, f32[64]{0:T(128)}, u32[]{:S(2)}) copy-start(f32[64]{0:T(128)} %gain.1) | copy-start | bytes 772
  9.9 34.9 %all-to-all-start = ((bf16[32,2,16,512]{3,2,1,0:T(8,128)(2,1)}), bf16[32,2,16,512]{3,2,1,0:T(8,128)(2,1)S(1)}, u32[]{:S(2)}, u32[]{:S(2)}) async-start(bf16[32,2,16,512]{3,2,1,0:T(8,128)(2,1)} %bitcast.8), calls=%async_computation | async-start | bytes 2097152 | tf_op jit(solution)/shard_map/all_to_all | solution.py:234
  49.2 2.8 %copy-start.5 = (f32[3,3,64]{2,1,0:T(4,128)S(1)}, f32[3,3,64]{2,1,0:T(4,128)}, u32[]{:S(2)}) copy-start(f32[3,3,64]{2,1,0:T(4,128)} %param.20) | copy-start | bytes 6916
  49.2 30.4 %copy-start = (bf16[32,1,2,16,512]{4,3,2,1,0:T(8,128)(2,1)S(1)}, bf16[32,1,2,16,512]{4,3,2,1,0:T(8,128)(2,1)}, u32[]{:S(2)}) copy-start(bf16[32,1,2,16,512]{4,3,2,1,0:T(8,128)(2,1)} %conv.1.stepped) | copy-start | bytes 3145732
  49.2 30.4 %all-to-all-start.1 = ((bf16[32,2,16,512]{3,2,1,0:T(8,128)(2,1)}), bf16[32,2,16,512]{3,2,1,0:T(8,128)(2,1)S(1)}, u32[]{:S(2)}, u32[]{:S(2)}) async-start(bf16[32,2,16,512]{3,2,1,0:T(8,128)(2,1)} %bitcast.6), calls=%async_computation.1 | async-start | bytes 2097152 | tf_op jit(solution)/shard_map/all_to_all | solution.py:234

commit v5 on v4

--- a/solution.py
+++ b/solution.py
@@ -74,35 +74,35 @@
     prod[wide + half :, :] = zeros
 
     def columns(source, depth, target, waits):
-        copies[waits[0]].wait()
-        copies[waits[1]].wait()
-        first = dot(source[0], turned[:depth, :])
-        if waits[2] is not None:
-            copies[waits[2]].wait()
-        second = dot(source[1], turned[:depth, :])
-        for k in range(2):
-            a = first[:, k * wide : (k + 1) * wide]
-            b = pltpu.roll(second[:, k * wide : (k + 1) * wide], pad, 1)
-            at = k * length
-            target[:, at : at + own] = a[:, :own].astype(BF16)
-            target[:, at + own : at + wide] = (a[:, own:] + b[:, :shared]).astype(BF16)
-            target[:, at + wide : at + length] = b[:, shared:].astype(BF16)
+        step = 128
+        for wait in waits[:2]:
+            copies[wait].wait()
+        for ch in range(2):
+            if ch and waits[2] is not None:
+                copies[waits[2]].wait()
+            for m in range(0, depth, step):
+                rows = slice(m, m + step)
+                part = jnp.concatenate(
+                    [dot(source[ch, rows, :], turned[:depth, n : n + 256]) for n in range(0, 2 * wide, 256)],
+                    axis=1,
+                )
+                for k in range(2):
+                    at = k * length
+                    one = part[:, k * wide : (k + 1) * wide]
+                    if ch == 0:
+                        target[rows, at : at + wide] = one.astype(BF16)
+                    else:
+                        one = pltpu.roll(one, pad, 1)
+                        both = one[:, :shared] + target[rows, at + own : at + wide].astype(F32)
+                        target[rows, at + own : at + wide] = both.astype(BF16)
+                        target[rows, at + wide : at + length] = one[:, shared:].astype(BF16)
 
     columns(psf, taps, cols_q, (0, 1, None))
     columns(model, img, cols_x, (2, 3, 4))
 
-    for k in range(2):
-        copies[5 + k].wait()
-        source = slice(pad + k * wide, pad + k * wide + half)
-        target = slice(k * half, (k + 1) * half)
-        spec_q[target, :] = dot(table[source, :taps], cols_q[...])
-        spec_x[target, :] = dot(table[source, :img], cols_x[...])
-
-    @pl.loop(0, half // 32)
-    def _(i):
-        for u in range(2):
-            at = pl.multiple_of(i * 32 + u * 16, 16)
-            c, s, t = pl.ds(at, 16), pl.ds(half + at, 16), pl.ds(wide + at, 16)
+    def products(start, count):
+        for row in range(start, start + count, 16):
+            c, s, t = (slice(at + row, at + row + 16) for at in (0, half, wide))
             for j in range(0, length, 128):
                 lc, ls = slice(j, j + 128), slice(length + j, length + j + 128)
                 xcc, xcs, xsc, xss = spec_x[c, lc], spec_x[c, ls], spec_x[s, lc], spec_x[s, ls]
@@ -112,8 +112,24 @@
                 prod[t, lc] = ((xcc * qsc - xss * qcs) + (xsc * qcc - xcs * qss)).astype(BF16)
                 prod[c, ls] = ((xcc * qcs - xss * qsc) + (xcs * qcc - xsc * qss)).astype(BF16)
 
+    copies[5].wait()
+    copies[6].wait()
+    step = half // 2
+    for start in range(0, half, step):
+        for k in range(2):
+            source = slice(pad + k * wide + start, pad + k * wide + start + step)
+            target = slice(k * half + start, k * half + start + step)
+            for n in range(0, 2 * length, 256):
+                lanes = slice(n, n + 256)
+                spec_q[target, lanes] = dot(table[source, :taps], cols_q[:, lanes])
+                spec_x[target, lanes] = dot(table[source, :img], cols_x[:, lanes])
+        products(start, step)
+
     copies[7].wait()
-    rows_y[...] = dot(turned[shift:, :], prod[...]).astype(BF16)
+    for n in range(0, 2 * length, 256):
+        for m in range(0, img, 128):
+            back = turned[shift + m : shift + m + 128, :]
+            rows_y[m : m + 128, n : n + 256] = dot(back, prod[:, n : n + 256]).astype(BF16)
 
     copies[8].wait()
     bands, parts, _, band, part = out.shape
@@ -129,7 +145,8 @@
             )
             back = table[pad * (1 - ch) : pad * (1 - ch) + 2 * wide, shift:]
             scale = rate[ch] * (4.0 / (length * length))
-            stepped = rate[ch] * dirty[ch, rows, :].astype(F32) - scale * dot(inner, back)
+            blurred = jnp.concatenate([dot(inner, back[:, n : n + 256]) for n in range(0, img, 256)], axis=1)
+            stepped = rate[ch] * dirty[ch, rows, :].astype(F32) - scale * blurred
             stepped = (model[ch, rows, :].astype(F32) + stepped).astype(BF16)
             for p in range(parts):
                 piece = stepped[:, p * part : (p + 1) * part]
@@ -159,12 +176,17 @@
         normed[:, g * band : (g + 1) * band, :] = swapped.reshape(band, band, part)
 
     a = math.sqrt(2.0 / math.pi)
+    blocks = [slice(n, min(n + 256, part)) for n in range(0, part, 256)]
     for r in range(band):
-        inner = (dot(w_in_t[...], normed[r]) + bias[...]).astype(BF16)
-        bent = inner * (BF16(a) + BF16(a * 0.044715) * (inner * inner))
-        hidden[r] = inner + inner * jnp.tanh(bent)
+        for lanes in blocks:
+            for h in range(0, hidden.shape[1], 128):
+                rows = slice(h, h + 128)
+                inner = (dot(w_in_t[rows, :], normed[r, :, lanes]) + bias[rows, lanes]).astype(BF16)
+                bent = inner * (BF16(a) + BF16(a * 0.044715) * (inner * inner))
+                hidden[r, rows, lanes] = inner + inner * jnp.tanh(bent)
     for r in range(band):
-        mixed[r] = (0.5 * dot(w_out_t[...], hidden[r])).astype(BF16)
+        for lanes in blocks:
+            mixed[r, :, lanes] = (0.5 * dot(w_out_t[...], hidden[r, :, lanes])).astype(BF16)
 
     for g in range(groups):
         block = mixed[:, g * band : (g + 1) * band, :].reshape(band * band, part)
@@ -210,13 +232,18 @@
                 total = base[:, n * 128 : (n + 1) * 128] + total
                 result[ch, at : at + size, n * 128 : (n + 1) * 128] = total.astype(BF16)
 
+        def leave(start):
+            down(start)
+            rows = pl.ds(start * band, size)
+            at = sems.at[ch * (bands // group) + start // group]
+            sends.append(pltpu.make_async_copy(result.at[ch, rows], out.at[ch, rows], at))
+            sends[-1].start()
+
         for start in range(0, bands, group):
             across(start)
             if start:
-                down(start - group)
-        down(bands - group)
-        sends.append(pltpu.make_async_copy(result.at[ch], out.at[ch], sems.at[ch]))
-        sends[-1].start()
+                leave(start - group)
+        leave(bands - group)
     for send in sends:
         send.wait()
 
@@ -301,7 +328,8 @@
         in_specs=[SMEM, SMEM, VMEM, VMEM],
         out_specs=HBM,
         scratch_shapes=[
-            plane, plane, plane, pltpu.VMEM((ch_dev, img, img), BF16), pltpu.SemaphoreType.DMA((ch_dev,)),
+            plane, plane, plane, pltpu.VMEM((ch_dev, img, img), BF16),
+            pltpu.SemaphoreType.DMA((ch_dev * bands // 4,)),
         ],
         compiler_params=params(24),
         name="spread",

time: 83.5 us -> 82.4 us (0.987)
  Pallas kernels: 17.9 us -> 16.8 us
    pallas_call x1, Pallas kernels: 9.82 us -> 8.77 us  [local(): pl.pallas_call(conv_kernel, out_shape=jax.ShapeDtypeStruct(blocks, BF16),...]
where the time goes in v5:
time: 82.4 us; the launch traced here: 82.1 us
  waiting for transfers between devices  54.8 us (67%)
  Pallas kernels  16.8 us (20%)
  starting transfers between devices  10.1 us (12%)
    all_to_all x2, waiting for transfers between devices, exchange(): lax.all_to_all(blocks, ('rows', 'cols'), split_axis=0, concat_axis=0, til...  54.8 us
    all_to_all x2, starting transfers between devices, exchange(): lax.all_to_all(blocks, ('rows', 'cols'), split_axis=0, concat_axis=0, til...  10.1 us
    pallas_call x1, Pallas kernels, local(): pl.pallas_call(conv_kernel, out_shape=jax.ShapeDtypeStruct(blocks, BF16),...  8.77 us
    pallas_call x1, Pallas kernels, local(): pl.pallas_call(mix_kernel, out_shape=jax.ShapeDtypeStruct((channels, BAND...  4.45 us
    pallas_call x1, Pallas kernels, local(): pl.pallas_call(spread_kernel, out_shape=jax.ShapeDtypeStruct((ch_dev, img...  3.54 us
  transfers between devices with their start and end apart: 2, of which 2 were waited for; matrix products, arithmetic and copies ran while one was open for 0% of the time, Pallas kernels for 0%

profile of v5, /device:TPU:0, one launch (start us, length us, event | category | flops | bytes accessed | tf_op | source)
XLA Modules:
  0.0 82.1 jit_solution(9026034355180434951)
XLA Ops:
  0.0 8.8 %conv.1.stepped = bf16[32,1,2,16,512]{4,3,2,1,0:T(8,128)(2,1)} custom-call(f32[2]{0:T(128)} %rate.1, bf16[2,512,512]{2,1,0:T(8,128)(2,1)} %model_h.1, bf16[2,512,512]{2,1,0:T(8,128)(2,1)} %dirty_h.1, bf16[2,256,256]{2,1,0:T(8,128)(2,1)} %psf_h.1, bf16[832,640]{1,0:T(8,128)(2,1)} %constant.18.clone.table_h, bf16[640,768]{1,0:T(8,128)(2,1)} %constant.19.clone.turned_h), custom_call_target="tpu_custom_call" | custom-call | tf_op jit(solution)/shard_map/conv/pallas_call | solution.py:278
  8.8 0.0 copy-start.6
  8.8 0.0 copy-start.4
  8.8 0.0 copy-start.1
  8.8 0.0 copy-start.2
  8.8 0.0 copy-start.3
  8.8 7.3 %all-to-all-start = ((bf16[32,2,16,512]{3,2,1,0:T(8,128)(2,1)}), bf16[32,2,16,512]{3,2,1,0:T(8,128)(2,1)S(1)}, u32[]{:S(2)}, u32[]{:S(2)}) async-start(bf16[32,2,16,512]{3,2,1,0:T(8,128)(2,1)} %bitcast.8), calls=%async_computation | async-start | bytes 2097152 | tf_op jit(solution)/shard_map/all_to_all | solution.py:261
  16.1 0.0 copy-done.6
  16.2 0.1 copy.15.b_in
  16.3 0.0 copy-done.4
  16.3 0.1 copy.14
  16.4 27.3 %all-to-all-done = bf16[32,2,16,512]{3,2,1,0:T(8,128)(2,1)S(1)} async-done(((bf16[32,2,16,512]{3,2,1,0:T(8,128)(2,1)}), bf16[32,2,16,512]{3,2,1,0:T(8,128)(2,1)S(1)}, u32[]{:S(2)}, u32[]{:S(2)}) %all-to-all-start) | async-done | bytes 1048608 | tf_op jit(solution)/shard_map/all_to_all | solution.py:261
  43.7 0.0 copy-done.1
  43.7 0.0 copy-done.2
  43.7 0.0 copy-done.3
  43.7 4.5 %mix.1 = bf16[64,16,512]{2,1,0:T(8,128)(2,1)} custom-call(f32[64]{0:T(128)S(1)} %copy-done.3, f32[256,1]{1,0:T(8,128)S(1)} %copy.15.b_in, bf16[256,64]{1,0:T(8,128)(2,1)S(1)} %bitcast.11, bf16[64,256]{1,0:T(8,128)(2,1)S(1)} %bitcast.12, bf16[256,256]{1,0:T(8,128)(2,1)S(1)} %copy-done.1, bf16[64,16,512]{2,1,0:T(8,128)(2,1)S(1)} %bitcast.9), custom_call_target="tpu_custom_call" | custom-call | tf_op jit(solution)/shard_map/mix/pallas_call | solution.py:306
  48.2 0.0 copy-start.5
  48.2 0.0 copy-start
  48.2 2.8 %all-to-all-start.1 = ((bf16[32,2,16,512]{3,2,1,0:T(8,128)(2,1)}), bf16[32,2,16,512]{3,2,1,0:T(8,128)(2,1)S(1)}, u32[]{:S(2)}, u32[]{:S(2)}) async-start(bf16[32,2,16,512]{3,2,1,0:T(8,128)(2,1)} %bitcast.6), calls=%async_computation.1 | async-start | bytes 2097152 | tf_op jit(solution)/shard_map/all_to_all | solution.py:261
  51.0 0.0 copy-done.5
  51.0 0.1 reshape.15.taps
  51.1 27.5 %all-to-all-done.1 = bf16[32,2,16,512]{3,2,1,0:T(8,128)(2,1)S(1)} async-done(((bf16[32,2,16,512]{3,2,1,0:T(8,128)(2,1)}), bf16[32,2,16,512]{3,2,1,0:T(8,128)(2,1)S(1)}, u32[]{:S(2)}, u32[]{:S(2)}) %all-to-all-start.1) | async-done | bytes 1048608 | tf_op jit(solution)/shard_map/all_to_all | solution.py:261
  78.6 0.0 copy-done
  78.6 3.5 %spread.1 = bf16[2,512,512]{2,1,0:T(8,128)(2,1)} custom-call(s32[1]{0:T(128)} %bitcast.first, f32[576]{0:T(1024)S(1)} %reshape.15.taps, bf16[32,1,2,16,512]{4,3,2,1,0:T(8,128)(2,1)S(1)} %copy-done, bf16[32,1,2,16,512]{4,3,2,1,0:T(8,128)(2,1)S(1)} %bitcast.10), custom_call_target="tpu_custom_call" | custom-call | tf_op jit(solution)/shard_map/spread/pallas_call | solution.py:325
Async XLA Ops:
  8.8 7.4 %copy-start.6 = (f32[256]{0:T(256)S(1)}, f32[256]{0:T(256)}, u32[]{:S(2)}) copy-start(f32[256]{0:T(256)} %param.18) | copy-start | bytes 3076
  8.8 7.5 %copy-start.4 = (bf16[64,256]{1,0:T(8,128)(2,1)S(1)}, bf16[64,256]{1,0:T(8,128)(2,1)}, u32[]{:S(2)}) copy-start(bf16[64,256]{1,0:T(8,128)(2,1)} %param.17) | copy-start | bytes 98308
  8.8 34.9 %copy-start.1 = (bf16[256,256]{1,0:T(8,128)(2,1)S(1)}, bf16[256,256]{1,0:T(8,128)(2,1)}, u32[]{:S(2)}) copy-start(bf16[256,256]{1,0:T(8,128)(2,1)} %constant.20.clone.swap) | copy-start | bytes 393220
  8.8 34.9 %copy-start.2 = (bf16[256,64]{0,1:T(8,128)(2,1)S(1)}, bf16[256,64]{0,1:T(8,128)(2,1)}, u32[]{:S(2)}) copy-start(bf16[256,64]{0,1:T(8,128)(2,1)} %param.19) | copy-start | bytes 98308
  8.8 34.9 %copy-start.3 = (f32[64]{0:T(128)S(1)}, f32[64]{0:T(128)}, u32[]{:S(2)}) copy-start(f32[64]{0:T(128)} %gain.1) | copy-start | bytes 772
  8.8 34.9 %all-to-all-start = ((bf16[32,2,16,512]{3,2,1,0:T(8,128)(2,1)}), bf16[32,2,16,512]{3,2,1,0:T(8,128)(2,1)S(1)}, u32[]{:S(2)}, u32[]{:S(2)}) async-start(bf16[32,2,16,512]{3,2,1,0:T(8,128)(2,1)} %bitcast.8), calls=%async_computation | async-start | bytes 2097152 | tf_op jit(solution)/shard_map/all_to_all | solution.py:261
  48.2 2.8 %copy-start.5 = (f32[3,3,64]{2,1,0:T(4,128)S(1)}, f32[3,3,64]{2,1,0:T(4,128)}, u32[]{:S(2)}) copy-start(f32[3,3,64]{2,1,0:T(4,128)} %param.20) | copy-start | bytes 6916
  48.2 30.4 %copy-start = (bf16[32,1,2,16,512]{4,3,2,1,0:T(8,128)(2,1)S(1)}, bf16[32,1,2,16,512]{4,3,2,1,0:T(8,128)(2,1)}, u32[]{:S(2)}) copy-start(bf16[32,1,2,16,512]{4,3,2,1,0:T(8,128)(2,1)} %conv.1.stepped) | copy-start | bytes 3145732
  48.2 30.4 %all-to-all-start.1 = ((bf16[32,2,16,512]{3,2,1,0:T(8,128)(2,1)}), bf16[32,2,16,512]{3,2,1,0:T(8,128)(2,1)S(1)}, u32[]{:S(2)}, u32[]{:S(2)}) async-start(bf16[32,2,16,512]{3,2,1,0:T(8,128)(2,1)} %bitcast.6), calls=%async_computation.1 | async-start | bytes 2097152 | tf_op jit(solution)/shard_map/all_to_all | solution.py:261

commit v6 on v5

v6 whole, which is shorter than its diff:
```python
import math

import jax
import jax.numpy as jnp
import ml_dtypes
import numpy as np
from jax import lax
from jax.experimental import pallas as pl
from jax.experimental.pallas import tpu as pltpu
from jax.sharding import Mesh
from jax.sharding import PartitionSpec as P

BAND = 16
MIB = 1024 * 1024
BF16, F32 = jnp.bfloat16, jnp.float32


def tables(img, psf):
    length = img + psf // 2
    half = length // 2
    pad = -half % 128
    phase = (2 * np.arange(half)[:, None] + 1) * np.arange(length)[None, :] % (2 * length)
    angle = phase * (math.pi / length)
    table = np.concatenate([np.pad(f(angle), ((0, pad), (0, 0))) for f in (np.cos, np.sin)])
    table = table.astype(ml_dtypes.bfloat16)
    return jnp.asarray(table), jnp.asarray(np.ascontiguousarray(table.T))


def shuffle_table():
    index = np.arange(BAND * BAND)
    source = (index % BAND) * BAND + index // BAND
    table = np.zeros((BAND * BAND, BAND * BAND), np.float32)
    table[index, source] = 1.0
    return jnp.asarray(table.astype(ml_dtypes.bfloat16))


def dot(a, b):
    return jnp.dot(a, b, preferred_element_type=F32)


def conv_kernel(ch, rate, half_no, model_h, dirty_h, psf_h, table_h, turned_h, *refs):
    own_first = refs[0] if ch else None
    own_h, cross_h, plane_h = refs[ch : ch + 3]
    (model, dirty, psf, table, turned, cols_x, cols_q, spec_x, spec_q, prod, rows_y, plane, blocks, sems, out_sems) = (
        refs[ch + 3 :]
    )
    img = model.shape[0]
    taps = psf.shape[0]
    shift = taps // 2
    length = table.shape[1]
    half = length // 2
    wide = table.shape[0] // 2

    def rows_of(source, target, start, count):
        return source.at[pl.ds(start, count)], target.at[pl.ds(start, count)]

    pairs = (
        (psf_h.at[ch], psf),
        rows_of(turned_h, turned, 0, taps),
        (model_h.at[ch], model),
        rows_of(turned_h, turned, taps, img - taps),
        rows_of(table_h, table, 0, wide),
        rows_of(table_h, table, wide, wide),
        rows_of(turned_h, turned, img, length - img),
        (dirty_h.at[ch], dirty),
    )
    copies = [pltpu.make_async_copy(*pair, sems.at[i]) for i, pair in enumerate(pairs)]
    for copy in copies:
        copy.start()
    sends = []

    def send(source, target):
        sends.append(pltpu.make_async_copy(source, target, out_sems.at[len(sends)]))
        sends[-1].start()

    if ch:
        send(own_first, own_h.at[:, :, 0])

    zeros = jnp.zeros((wide - half, 2 * wide), BF16)
    prod[half:wide, :] = zeros
    prod[wide + half :, :] = zeros

    def columns(source, depth, target):
        for n in range(0, 2 * wide, 256):
            for m in range(0, depth, 128):
                one = dot(source[m : m + 128, :], turned[:depth, n : n + 256])
                target[m : m + 128, n : n + 256] = one.astype(BF16)

    copies[0].wait()
    copies[1].wait()
    columns(psf, taps, cols_q)
    copies[2].wait()
    copies[3].wait()
    columns(model, img, cols_x)

    def products(start, count):
        for row in range(start, start + count, 16):
            c, s, t = (slice(at + row, at + row + 16) for at in (0, half, wide))
            for j in range(0, wide, 128):
                lc, ls = slice(j, j + 128), slice(wide + j, wide + j + 128)
                xcc, xcs, xsc, xss = spec_x[c, lc], spec_x[c, ls], spec_x[s, lc], spec_x[s, ls]
                qcc, qcs, qsc, qss = spec_q[c, lc], spec_q[c, ls], spec_q[s, lc], spec_q[s, ls]
                prod[c, lc] = ((xcc * qcc + xss * qss) - (xsc * qsc + xcs * qcs)).astype(BF16)
                prod[t, ls] = ((xcc * qss + xss * qcc) + (xsc * qcs + xcs * qsc)).astype(BF16)
                prod[t, lc] = ((xcc * qsc - xss * qcs) + (xsc * qcc - xcs * qss)).astype(BF16)
                prod[c, ls] = ((xcc * qcs - xss * qsc) + (xcs * qcc - xsc * qss)).astype(BF16)

    copies[4].wait()
    copies[5].wait()
    step = half // 2
    for start in range(0, half, step):
        for k in range(2):
            source = slice(k * wide + start, k * wide + start + step)
            target = slice(k * half + start, k * half + start + step)
            for n in range(0, 2 * wide, 256):
                lanes = slice(n, n + 256)
                spec_q[target, lanes] = dot(table[source, :taps], cols_q[:, lanes])
                spec_x[target, lanes] = dot(table[source, :img], cols_x[:, lanes])
        products(start, step)

    copies[6].wait()
    for n in range(0, 2 * wide, 256):
        for m in range(0, img, 128):
            back = turned[shift + m : shift + m + 128, :]
            rows_y[m : m + 128, n : n + 256] = dot(back, prod[:, n : n + 256]).astype(BF16)

    copies[7].wait()
    bands, parts, band, part = blocks.shape[1:]
    scale = rate[ch] * (4.0 / (length * length))
    step = 128
    for i in range(img // step):
        rows = slice(i * step, (i + 1) * step)
        inner = rows_y[rows, :]
        blurred = jnp.concatenate(
            [dot(inner, table[:, shift + n : shift + n + 256]) for n in range(0, img, 256)], axis=1
        )
        stepped = rate[ch] * dirty[rows, :].astype(F32) - scale * blurred
        stepped = (model[rows, :].astype(F32) + stepped).astype(BF16)
        plane[rows, :] = stepped
        side, at = i * step // (bands * band), i * step % (bands * band) // band
        other = 1 - half_no[0] if side else half_no[0]
        for p in range(parts):
            piece = stepped[:, p * part : (p + 1) * part]
            blocks[other, at : at + step // band, p] = piece.reshape(step // band, band, part)
    send(blocks.at[1], cross_h)
    send(blocks.at[0], own_h.at[:, :, 1] if ch else own_h)
    send(plane, plane_h)
    for copy in sends:
        copy.wait()


def mix_kernel(q, gain, b_in, w_in_t, w_out_t, swap, own, cross_0, cross_1, *refs):
    earlier, refs = (refs[0], refs[1:]) if q else (None, refs)
    own_out, cross_out, bias, normed, hidden, mixed = refs
    sources, _, band, part = cross_out.shape
    channels = 4 * sources
    groups = channels // band
    lane = slice(q * part, (q + 1) * part)

    def tile(j):
        other, e, c = j // (2 * sources), j // 2 % sources, j % 2
        block = (cross_1 if c else cross_0)[e, :, lane] if other else own[e, c, :, lane]
        return block.astype(F32)

    bias[...] = jnp.broadcast_to(b_in[...], bias.shape)
    power = jnp.zeros((band, part), F32)
    for j in range(channels):
        v = tile(j)
        power = power + v * v
    inverse = lax.rsqrt(power * (1.0 / channels) + 1e-06)
    for g in range(groups):
        rows = [(tile(j) * inverse * gain[j]).astype(BF16) for j in range(g * band, (g + 1) * band)]
        swapped = dot(swap[...], jnp.concatenate(rows, axis=0)).astype(BF16)
        normed[:, g * band : (g + 1) * band, :] = swapped.reshape(band, band, part)

    a = math.sqrt(2.0 / math.pi)
    blocks = [slice(n, min(n + 256, part)) for n in range(0, part, 256)]
    for r in range(band):
        for lanes in blocks:
            for h in range(0, hidden.shape[1], 128):
                rows = slice(h, h + 128)
                inner = (dot(w_in_t[rows, :], normed[r, :, lanes]) + bias[rows, lanes]).astype(BF16)
                bent = inner * (BF16(a) + BF16(a * 0.044715) * (inner * inner))
                hidden[r, rows, lanes] = inner + inner * jnp.tanh(bent)
    for r in range(band):
        for lanes in blocks:
            mixed[r, :, lanes] = (0.5 * dot(w_out_t[...], hidden[r, :, lanes])).astype(BF16)

    if q:
        own_out[:, :q] = earlier[...]
    for g in range(groups):
        block = mixed[:, g * band : (g + 1) * band, :].reshape(band * band, part)
        swapped = dot(swap[...], block).astype(BF16).reshape(band // 2, 2, band, part)
        other, e = g // (groups // 2), g % (groups // 2) * (band // 2)
        if other:
            cross_out[e : e + band // 2] = swapped
        else:
            own_out[e : e + band // 2, q] = swapped


def spread_kernel(first, half_no, taps, plane_0, plane_1, own, *refs):
    bands, parts, chunks, ch_dev, band, part = own.shape
    cross, refs = refs[:chunks], refs[chunks:]
    out, above, middle, below, result, sems = refs
    channels = taps.shape[0] // 9
    img = parts * part * chunks
    group = 4
    size = group * band

    def rows_of(other, start, ch):
        pieces = []
        for p in range(parts):
            for q in range(chunks):
                where = slice(start, start + group)
                block = cross[q][where, p, ch] if other else own[where, p, q, ch]
                pieces.append(block.reshape(size, part))
        return jnp.concatenate(pieces, axis=1).astype(F32)

    zero = jnp.zeros((img // 128, 8, 128), F32)
    above[:, 0:8, :] = zero
    below[:, img : img + 8, :] = zero
    lane = lax.broadcasted_iota(jnp.int32, (size, img), 1)
    sends = []
    for ch in range(ch_dev):
        k = [[taps[(3 * i + j) * channels + first[0] + ch] for j in range(3)] for i in range(3)]

        def across(other, start):
            x = rows_of(other, start, ch)
            low = jnp.where(lane == 0, 0.0, pltpu.roll(x, 1, 1))
            high = jnp.where(lane == img - 1, 0.0, pltpu.roll(x, img - 1, 1))
            side = 1 - half_no[0] if other else half_no[0]
            at = side * (img // 2) + start * band
            for target, row, off in ((above, 0, 8), (middle, 1, 0), (below, 2, 0)):
                value = k[row][0] * low + k[row][1] * x + k[row][2] * high
                where = pl.ds(pl.multiple_of(at + off, 8), size)
                for n in range(img // 128):
                    target[n, where, :] = value[:, n * 128 : (n + 1) * 128]

        def leave(at):
            rows = slice(at, at + size)
            base = (plane_1 if ch else plane_0)[rows, :].astype(F32)
            for n in range(img // 128):
                total = above[n, at + 7 : at + 7 + size, :] + below[n, at + 1 : at + 1 + size, :]
                total = total + middle[n, rows, :]
                total = base[:, n * 128 : (n + 1) * 128] + total
                result[ch, rows, n * 128 : (n + 1) * 128] = total.astype(BF16)
            sem = sems.at[(ch * img + at) // size]
            sends.append(pltpu.make_async_copy(result.at[ch, pl.ds(at, size)], out.at[ch, pl.ds(at, size)], sem))
            sends[-1].start()

        for other in range(2):
            for start in range(0, bands, group):
                across(other, start)
        for at in range(0, img, size):
            leave(at)
    for send in sends:
        send.wait()


VMEM = pl.BlockSpec(memory_space=pltpu.VMEM)
SMEM = pl.BlockSpec(memory_space=pltpu.SMEM)
HBM = pl.BlockSpec(memory_space=pltpu.HBM)


def params(mib):
    return pltpu.CompilerParams(vmem_limit_bytes=mib * MIB)


def exchange(blocks):
    return lax.all_to_all(blocks, ("rows", "side"), split_axis=0, concat_axis=0, tiled=True)


def swap_halves(blocks):
    return lax.ppermute(blocks, "half", [(0, 1), (1, 0)])


def local(model, dirty, psf, step_size, gain, w_in, b_in, w_out, kernel):
    ch_dev, img, _ = model.shape
    psf_len = psf.shape[1]
    assert ch_dev == 2
    n_rows, n_side = lax.axis_size("rows"), lax.axis_size("side")
    n_half = n_rows * n_side
    channels = gain.shape[0]
    hidden = b_in.shape[0]
    part = img * img // (2 * n_half * BAND)
    parts = img // part
    bands = img // BAND // 2
    chunks = 2 if part % 256 == 0 else 1
    lanes = part // chunks
    table, turned = tables(img, psf_len)
    length, wide = turned.shape[0], table.shape[0] // 2
    half_no = lax.axis_index("half").astype(jnp.int32)

    def conv(ch, model, *own_first):
        one = jax.ShapeDtypeStruct((bands, parts, BAND, part), BF16)
        two = jax.ShapeDtypeStruct((bands, parts, 2, BAND, part), BF16)
        return pl.pallas_call(
            lambda *refs: conv_kernel(ch, *refs),
            out_shape=[two if ch else one, one, jax.ShapeDtypeStruct((img, img), BF16)],
            in_specs=[SMEM, SMEM] + [HBM] * (5 + ch),
            out_specs=[HBM] * 3,
            scratch_shapes=[
                pltpu.VMEM((img, img), BF16),
                pltpu.VMEM((img, img), BF16),
                pltpu.VMEM((psf_len, psf_len), BF16),
                pltpu.VMEM(table.shape, BF16),
                pltpu.VMEM(turned.shape, BF16),
                pltpu.VMEM((img, 2 * wide), BF16),
                pltpu.VMEM((psf_len, 2 * wide), BF16),
                pltpu.VMEM((length, 2 * wide), F32),
                pltpu.VMEM((length, 2 * wide), F32),
                pltpu.VMEM((2 * wide, 2 * wide), BF16),
                pltpu.VMEM((img, 2 * wide), BF16),
                pltpu.VMEM((img, img), BF16),
                pltpu.VMEM((2, bands, parts, BAND, part), BF16),
                pltpu.SemaphoreType.DMA((8,)),
                pltpu.SemaphoreType.DMA((4,)),
            ],
            compiler_params=params(58),
            cost_estimate=pl.CostEstimate(flops=6_000_000_000, bytes_accessed=4_000_000, transcendentals=0),
            name="conv",
        )(step_size, half_no[None], model, dirty, psf, table, turned, *own_first)

    def mix(q, *blocks):
        one = jax.ShapeDtypeStruct((n_half, ch_dev, BAND, lanes), BF16)
        own = jax.ShapeDtypeStruct((n_half, q + 1, ch_dev, BAND, lanes), BF16)
        return pl.pallas_call(
            lambda *refs: mix_kernel(q, *refs),
            out_shape=[own, one],
            in_specs=[SMEM] + [VMEM] * (4 + len(blocks)),
            out_specs=[VMEM] * 2,
            scratch_shapes=[
                pltpu.VMEM((hidden, lanes), F32),
                pltpu.VMEM((BAND, channels, lanes), BF16),
                pltpu.VMEM((BAND, hidden, lanes), BF16),
                pltpu.VMEM((BAND, channels, lanes), BF16),
            ],
            compiler_params=params(24),
            cost_estimate=pl.CostEstimate(flops=3_000_000_000, bytes_accessed=2_000_000, transcendentals=0),
            name="mix",
        )(gain, b_in[:, None], w_in.T, w_out, shuffle_table(), *blocks)

    def by_half(values):
        grid = values.reshape(n_rows, 2, n_side, ch_dev, -1).transpose(1, 0, 2, 3, 4)
        return jnp.where(half_no == 0, grid, grid[::-1]).reshape(channels, -1)

    own_first, cross_0, plane_0 = conv(0, model)
    own_first, cross_0, model = lax.optimization_barrier((own_first, cross_0, model))
    got_0 = swap_halves(cross_0.reshape(n_half, BAND, part))
    own, cross_1, plane_1 = conv(1, model, own_first)
    own, cross_1, gain, w_in, b_in, w_out, kernel = lax.optimization_barrier(
        (own, cross_1, gain, w_in, b_in, w_out, kernel)
    )
    got_1 = swap_halves(cross_1.reshape(n_half, BAND, part))
    tiles = exchange(own.reshape(n_half, ch_dev, BAND, part))
    tiles_0 = exchange(got_0)
    tiles_1 = exchange(got_1)

    gain = by_half(gain)[:, 0]
    w_in = by_half(w_in)
    w_out = by_half(w_out.T)

    earlier, returned = [], []
    for q in range(chunks):
        mixed, cross = mix(q, tiles, tiles_0, tiles_1, *earlier)
        earlier = [mixed]
        returned.append(swap_halves(cross))
    mixed = exchange(mixed).reshape(bands, parts, chunks, ch_dev, BAND, lanes)
    returned = [exchange(block).reshape(bands, parts, ch_dev, BAND, lanes) for block in returned]
    position = lax.axis_index(("rows", "half", "side")).astype(jnp.int32) * ch_dev
    scratch = pltpu.VMEM((img // 128, img + 8, 128), F32)

    return pl.pallas_call(
        spread_kernel,
        out_shape=jax.ShapeDtypeStruct((ch_dev, img, img), BF16),
        in_specs=[SMEM, SMEM, SMEM] + [VMEM] * (3 + chunks),
        out_specs=HBM,
        scratch_shapes=[
            scratch, scratch, scratch, pltpu.VMEM((ch_dev, img, img), BF16),
            pltpu.SemaphoreType.DMA((ch_dev * img // 64,)),
        ],
        compiler_params=params(24),
        name="spread",
    )(position[None], half_no[None], kernel.reshape(-1), plane_0, plane_1, mixed, *returned)


def solution(mesh):
    grid = mesh.devices
    halves = Mesh(grid.reshape(grid.shape[0], 2, grid.shape[1] // 2), ("rows", "half", "side"))
    every = ("rows", "half", "side")
    planes = P(every, None, None)
    return jax.shard_map(
        local,
        mesh=halves,
        in_specs=(planes, planes, planes, P(every), P(), P(), P(), P(), P()),
        out_specs=planes,
        check_vma=False,
    )
```

time: 82.4 us -> 147 us (1.78)
  blocking collectives: 0 us -> 23.1 us
  starting transfers between devices: 10.1 us -> 28.3 us
  waiting for transfers between devices: 54.8 us -> 67.6 us
  Pallas kernels: 16.8 us -> 25 us
  local copies, waits for them, and re-layouts: 0.36 us -> 1.96 us
    ppermute x0 -> x4, waiting for transfers between devices: none -> 48.9 us  [swap_halves(): return lax.ppermute(blocks, 'half', [(0, 1), (1, 0)])]
    all_to_all x2 -> x4, waiting for transfers between devices: 54.8 us -> 18.7 us  [exchange(): lax.all_to_all(blocks, ('rows', 'side'), split_axis=0, concat_axis=0, til...]
    all_to_all x0 -> x2, blocking collectives: none -> 23.1 us  [exchange(): lax.all_to_all(blocks, ('rows', 'side'), split_axis=0, concat_axis=0, til...]
    ppermute x0 -> x4, starting transfers between devices: none -> 13.1 us  [swap_halves(): return lax.ppermute(blocks, 'half', [(0, 1), (1, 0)])]
    pallas_call x2 -> x4, Pallas kernels: 13.2 us -> 21.4 us  [the longest x2 16.2 us: conv(): pl.pallas_call(lambda *refs: conv_kernel(ch, *refs), out_shape=[two if ch...]
    all_to_all x2 -> x4, starting transfers between devices: 10.1 us -> 15.2 us  [exchange(): lax.all_to_all(blocks, ('rows', 'side'), split_axis=0, concat_axis=0, til...]
  transfers between devices with their start and end apart: 2 -> 8, of which waited for: 2 -> 6; matrix products, arithmetic and copies ran while one was open for 0% -> 1% of each run, Pallas kernels for 0% -> 0%
where the time goes in v6:
time: 147 us; the launch traced here: 146 us
  waiting for transfers between devices  67.6 us (46%)
  starting transfers between devices  28.3 us (19%)
  Pallas kernels  25 us (17%)
  blocking collectives  23.1 us (16%)
  local copies, waits for them, and re-layouts  1.96 us (1%)
    ppermute x4, waiting for transfers between devices, swap_halves(): return lax.ppermute(blocks, 'half', [(0, 1), (1, 0)])  48.9 us
    all_to_all x2, blocking collectives, exchange(): lax.all_to_all(blocks, ('rows', 'side'), split_axis=0, concat_axis=0, til...  23.1 us
    all_to_all x4, waiting for transfers between devices, exchange(): lax.all_to_all(blocks, ('rows', 'side'), split_axis=0, concat_axis=0, til...  18.7 us
    pallas_call x2, Pallas kernels, conv(): pl.pallas_call(lambda *refs: conv_kernel(ch, *refs), out_shape=[two if ch...  16.2 us
    all_to_all x4, starting transfers between devices, exchange(): lax.all_to_all(blocks, ('rows', 'side'), split_axis=0, concat_axis=0, til...  15.2 us
    ppermute x4, starting transfers between devices, swap_halves(): return lax.ppermute(blocks, 'half', [(0, 1), (1, 0)])  13.1 us
    pallas_call x2, Pallas kernels, mix(): pl.pallas_call(lambda *refs: mix_kernel(q, *refs), out_shape=[own, one],...  5.26 us
    pallas_call x1, Pallas kernels, local(): pl.pallas_call(spread_kernel, out_shape=jax.ShapeDtypeStruct((ch_dev, img...  3.55 us
  transfers between devices with their start and end apart: 8, of which 6 were waited for; matrix products, arithmetic and copies ran while one was open for 1% of the time, Pallas kernels for 0%

profile of v6, /device:TPU:0, one launch (start us, length us, event | category | flops | bytes accessed | tf_op | source)
XLA Modules:
  0.0 146.4 jit_solution(15107067185821954142)
XLA Ops:
  0.0 6.3 %conv.2 = (bf16[16,1,16,512]{3,2,1,0:T(8,128)(2,1)}, bf16[16,1,16,512]{3,2,1,0:T(8,128)(2,1)}, bf16[512,512]{1,0:T(8,128)(2,1)}) custom-call(f32[2]{0:T(128)} %refs_0_.3, s32[1]{0:T(128)} %bitcast.1.refs_1_.half_no, bf16[2,512,512]{2,1,0:T(8,128)(2,1)} %refs_2_.2, bf16[2,512,512]{2,1,0:T(8,128)(2,1)} %refs_3_.3, bf16[2,256,256]{2,1,0:T(8,128)(2,1)} %refs_4_.5, ...), custom_call_target="tpu_custom_call" | custom-call | flops 6000000000 | bytes 4000000 | tf_op jit(solution)/shard_map/conv/pallas_call | solution.py:297
  6.4 9.8 %conv.3 = (bf16[16,1,2,16,512]{4,3,2,1,0:T(8,128)(2,1)}, bf16[16,1,16,512]{3,2,1,0:T(8,128)(2,1)}, bf16[512,512]{1,0:T(8,128)(2,1)}) custom-call(f32[2]{0:T(128)} %refs_0_.3, s32[1]{0:T(128)} %bitcast.1.refs_1_.half_no, bf16[2,512,512]{2,1,0:T(8,128)(2,1)} %refs_2_.2, bf16[2,512,512]{2,1,0:T(8,128)(2,1)} %refs_3_.3, bf16[2,256,256]{2,1,0:T(8,128)(2,1)} %refs_4_.5, ...), custom_call_target="tpu_custom_call" | custom-call | flops 6000000000 | bytes 4000000 | tf_op jit(solution)/shard_map/conv/pallas_call | solution.py:297
  16.2 4.1 %collective-permute-start.1 = (bf16[16,16,512]{2,1,0:T(8,128)(2,1)}, bf16[16,16,512]{2,1,0:T(8,128)(2,1)}, u32[]{:S(2)}, u32[]{:S(2)}) collective-permute-start(bf16[16,16,512]{2,1,0:T(8,128)(2,1)} %bitcast.31), channel_id=1, source_target_pairs={{0,4},{4,0},{1,5},{5,1},{2,6},{6,2},{3,7},{7,3},{8,12},{12,8},{9,1... | collective-permute-start | bytes 786440 | tf_op jit(solution)/shard_map/ppermute | solution.py:274
  20.3 12.2 %collective-permute-done.1 = bf16[16,16,512]{2,1,0:T(8,128)(2,1)} collective-permute-done((bf16[16,16,512]{2,1,0:T(8,128)(2,1)}, bf16[16,16,512]{2,1,0:T(8,128)(2,1)}, u32[]{:S(2)}, u32[]{:S(2)}) %collective-permute-start.1) | collective-permute-done | bytes 262176 | tf_op jit(solution)/shard_map/ppermute | solution.py:274
  32.5 4.0 %all-to-all-start.2 = ((bf16[16,16,512]{2,1,0:T(8,128)(2,1)}), bf16[16,16,512]{2,1,0:T(8,128)(2,1)S(1)}, u32[]{:S(2)}, u32[]{:S(2)}) async-start(bf16[16,16,512]{2,1,0:T(8,128)(2,1)} %collective-permute-done.1), calls=%async_computation.2 | async-start | bytes 524288 | tf_op jit(solution)/shard_map/all_to_all | solution.py:270
  36.6 3.4 %collective-permute-start = (bf16[16,16,512]{2,1,0:T(8,128)(2,1)S(1)}, bf16[16,16,512]{2,1,0:T(8,128)(2,1)S(1)}, u32[]{:S(2)}, u32[]{:S(2)}) collective-permute-start(bf16[16,16,512]{2,1,0:T(8,128)(2,1)S(1)} %bitcast.30), channel_id=1, source_target_pairs={{0,4},{4,0},{1,5},{5,1},{2,6},{6,2},{3,7},{7,3},{8,12},{12,8},{9,1... | collective-permute-start | bytes 786440 | tf_op jit(solution)/shard_map/ppermute | solution.py:274
  40.0 12.5 %collective-permute-done = bf16[16,16,512]{2,1,0:T(8,128)(2,1)S(1)} collective-permute-done((bf16[16,16,512]{2,1,0:T(8,128)(2,1)S(1)}, bf16[16,16,512]{2,1,0:T(8,128)(2,1)S(1)}, u32[]{:S(2)}, u32[]{:S(2)}) %collective-permute-start) | collective-permute-done | bytes 262176 | tf_op jit(solution)/shard_map/ppermute | solution.py:274
  52.5 0.0 all-to-all-done.2.refs_7_
  52.5 11.6 %all_to_all.30.refs_6_ = bf16[16,16,512]{2,1,0:T(8,128)(2,1)S(1)} all-to-all(bf16[16,16,512]{2,1,0:T(8,128)(2,1)S(1)} %collective-permute-done), channel_id=1, replica_groups=mesh['rows'=4,'half'=2,'side'=4] {'rows','side'}, dimensions={0} | all-to-all | bytes 524288 | tf_op jit(solution)/shard_map/all_to_all | solution.py:270
  64.2 3.7 %all-to-all-start = ((bf16[16,2,16,512]{3,2,1,0:T(8,128)(2,1)}), bf16[16,2,16,512]{3,2,1,0:T(8,128)(2,1)S(1)}, u32[]{:S(2)}, u32[]{:S(2)}) async-start(bf16[16,2,16,512]{3,2,1,0:T(8,128)(2,1)} %bitcast.8), calls=%async_computation | async-start | bytes 1048576 | tf_op jit(solution)/shard_map/all_to_all | solution.py:270
  68.0 0.0 copy-start.6
  68.0 0.0 copy-start.4
  68.0 0.1 copy.20
  68.1 0.6 copy-done.4
  68.9 0.0 copy-start.7
  68.9 0.6 copy-done.7
  69.5 0.1 reshape.37
  69.7 0.1 squeeze_reshape.3.refs_0_
  69.8 0.1 copy.23.refs_1_
  69.9 8.4 %all-to-all-done.refs_5_ = bf16[16,2,16,512]{3,2,1,0:T(8,128)(2,1)S(1)} async-done(((bf16[16,2,16,512]{3,2,1,0:T(8,128)(2,1)}), bf16[16,2,16,512]{3,2,1,0:T(8,128)(2,1)S(1)}, u32[]{:S(2)}, u32[]{:S(2)}) %all-to-all-start) | async-done | bytes 524320 | tf_op jit(solution)/shard_map/all_to_all | solution.py:270
  78.4 2.2 %mix.2 = (bf16[16,1,2,16,256]{4,3,2,1,0:T(8,128)(2,1)S(1)}, bf16[16,2,16,256]{3,2,1,0:T(8,128)(2,1)S(1)}) custom-call(f32[64]{0:T(128)S(1)} %squeeze_reshape.3.refs_0_, f32[256,1]{1,0:T(8,128)S(1)} %copy.23.refs_1_, bf16[256,64]{1,0:T(8,128)(2,1)S(1)} %bitcast.23, bf16[64,256]{1,0:T(8,128)(2,1)S(1)} %reshape.41.refs_3_, bf16[256,256]{1,0:T(8,128)(2,1)S(1)} %copy-done.2, ...), custom_call_target="tpu_custom_call" | custom-call | flops 3000000000 | bytes 2000000 | tf_op jit(solution)/shard_map/mix/pallas_call | solution.py:327
  80.6 3.0 %mix.3 = (bf16[16,2,2,16,256]{4,3,2,1,0:T(8,128)(2,1)}, bf16[16,2,16,256]{3,2,1,0:T(8,128)(2,1)S(1)}) custom-call(f32[64]{0:T(128)S(1)} %squeeze_reshape.3.refs_0_, f32[256,1]{1,0:T(8,128)S(1)} %copy.23.refs_1_, bf16[256,64]{1,0:T(8,128)(2,1)S(1)} %bitcast.24, bf16[64,256]{1,0:T(8,128)(2,1)S(1)} %reshape.41.refs_3_, bf16[256,256]{1,0:T(8,128)(2,1)S(1)} %copy-done.2, ...), custom_call_target="tpu_custom_call" | custom-call | flops 3000000000 | bytes 2000000 | tf_op jit(solution)/shard_map/mix/pallas_call | solution.py:327
  83.6 3.4 %collective-permute-start.3 = (bf16[16,2,16,256]{3,2,1,0:T(8,128)(2,1)S(1)}, bf16[16,2,16,256]{3,2,1,0:T(8,128)(2,1)}, u32[]{:S(2)}, u32[]{:S(2)}) collective-permute-start(bf16[16,2,16,256]{3,2,1,0:T(8,128)(2,1)S(1)} %get-tuple-element.44), channel_id=1, source_target_pairs={{0,4},{4,0},{1,5},{5,1},{2,6},{6,2},{3,7},{7,3},{8,12},{12,8},{9,1... | collective-permute-start | bytes 786440 | tf_op jit(solution)/shard_map/ppermute | solution.py:274
  87.0 11.2 %collective-permute-done.3 = bf16[16,2,16,256]{3,2,1,0:T(8,128)(2,1)} collective-permute-done((bf16[16,2,16,256]{3,2,1,0:T(8,128)(2,1)S(1)}, bf16[16,2,16,256]{3,2,1,0:T(8,128)(2,1)}, u32[]{:S(2)}, u32[]{:S(2)}) %collective-permute-start.3) | collective-permute-done | bytes 262176 | tf_op jit(solution)/shard_map/ppermute | solution.py:274
  98.2 3.7 %all-to-all-start.5 = ((bf16[16,2,16,256]{3,2,1,0:T(8,128)(2,1)}), bf16[16,2,16,256]{3,2,1,0:T(8,128)(2,1)S(1)}, u32[]{:S(2)}, u32[]{:S(2)}) async-start(bf16[16,2,16,256]{3,2,1,0:T(8,128)(2,1)} %collective-permute-done.3), calls=%async_computation.5 | async-start | bytes 524288 | tf_op jit(solution)/shard_map/all_to_all | solution.py:270
  101.9 2.2 %collective-permute-start.2 = (bf16[16,2,16,256]{3,2,1,0:T(8,128)(2,1)S(1)}, bf16[16,2,16,256]{3,2,1,0:T(8,128)(2,1)S(1)}, u32[]{:S(2)}, u32[]{:S(2)}) collective-permute-start(bf16[16,2,16,256]{3,2,1,0:T(8,128)(2,1)S(1)} %get-tuple-element.43), channel_id=1, source_target_pairs={{0,4},{4,0},{1,5},{5,1},{2,6},{6,2},{3,7},{7,3},{8,12},{12,8},{9,1... | collective-permute-start | bytes 786440 | tf_op jit(solution)/shard_map/ppermute | solution.py:274
  104.1 12.9 %collective-permute-done.2 = bf16[16,2,16,256]{3,2,1,0:T(8,128)(2,1)S(1)} collective-permute-done((bf16[16,2,16,256]{3,2,1,0:T(8,128)(2,1)S(1)}, bf16[16,2,16,256]{3,2,1,0:T(8,128)(2,1)S(1)}, u32[]{:S(2)}, u32[]{:S(2)}) %collective-permute-start.2) | collective-permute-done | bytes 262176 | tf_op jit(solution)/shard_map/ppermute | solution.py:274
  117.0 11.5 %all_to_all.31 = bf16[16,2,16,256]{3,2,1,0:T(8,128)(2,1)S(1)} all-to-all(bf16[16,2,16,256]{3,2,1,0:T(8,128)(2,1)S(1)} %collective-permute-done.2), channel_id=1, replica_groups=mesh['rows'=4,'half'=2,'side'=4] {'rows','side'}, dimensions={0} | all-to-all | bytes 524288 | tf_op jit(solution)/shard_map/all_to_all | solution.py:270
  128.5 3.9 %all-to-all-start.3 = ((bf16[16,2,2,16,256]{4,3,2,1,0:T(8,128)(2,1)}), bf16[16,2,2,16,256]{4,3,2,1,0:T(8,128)(2,1)S(1)}, u32[]{:S(2)}, u32[]{:S(2)}) async-start(bf16[16,2,2,16,256]{4,3,2,1,0:T(8,128)(2,1)} %get-tuple-element.42), calls=%async_computation.3 | async-start | bytes 1048576 | tf_op jit(solution)/shard_map/all_to_all | solution.py:270
  132.4 0.1 reshape.36.taps
  132.5 10.2 %all-to-all-done.3 = bf16[16,2,2,16,256]{4,3,2,1,0:T(8,128)(2,1)S(1)} async-done(((bf16[16,2,2,16,256]{4,3,2,1,0:T(8,128)(2,1)}), bf16[16,2,2,16,256]{4,3,2,1,0:T(8,128)(2,1)S(1)}, u32[]{:S(2)}, u32[]{:S(2)}) %all-to-all-start.3) | async-done | bytes 524320 | tf_op jit(solution)/shard_map/all_to_all | solution.py:270
  142.7 3.5 %spread.1 = bf16[2,512,512]{2,1,0:T(8,128)(2,1)} custom-call(s32[1]{0:T(128)} %bitcast.first, s32[1]{0:T(128)} %bitcast.1.refs_1_.half_no, f32[576]{0:T(1024)S(1)} %reshape.36.taps, bf16[512,512]{1,0:T(8,128)(2,1)S(1)} %copy-done, bf16[512,512]{1,0:T(8,128)(2,1)S(1)} %copy-done.1, bf16[16,1,2,2,16,256]{5,4,3,2,1,0:T(8,128)(2,1)S(1)} %bitcast.20, ...), custom_call_target="tpu_custom_call" | custom-call | tf_op jit(solution)/shard_map/spread/pallas_call | solution.py:373
  (24 shorter events, 0.2 us)
Async XLA Ops:
  16.2 20.4 %copy-start.8 = (bf16[16,1,16,512]{3,2,1,0:T(8,128)(2,1)S(1)}, bf16[16,1,16,512]{3,2,1,0:T(8,128)(2,1)}, u32[]{:S(2)}) copy-start(bf16[16,1,16,512]{3,2,1,0:T(8,128)(2,1)} %get-tuple-element.39) | copy-start | bytes 786436
  16.2 16.3 %collective-permute-start.1 = (bf16[16,16,512]{2,1,0:T(8,128)(2,1)}, bf16[16,16,512]{2,1,0:T(8,128)(2,1)}, u32[]{:S(2)}, u32[]{:S(2)}) collective-permute-start(bf16[16,16,512]{2,1,0:T(8,128)(2,1)} %bitcast.31), channel_id=1, source_target_pairs={{0,4},{4,0},{1,5},{5,1},{2,6},{6,2},{3,7},{7,3},{8,12},{12,8},{9,1... | collective-permute-start | bytes 786440 | tf_op jit(solution)/shard_map/ppermute | solution.py:274
  32.5 20.0 %all-to-all-start.2 = ((bf16[16,16,512]{2,1,0:T(8,128)(2,1)}), bf16[16,16,512]{2,1,0:T(8,128)(2,1)S(1)}, u32[]{:S(2)}, u32[]{:S(2)}) async-start(bf16[16,16,512]{2,1,0:T(8,128)(2,1)} %collective-permute-done.1), calls=%async_computation.2 | async-start | bytes 524288 | tf_op jit(solution)/shard_map/all_to_all | solution.py:270
  36.6 16.0 %collective-permute-start = (bf16[16,16,512]{2,1,0:T(8,128)(2,1)S(1)}, bf16[16,16,512]{2,1,0:T(8,128)(2,1)S(1)}, u32[]{:S(2)}, u32[]{:S(2)}) collective-permute-start(bf16[16,16,512]{2,1,0:T(8,128)(2,1)S(1)} %bitcast.30), channel_id=1, source_target_pairs={{0,4},{4,0},{1,5},{5,1},{2,6},{6,2},{3,7},{7,3},{8,12},{12,8},{9,1... | collective-permute-start | bytes 786440 | tf_op jit(solution)/shard_map/ppermute | solution.py:274
  64.2 3.7 %copy-start.3 = (bf16[64,256]{1,0:T(8,128)(2,1)S(1)}, bf16[64,256]{1,0:T(8,128)(2,1)}, u32[]{:S(2)}) copy-start(bf16[64,256]{1,0:T(8,128)(2,1)} %param.18) | copy-start | bytes 98308
  64.2 14.2 %all-to-all-start = ((bf16[16,2,16,512]{3,2,1,0:T(8,128)(2,1)}), bf16[16,2,16,512]{3,2,1,0:T(8,128)(2,1)S(1)}, u32[]{:S(2)}, u32[]{:S(2)}) async-start(bf16[16,2,16,512]{3,2,1,0:T(8,128)(2,1)} %bitcast.8), calls=%async_computation | async-start | bytes 1048576 | tf_op jit(solution)/shard_map/all_to_all | solution.py:270
  68.0 1.8 %copy-start.6 = (f32[256]{0:T(256)S(1)}, f32[256]{0:T(256)}, u32[]{:S(2)}) copy-start(f32[256]{0:T(256)} %param.19) | copy-start | bytes 3076
  68.0 0.8 copy-start.4
  68.9 0.7 copy-start.7
  69.5 8.9 %copy-start.2 = (bf16[256,256]{1,0:T(8,128)(2,1)S(1)}, bf16[256,256]{1,0:T(8,128)(2,1)}, u32[]{:S(2)}) copy-start(bf16[256,256]{1,0:T(8,128)(2,1)} %constant.28.clone.refs_4_) | copy-start | bytes 393220
  83.6 14.6 %collective-permute-start.3 = (bf16[16,2,16,256]{3,2,1,0:T(8,128)(2,1)S(1)}, bf16[16,2,16,256]{3,2,1,0:T(8,128)(2,1)}, u32[]{:S(2)}, u32[]{:S(2)}) collective-permute-start(bf16[16,2,16,256]{3,2,1,0:T(8,128)(2,1)S(1)} %get-tuple-element.44), channel_id=1, source_target_pairs={{0,4},{4,0},{1,5},{5,1},{2,6},{6,2},{3,7},{7,3},{8,12},{12,8},{9,1... | collective-permute-start | bytes 786440 | tf_op jit(solution)/shard_map/ppermute | solution.py:274
  98.2 34.2 %copy-start.5 = (f32[3,3,64]{2,1,0:T(4,128)S(1)}, f32[3,3,64]{2,1,0:T(4,128)}, u32[]{:S(2)}) copy-start(f32[3,3,64]{2,1,0:T(4,128)} %param.21) | copy-start | bytes 6916
  98.2 18.7 %all-to-all-start.5 = ((bf16[16,2,16,256]{3,2,1,0:T(8,128)(2,1)}), bf16[16,2,16,256]{3,2,1,0:T(8,128)(2,1)S(1)}, u32[]{:S(2)}, u32[]{:S(2)}) async-start(bf16[16,2,16,256]{3,2,1,0:T(8,128)(2,1)} %collective-permute-done.3), calls=%async_computation.5 | async-start | bytes 524288 | tf_op jit(solution)/shard_map/all_to_all | solution.py:270
  101.9 15.1 %collective-permute-start.2 = (bf16[16,2,16,256]{3,2,1,0:T(8,128)(2,1)S(1)}, bf16[16,2,16,256]{3,2,1,0:T(8,128)(2,1)S(1)}, u32[]{:S(2)}, u32[]{:S(2)}) collective-permute-start(bf16[16,2,16,256]{3,2,1,0:T(8,128)(2,1)S(1)} %get-tuple-element.43), channel_id=1, source_target_pairs={{0,4},{4,0},{1,5},{5,1},{2,6},{6,2},{3,7},{7,3},{8,12},{12,8},{9,1... | collective-permute-start | bytes 786440 | tf_op jit(solution)/shard_map/ppermute | solution.py:274
  128.5 14.2 %copy-start = (bf16[512,512]{1,0:T(8,128)(2,1)S(1)}, bf16[512,512]{1,0:T(8,128)(2,1)}, u32[]{:S(2)}) copy-start(bf16[512,512]{1,0:T(8,128)(2,1)} %get-tuple-element.32.plane_0) | copy-start | bytes 1572868
  128.5 14.2 %copy-start.1 = (bf16[512,512]{1,0:T(8,128)(2,1)S(1)}, bf16[512,512]{1,0:T(8,128)(2,1)}, u32[]{:S(2)}) copy-start(bf16[512,512]{1,0:T(8,128)(2,1)} %get-tuple-element.33.plane_1) | copy-start | bytes 1572868
  128.5 14.2 %all-to-all-start.3 = ((bf16[16,2,2,16,256]{4,3,2,1,0:T(8,128)(2,1)}), bf16[16,2,2,16,256]{4,3,2,1,0:T(8,128)(2,1)S(1)}, u32[]{:S(2)}, u32[]{:S(2)}) async-start(bf16[16,2,2,16,256]{4,3,2,1,0:T(8,128)(2,1)} %get-tuple-element.42), calls=%async_computation.3 | async-start | bytes 1048576 | tf_op jit(solution)/shard_map/all_to_all | solution.py:270

commit v7 on v5

--- a/solution.py
+++ b/solution.py
@@ -66,7 +66,7 @@
         (dirty_h, dirty),
     )
     copies = [pltpu.make_async_copy(*pair, sems.at[i]) for i, pair in enumerate(pairs)]
-    for copy in copies:
+    for copy in copies[:5]:
         copy.start()
 
     zeros = jnp.zeros((pad, 2 * length), BF16)
@@ -77,6 +77,8 @@
         step = 128
         for wait in waits[:2]:
             copies[wait].wait()
+        for copy in copies[waits[3]]:
+            copy.start()
         for ch in range(2):
             if ch and waits[2] is not None:
                 copies[waits[2]].wait()
@@ -97,8 +99,8 @@
                         target[rows, at + own : at + wide] = both.astype(BF16)
                         target[rows, at + wide : at + length] = one[:, shared:].astype(BF16)
 
-    columns(psf, taps, cols_q, (0, 1, None))
-    columns(model, img, cols_x, (2, 3, 4))
+    columns(psf, taps, cols_q, (0, 1, None, slice(5, 7)))
+    columns(model, img, cols_x, (2, 3, 4, slice(7, 9)))
 
     def products(start, count):
         for row in range(start, start + count, 16):
@@ -133,11 +135,12 @@
 
     copies[8].wait()
     bands, parts, _, band, part = out.shape
-    step = 128
     sends = []
-    for i in range(img // step):
-        rows = slice(i * step, (i + 1) * step)
-        where = slice(i * step // band, (i + 1) * step // band)
+    cuts = [*range(0, img - 63, 128), img - 64, img]
+    for i, (start, stop) in enumerate(zip(cuts, cuts[1:])):
+        step = stop - start
+        rows = slice(start, stop)
+        where = slice(start // band, stop // band)
         for ch in range(2):
             at = ch * own
             inner = jnp.concatenate(
@@ -157,11 +160,11 @@
         send.wait()
 
 
-def mix_kernel(gain, b_in, w_in_t, w_out_t, swap, tiles, out, bias, normed, hidden, mixed):
+def mix_kernel(gain, w_in_t, w_out_t, swap, tiles, out, normed, hidden, mixed):
     channels, band, part = tiles.shape
     groups = channels // band
 
-    bias[...] = jnp.broadcast_to(b_in[...], bias.shape)
+    normed[:, channels:, :] = jnp.ones((band, band, part), BF16)
     power = jnp.zeros((band, part), F32)
     for c in range(channels):
         v = tiles[c].astype(F32)
@@ -181,7 +184,7 @@
         for lanes in blocks:
             for h in range(0, hidden.shape[1], 128):
                 rows = slice(h, h + 128)
-                inner = (dot(w_in_t[rows, :], normed[r, :, lanes]) + bias[rows, lanes]).astype(BF16)
+                inner = dot(w_in_t[rows, :], normed[r, :, lanes]).astype(BF16)
                 bent = inner * (BF16(a) + BF16(a * 0.044715) * (inner * inner))
                 hidden[r, rows, lanes] = inner + inner * jnp.tanh(bent)
     for r in range(band):
@@ -208,15 +211,17 @@
     zero = jnp.zeros((img // 128, 8, 128), F32)
     above[:, 0:8, :] = zero
     below[:, img : img + 8, :] = zero
-    lane = lax.broadcasted_iota(jnp.int32, (size, img), 1)
+    lane = lax.broadcasted_iota(jnp.int32, (size, 128), 1)
     sends = []
     for ch in range(ch_dev):
         k = [[taps[(3 * i + j) * channels + first[0] + ch] for j in range(3)] for i in range(3)]
 
         def across(start):
             x = rows_of(mixed, start, ch)
-            low = jnp.where(lane == 0, 0.0, pltpu.roll(x, 1, 1))
-            high = jnp.where(lane == img - 1, 0.0, pltpu.roll(x, img - 1, 1))
+            low = pltpu.roll(x, 1, 1)
+            low = jnp.concatenate([jnp.where(lane == 0, 0.0, low[:, :128]), low[:, 128:]], axis=1)
+            high = pltpu.roll(x, img - 1, 1)
+            high = jnp.concatenate([high[:, :-128], jnp.where(lane == 127, 0.0, high[:, -128:])], axis=1)
             at = start * band
             for target, row, off in ((above, 0, 8), (middle, 1, 0), (below, 2, 0)):
                 value = k[row][0] * low + k[row][1] * x + k[row][2] * high
@@ -259,6 +264,15 @@
 
 def exchange(blocks):
     return lax.all_to_all(blocks, ("rows", "cols"), split_axis=0, concat_axis=0, tiled=True)
+
+
+def with_bias(w_in, b_in):
+    columns = []
+    for _ in range(3):
+        columns.append(lax.reduce_precision(b_in, 8, 7))
+        b_in = b_in - columns[-1]
+    bias = jnp.stack(columns, axis=1).astype(BF16)
+    return jnp.concatenate([w_in.T, jnp.pad(bias, ((0, 0), (0, BAND - 3)))], axis=1)
 
 
 def local(model, dirty, psf, step_size, gain, w_in, b_in, w_out, kernel):
@@ -294,7 +308,7 @@
             pltpu.VMEM((img, 2 * length), BF16),
             pltpu.VMEM(blocks, BF16),
             pltpu.SemaphoreType.DMA((9,)),
-            pltpu.SemaphoreType.DMA((img // 128,)),
+            pltpu.SemaphoreType.DMA((img // 128 + 1,)),
         ],
         compiler_params=params(58),
         name="conv",
@@ -306,17 +320,16 @@
     mixed = pl.pallas_call(
         mix_kernel,
         out_shape=jax.ShapeDtypeStruct((channels, BAND, part), BF16),
-        in_specs=[SMEM] + [VMEM] * 5,
+        in_specs=[SMEM] + [VMEM] * 4,
         out_specs=VMEM,
         scratch_shapes=[
-            pltpu.VMEM((hidden, part), F32),
-            pltpu.VMEM((BAND, channels, part), BF16),
+            pltpu.VMEM((BAND, channels + BAND, part), BF16),
             pltpu.VMEM((BAND, hidden, part), BF16),
             pltpu.VMEM((BAND, channels, part), BF16),
         ],
         compiler_params=params(24),
         name="mix",
-    )(gain, b_in[:, None], w_in.T, w_out.T, shuffle_table(), tiles)
+    )(gain, with_bias(w_in, b_in), w_out.T, shuffle_table(), tiles)
 
     returned = exchange(mixed.reshape(n_dev, ch_dev, BAND, part)).reshape(blocks)
     position = lax.axis_index(("rows", "cols")).astype(jnp.int32) * ch_dev

time: 82.4 us -> 82.6 us (level)
  transfers between devices with their start and end apart: 2 -> 2, of which waited for: 2 -> 2; matrix products, arithmetic and copies ran while one was open for 0% -> 1% of each run, Pallas kernels for 0% -> 0%
where the time goes in v7:
time: 82.6 us; the launch traced here: 82.3 us
  waiting for transfers between devices  54.6 us (66%)
  Pallas kernels  16.9 us (20%)
  starting transfers between devices  10.1 us (12%)
    all_to_all x2, waiting for transfers between devices, exchange(): lax.all_to_all(blocks, ('rows', 'cols'), split_axis=0, concat_axis=0, til...  54.6 us
    all_to_all x2, starting transfers between devices, exchange(): lax.all_to_all(blocks, ('rows', 'cols'), split_axis=0, concat_axis=0, til...  10.1 us
    pallas_call x1, Pallas kernels, local(): pl.pallas_call(conv_kernel, out_shape=jax.ShapeDtypeStruct(blocks, BF16),...  9.02 us
    pallas_call x1, Pallas kernels, local(): pl.pallas_call(mix_kernel, out_shape=jax.ShapeDtypeStruct((channels, BAND...  4.36 us
    pallas_call x1, Pallas kernels, local(): pl.pallas_call(spread_kernel, out_shape=jax.ShapeDtypeStruct((ch_dev, img...  3.54 us
  transfers between devices with their start and end apart: 2, of which 2 were waited for; matrix products, arithmetic and copies ran while one was open for 1% of the time, Pallas kernels for 0%

profile of v7, /device:TPU:0, one launch (start us, length us, event | category | flops | bytes accessed | tf_op | source)
XLA Modules:
  0.0 82.3 jit_solution(5094792767536591839)
XLA Ops:
  0.0 9.0 %conv.1.stepped = bf16[32,1,2,16,512]{4,3,2,1,0:T(8,128)(2,1)} custom-call(f32[2]{0:T(128)} %rate.1, bf16[2,512,512]{2,1,0:T(8,128)(2,1)} %model_h.1, bf16[2,512,512]{2,1,0:T(8,128)(2,1)} %dirty_h.1, bf16[2,256,256]{2,1,0:T(8,128)(2,1)} %psf_h.1, bf16[832,640]{1,0:T(8,128)(2,1)} %constant.21.clone.table_h, bf16[640,768]{1,0:T(8,128)(2,1)} %constant.22.clone.turned_h), custom_call_target="tpu_custom_call" | custom-call | tf_op jit(solution)/shard_map/conv/pallas_call | solution.py:292
  9.0 0.0 copy-start.6
  9.0 0.0 copy-start.4
  9.1 0.0 copy-start.1
  9.1 0.0 copy-start.2
  9.1 0.0 copy-start.3
  9.1 7.3 %all-to-all-start = ((bf16[32,2,16,512]{3,2,1,0:T(8,128)(2,1)}), bf16[32,2,16,512]{3,2,1,0:T(8,128)(2,1)S(1)}, u32[]{:S(2)}, u32[]{:S(2)}) async-start(bf16[32,2,16,512]{3,2,1,0:T(8,128)(2,1)} %bitcast.7), calls=%async_computation | async-start | bytes 2097152 | tf_op jit(solution)/shard_map/all_to_all | solution.py:266
  16.4 0.0 copy-done.6
  16.5 0.1 copy.19
  16.6 0.0 copy-done.4
  16.6 0.1 copy.18
  16.8 0.1 fusion.1.w_in_t
  16.9 27.1 %all-to-all-done = bf16[32,2,16,512]{3,2,1,0:T(8,128)(2,1)S(1)} async-done(((bf16[32,2,16,512]{3,2,1,0:T(8,128)(2,1)}), bf16[32,2,16,512]{3,2,1,0:T(8,128)(2,1)S(1)}, u32[]{:S(2)}, u32[]{:S(2)}) %all-to-all-start) | async-done | bytes 1048608 | tf_op jit(solution)/shard_map/all_to_all | solution.py:266
  44.0 0.0 copy-done.1
  44.0 0.0 copy-done.2
  44.0 0.0 copy-done.3
  44.0 4.4 %mix.1 = bf16[64,16,512]{2,1,0:T(8,128)(2,1)} custom-call(f32[64]{0:T(128)S(1)} %copy-done.3, bf16[256,80]{1,0:T(8,128)(2,1)S(1)} %fusion.1.w_in_t, bf16[64,256]{1,0:T(8,128)(2,1)S(1)} %bitcast.10, bf16[256,256]{1,0:T(8,128)(2,1)S(1)} %copy-done.1, bf16[64,16,512]{2,1,0:T(8,128)(2,1)S(1)} %bitcast.8), custom_call_target="tpu_custom_call" | custom-call | tf_op jit(solution)/shard_map/mix/pallas_call | solution.py:320
  48.4 0.0 copy-start.5
  48.4 0.0 copy-start
  48.4 2.8 %all-to-all-start.1 = ((bf16[32,2,16,512]{3,2,1,0:T(8,128)(2,1)}), bf16[32,2,16,512]{3,2,1,0:T(8,128)(2,1)S(1)}, u32[]{:S(2)}, u32[]{:S(2)}) async-start(bf16[32,2,16,512]{3,2,1,0:T(8,128)(2,1)} %bitcast.5), calls=%async_computation.1 | async-start | bytes 2097152 | tf_op jit(solution)/shard_map/all_to_all | solution.py:266
  51.2 0.0 copy-done.5
  51.2 0.1 reshape.15.taps
  51.2 27.5 %all-to-all-done.1 = bf16[32,2,16,512]{3,2,1,0:T(8,128)(2,1)S(1)} async-done(((bf16[32,2,16,512]{3,2,1,0:T(8,128)(2,1)}), bf16[32,2,16,512]{3,2,1,0:T(8,128)(2,1)S(1)}, u32[]{:S(2)}, u32[]{:S(2)}) %all-to-all-start.1) | async-done | bytes 1048608 | tf_op jit(solution)/shard_map/all_to_all | solution.py:266
  78.7 0.0 copy-done
  78.7 3.5 %spread.1 = bf16[2,512,512]{2,1,0:T(8,128)(2,1)} custom-call(s32[1]{0:T(128)} %bitcast.first, f32[576]{0:T(1024)S(1)} %reshape.15.taps, bf16[32,1,2,16,512]{4,3,2,1,0:T(8,128)(2,1)S(1)} %copy-done, bf16[32,1,2,16,512]{4,3,2,1,0:T(8,128)(2,1)S(1)} %bitcast.9), custom_call_target="tpu_custom_call" | custom-call | tf_op jit(solution)/shard_map/spread/pallas_call | solution.py:338
  (5 shorter events, 0.0 us)
Async XLA Ops:
  9.0 7.4 %copy-start.6 = (f32[256]{0:T(256)S(1)}, f32[256]{0:T(256)}, u32[]{:S(2)}) copy-start(f32[256]{0:T(256)} %param.18) | copy-start | bytes 3076
  9.0 7.6 %copy-start.4 = (bf16[64,256]{1,0:T(8,128)(2,1)S(1)}, bf16[64,256]{1,0:T(8,128)(2,1)}, u32[]{:S(2)}) copy-start(bf16[64,256]{1,0:T(8,128)(2,1)} %param.17) | copy-start | bytes 98308
  9.1 34.9 %copy-start.1 = (bf16[256,256]{1,0:T(8,128)(2,1)S(1)}, bf16[256,256]{1,0:T(8,128)(2,1)}, u32[]{:S(2)}) copy-start(bf16[256,256]{1,0:T(8,128)(2,1)} %constant.23.clone.swap) | copy-start | bytes 393220
  9.1 34.9 %copy-start.2 = (bf16[256,64]{0,1:T(8,128)(2,1)S(1)}, bf16[256,64]{0,1:T(8,128)(2,1)}, u32[]{:S(2)}) copy-start(bf16[256,64]{0,1:T(8,128)(2,1)} %param.19) | copy-start | bytes 98308
  9.1 34.9 %copy-start.3 = (f32[64]{0:T(128)S(1)}, f32[64]{0:T(128)}, u32[]{:S(2)}) copy-start(f32[64]{0:T(128)} %gain.1) | copy-start | bytes 772
  9.1 34.9 %all-to-all-start = ((bf16[32,2,16,512]{3,2,1,0:T(8,128)(2,1)}), bf16[32,2,16,512]{3,2,1,0:T(8,128)(2,1)S(1)}, u32[]{:S(2)}, u32[]{:S(2)}) async-start(bf16[32,2,16,512]{3,2,1,0:T(8,128)(2,1)} %bitcast.7), calls=%async_computation | async-start | bytes 2097152 | tf_op jit(solution)/shard_map/all_to_all | solution.py:266
  48.4 2.8 %copy-start.5 = (f32[3,3,64]{2,1,0:T(4,128)S(1)}, f32[3,3,64]{2,1,0:T(4,128)}, u32[]{:S(2)}) copy-start(f32[3,3,64]{2,1,0:T(4,128)} %param.20) | copy-start | bytes 6916
  48.4 30.4 %copy-start = (bf16[32,1,2,16,512]{4,3,2,1,0:T(8,128)(2,1)S(1)}, bf16[32,1,2,16,512]{4,3,2,1,0:T(8,128)(2,1)}, u32[]{:S(2)}) copy-start(bf16[32,1,2,16,512]{4,3,2,1,0:T(8,128)(2,1)} %conv.1.stepped) | copy-start | bytes 3145732
  48.4 30.4 %all-to-all-start.1 = ((bf16[32,2,16,512]{3,2,1,0:T(8,128)(2,1)}), bf16[32,2,16,512]{3,2,1,0:T(8,128)(2,1)S(1)}, u32[]{:S(2)}, u32[]{:S(2)}) async-start(bf16[32,2,16,512]{3,2,1,0:T(8,128)(2,1)} %bitcast.5), calls=%async_computation.1 | async-start | bytes 2097152 | tf_op jit(solution)/shard_map/all_to_all | solution.py:266

commit v8 on v7

--- a/solution.py
+++ b/solution.py
@@ -38,8 +38,8 @@
 
 
 def conv_kernel(
-    rate, model_h, dirty_h, psf_h, table_h, turned_h, out_h,
-    model, dirty, psf, table, turned, cols_x, cols_q, spec_x, spec_q, prod, rows_y, out, sems, out_sems,
+    rate_h, model_h, dirty_h, psf_h, table_h, turned_h, out_h,
+    rate, model, dirty, psf, table, turned, cols_x, cols_q, spec_x, spec_q, prod, rows_y, out, sems, out_sems,
 ):
     img = model.shape[1]
     taps = psf.shape[1]
@@ -51,23 +51,30 @@
     own = length - wide
     shared = wide - own
 
-    def rows_of(source, target, start, count):
-        return source.at[pl.ds(start, count)], target.at[pl.ds(start, count)]
-
-    pairs = (
-        (psf_h, psf),
-        rows_of(turned_h, turned, 0, taps),
-        (model_h.at[0], model.at[0]),
-        rows_of(turned_h, turned, taps, img - taps),
-        (model_h.at[1], model.at[1]),
-        rows_of(table_h, table, 0, pad + wide),
-        rows_of(table_h, table, pad + wide, wide),
-        rows_of(turned_h, turned, img, length - img),
-        (dirty_h, dirty),
-    )
-    copies = [pltpu.make_async_copy(*pair, sems.at[i]) for i, pair in enumerate(pairs)]
-    for copy in copies[:5]:
-        copy.start()
+    loads = {}
+
+    def load(name, source, target, start, count, pieces):
+        for i in range(pieces):
+            rows = pl.ds(start + i * count // pieces, count // pieces)
+            copy = pltpu.make_async_copy(source.at[rows], target.at[rows], sems.at[sum(map(len, loads.values()))])
+            copy.start()
+            loads.setdefault(name, []).append(copy)
+
+    def arrived(name):
+        for copy in loads[name]:
+            copy.wait()
+
+    load("psf", psf_h.at[0], psf.at[0], 0, taps, 1)
+    load("turned_0", turned_h, turned, 0, taps, 4)
+    load("psf", psf_h.at[1], psf.at[1], 0, taps, 1)
+    load("model_0", model_h.at[0], model.at[0], 0, img, 2)
+    load("turned_1", turned_h, turned, taps, img - taps, 2)
+    load("model_1", model_h.at[1], model.at[1], 0, img, 2)
+    load("table", table_h, table, 0, table.shape[0], 4)
+    load("rest", turned_h, turned, img, length - img, 1)
+    load("dirty", dirty_h, dirty, 0, 2, 2)
+    loads["rate"] = [pltpu.make_async_copy(rate_h, rate, sems.at[sum(map(len, loads.values()))])]
+    loads["rate"][0].start()
 
     zeros = jnp.zeros((pad, 2 * length), BF16)
     prod[half:wide, :] = zeros
@@ -75,13 +82,9 @@
 
     def columns(source, depth, target, waits):
         step = 128
-        for wait in waits[:2]:
-            copies[wait].wait()
-        for copy in copies[waits[3]]:
-            copy.start()
         for ch in range(2):
-            if ch and waits[2] is not None:
-                copies[waits[2]].wait()
+            for wait in waits[ch]:
+                arrived(wait)
             for m in range(0, depth, step):
                 rows = slice(m, m + step)
                 part = jnp.concatenate(
@@ -99,8 +102,8 @@
                         target[rows, at + own : at + wide] = both.astype(BF16)
                         target[rows, at + wide : at + length] = one[:, shared:].astype(BF16)
 
-    columns(psf, taps, cols_q, (0, 1, None, slice(5, 7)))
-    columns(model, img, cols_x, (2, 3, 4, slice(7, 9)))
+    columns(psf, taps, cols_q, (("psf", "turned_0"), ()))
+    columns(model, img, cols_x, (("model_0", "turned_1"), ("model_1",)))
 
     def products(start, count):
         for row in range(start, start + count, 16):
@@ -114,8 +117,7 @@
                 prod[t, lc] = ((xcc * qsc - xss * qcs) + (xsc * qcc - xcs * qss)).astype(BF16)
                 prod[c, ls] = ((xcc * qcs - xss * qsc) + (xcs * qcc - xsc * qss)).astype(BF16)
 
-    copies[5].wait()
-    copies[6].wait()
+    arrived("table")
     step = half // 2
     for start in range(0, half, step):
         for k in range(2):
@@ -127,20 +129,20 @@
                 spec_x[target, lanes] = dot(table[source, :img], cols_x[:, lanes])
         products(start, step)
 
-    copies[7].wait()
+    arrived("rest")
     for n in range(0, 2 * length, 256):
         for m in range(0, img, 128):
             back = turned[shift + m : shift + m + 128, :]
             rows_y[m : m + 128, n : n + 256] = dot(back, prod[:, n : n + 256]).astype(BF16)
 
-    copies[8].wait()
+    arrived("dirty")
+    arrived("rate")
     bands, parts, _, band, part = out.shape
+    step = 128
     sends = []
-    cuts = [*range(0, img - 63, 128), img - 64, img]
-    for i, (start, stop) in enumerate(zip(cuts, cuts[1:])):
-        step = stop - start
-        rows = slice(start, stop)
-        where = slice(start // band, stop // band)
+    for i in range(img // step):
+        rows = slice(i * step, (i + 1) * step)
+        where = slice(i * step // band, (i + 1) * step // band)
         for ch in range(2):
             at = ch * own
             inner = jnp.concatenate(
@@ -160,7 +162,7 @@
         send.wait()
 
 
-def mix_kernel(gain, w_in_t, w_out_t, swap, tiles, out, normed, hidden, mixed):
+def mix_kernel(gain, w_in_t, w_out_t, swap, tiles, out_h, normed, hidden, mixed, out, sems):
     channels, band, part = tiles.shape
     groups = channels // band
 
@@ -172,7 +174,7 @@
     inverse = lax.rsqrt(power * (1.0 / channels) + 1e-06)
     for g in range(groups):
         rows = [
-            (tiles[c].astype(F32) * inverse * gain[c]).astype(BF16)
+            (tiles[c].astype(F32) * inverse * gain[c : c + 1, :]).astype(BF16)
             for c in range(g * band, (g + 1) * band)
         ]
         swapped = dot(swap[...], jnp.concatenate(rows, axis=0)).astype(BF16)
@@ -191,14 +193,19 @@
         for lanes in blocks:
             mixed[r, :, lanes] = (0.5 * dot(w_out_t[...], hidden[r, :, lanes])).astype(BF16)
 
+    sends = []
     for g in range(groups):
         block = mixed[:, g * band : (g + 1) * band, :].reshape(band * band, part)
         swapped = dot(swap[...], block).astype(BF16)
-        out[g * band : (g + 1) * band] = swapped.reshape(band, band, part)
-
-
-def spread_kernel(first, taps, stepped, mixed, out, above, middle, below, result, sems):
-    channels = taps.shape[0] // 9
+        where = pl.ds(g * band, band)
+        out[where] = swapped.reshape(band, band, part)
+        sends.append(pltpu.make_async_copy(out.at[where], out_h.at[where], sems.at[g]))
+        sends[-1].start()
+    for send in sends:
+        send.wait()
+
+
+def spread_kernel(taps, stepped, mixed, out, above, middle, below, result, sems):
     bands, parts, ch_dev, band, part = stepped.shape
     img = parts * part
     group = 4
@@ -214,19 +221,22 @@
     lane = lax.broadcasted_iota(jnp.int32, (size, 128), 1)
     sends = []
     for ch in range(ch_dev):
-        k = [[taps[(3 * i + j) * channels + first[0] + ch] for j in range(3)] for i in range(3)]
+        k = [[taps[i, j, ch : ch + 1, :] for j in range(3)] for i in range(3)]
 
         def across(start):
             x = rows_of(mixed, start, ch)
-            low = pltpu.roll(x, 1, 1)
-            low = jnp.concatenate([jnp.where(lane == 0, 0.0, low[:, :128]), low[:, 128:]], axis=1)
-            high = pltpu.roll(x, img - 1, 1)
-            high = jnp.concatenate([high[:, :-128], jnp.where(lane == 127, 0.0, high[:, -128:])], axis=1)
+            low, high = pltpu.roll(x, 1, 1), pltpu.roll(x, img - 1, 1)
             at = start * band
-            for target, row, off in ((above, 0, 8), (middle, 1, 0), (below, 2, 0)):
-                value = k[row][0] * low + k[row][1] * x + k[row][2] * high
-                for n in range(img // 128):
-                    target[n, at + off : at + off + size, :] = value[:, n * 128 : (n + 1) * 128]
+            for n in range(img // 128):
+                lanes = slice(n * 128, (n + 1) * 128)
+                left, here, right = low[:, lanes], x[:, lanes], high[:, lanes]
+                if n == 0:
+                    left = jnp.where(lane == 0, 0.0, left)
+                if n == img // 128 - 1:
+                    right = jnp.where(lane == 127, 0.0, right)
+                for target, row, off in ((above, 0, 8), (middle, 1, 0), (below, 2, 0)):
+                    value = k[row][0] * left + k[row][1] * here + k[row][2] * right
+                    target[n, at + off : at + off + size, :] = value
 
         def down(start):
             at = start * band
@@ -292,9 +302,10 @@
     stepped = pl.pallas_call(
         conv_kernel,
         out_shape=jax.ShapeDtypeStruct(blocks, BF16),
-        in_specs=[SMEM] + [HBM] * 5,
+        in_specs=[HBM] * 6,
         out_specs=HBM,
         scratch_shapes=[
+            pltpu.SMEM(step_size.shape, F32),
             pltpu.VMEM(model.shape, BF16),
             pltpu.VMEM(model.shape, BF16),
             pltpu.VMEM(psf.shape, BF16),
@@ -307,38 +318,44 @@
             pltpu.VMEM((2 * wide, 2 * length), BF16),
             pltpu.VMEM((img, 2 * length), BF16),
             pltpu.VMEM(blocks, BF16),
-            pltpu.SemaphoreType.DMA((9,)),
-            pltpu.SemaphoreType.DMA((img // 128 + 1,)),
+            pltpu.SemaphoreType.DMA((20,)),
+            pltpu.SemaphoreType.DMA((img // 128,)),
         ],
         compiler_params=params(58),
         name="conv",
     )(step_size, model, dirty, psf, table, turned)
-    stepped, w_in, b_in, w_out, kernel = lax.optimization_barrier((stepped, w_in, b_in, w_out, kernel))
+    stepped, gain, w_in, b_in, w_out, kernel = lax.optimization_barrier(
+        (stepped, gain, w_in, b_in, w_out, kernel)
+    )
 
     tiles = exchange(stepped.reshape(n_dev, ch_dev, BAND, part)).reshape(channels, BAND, part)
 
     mixed = pl.pallas_call(
         mix_kernel,
         out_shape=jax.ShapeDtypeStruct((channels, BAND, part), BF16),
-        in_specs=[SMEM] + [VMEM] * 4,
-        out_specs=VMEM,
+        in_specs=[VMEM] * 5,
+        out_specs=HBM,
         scratch_shapes=[
             pltpu.VMEM((BAND, channels + BAND, part), BF16),
             pltpu.VMEM((BAND, hidden, part), BF16),
             pltpu.VMEM((BAND, channels, part), BF16),
+            pltpu.VMEM((channels, BAND, part), BF16),
+            pltpu.SemaphoreType.DMA((channels // BAND,)),
         ],
         compiler_params=params(24),
         name="mix",
-    )(gain, with_bias(w_in, b_in), w_out.T, shuffle_table(), tiles)
+    )(jnp.broadcast_to(gain[:, None], (channels, part)), with_bias(w_in, b_in), w_out.T, shuffle_table(), tiles)
 
     returned = exchange(mixed.reshape(n_dev, ch_dev, BAND, part)).reshape(blocks)
     position = lax.axis_index(("rows", "cols")).astype(jnp.int32) * ch_dev
+    taps = lax.dynamic_slice_in_dim(kernel, position, ch_dev, axis=2)
+    taps = jnp.broadcast_to(taps[..., None], (3, 3, ch_dev, 128))
     plane = pltpu.VMEM((img // 128, img + 8, 128), F32)
 
     return pl.pallas_call(
         spread_kernel,
         out_shape=jax.ShapeDtypeStruct((ch_dev, img, img), BF16),
-        in_specs=[SMEM, SMEM, VMEM, VMEM],
+        in_specs=[VMEM] * 3,
         out_specs=HBM,
         scratch_shapes=[
             plane, plane, plane, pltpu.VMEM((ch_dev, img, img), BF16),
@@ -346,7 +363,7 @@
         ],
         compiler_params=params(24),
         name="spread",
-    )(position[None], kernel.reshape(-1), stepped, returned)
+    )(taps, stepped, returned)
 
 
 def solution(mesh):

time: 82.6 us -> 80.9 us (0.979)
  Pallas kernels: 16.9 us -> 15.1 us
where the time goes in v8:
time: 80.9 us; the launch traced here: 80.6 us
  waiting for transfers between devices  54.6 us (67%)
  Pallas kernels  15.1 us (19%)
  starting transfers between devices  10.1 us (12%)
    all_to_all x2, waiting for transfers between devices, exchange(): lax.all_to_all(blocks, ('rows', 'cols'), split_axis=0, concat_axis=0, til...  54.6 us
    all_to_all x2, starting transfers between devices, exchange(): lax.all_to_all(blocks, ('rows', 'cols'), split_axis=0, concat_axis=0, til...  10.1 us
    pallas_call x1, Pallas kernels, local(): pl.pallas_call(conv_kernel, out_shape=jax.ShapeDtypeStruct(blocks, BF16),...  8.32 us
    pallas_call x1, Pallas kernels, local(): pl.pallas_call(mix_kernel, out_shape=jax.ShapeDtypeStruct((channels, BAND...  3.71 us
    pallas_call x1, Pallas kernels, local(): pl.pallas_call(spread_kernel, out_shape=jax.ShapeDtypeStruct((ch_dev, img...  3.04 us
  transfers between devices with their start and end apart: 2, of which 2 were waited for; matrix products, arithmetic and copies ran while one was open for 1% of the time, Pallas kernels for 0%

profile of v8, /device:TPU:0, one launch (start us, length us, event | category | flops | bytes accessed | tf_op | source)
XLA Modules:
  0.0 80.6 jit_solution(12190550728146293411)
XLA Ops:
  0.0 0.0 copy-start
  0.0 8.3 %conv.1.stepped = bf16[32,1,2,16,512]{4,3,2,1,0:T(8,128)(2,1)} custom-call(f32[2]{0:T(128)} %rate_h.1, bf16[2,512,512]{2,1,0:T(8,128)(2,1)} %model_h.1, bf16[2,512,512]{2,1,0:T(8,128)(2,1)} %dirty_h.1, bf16[2,256,256]{2,1,0:T(8,128)(2,1)} %psf_h.1, bf16[832,640]{1,0:T(8,128)(2,1)} %constant.24.clone.table_h, bf16[640,768]{1,0:T(8,128)(2,1)} %constant.25.clone.turned_h), custom_call_target="tpu_custom_call" | custom-call | tf_op jit(solution)/shard_map/conv/pallas_call | solution.py:302
  8.3 0.0 copy-start.5
  8.3 0.0 copy-start.4
  8.4 0.0 copy-start.6
  8.4 0.0 copy-start.2
  8.4 0.0 copy-start.3
  8.4 7.3 %all-to-all-start = ((bf16[32,2,16,512]{3,2,1,0:T(8,128)(2,1)}), bf16[32,2,16,512]{3,2,1,0:T(8,128)(2,1)S(1)}, u32[]{:S(2)}, u32[]{:S(2)}) async-start(bf16[32,2,16,512]{3,2,1,0:T(8,128)(2,1)} %bitcast.6), calls=%async_computation | async-start | bytes 2097152 | tf_op jit(solution)/shard_map/all_to_all | solution.py:276
  15.7 0.0 copy-done.5
  15.8 0.1 copy.19
  15.9 0.0 copy-done.4
  15.9 0.1 copy.18
  16.0 0.1 fusion.1.w_in_t
  16.2 27.1 %all-to-all-done = bf16[32,2,16,512]{3,2,1,0:T(8,128)(2,1)S(1)} async-done(((bf16[32,2,16,512]{3,2,1,0:T(8,128)(2,1)}), bf16[32,2,16,512]{3,2,1,0:T(8,128)(2,1)S(1)}, u32[]{:S(2)}, u32[]{:S(2)}) %all-to-all-start) | async-done | bytes 1048608 | tf_op jit(solution)/shard_map/all_to_all | solution.py:276
  43.3 0.0 copy-done.6
  43.3 0.1 broadcast_in_dim.5.gain
  43.4 0.0 copy-done.2
  43.4 0.0 copy-done.3
  43.4 3.7 %mix.1 = bf16[64,16,512]{2,1,0:T(8,128)(2,1)} custom-call(f32[64,512]{1,0:T(8,128)S(1)} %broadcast_in_dim.5.gain, bf16[256,80]{1,0:T(8,128)(2,1)S(1)} %fusion.1.w_in_t, bf16[64,256]{1,0:T(8,128)(2,1)S(1)} %bitcast.9, bf16[256,256]{1,0:T(8,128)(2,1)S(1)} %copy-done.2, bf16[64,16,512]{2,1,0:T(8,128)(2,1)S(1)} %bitcast.7), custom_call_target="tpu_custom_call" | custom-call | tf_op jit(solution)/shard_map/mix/pallas_call | solution.py:333
  47.1 0.0 copy-start.1
  47.1 2.8 %all-to-all-start.1 = ((bf16[32,2,16,512]{3,2,1,0:T(8,128)(2,1)}), bf16[32,2,16,512]{3,2,1,0:T(8,128)(2,1)S(1)}, u32[]{:S(2)}, u32[]{:S(2)}) async-start(bf16[32,2,16,512]{3,2,1,0:T(8,128)(2,1)} %bitcast.4), calls=%async_computation.1 | async-start | bytes 2097152 | tf_op jit(solution)/shard_map/all_to_all | solution.py:276
  49.9 0.0 copy-done
  49.9 0.1 constant_dynamic-slice_fusion
  50.0 27.5 %all-to-all-done.1 = bf16[32,2,16,512]{3,2,1,0:T(8,128)(2,1)S(1)} async-done(((bf16[32,2,16,512]{3,2,1,0:T(8,128)(2,1)}), bf16[32,2,16,512]{3,2,1,0:T(8,128)(2,1)S(1)}, u32[]{:S(2)}, u32[]{:S(2)}) %all-to-all-start.1) | async-done | bytes 1048608 | tf_op jit(solution)/shard_map/all_to_all | solution.py:276
  77.5 0.1 broadcast_in_dim.4.taps
  77.6 0.0 copy-done.1
  77.6 3.0 %spread.1 = bf16[2,512,512]{2,1,0:T(8,128)(2,1)} custom-call(f32[3,3,2,128]{3,2,1,0:T(2,128)S(1)} %broadcast_in_dim.4.taps, bf16[32,1,2,16,512]{4,3,2,1,0:T(8,128)(2,1)S(1)} %copy-done.1, bf16[32,1,2,16,512]{4,3,2,1,0:T(8,128)(2,1)S(1)} %bitcast.8), custom_call_target="tpu_custom_call" | custom-call | tf_op jit(solution)/shard_map/spread/pallas_call | solution.py:355
  (5 shorter events, 0.0 us)
Async XLA Ops:
  0.0 49.9 %copy-start = (f32[3,3,64]{2,1,0:T(4,128)S(1)}, f32[3,3,64]{2,1,0:T(4,128)}, u32[]{:S(2)}) copy-start(f32[3,3,64]{2,1,0:T(4,128)} %param.20) | copy-start | bytes 6916
  8.3 7.4 %copy-start.5 = (f32[256]{0:T(256)S(1)}, f32[256]{0:T(256)}, u32[]{:S(2)}) copy-start(f32[256]{0:T(256)} %param.18) | copy-start | bytes 3076
  8.3 7.6 %copy-start.4 = (bf16[64,256]{1,0:T(8,128)(2,1)S(1)}, bf16[64,256]{1,0:T(8,128)(2,1)}, u32[]{:S(2)}) copy-start(bf16[64,256]{1,0:T(8,128)(2,1)} %param.17) | copy-start | bytes 98308
  8.4 34.9 %copy-start.6 = (f32[64]{0:T(128)S(1)}, f32[64]{0:T(128)}, u32[]{:S(2)}) copy-start(f32[64]{0:T(128)} %param.16) | copy-start | bytes 772
  8.4 35.0 %copy-start.2 = (bf16[256,256]{1,0:T(8,128)(2,1)S(1)}, bf16[256,256]{1,0:T(8,128)(2,1)}, u32[]{:S(2)}) copy-start(bf16[256,256]{1,0:T(8,128)(2,1)} %constant.26.clone.swap) | copy-start | bytes 393220
  8.4 35.0 %copy-start.3 = (bf16[256,64]{0,1:T(8,128)(2,1)S(1)}, bf16[256,64]{0,1:T(8,128)(2,1)}, u32[]{:S(2)}) copy-start(bf16[256,64]{0,1:T(8,128)(2,1)} %param.19) | copy-start | bytes 98308
  8.4 34.9 %all-to-all-start = ((bf16[32,2,16,512]{3,2,1,0:T(8,128)(2,1)}), bf16[32,2,16,512]{3,2,1,0:T(8,128)(2,1)S(1)}, u32[]{:S(2)}, u32[]{:S(2)}) async-start(bf16[32,2,16,512]{3,2,1,0:T(8,128)(2,1)} %bitcast.6), calls=%async_computation | async-start | bytes 2097152 | tf_op jit(solution)/shard_map/all_to_all | solution.py:276
  47.1 30.5 %copy-start.1 = (bf16[32,1,2,16,512]{4,3,2,1,0:T(8,128)(2,1)S(1)}, bf16[32,1,2,16,512]{4,3,2,1,0:T(8,128)(2,1)}, u32[]{:S(2)}) copy-start(bf16[32,1,2,16,512]{4,3,2,1,0:T(8,128)(2,1)} %conv.1.stepped) | copy-start | bytes 3145732
  47.1 30.4 %all-to-all-start.1 = ((bf16[32,2,16,512]{3,2,1,0:T(8,128)(2,1)}), bf16[32,2,16,512]{3,2,1,0:T(8,128)(2,1)S(1)}, u32[]{:S(2)}, u32[]{:S(2)}) async-start(bf16[32,2,16,512]{3,2,1,0:T(8,128)(2,1)} %bitcast.4), calls=%async_computation.1 | async-start | bytes 2097152 | tf_op jit(solution)/shard_map/all_to_all | solution.py:276

commit v9 on v8

--- a/solution.py
+++ b/solution.py
@@ -1,3 +1,4 @@
+import functools
 import math
 
 import jax
@@ -10,6 +11,7 @@
 from jax.sharding import PartitionSpec as P
 
 BAND = 16
+GROUP = 64
 MIB = 1024 * 1024
 BF16, F32 = jnp.bfloat16, jnp.float32
 
@@ -17,12 +19,11 @@
 def tables(img, psf):
     length = img + psf // 2
     half = length // 2
-    pad = -half % 128
     phase = (2 * np.arange(half)[:, None] + 1) * np.arange(length)[None, :] % (2 * length)
-    angle = phase * (math.pi / length)
-    table = np.concatenate([np.pad(f(angle), ((pad, 0), (0, 0))) for f in (np.cos, np.sin)])
-    table = np.pad(table, ((0, pad), (0, 0))).astype(ml_dtypes.bfloat16)
-    return jnp.asarray(table), jnp.asarray(np.ascontiguousarray(table[pad:].T))
+    angle = (phase * (math.pi / length)).reshape(half // GROUP, 1, GROUP, length)
+    table = np.concatenate([np.cos(angle), np.sin(angle)], axis=1).reshape(length, length)
+    table = table.astype(ml_dtypes.bfloat16)
+    return jnp.asarray(table), jnp.asarray(np.ascontiguousarray(table.T))
 
 
 def shuffle_table():
@@ -35,6 +36,15 @@
 
 def dot(a, b):
     return jnp.dot(a, b, preferred_element_type=F32)
+
+
+def interleave(first, second):
+    done = 0
+    for i, step in enumerate(first):
+        step()
+        while done * len(first) < (i + 1) * len(second):
+            second[done]()
+            done += 1
 
 
 def conv_kernel(
@@ -45,12 +55,7 @@
     taps = psf.shape[1]
     shift = taps // 2
     length = table.shape[1]
-    half = length // 2
-    wide = turned.shape[1] // 2
-    pad = wide - half
-    own = length - wide
-    shared = wide - own
-
+    tiles = [slice(n, n + 256) for n in range(0, 2 * length, 256)]
     loads = {}
 
     def load(name, source, target, start, count, pieces):
@@ -70,70 +75,76 @@
     load("model_0", model_h.at[0], model.at[0], 0, img, 2)
     load("turned_1", turned_h, turned, taps, img - taps, 2)
     load("model_1", model_h.at[1], model.at[1], 0, img, 2)
-    load("table", table_h, table, 0, table.shape[0], 4)
+    load("table", table_h, table, 0, length, 4)
     load("rest", turned_h, turned, img, length - img, 1)
     load("dirty", dirty_h, dirty, 0, 2, 2)
     loads["rate"] = [pltpu.make_async_copy(rate_h, rate, sems.at[sum(map(len, loads.values()))])]
     loads["rate"][0].start()
 
-    zeros = jnp.zeros((pad, 2 * length), BF16)
-    prod[half:wide, :] = zeros
-    prod[wide + half :, :] = zeros
-
     def columns(source, depth, target, waits):
-        step = 128
         for ch in range(2):
             for wait in waits[ch]:
                 arrived(wait)
-            for m in range(0, depth, step):
-                rows = slice(m, m + step)
-                part = jnp.concatenate(
-                    [dot(source[ch, rows, :], turned[:depth, n : n + 256]) for n in range(0, 2 * wide, 256)],
-                    axis=1,
-                )
-                for k in range(2):
-                    at = k * length
-                    one = part[:, k * wide : (k + 1) * wide]
-                    if ch == 0:
-                        target[rows, at : at + wide] = one.astype(BF16)
-                    else:
-                        one = pltpu.roll(one, pad, 1)
-                        both = one[:, :shared] + target[rows, at + own : at + wide].astype(F32)
-                        target[rows, at + own : at + wide] = both.astype(BF16)
-                        target[rows, at + wide : at + length] = one[:, shared:].astype(BF16)
+            for m in range(0, depth, 128):
+                rows = slice(m, m + 128)
+                for n in range(0, length, 256):
+                    lanes = slice(n, min(n + 256, length))
+                    to = slice(ch * length + lanes.start, ch * length + lanes.stop)
+                    target[rows, to] = dot(source[ch, rows, :], turned[:depth, lanes]).astype(BF16)
 
     columns(psf, taps, cols_q, (("psf", "turned_0"), ()))
     columns(model, img, cols_x, (("model_0", "turned_1"), ("model_1",)))
 
-    def products(start, count):
-        for row in range(start, start + count, 16):
-            c, s, t = (slice(at + row, at + row + 16) for at in (0, half, wide))
-            for j in range(0, length, 128):
-                lc, ls = slice(j, j + 128), slice(length + j, length + j + 128)
-                xcc, xcs, xsc, xss = spec_x[c, lc], spec_x[c, ls], spec_x[s, lc], spec_x[s, ls]
-                qcc, qcs, qsc, qss = spec_q[c, lc], spec_q[c, ls], spec_q[s, lc], spec_q[s, ls]
-                prod[c, lc] = ((xcc * qcc + xss * qss) - (xsc * qsc + xcs * qcs)).astype(BF16)
-                prod[t, ls] = ((xcc * qss + xss * qcc) + (xsc * qcs + xcs * qsc)).astype(BF16)
-                prod[t, lc] = ((xcc * qsc - xss * qcs) + (xsc * qcc - xcs * qss)).astype(BF16)
-                prod[c, ls] = ((xcc * qcs - xss * qsc) + (xcs * qcc - xsc * qss)).astype(BF16)
+    def spectra(lanes):
+        def one(target, source, depth, m):
+            target[m : m + 160, lanes] = dot(table[m : m + 160, :depth], source[:, lanes])
+
+        return [
+            functools.partial(one, target, source, depth, m)
+            for m in range(0, length, 160)
+            for target, source, depth in ((spec_q, cols_q, taps), (spec_x, cols_x, img))
+        ]
+
+    lane = lax.broadcasted_iota(jnp.int32, (16, 2 * GROUP), 1)
+    sign = jnp.where(lane < GROUP, -1.0, 1.0)
+
+    def products(lanes):
+        def one(row, at):
+            c, s, columns = slice(row, row + 16), slice(row + GROUP, row + GROUP + 16), slice(at, at + 2 * GROUP)
+
+            def parts(value):
+                turn = pltpu.roll(value, GROUP, 1)
+                return jnp.where(lane < GROUP, value, turn), jnp.where(lane < GROUP, turn, value)
+
+            (c_re, c_im), (s_re, s_im) = parts(spec_x[c, columns]), parts(spec_x[s, columns])
+            q_c, q_s = spec_q[c, columns], spec_q[s, columns]
+            t_c, t_s = pltpu.roll(q_c, GROUP, 1) * sign, pltpu.roll(q_s, GROUP, 1) * sign
+            prod[c, columns] = ((c_re * q_c + c_im * t_c) - (s_re * q_s + s_im * t_s)).astype(BF16)
+            prod[s, columns] = ((s_re * q_c + s_im * t_c) + (c_re * q_s + c_im * t_s)).astype(BF16)
+
+        return [
+            functools.partial(one, base + row, at)
+            for base in range(0, length, 2 * GROUP)
+            for row in range(0, GROUP, 16)
+            for at in range(lanes.start, lanes.stop, 2 * GROUP)
+        ]
+
+    def inverse(lanes):
+        def one(m):
+            back = turned[shift + m : shift + m + 128, :]
+            rows_y[m : m + 128, lanes] = dot(back, prod[:, lanes]).astype(BF16)
+
+        return [functools.partial(one, m) for m in range(0, img, 128)]
 
     arrived("table")
-    step = half // 2
-    for start in range(0, half, step):
-        for k in range(2):
-            source = slice(pad + k * wide + start, pad + k * wide + start + step)
-            target = slice(k * half + start, k * half + start + step)
-            for n in range(0, 2 * length, 256):
-                lanes = slice(n, n + 256)
-                spec_q[target, lanes] = dot(table[source, :taps], cols_q[:, lanes])
-                spec_x[target, lanes] = dot(table[source, :img], cols_x[:, lanes])
-        products(start, step)
-
     arrived("rest")
-    for n in range(0, 2 * length, 256):
-        for m in range(0, img, 128):
-            back = turned[shift + m : shift + m + 128, :]
-            rows_y[m : m + 128, n : n + 256] = dot(back, prod[:, n : n + 256]).astype(BF16)
+    for step in spectra(tiles[0]):
+        step()
+    for t in range(len(tiles)):
+        matrix = (inverse(tiles[t - 1]) if t else []) + (spectra(tiles[t + 1]) if t + 1 < len(tiles) else [])
+        interleave(products(tiles[t]), matrix)
+    for step in inverse(tiles[-1]):
+        step()
 
     arrived("dirty")
     arrived("rate")
@@ -144,13 +155,11 @@
         rows = slice(i * step, (i + 1) * step)
         where = slice(i * step // band, (i + 1) * step // band)
         for ch in range(2):
-            at = ch * own
-            inner = jnp.concatenate(
-                [rows_y[rows, at : at + wide], rows_y[rows, length + at : length + at + wide]], axis=1
+            inner = rows_y[rows, ch * length : (ch + 1) * length]
+            blurred = jnp.concatenate(
+                [dot(inner, table[:, shift + n : shift + n + 256]) for n in range(0, img, 256)], axis=1
             )
-            back = table[pad * (1 - ch) : pad * (1 - ch) + 2 * wide, shift:]
             scale = rate[ch] * (4.0 / (length * length))
-            blurred = jnp.concatenate([dot(inner, back[:, n : n + 256]) for n in range(0, img, 256)], axis=1)
             stepped = rate[ch] * dirty[ch, rows, :].astype(F32) - scale * blurred
             stepped = (model[ch, rows, :].astype(F32) + stepped).astype(BF16)
             for p in range(parts):
@@ -167,40 +176,54 @@
     groups = channels // band
 
     normed[:, channels:, :] = jnp.ones((band, band, part), BF16)
-    power = jnp.zeros((band, part), F32)
-    for c in range(channels):
-        v = tiles[c].astype(F32)
-        power = power + v * v
-    inverse = lax.rsqrt(power * (1.0 / channels) + 1e-06)
-    for g in range(groups):
-        rows = [
-            (tiles[c].astype(F32) * inverse * gain[c : c + 1, :]).astype(BF16)
-            for c in range(g * band, (g + 1) * band)
-        ]
-        swapped = dot(swap[...], jnp.concatenate(rows, axis=0)).astype(BF16)
-        normed[:, g * band : (g + 1) * band, :] = swapped.reshape(band, band, part)
-
     a = math.sqrt(2.0 / math.pi)
-    blocks = [slice(n, min(n + 256, part)) for n in range(0, part, 256)]
-    for r in range(band):
-        for lanes in blocks:
+    sends = []
+
+    def norm(lanes):
+        size = lanes.stop - lanes.start
+        power = jnp.zeros((band, size), F32)
+        for c in range(channels):
+            v = tiles[c, :, lanes].astype(F32)
+            power = power + v * v
+        inverse = lax.rsqrt(power * (1.0 / channels) + 1e-06)
+        for g in range(groups):
+            rows = [
+                (tiles[c, :, lanes].astype(F32) * inverse * gain[c : c + 1, lanes]).astype(BF16)
+                for c in range(g * band, (g + 1) * band)
+            ]
+            swapped = dot(swap[...], jnp.concatenate(rows, axis=0)).astype(BF16)
+            normed[:, g * band : (g + 1) * band, lanes] = swapped.reshape(band, band, size)
+
+    def first_layer(lanes):
+        for r in range(band):
             for h in range(0, hidden.shape[1], 128):
                 rows = slice(h, h + 128)
                 inner = dot(w_in_t[rows, :], normed[r, :, lanes]).astype(BF16)
                 bent = inner * (BF16(a) + BF16(a * 0.044715) * (inner * inner))
                 hidden[r, rows, lanes] = inner + inner * jnp.tanh(bent)
-    for r in range(band):
-        for lanes in blocks:
+
+    def second_layer(lanes):
+        for r in range(band):
             mixed[r, :, lanes] = (0.5 * dot(w_out_t[...], hidden[r, :, lanes])).astype(BF16)
 
-    sends = []
-    for g in range(groups):
-        block = mixed[:, g * band : (g + 1) * band, :].reshape(band * band, part)
-        swapped = dot(swap[...], block).astype(BF16)
-        where = pl.ds(g * band, band)
-        out[where] = swapped.reshape(band, band, part)
-        sends.append(pltpu.make_async_copy(out.at[where], out_h.at[where], sems.at[g]))
-        sends[-1].start()
+    def leave(lanes):
+        size = lanes.stop - lanes.start
+        for g in range(groups):
+            block = mixed[:, g * band : (g + 1) * band, lanes].reshape(band * band, size)
+            swapped = dot(swap[...], block).astype(BF16)
+            where = pl.ds(g * band, band), slice(None), pl.ds(lanes.start, size)
+            out[g * band : (g + 1) * band, :, lanes] = swapped.reshape(band, band, size)
+            sends.append(pltpu.make_async_copy(out.at[where], out_h.at[where], sems.at[len(sends)]))
+            sends[-1].start()
+
+    blocks = [slice(n, min(n + 256, part)) for n in range(0, part, 256)]
+    norm(blocks[0])
+    for i, lanes in enumerate(blocks):
+        first_layer(lanes)
+        if i + 1 < len(blocks):
+            norm(blocks[i + 1])
+        second_layer(lanes)
+        leave(lanes)
     for send in sends:
         send.wait()
 
@@ -296,7 +319,7 @@
     parts = img // part
     bands = img // BAND
     table, turned = tables(img, psf_len)
-    length, wide = turned.shape[0], turned.shape[1] // 2
+    length = table.shape[0]
     blocks = (bands, parts, ch_dev, BAND, part)
 
     stepped = pl.pallas_call(
@@ -315,7 +338,7 @@
             pltpu.VMEM((psf_len, 2 * length), BF16),
             pltpu.VMEM((length, 2 * length), F32),
             pltpu.VMEM((length, 2 * length), F32),
-            pltpu.VMEM((2 * wide, 2 * length), BF16),
+            pltpu.VMEM((length, 2 * length), BF16),
             pltpu.VMEM((img, 2 * length), BF16),
             pltpu.VMEM(blocks, BF16),
             pltpu.SemaphoreType.DMA((20,)),
@@ -340,7 +363,7 @@
             pltpu.VMEM((BAND, hidden, part), BF16),
             pltpu.VMEM((BAND, channels, part), BF16),
             pltpu.VMEM((channels, BAND, part), BF16),
-            pltpu.SemaphoreType.DMA((channels // BAND,)),
+            pltpu.SemaphoreType.DMA((channels // BAND * max(1, part // 256),)),
         ],
         compiler_params=params(24),
         name="mix",

time: 80.9 us -> 81.2 us (level)
  local copies, waits for them, and re-layouts: 0.54 us -> 1.8 us
    unnamed x14, local copies, waits for them, and re-layouts: 0.04 us -> 1.31 us
where the time goes in v9:
time: 81.2 us; the launch traced here: 80.8 us
  waiting for transfers between devices  54 us (67%)
  Pallas kernels  14.7 us (18%)
  starting transfers between devices  10.1 us (12%)
  local copies, waits for them, and re-layouts  1.8 us (2%)
    all_to_all x2, waiting for transfers between devices, exchange(): lax.all_to_all(blocks, ('rows', 'cols'), split_axis=0, concat_axis=0, til...  54 us
    all_to_all x2, starting transfers between devices, exchange(): lax.all_to_all(blocks, ('rows', 'cols'), split_axis=0, concat_axis=0, til...  10.1 us
    pallas_call x1, Pallas kernels, local(): pl.pallas_call(conv_kernel, out_shape=jax.ShapeDtypeStruct(blocks, BF16),...  7.62 us
    pallas_call x1, Pallas kernels, local(): pl.pallas_call(mix_kernel, out_shape=jax.ShapeDtypeStruct((channels, BAND...  4.01 us
    pallas_call x1, Pallas kernels, local(): pl.pallas_call(spread_kernel, out_shape=jax.ShapeDtypeStruct((ch_dev, img...  3.04 us
  transfers between devices with their start and end apart: 2, of which 2 were waited for; matrix products, arithmetic and copies ran while one was open for 1% of the time, Pallas kernels for 0%

profile of v9, /device:TPU:0, one launch (start us, length us, event | category | flops | bytes accessed | tf_op | source)
XLA Modules:
  0.0 80.8 jit_solution(10974180594447681779)
XLA Ops:
  0.0 0.0 copy-start
  0.0 7.6 %conv.1.stepped = bf16[32,1,2,16,512]{4,3,2,1,0:T(8,128)(2,1)} custom-call(f32[2]{0:T(128)} %rate_h.1, bf16[2,512,512]{2,1,0:T(8,128)(2,1)} %model_h.1, bf16[2,512,512]{2,1,0:T(8,128)(2,1)} %dirty_h.1, bf16[2,256,256]{2,1,0:T(8,128)(2,1)} %psf_h.1, bf16[640,640]{1,0:T(8,128)(2,1)} %constant.24.clone.table_h, bf16[640,640]{1,0:T(8,128)(2,1)} %constant.25.clone.turned_h), custom_call_target="tpu_custom_call" | custom-call | tf_op jit(solution)/shard_map/conv/pallas_call | solution.py:325
  7.6 0.0 copy-start.5
  7.6 7.3 %all-to-all-start = ((bf16[32,2,16,512]{3,2,1,0:T(8,128)(2,1)}), bf16[32,2,16,512]{3,2,1,0:T(8,128)(2,1)S(1)}, u32[]{:S(2)}, u32[]{:S(2)}) async-start(bf16[32,2,16,512]{3,2,1,0:T(8,128)(2,1)} %bitcast.6), calls=%async_computation | async-start | bytes 2097152 | tf_op jit(solution)/shard_map/all_to_all | solution.py:299
  15.0 0.0 copy-done.5
  15.0 0.0 copy-start.4
  15.0 0.1 copy.19
  15.2 0.6 copy-done.4
  15.8 0.1 copy.18
  15.9 0.0 copy-start.2
  15.9 0.1 fusion.1.w_in_t
  16.0 0.0 copy-start.6
  16.0 26.5 %all-to-all-done = bf16[32,2,16,512]{3,2,1,0:T(8,128)(2,1)S(1)} async-done(((bf16[32,2,16,512]{3,2,1,0:T(8,128)(2,1)}), bf16[32,2,16,512]{3,2,1,0:T(8,128)(2,1)S(1)}, u32[]{:S(2)}, u32[]{:S(2)}) %all-to-all-start) | async-done | bytes 1048608 | tf_op jit(solution)/shard_map/all_to_all | solution.py:299
  42.5 0.0 copy-done.6
  42.5 0.0 copy-start.3
  42.5 0.1 broadcast_in_dim.5.gain
  42.6 0.0 copy-done.2
  42.6 0.7 copy-done.3
  43.3 4.0 %mix.1 = bf16[64,16,512]{2,1,0:T(8,128)(2,1)} custom-call(f32[64,512]{1,0:T(8,128)S(1)} %broadcast_in_dim.5.gain, bf16[256,80]{1,0:T(8,128)(2,1)S(1)} %fusion.1.w_in_t, bf16[64,256]{1,0:T(8,128)(2,1)S(1)} %bitcast.9, bf16[256,256]{1,0:T(8,128)(2,1)S(1)} %copy-done.2, bf16[64,16,512]{2,1,0:T(8,128)(2,1)S(1)} %bitcast.7), custom_call_target="tpu_custom_call" | custom-call | tf_op jit(solution)/shard_map/mix/pallas_call | solution.py:356
  47.3 0.0 copy-start.1
  47.3 2.8 %all-to-all-start.1 = ((bf16[32,2,16,512]{3,2,1,0:T(8,128)(2,1)}), bf16[32,2,16,512]{3,2,1,0:T(8,128)(2,1)S(1)}, u32[]{:S(2)}, u32[]{:S(2)}) async-start(bf16[32,2,16,512]{3,2,1,0:T(8,128)(2,1)} %bitcast.4), calls=%async_computation.1 | async-start | bytes 2097152 | tf_op jit(solution)/shard_map/all_to_all | solution.py:299
  50.1 0.0 copy-done
  50.2 0.1 constant_dynamic-slice_fusion
  50.2 27.5 %all-to-all-done.1 = bf16[32,2,16,512]{3,2,1,0:T(8,128)(2,1)S(1)} async-done(((bf16[32,2,16,512]{3,2,1,0:T(8,128)(2,1)}), bf16[32,2,16,512]{3,2,1,0:T(8,128)(2,1)S(1)}, u32[]{:S(2)}, u32[]{:S(2)}) %all-to-all-start.1) | async-done | bytes 1048608 | tf_op jit(solution)/shard_map/all_to_all | solution.py:299
  77.7 0.1 broadcast_in_dim.4.taps
  77.8 0.0 copy-done.1
  77.8 3.0 %spread.1 = bf16[2,512,512]{2,1,0:T(8,128)(2,1)} custom-call(f32[3,3,2,128]{3,2,1,0:T(2,128)S(1)} %broadcast_in_dim.4.taps, bf16[32,1,2,16,512]{4,3,2,1,0:T(8,128)(2,1)S(1)} %copy-done.1, bf16[32,1,2,16,512]{4,3,2,1,0:T(8,128)(2,1)S(1)} %bitcast.8), custom_call_target="tpu_custom_call" | custom-call | tf_op jit(solution)/shard_map/spread/pallas_call | solution.py:378
  (5 shorter events, 0.0 us)
Async XLA Ops:
  0.0 50.1 %copy-start = (f32[3,3,64]{2,1,0:T(4,128)S(1)}, f32[3,3,64]{2,1,0:T(4,128)}, u32[]{:S(2)}) copy-start(f32[3,3,64]{2,1,0:T(4,128)} %param.20) | copy-start | bytes 6916
  7.6 7.3 %copy-start.5 = (f32[256]{0:T(256)S(1)}, f32[256]{0:T(256)}, u32[]{:S(2)}) copy-start(f32[256]{0:T(256)} %param.18) | copy-start | bytes 3076
  7.6 34.9 %all-to-all-start = ((bf16[32,2,16,512]{3,2,1,0:T(8,128)(2,1)}), bf16[32,2,16,512]{3,2,1,0:T(8,128)(2,1)S(1)}, u32[]{:S(2)}, u32[]{:S(2)}) async-start(bf16[32,2,16,512]{3,2,1,0:T(8,128)(2,1)} %bitcast.6), calls=%async_computation | async-start | bytes 2097152 | tf_op jit(solution)/shard_map/all_to_all | solution.py:299
  15.0 0.8 copy-start.4
  15.9 26.7 %copy-start.2 = (bf16[256,256]{1,0:T(8,128)(2,1)S(1)}, bf16[256,256]{1,0:T(8,128)(2,1)}, u32[]{:S(2)}) copy-start(bf16[256,256]{1,0:T(8,128)(2,1)} %constant.26.clone.swap) | copy-start | bytes 393220
  16.0 26.5 %copy-start.6 = (f32[64]{0:T(128)S(1)}, f32[64]{0:T(128)}, u32[]{:S(2)}) copy-start(f32[64]{0:T(128)} %param.16) | copy-start | bytes 772
  42.5 0.8 copy-start.3
  47.3 30.5 %copy-start.1 = (bf16[32,1,2,16,512]{4,3,2,1,0:T(8,128)(2,1)S(1)}, bf16[32,1,2,16,512]{4,3,2,1,0:T(8,128)(2,1)}, u32[]{:S(2)}) copy-start(bf16[32,1,2,16,512]{4,3,2,1,0:T(8,128)(2,1)} %conv.1.stepped) | copy-start | bytes 3145732
  47.3 30.4 %all-to-all-start.1 = ((bf16[32,2,16,512]{3,2,1,0:T(8,128)(2,1)}), bf16[32,2,16,512]{3,2,1,0:T(8,128)(2,1)S(1)}, u32[]{:S(2)}, u32[]{:S(2)}) async-start(bf16[32,2,16,512]{3,2,1,0:T(8,128)(2,1)} %bitcast.4), calls=%async_computation.1 | async-start | bytes 2097152 | tf_op jit(solution)/shard_map/all_to_all | solution.py:299

commit v10 on v9

--- a/solution.py
+++ b/solution.py
@@ -24,14 +24,6 @@
     table = np.concatenate([np.cos(angle), np.sin(angle)], axis=1).reshape(length, length)
     table = table.astype(ml_dtypes.bfloat16)
     return jnp.asarray(table), jnp.asarray(np.ascontiguousarray(table.T))
-
-
-def shuffle_table():
-    index = np.arange(BAND * BAND)
-    source = (index % BAND) * BAND + index // BAND
-    table = np.zeros((BAND * BAND, BAND * BAND), np.float32)
-    table[index, source] = 1.0
-    return jnp.asarray(table.astype(ml_dtypes.bfloat16))
 
 
 def dot(a, b):
@@ -56,6 +48,7 @@
     shift = taps // 2
     length = table.shape[1]
     tiles = [slice(n, n + 256) for n in range(0, 2 * length, 256)]
+    tall = length // 2
     loads = {}
 
     def load(name, source, target, start, count, pieces):
@@ -85,8 +78,8 @@
         for ch in range(2):
             for wait in waits[ch]:
                 arrived(wait)
-            for m in range(0, depth, 128):
-                rows = slice(m, m + 128)
+            for m in range(0, depth, 256):
+                rows = slice(m, m + 256)
                 for n in range(0, length, 256):
                     lanes = slice(n, min(n + 256, length))
                     to = slice(ch * length + lanes.start, ch * length + lanes.stop)
@@ -97,11 +90,11 @@
 
     def spectra(lanes):
         def one(target, source, depth, m):
-            target[m : m + 160, lanes] = dot(table[m : m + 160, :depth], source[:, lanes])
+            target[m : m + tall, lanes] = dot(table[m : m + tall, :depth], source[:, lanes])
 
         return [
             functools.partial(one, target, source, depth, m)
-            for m in range(0, length, 160)
+            for m in range(0, length, tall)
             for target, source, depth in ((spec_q, cols_q, taps), (spec_x, cols_x, img))
         ]
 
@@ -131,10 +124,10 @@
 
     def inverse(lanes):
         def one(m):
-            back = turned[shift + m : shift + m + 128, :]
-            rows_y[m : m + 128, lanes] = dot(back, prod[:, lanes]).astype(BF16)
-
-        return [functools.partial(one, m) for m in range(0, img, 128)]
+            back = turned[shift + m : shift + m + 256, :]
+            rows_y[m : m + 256, lanes] = dot(back, prod[:, lanes]).astype(BF16)
+
+        return [functools.partial(one, m) for m in range(0, img, 256)]
 
     arrived("table")
     arrived("rest")
@@ -149,81 +142,75 @@
     arrived("dirty")
     arrived("rate")
     bands, parts, _, band, part = out.shape
-    step = 128
+    step = 256
     sends = []
     for i in range(img // step):
         rows = slice(i * step, (i + 1) * step)
         where = slice(i * step // band, (i + 1) * step // band)
         for ch in range(2):
+            scale = rate[ch] * (4.0 / (length * length))
             inner = rows_y[rows, ch * length : (ch + 1) * length]
-            blurred = jnp.concatenate(
-                [dot(inner, table[:, shift + n : shift + n + 256]) for n in range(0, img, 256)], axis=1
-            )
-            scale = rate[ch] * (4.0 / (length * length))
-            stepped = rate[ch] * dirty[ch, rows, :].astype(F32) - scale * blurred
-            stepped = (model[ch, rows, :].astype(F32) + stepped).astype(BF16)
-            for p in range(parts):
-                piece = stepped[:, p * part : (p + 1) * part]
-                out[where, p, ch] = piece.reshape(step // band, band, part)
-        sends.append(pltpu.make_async_copy(out.at[where], out_h.at[where], out_sems.at[i]))
-        sends[-1].start()
+            for n in range(0, img, 256):
+                lanes = slice(n, n + 256)
+                blurred = dot(inner, table[:, shift + n : shift + n + 256])
+                stepped = rate[ch] * dirty[ch, rows, lanes].astype(F32) - scale * blurred
+                stepped = (model[ch, rows, lanes].astype(F32) + stepped).astype(BF16)
+                size = min(part, 256)
+                for k in range(0, 256, size):
+                    piece = stepped[:, k : k + size].reshape(step // band, band, size)
+                    at = (n + k) % part
+                    out[where, (n + k) // part, ch, :, at : at + size] = piece
+            place = where, slice(None), ch
+            sends.append(pltpu.make_async_copy(out.at[place], out_h.at[place], out_sems.at[len(sends)]))
+            sends[-1].start()
     for send in sends:
         send.wait()
 
 
-def mix_kernel(gain, w_in_t, w_out_t, swap, tiles, out_h, normed, hidden, mixed, out, sems):
+def mix_kernel(gain, weights, tiles, out_h, w_in_t, swap, normed, hidden, mixed, out, sems):
     channels, band, part = tiles.shape
     groups = channels // band
 
+    depth = channels + band
+    w_in_t[...] = weights[: w_in_t.shape[1], :].astype(F32).T.astype(BF16)
+    w_out_t = weights[w_in_t.shape[1] :, :]
+    place = [lax.broadcasted_iota(jnp.int32, swap.shape, axis) for axis in range(2)]
+    swap[...] = jnp.where(place[0] % band * band + place[0] // band == place[1], 1.0, 0.0).astype(BF16)
     normed[:, channels:, :] = jnp.ones((band, band, part), BF16)
+    power = jnp.zeros((band, part), F32)
+    for c in range(channels):
+        v = tiles[c].astype(F32)
+        power = power + v * v
+    inverse = lax.rsqrt(power * (1.0 / channels) + 1e-06)
+    for g in range(groups):
+        rows = [
+            (tiles[c].astype(F32) * inverse * gain[c : c + 1, :]).astype(BF16)
+            for c in range(g * band, (g + 1) * band)
+        ]
+        swapped = dot(swap[...], jnp.concatenate(rows, axis=0)).astype(BF16)
+        normed[:, g * band : (g + 1) * band, :] = swapped.reshape(band, band, part)
+
     a = math.sqrt(2.0 / math.pi)
-    sends = []
-
-    def norm(lanes):
-        size = lanes.stop - lanes.start
-        power = jnp.zeros((band, size), F32)
-        for c in range(channels):
-            v = tiles[c, :, lanes].astype(F32)
-            power = power + v * v
-        inverse = lax.rsqrt(power * (1.0 / channels) + 1e-06)
-        for g in range(groups):
-            rows = [
-                (tiles[c, :, lanes].astype(F32) * inverse * gain[c : c + 1, lanes]).astype(BF16)
-                for c in range(g * band, (g + 1) * band)
-            ]
-            swapped = dot(swap[...], jnp.concatenate(rows, axis=0)).astype(BF16)
-            normed[:, g * band : (g + 1) * band, lanes] = swapped.reshape(band, band, size)
-
-    def first_layer(lanes):
-        for r in range(band):
+    blocks = [slice(n, min(n + 256, part)) for n in range(0, part, 256)]
+    for r in range(band):
+        for lanes in blocks:
             for h in range(0, hidden.shape[1], 128):
                 rows = slice(h, h + 128)
-                inner = dot(w_in_t[rows, :], normed[r, :, lanes]).astype(BF16)
+                inner = dot(w_in_t[rows, :depth], normed[r, :, lanes]).astype(BF16)
                 bent = inner * (BF16(a) + BF16(a * 0.044715) * (inner * inner))
                 hidden[r, rows, lanes] = inner + inner * jnp.tanh(bent)
-
-    def second_layer(lanes):
-        for r in range(band):
-            mixed[r, :, lanes] = (0.5 * dot(w_out_t[...], hidden[r, :, lanes])).astype(BF16)
-
-    def leave(lanes):
-        size = lanes.stop - lanes.start
-        for g in range(groups):
-            block = mixed[:, g * band : (g + 1) * band, lanes].reshape(band * band, size)
-            swapped = dot(swap[...], block).astype(BF16)
-            where = pl.ds(g * band, band), slice(None), pl.ds(lanes.start, size)
-            out[g * band : (g + 1) * band, :, lanes] = swapped.reshape(band, band, size)
-            sends.append(pltpu.make_async_copy(out.at[where], out_h.at[where], sems.at[len(sends)]))
-            sends[-1].start()
-
-    blocks = [slice(n, min(n + 256, part)) for n in range(0, part, 256)]
-    norm(blocks[0])
-    for i, lanes in enumerate(blocks):
-        first_layer(lanes)
-        if i + 1 < len(blocks):
-            norm(blocks[i + 1])
-        second_layer(lanes)
-        leave(lanes)
+    for r in range(band):
+        for lanes in blocks:
+            mixed[r, :, lanes] = (0.5 * dot(w_out_t, hidden[r, :, lanes])).astype(BF16)
+
+    sends = []
+    for g in range(groups):
+        block = mixed[:, g * band : (g + 1) * band, :].reshape(band * band, part)
+        swapped = dot(swap[...], block).astype(BF16)
+        where = pl.ds(g * band, band)
+        out[where] = swapped.reshape(band, band, part)
+        sends.append(pltpu.make_async_copy(out.at[where], out_h.at[where], sems.at[g]))
+        sends[-1].start()
     for send in sends:
         send.wait()
 
@@ -299,13 +286,13 @@
     return lax.all_to_all(blocks, ("rows", "cols"), split_axis=0, concat_axis=0, tiled=True)
 
 
-def with_bias(w_in, b_in):
-    columns = []
+def layers(w_in, b_in, w_out, wide):
+    rows = []
     for _ in range(3):
-        columns.append(lax.reduce_precision(b_in, 8, 7))
-        b_in = b_in - columns[-1]
-    bias = jnp.stack(columns, axis=1).astype(BF16)
-    return jnp.concatenate([w_in.T, jnp.pad(bias, ((0, 0), (0, BAND - 3)))], axis=1)
+        rows.append(lax.reduce_precision(b_in, 8, 7))
+        b_in = b_in - rows[-1]
+    zeros = jnp.zeros((wide - w_in.shape[0] - 3, w_in.shape[1]), BF16)
+    return jnp.concatenate([w_in, jnp.stack(rows).astype(BF16), zeros, w_out.T], axis=0)
 
 
 def local(model, dirty, psf, step_size, gain, w_in, b_in, w_out, kernel):
@@ -320,6 +307,7 @@
     bands = img // BAND
     table, turned = tables(img, psf_len)
     length = table.shape[0]
+    wide = -(-(channels + BAND) // 128) * 128
     blocks = (bands, parts, ch_dev, BAND, part)
 
     stepped = pl.pallas_call(
@@ -356,18 +344,20 @@
     mixed = pl.pallas_call(
         mix_kernel,
         out_shape=jax.ShapeDtypeStruct((channels, BAND, part), BF16),
-        in_specs=[VMEM] * 5,
+        in_specs=[VMEM] * 3,
         out_specs=HBM,
         scratch_shapes=[
+            pltpu.VMEM((hidden, wide), BF16),
+            pltpu.VMEM((BAND * BAND, BAND * BAND), BF16),
             pltpu.VMEM((BAND, channels + BAND, part), BF16),
             pltpu.VMEM((BAND, hidden, part), BF16),
             pltpu.VMEM((BAND, channels, part), BF16),
             pltpu.VMEM((channels, BAND, part), BF16),
-            pltpu.SemaphoreType.DMA((channels // BAND * max(1, part // 256),)),
+            pltpu.SemaphoreType.DMA((channels // BAND,)),
         ],
         compiler_params=params(24),
         name="mix",
-    )(jnp.broadcast_to(gain[:, None], (channels, part)), with_bias(w_in, b_in), w_out.T, shuffle_table(), tiles)
+    )(jnp.broadcast_to(gain[:, None], (channels, part)), layers(w_in, b_in, w_out, wide), tiles)
 
     returned = exchange(mixed.reshape(n_dev, ch_dev, BAND, part)).reshape(blocks)
     position = lax.axis_index(("rows", "cols")).astype(jnp.int32) * ch_dev

time: 81.2 us -> 80.2 us (0.988)
  transfers between devices with their start and end apart: 2 -> 2, of which waited for: 2 -> 2; matrix products, arithmetic and copies ran while one was open for 1% -> 0% of each run, Pallas kernels for 0% -> 0%
where the time goes in v10:
time: 80.2 us; the launch traced here: 79.8 us
  waiting for transfers between devices  54.1 us (67%)
  Pallas kernels  14.4 us (18%)
  starting transfers between devices  10.1 us (13%)
  local copies, waits for them, and re-layouts  1.14 us (1%)
    all_to_all x2, waiting for transfers between devices, exchange(): lax.all_to_all(blocks, ('rows', 'cols'), split_axis=0, concat_axis=0, til...  54.1 us
    all_to_all x2, starting transfers between devices, exchange(): lax.all_to_all(blocks, ('rows', 'cols'), split_axis=0, concat_axis=0, til...  10.1 us
    pallas_call x1, Pallas kernels, local(): pl.pallas_call(conv_kernel, out_shape=jax.ShapeDtypeStruct(blocks, BF16),...  7.61 us
    pallas_call x1, Pallas kernels, local(): pl.pallas_call(mix_kernel, out_shape=jax.ShapeDtypeStruct((channels, BAND...  3.71 us
    pallas_call x1, Pallas kernels, local(): pl.pallas_call(spread_kernel, out_shape=jax.ShapeDtypeStruct((ch_dev, img...  3.04 us
  transfers between devices with their start and end apart: 2, of which 2 were waited for; matrix products, arithmetic and copies ran while one was open for 0% of the time, Pallas kernels for 0%

profile of v10, /device:TPU:0, one launch (start us, length us, event | category | flops | bytes accessed | tf_op | source)
XLA Modules:
  0.0 79.8 jit_solution(8139928209354076696)
XLA Ops:
  0.0 0.0 copy-start
  0.0 7.6 %conv.1.stepped = bf16[32,1,2,16,512]{4,3,2,1,0:T(8,128)(2,1)} custom-call(f32[2]{0:T(128)} %rate_h.1, bf16[2,512,512]{2,1,0:T(8,128)(2,1)} %model_h.1, bf16[2,512,512]{2,1,0:T(8,128)(2,1)} %dirty_h.1, bf16[2,256,256]{2,1,0:T(8,128)(2,1)} %psf_h.1, bf16[640,640]{1,0:T(8,128)(2,1)} %constant.22.clone.table_h, bf16[640,640]{1,0:T(8,128)(2,1)} %constant.23.clone.turned_h), custom_call_target="tpu_custom_call" | custom-call | tf_op jit(solution)/shard_map/conv/pallas_call | solution.py:313
  7.6 0.0 copy-start.4
  7.6 0.0 copy-start.3
  7.6 7.3 %all-to-all-start = ((bf16[32,2,16,512]{3,2,1,0:T(8,128)(2,1)}), bf16[32,2,16,512]{3,2,1,0:T(8,128)(2,1)S(1)}, u32[]{:S(2)}, u32[]{:S(2)}) async-start(bf16[32,2,16,512]{3,2,1,0:T(8,128)(2,1)} %bitcast.5), calls=%async_computation | async-start | bytes 2097152 | tf_op jit(solution)/shard_map/all_to_all | solution.py:286
  15.0 0.0 copy-done.4
  15.0 0.0 copy-start.2
  15.0 0.0 copy-done.3
  15.1 0.7 copy-done.2
  15.7 0.2 concatenate.4.weights
  15.9 0.0 copy-start.5
  15.9 26.6 %all-to-all-done = bf16[32,2,16,512]{3,2,1,0:T(8,128)(2,1)S(1)} async-done(((bf16[32,2,16,512]{3,2,1,0:T(8,128)(2,1)}), bf16[32,2,16,512]{3,2,1,0:T(8,128)(2,1)S(1)}, u32[]{:S(2)}, u32[]{:S(2)}) %all-to-all-start) | async-done | bytes 1048608 | tf_op jit(solution)/shard_map/all_to_all | solution.py:286
  42.5 0.0 copy-done.5
  42.5 0.1 broadcast_in_dim.7.gain
  42.6 3.7 %mix.1 = bf16[64,16,512]{2,1,0:T(8,128)(2,1)} custom-call(f32[64,512]{1,0:T(8,128)S(1)} %broadcast_in_dim.7.gain, bf16[192,256]{1,0:T(8,128)(2,1)S(1)} %concatenate.4.weights, bf16[64,16,512]{2,1,0:T(8,128)(2,1)S(1)} %bitcast.7), custom_call_target="tpu_custom_call" | custom-call | tf_op jit(solution)/shard_map/mix/pallas_call | solution.py:344
  46.3 0.0 copy-start.1
  46.3 2.8 %all-to-all-start.1 = ((bf16[32,2,16,512]{3,2,1,0:T(8,128)(2,1)}), bf16[32,2,16,512]{3,2,1,0:T(8,128)(2,1)S(1)}, u32[]{:S(2)}, u32[]{:S(2)}) async-start(bf16[32,2,16,512]{3,2,1,0:T(8,128)(2,1)} %bitcast.3), calls=%async_computation.1 | async-start | bytes 2097152 | tf_op jit(solution)/shard_map/all_to_all | solution.py:286
  49.2 0.0 copy-done
  49.2 0.1 constant_dynamic-slice_fusion
  49.2 27.5 %all-to-all-done.1 = bf16[32,2,16,512]{3,2,1,0:T(8,128)(2,1)S(1)} async-done(((bf16[32,2,16,512]{3,2,1,0:T(8,128)(2,1)}), bf16[32,2,16,512]{3,2,1,0:T(8,128)(2,1)S(1)}, u32[]{:S(2)}, u32[]{:S(2)}) %all-to-all-start.1) | async-done | bytes 1048608 | tf_op jit(solution)/shard_map/all_to_all | solution.py:286
  76.7 0.1 broadcast_in_dim.6.taps
  76.8 0.0 copy-done.1
  76.8 3.0 %spread.1 = bf16[2,512,512]{2,1,0:T(8,128)(2,1)} custom-call(f32[3,3,2,128]{3,2,1,0:T(2,128)S(1)} %broadcast_in_dim.6.taps, bf16[32,1,2,16,512]{4,3,2,1,0:T(8,128)(2,1)S(1)} %copy-done.1, bf16[32,1,2,16,512]{4,3,2,1,0:T(8,128)(2,1)S(1)} %bitcast.6), custom_call_target="tpu_custom_call" | custom-call | tf_op jit(solution)/shard_map/spread/pallas_call | solution.py:368
  (5 shorter events, 0.0 us)
Async XLA Ops:
  0.0 49.2 %copy-start = (f32[3,3,64]{2,1,0:T(4,128)S(1)}, f32[3,3,64]{2,1,0:T(4,128)}, u32[]{:S(2)}) copy-start(f32[3,3,64]{2,1,0:T(4,128)} %param.19) | copy-start | bytes 6916
  7.6 7.3 %copy-start.4 = (f32[256]{0:T(256)S(1)}, f32[256]{0:T(256)}, u32[]{:S(2)}) copy-start(f32[256]{0:T(256)} %param.17) | copy-start | bytes 3076
  7.6 7.4 %copy-start.3 = (bf16[256,64]{0,1:T(8,128)(2,1)S(1)}, bf16[256,64]{0,1:T(8,128)(2,1)}, u32[]{:S(2)}) copy-start(bf16[256,64]{0,1:T(8,128)(2,1)} %param.18) | copy-start | bytes 98308
  7.6 34.9 %all-to-all-start = ((bf16[32,2,16,512]{3,2,1,0:T(8,128)(2,1)}), bf16[32,2,16,512]{3,2,1,0:T(8,128)(2,1)S(1)}, u32[]{:S(2)}, u32[]{:S(2)}) async-start(bf16[32,2,16,512]{3,2,1,0:T(8,128)(2,1)} %bitcast.5), calls=%async_computation | async-start | bytes 2097152 | tf_op jit(solution)/shard_map/all_to_all | solution.py:286
  15.0 0.8 copy-start.2
  15.9 26.6 %copy-start.5 = (f32[64]{0:T(128)S(1)}, f32[64]{0:T(128)}, u32[]{:S(2)}) copy-start(f32[64]{0:T(128)} %param.15) | copy-start | bytes 772
  46.3 30.5 %copy-start.1 = (bf16[32,1,2,16,512]{4,3,2,1,0:T(8,128)(2,1)S(1)}, bf16[32,1,2,16,512]{4,3,2,1,0:T(8,128)(2,1)}, u32[]{:S(2)}) copy-start(bf16[32,1,2,16,512]{4,3,2,1,0:T(8,128)(2,1)} %conv.1.stepped) | copy-start | bytes 3145732
  46.3 30.4 %all-to-all-start.1 = ((bf16[32,2,16,512]{3,2,1,0:T(8,128)(2,1)}), bf16[32,2,16,512]{3,2,1,0:T(8,128)(2,1)S(1)}, u32[]{:S(2)}, u32[]{:S(2)}) async-start(bf16[32,2,16,512]{3,2,1,0:T(8,128)(2,1)} %bitcast.3), calls=%async_computation.1 | async-start | bytes 2097152 | tf_op jit(solution)/shard_map/all_to_all | solution.py:286

commit v11 on v10

--- a/solution.py
+++ b/solution.py
@@ -8,6 +8,7 @@
 from jax import lax
 from jax.experimental import pallas as pl
 from jax.experimental.pallas import tpu as pltpu
+from jax.sharding import Mesh
 from jax.sharding import PartitionSpec as P
 
 BAND = 16
@@ -282,24 +283,27 @@
     return pltpu.CompilerParams(vmem_limit_bytes=mib * MIB)
 
 
-def exchange(blocks):
-    return lax.all_to_all(blocks, ("rows", "cols"), split_axis=0, concat_axis=0, tiled=True)
-
-
-def layers(w_in, b_in, w_out, wide):
+def exchange(blocks, order):
+    return lax.all_to_all(
+        blocks, "all", split_axis=0, concat_axis=0, axis_index_groups=[order], tiled=True
+    )
+
+
+def layers(w_in, b_in, w_out_t, wide):
     rows = []
     for _ in range(3):
         rows.append(lax.reduce_precision(b_in, 8, 7))
         b_in = b_in - rows[-1]
     zeros = jnp.zeros((wide - w_in.shape[0] - 3, w_in.shape[1]), BF16)
-    return jnp.concatenate([w_in, jnp.stack(rows).astype(BF16), zeros, w_out.T], axis=0)
-
-
-def local(model, dirty, psf, step_size, gain, w_in, b_in, w_out, kernel):
+    return jnp.concatenate([w_in, jnp.stack(rows).astype(BF16), zeros, w_out_t], axis=0)
+
+
+def local(n_rows, n_cols, model, dirty, psf, step_size, gain, w_in, b_in, w_out, kernel):
     ch_dev, img, _ = model.shape
     psf_len = psf.shape[1]
     assert ch_dev == 2
-    n_dev = lax.axis_size("rows") * lax.axis_size("cols")
+    n_dev = n_rows * n_cols
+    order = [r * n_cols + (c + n_cols // 2) % n_cols for r in range(n_rows) for c in range(n_cols)]
     channels = gain.shape[0]
     hidden = b_in.shape[0]
     part = img * img // (n_dev * BAND)
@@ -339,7 +343,10 @@
         (stepped, gain, w_in, b_in, w_out, kernel)
     )
 
-    tiles = exchange(stepped.reshape(n_dev, ch_dev, BAND, part)).reshape(channels, BAND, part)
+    def ordered(values):
+        return values.reshape(n_rows, 2, channels // (2 * n_rows), -1)[:, ::-1].reshape(values.shape)
+
+    tiles = exchange(stepped.reshape(n_dev, ch_dev, BAND, part), order).reshape(channels, BAND, part)
 
     mixed = pl.pallas_call(
         mix_kernel,
@@ -357,10 +364,14 @@
         ],
         compiler_params=params(24),
         name="mix",
-    )(jnp.broadcast_to(gain[:, None], (channels, part)), layers(w_in, b_in, w_out, wide), tiles)
-
-    returned = exchange(mixed.reshape(n_dev, ch_dev, BAND, part)).reshape(blocks)
-    position = lax.axis_index(("rows", "cols")).astype(jnp.int32) * ch_dev
+    )(
+        jnp.broadcast_to(ordered(gain)[:, None], (channels, part)),
+        layers(ordered(w_in), b_in, ordered(w_out.T), wide),
+        tiles,
+    )
+
+    returned = exchange(mixed.reshape(n_dev, ch_dev, BAND, part), order).reshape(blocks)
+    position = lax.axis_index("all").astype(jnp.int32) * ch_dev
     taps = lax.dynamic_slice_in_dim(kernel, position, ch_dev, axis=2)
     taps = jnp.broadcast_to(taps[..., None], (3, 3, ch_dev, 128))
     plane = pltpu.VMEM((img // 128, img + 8, 128), F32)
@@ -380,20 +391,12 @@
 
 
 def solution(mesh):
+    line = Mesh(mesh.devices.reshape(-1), ("all",))
+    planes = P("all", None, None)
     return jax.shard_map(
-        local,
-        mesh=mesh,
-        in_specs=(
-            P(("rows", "cols"), None, None),
-            P(("rows", "cols"), None, None),
-            P(("rows", "cols"), None, None),
-            P(("rows", "cols")),
-            P(),
-            P(),
-            P(),
-            P(),
-            P(),
-        ),
-        out_specs=P(("rows", "cols"), None, None),
+        functools.partial(local, *mesh.devices.shape),
+        mesh=line,
+        in_specs=(planes, planes, planes, P("all"), P(), P(), P(), P(), P()),
+        out_specs=planes,
         check_vma=False,
     )

time: 80.2 us -> 79.2 us (0.988)
  the two profiles are of different devices: /device:TPU:0 before, /device:TPU:1 now
where the time goes in v11:
time: 79.2 us; the launch traced here: 78.8 us
  waiting for transfers between devices  52.6 us (66%)
  Pallas kernels  14.4 us (18%)
  starting transfers between devices  9.64 us (12%)
  local copies, waits for them, and re-layouts  2.06 us (3%)
    all_to_all x2, waiting for transfers between devices, exchange(): lax.all_to_all(blocks, 'all', split_axis=0, concat_axis=0, axis_index_gro...  52.6 us
    all_to_all x2, starting transfers between devices, exchange(): lax.all_to_all(blocks, 'all', split_axis=0, concat_axis=0, axis_index_gro...  9.64 us
    pallas_call x1, Pallas kernels, local(): pl.pallas_call(conv_kernel, out_shape=jax.ShapeDtypeStruct(blocks, BF16),...  7.62 us
    pallas_call x1, Pallas kernels, local(): pl.pallas_call(mix_kernel, out_shape=jax.ShapeDtypeStruct((channels, BAND...  3.71 us
    pallas_call x1, Pallas kernels, local(): pl.pallas_call(spread_kernel, out_shape=jax.ShapeDtypeStruct((ch_dev, img...  3.04 us
  transfers between devices with their start and end apart: 2, of which 2 were waited for; matrix products, arithmetic and copies ran while one was open for 1% of the time, Pallas kernels for 0%

profile of v11, /device:TPU:1, one launch (start us, length us, event | category | flops | bytes accessed | tf_op | source)
XLA Modules:
  0.0 78.8 jit_solution(4129350712851425746)
XLA Ops:
  0.0 0.0 copy-start
  0.0 7.6 %conv.1.stepped = bf16[32,1,2,16,512]{4,3,2,1,0:T(8,128)(2,1)} custom-call(f32[2]{0:T(128)} %rate_h.1, bf16[2,512,512]{2,1,0:T(8,128)(2,1)} %model_h.1, bf16[2,512,512]{2,1,0:T(8,128)(2,1)} %dirty_h.1, bf16[2,256,256]{2,1,0:T(8,128)(2,1)} %psf_h.1, bf16[640,640]{1,0:T(8,128)(2,1)} %constant.16.clone.table_h, bf16[640,640]{1,0:T(8,128)(2,1)} %constant.17.clone.turned_h), custom_call_target="tpu_custom_call" | custom-call | tf_op jit(solution)/shard_map/conv/pallas_call | solution.py:317
  7.6 0.0 copy-start.4
  7.6 0.0 copy-start.2
  7.7 7.1 %all-to-all-start = ((bf16[32,2,16,512]{3,2,1,0:T(8,128)(2,1)}), bf16[32,2,16,512]{3,2,1,0:T(8,128)(2,1)S(1)}, u32[]{:S(2)}, u32[]{:S(2)}) async-start(bf16[32,2,16,512]{3,2,1,0:T(8,128)(2,1)} %bitcast.12), calls=%async_computation | async-start | bytes 2097152 | tf_op jit(solution)/shard_map/all_to_all | solution.py:287
  14.8 0.0 copy-done.4
  14.8 0.0 copy-done.2
  14.8 0.0 copy-start.3
  14.8 0.7 copy-done.3
  15.6 0.0 copy-start.5
  15.6 0.6 copy-done.5
  16.2 0.1 reshape.29
  16.4 0.1 broadcast_in_dim.17
  16.5 0.2 concatenate.4.weights
  16.7 25.4 %all-to-all-done = bf16[32,2,16,512]{3,2,1,0:T(8,128)(2,1)S(1)} async-done(((bf16[32,2,16,512]{3,2,1,0:T(8,128)(2,1)}), bf16[32,2,16,512]{3,2,1,0:T(8,128)(2,1)S(1)}, u32[]{:S(2)}, u32[]{:S(2)}) %all-to-all-start) | async-done | bytes 1048608 | tf_op jit(solution)/shard_map/all_to_all | solution.py:287
  42.0 0.1 broadcast_in_dim.18.gain
  42.1 3.7 %mix.1 = bf16[64,16,512]{2,1,0:T(8,128)(2,1)} custom-call(f32[64,512]{1,0:T(8,128)S(1)} %broadcast_in_dim.18.gain, bf16[192,256]{1,0:T(8,128)(2,1)S(1)} %concatenate.4.weights, bf16[64,16,512]{2,1,0:T(8,128)(2,1)S(1)} %bitcast.13), custom_call_target="tpu_custom_call" | custom-call | tf_op jit(solution)/shard_map/mix/pallas_call | solution.py:351
  45.8 0.0 copy-start.1
  45.8 2.5 %all-to-all-start.1 = ((bf16[32,2,16,512]{3,2,1,0:T(8,128)(2,1)}), bf16[32,2,16,512]{3,2,1,0:T(8,128)(2,1)S(1)}, u32[]{:S(2)}, u32[]{:S(2)}) async-start(bf16[32,2,16,512]{3,2,1,0:T(8,128)(2,1)} %bitcast.7), calls=%async_computation.1 | async-start | bytes 2097152 | tf_op jit(solution)/shard_map/all_to_all | solution.py:287
  48.4 0.0 copy-done
  48.4 0.1 constant_dynamic-slice_fusion
  48.5 27.2 %all-to-all-done.1 = bf16[32,2,16,512]{3,2,1,0:T(8,128)(2,1)S(1)} async-done(((bf16[32,2,16,512]{3,2,1,0:T(8,128)(2,1)}), bf16[32,2,16,512]{3,2,1,0:T(8,128)(2,1)S(1)}, u32[]{:S(2)}, u32[]{:S(2)}) %all-to-all-start.1) | async-done | bytes 1048608 | tf_op jit(solution)/shard_map/all_to_all | solution.py:287
  75.7 0.1 broadcast_in_dim.16.taps
  75.7 0.0 copy-done.1
  75.7 3.0 %spread.1 = bf16[2,512,512]{2,1,0:T(8,128)(2,1)} custom-call(f32[3,3,2,128]{3,2,1,0:T(2,128)S(1)} %broadcast_in_dim.16.taps, bf16[32,1,2,16,512]{4,3,2,1,0:T(8,128)(2,1)S(1)} %copy-done.1, bf16[32,1,2,16,512]{4,3,2,1,0:T(8,128)(2,1)S(1)} %bitcast.14), custom_call_target="tpu_custom_call" | custom-call | tf_op jit(solution)/shard_map/spread/pallas_call | solution.py:379
  (8 shorter events, 0.1 us)
Async XLA Ops:
  0.0 48.4 %copy-start = (f32[3,3,64]{2,1,0:T(4,128)S(1)}, f32[3,3,64]{2,1,0:T(4,128)}, u32[]{:S(2)}) copy-start(f32[3,3,64]{2,1,0:T(4,128)} %param.19) | copy-start | bytes 6916
  7.6 7.1 %copy-start.4 = (f32[256]{0:T(256)S(1)}, f32[256]{0:T(256)}, u32[]{:S(2)}) copy-start(f32[256]{0:T(256)} %param.17) | copy-start | bytes 3076
  7.6 7.2 %copy-start.2 = (bf16[64,256]{1,0:T(8,128)(2,1)S(1)}, bf16[64,256]{1,0:T(8,128)(2,1)}, u32[]{:S(2)}) copy-start(bf16[64,256]{1,0:T(8,128)(2,1)} %param.16) | copy-start | bytes 98308
  7.7 34.4 %all-to-all-start = ((bf16[32,2,16,512]{3,2,1,0:T(8,128)(2,1)}), bf16[32,2,16,512]{3,2,1,0:T(8,128)(2,1)S(1)}, u32[]{:S(2)}, u32[]{:S(2)}) async-start(bf16[32,2,16,512]{3,2,1,0:T(8,128)(2,1)} %bitcast.12), calls=%async_computation | async-start | bytes 2097152 | tf_op jit(solution)/shard_map/all_to_all | solution.py:287
  14.8 0.8 copy-start.3
  15.6 0.7 copy-start.5
  45.8 29.9 %copy-start.1 = (bf16[32,1,2,16,512]{4,3,2,1,0:T(8,128)(2,1)S(1)}, bf16[32,1,2,16,512]{4,3,2,1,0:T(8,128)(2,1)}, u32[]{:S(2)}) copy-start(bf16[32,1,2,16,512]{4,3,2,1,0:T(8,128)(2,1)} %conv.1.stepped) | copy-start | bytes 3145732
  45.8 29.8 %all-to-all-start.1 = ((bf16[32,2,16,512]{3,2,1,0:T(8,128)(2,1)}), bf16[32,2,16,512]{3,2,1,0:T(8,128)(2,1)S(1)}, u32[]{:S(2)}, u32[]{:S(2)}) async-start(bf16[32,2,16,512]{3,2,1,0:T(8,128)(2,1)} %bitcast.7), calls=%async_computation.1 | async-start | bytes 2097152 | tf_op jit(solution)/shard_map/all_to_all | solution.py:287

commit v12 on v11

--- a/solution.py
+++ b/solution.py
@@ -303,7 +303,8 @@
     psf_len = psf.shape[1]
     assert ch_dev == 2
     n_dev = n_rows * n_cols
-    order = [r * n_cols + (c + n_cols // 2) % n_cols for r in range(n_rows) for c in range(n_cols)]
+    side = n_cols // 2
+    order = [r * n_cols + half * side + k for r in range(n_rows) for k in range(side) for half in (1, 0)]
     channels = gain.shape[0]
     hidden = b_in.shape[0]
     part = img * img // (n_dev * BAND)
@@ -344,7 +345,8 @@
     )
 
     def ordered(values):
-        return values.reshape(n_rows, 2, channels // (2 * n_rows), -1)[:, ::-1].reshape(values.shape)
+        grid = values.reshape(n_rows, 2, side, ch_dev, -1)[:, ::-1]
+        return grid.transpose(0, 2, 1, 3, 4).reshape(values.shape)
 
     tiles = exchange(stepped.reshape(n_dev, ch_dev, BAND, part), order).reshape(channels, BAND, part)
 

time: 79.2 us -> 77 us (0.972)
  waiting for transfers between devices: 52.6 us -> 49.4 us
    all_to_all x2, waiting for transfers between devices: 52.6 us -> 49.4 us  [exchange(): lax.all_to_all(blocks, 'all', split_axis=0, concat_axis=0, axis_index_gro...]
where the time goes in v12:
time: 77 us; the launch traced here: 76.6 us
  waiting for transfers between devices  49.4 us (64%)
  Pallas kernels  14.4 us (19%)
  starting transfers between devices  10.4 us (14%)
  local copies, waits for them, and re-layouts  2.22 us (3%)
    all_to_all x2, waiting for transfers between devices, exchange(): lax.all_to_all(blocks, 'all', split_axis=0, concat_axis=0, axis_index_gro...  49.4 us
    all_to_all x2, starting transfers between devices, exchange(): lax.all_to_all(blocks, 'all', split_axis=0, concat_axis=0, axis_index_gro...  10.4 us
    pallas_call x1, Pallas kernels, local(): pl.pallas_call(conv_kernel, out_shape=jax.ShapeDtypeStruct(blocks, BF16),...  7.62 us
    pallas_call x1, Pallas kernels, local(): pl.pallas_call(mix_kernel, out_shape=jax.ShapeDtypeStruct((channels, BAND...  3.71 us
    pallas_call x1, Pallas kernels, local(): pl.pallas_call(spread_kernel, out_shape=jax.ShapeDtypeStruct((ch_dev, img...  3.04 us
  transfers between devices with their start and end apart: 2, of which 2 were waited for; matrix products, arithmetic and copies ran while one was open for 1% of the time, Pallas kernels for 0%

profile of v12, /device:TPU:1, one launch (start us, length us, event | category | flops | bytes accessed | tf_op | source)
XLA Modules:
  0.0 76.6 jit_solution(840376989915547961)
XLA Ops:
  0.0 0.0 copy-start
  0.0 7.6 %conv.1.stepped = bf16[32,1,2,16,512]{4,3,2,1,0:T(8,128)(2,1)} custom-call(f32[2]{0:T(128)} %rate_h.1, bf16[2,512,512]{2,1,0:T(8,128)(2,1)} %model_h.1, bf16[2,512,512]{2,1,0:T(8,128)(2,1)} %dirty_h.1, bf16[2,256,256]{2,1,0:T(8,128)(2,1)} %psf_h.1, bf16[640,640]{1,0:T(8,128)(2,1)} %constant.16.clone.table_h, bf16[640,640]{1,0:T(8,128)(2,1)} %constant.17.clone.turned_h), custom_call_target="tpu_custom_call" | custom-call | tf_op jit(solution)/shard_map/conv/pallas_call | solution.py:318
  7.6 0.0 copy-start.4
  7.6 0.0 copy-start.2
  7.7 7.1 %all-to-all-start = ((bf16[32,2,16,512]{3,2,1,0:T(8,128)(2,1)}), bf16[32,2,16,512]{3,2,1,0:T(8,128)(2,1)S(1)}, u32[]{:S(2)}, u32[]{:S(2)}) async-start(bf16[32,2,16,512]{3,2,1,0:T(8,128)(2,1)} %bitcast.13), calls=%async_computation | async-start | bytes 2097152 | tf_op jit(solution)/shard_map/all_to_all | solution.py:287
  14.8 0.0 copy-done.4
  14.8 0.0 copy-done.2
  14.9 0.0 copy-start.3
  15.0 0.7 copy-done.3
  15.8 0.0 copy-start.5
  15.8 0.6 copy-done.5
  16.4 0.1 reshape.29
  16.6 0.1 broadcast_in_dim.17
  16.7 0.2 concatenate.4.weights
  16.9 23.7 %all-to-all-done = bf16[32,2,16,512]{3,2,1,0:T(8,128)(2,1)S(1)} async-done(((bf16[32,2,16,512]{3,2,1,0:T(8,128)(2,1)}), bf16[32,2,16,512]{3,2,1,0:T(8,128)(2,1)S(1)}, u32[]{:S(2)}, u32[]{:S(2)}) %all-to-all-start) | async-done | bytes 1048608 | tf_op jit(solution)/shard_map/all_to_all | solution.py:287
  40.6 0.1 broadcast_in_dim.18.gain
  40.6 3.7 %mix.1 = bf16[64,16,512]{2,1,0:T(8,128)(2,1)} custom-call(f32[64,512]{1,0:T(8,128)S(1)} %broadcast_in_dim.18.gain, bf16[192,256]{1,0:T(8,128)(2,1)S(1)} %concatenate.4.weights, bf16[64,16,512]{2,1,0:T(8,128)(2,1)S(1)} %bitcast.14), custom_call_target="tpu_custom_call" | custom-call | tf_op jit(solution)/shard_map/mix/pallas_call | solution.py:353
  44.4 0.0 copy-start.1
  44.4 3.3 %all-to-all-start.1 = ((bf16[32,2,16,512]{3,2,1,0:T(8,128)(2,1)}), bf16[32,2,16,512]{3,2,1,0:T(8,128)(2,1)S(1)}, u32[]{:S(2)}, u32[]{:S(2)}) async-start(bf16[32,2,16,512]{3,2,1,0:T(8,128)(2,1)} %bitcast.6), calls=%async_computation.1 | async-start | bytes 2097152 | tf_op jit(solution)/shard_map/all_to_all | solution.py:287
  47.7 0.0 copy-done
  47.7 0.1 constant_dynamic-slice_fusion
  47.8 25.7 %all-to-all-done.1 = bf16[32,2,16,512]{3,2,1,0:T(8,128)(2,1)S(1)} async-done(((bf16[32,2,16,512]{3,2,1,0:T(8,128)(2,1)}), bf16[32,2,16,512]{3,2,1,0:T(8,128)(2,1)S(1)}, u32[]{:S(2)}, u32[]{:S(2)}) %all-to-all-start.1) | async-done | bytes 1048608 | tf_op jit(solution)/shard_map/all_to_all | solution.py:287
  73.5 0.1 broadcast_in_dim.16.taps
  73.6 0.0 copy-done.1
  73.6 3.0 %spread.1 = bf16[2,512,512]{2,1,0:T(8,128)(2,1)} custom-call(f32[3,3,2,128]{3,2,1,0:T(2,128)S(1)} %broadcast_in_dim.16.taps, bf16[32,1,2,16,512]{4,3,2,1,0:T(8,128)(2,1)S(1)} %copy-done.1, bf16[32,1,2,16,512]{4,3,2,1,0:T(8,128)(2,1)S(1)} %bitcast.15), custom_call_target="tpu_custom_call" | custom-call | tf_op jit(solution)/shard_map/spread/pallas_call | solution.py:381
  (15 shorter events, 0.2 us)
Async XLA Ops:
  0.0 47.7 %copy-start = (f32[3,3,64]{2,1,0:T(4,128)S(1)}, f32[3,3,64]{2,1,0:T(4,128)}, u32[]{:S(2)}) copy-start(f32[3,3,64]{2,1,0:T(4,128)} %param.19) | copy-start | bytes 6916
  7.6 7.1 %copy-start.4 = (f32[256]{0:T(256)S(1)}, f32[256]{0:T(256)}, u32[]{:S(2)}) copy-start(f32[256]{0:T(256)} %param.17) | copy-start | bytes 3076
  7.6 7.2 %copy-start.2 = (bf16[64,256]{1,0:T(8,128)(2,1)S(1)}, bf16[64,256]{1,0:T(8,128)(2,1)}, u32[]{:S(2)}) copy-start(bf16[64,256]{1,0:T(8,128)(2,1)} %param.16) | copy-start | bytes 98308
  7.7 32.9 %all-to-all-start = ((bf16[32,2,16,512]{3,2,1,0:T(8,128)(2,1)}), bf16[32,2,16,512]{3,2,1,0:T(8,128)(2,1)S(1)}, u32[]{:S(2)}, u32[]{:S(2)}) async-start(bf16[32,2,16,512]{3,2,1,0:T(8,128)(2,1)} %bitcast.13), calls=%async_computation | async-start | bytes 2097152 | tf_op jit(solution)/shard_map/all_to_all | solution.py:287
  14.9 0.8 copy-start.3
  15.8 0.7 copy-start.5
  44.4 29.2 %copy-start.1 = (bf16[32,1,2,16,512]{4,3,2,1,0:T(8,128)(2,1)S(1)}, bf16[32,1,2,16,512]{4,3,2,1,0:T(8,128)(2,1)}, u32[]{:S(2)}) copy-start(bf16[32,1,2,16,512]{4,3,2,1,0:T(8,128)(2,1)} %conv.1.stepped) | copy-start | bytes 3145732
  44.4 29.1 %all-to-all-start.1 = ((bf16[32,2,16,512]{3,2,1,0:T(8,128)(2,1)}), bf16[32,2,16,512]{3,2,1,0:T(8,128)(2,1)S(1)}, u32[]{:S(2)}, u32[]{:S(2)}) async-start(bf16[32,2,16,512]{3,2,1,0:T(8,128)(2,1)} %bitcast.6), calls=%async_computation.1 | async-start | bytes 2097152 | tf_op jit(solution)/shard_map/all_to_all | solution.py:287

commit v13 on v11

--- a/solution.py
+++ b/solution.py
@@ -283,6 +283,17 @@
     return pltpu.CompilerParams(vmem_limit_bytes=mib * MIB)
 
 
+def partner_order(n_rows, n_cols):
+    y, x = n_rows // 2 * n_cols, n_rows // 4 * n_cols
+    half, near, core = n_cols // 2, n_cols // 4, 1
+    steps = [y | x | half | near, core, y | half, y, x]
+    steps += [bit for bit in (1 << k for k in range(1, 16)) if bit < n_rows * n_cols and bit not in (y, x, half, near)]
+    order = [half]
+    for step in steps:
+        order += [device ^ step for device in order]
+    return order
+
+
 def exchange(blocks, order):
     return lax.all_to_all(
         blocks, "all", split_axis=0, concat_axis=0, axis_index_groups=[order], tiled=True
@@ -303,7 +314,7 @@
     psf_len = psf.shape[1]
     assert ch_dev == 2
     n_dev = n_rows * n_cols
-    order = [r * n_cols + (c + n_cols // 2) % n_cols for r in range(n_rows) for c in range(n_cols)]
+    order = partner_order(n_rows, n_cols)
     channels = gain.shape[0]
     hidden = b_in.shape[0]
     part = img * img // (n_dev * BAND)
@@ -344,7 +355,7 @@
     )
 
     def ordered(values):
-        return values.reshape(n_rows, 2, channels // (2 * n_rows), -1)[:, ::-1].reshape(values.shape)
+        return jnp.concatenate([values[d * ch_dev : (d + 1) * ch_dev] for d in order], axis=0)
 
     tiles = exchange(stepped.reshape(n_dev, ch_dev, BAND, part), order).reshape(channels, BAND, part)
 

time: 79.2 us -> 79.3 us (level)
  the two profiles are of different devices: /device:TPU:1 before, /device:TPU:0 now
where the time goes in v13:
time: 79.3 us; the launch traced here: 78.9 us
  waiting for transfers between devices  51.8 us (65%)
  Pallas kernels  14.3 us (18%)
  starting transfers between devices  10.1 us (13%)
  local copies, waits for them, and re-layouts  2.45 us (3%)
    all_to_all x2, waiting for transfers between devices, exchange(): lax.all_to_all(blocks, 'all', split_axis=0, concat_axis=0, axis_index_gro...  51.8 us
    all_to_all x2, starting transfers between devices, exchange(): lax.all_to_all(blocks, 'all', split_axis=0, concat_axis=0, axis_index_gro...  10.1 us
    pallas_call x1, Pallas kernels, local(): pl.pallas_call(conv_kernel, out_shape=jax.ShapeDtypeStruct(blocks, BF16),...  7.61 us
    pallas_call x1, Pallas kernels, local(): pl.pallas_call(mix_kernel, out_shape=jax.ShapeDtypeStruct((channels, BAND...  3.7 us
    pallas_call x1, Pallas kernels, local(): pl.pallas_call(spread_kernel, out_shape=jax.ShapeDtypeStruct((ch_dev, img...  3.04 us
  transfers between devices with their start and end apart: 2, of which 2 were waited for; matrix products, arithmetic and copies ran while one was open for 1% of the time, Pallas kernels for 0%

profile of v13, /device:TPU:0, one launch (start us, length us, event | category | flops | bytes accessed | tf_op | source)
XLA Modules:
  0.0 78.9 jit_solution(7402156907213243891)
XLA Ops:
  0.0 0.0 copy-start
  0.0 7.6 %conv.1.stepped = bf16[32,1,2,16,512]{4,3,2,1,0:T(8,128)(2,1)} custom-call(f32[2]{0:T(128)} %rate_h.1, bf16[2,512,512]{2,1,0:T(8,128)(2,1)} %model_h.1, bf16[2,512,512]{2,1,0:T(8,128)(2,1)} %dirty_h.1, bf16[2,256,256]{2,1,0:T(8,128)(2,1)} %psf_h.1, bf16[640,640]{1,0:T(8,128)(2,1)} %constant.16.clone.table_h, bf16[640,640]{1,0:T(8,128)(2,1)} %constant.17.clone.turned_h), custom_call_target="tpu_custom_call" | custom-call | tf_op jit(solution)/shard_map/conv/pallas_call | solution.py:328
  7.6 0.0 copy-start.5
  7.6 7.3 %all-to-all-start = ((bf16[32,2,16,512]{3,2,1,0:T(8,128)(2,1)}), bf16[32,2,16,512]{3,2,1,0:T(8,128)(2,1)S(1)}, u32[]{:S(2)}, u32[]{:S(2)}) async-start(bf16[32,2,16,512]{3,2,1,0:T(8,128)(2,1)} %bitcast.5), calls=%async_computation | async-start | bytes 2097152 | tf_op jit(solution)/shard_map/all_to_all | solution.py:298
  14.9 0.0 copy-done.5
  15.0 0.0 copy-start.2
  15.0 0.6 copy-done.2
  15.7 0.1 fusion.7
  15.7 0.1 fusion.6
  15.8 0.0 copy-start.3
  15.8 0.0 copy-start.4
  15.8 0.1 concatenate.7
  15.9 0.6 copy-done.3
  16.6 0.0 copy-done.4
  16.7 0.6 concatenate.8.weights
  17.3 24.8 %all-to-all-done = bf16[32,2,16,512]{3,2,1,0:T(8,128)(2,1)S(1)} async-done(((bf16[32,2,16,512]{3,2,1,0:T(8,128)(2,1)}), bf16[32,2,16,512]{3,2,1,0:T(8,128)(2,1)S(1)}, u32[]{:S(2)}, u32[]{:S(2)}) %all-to-all-start) | async-done | bytes 1048608 | tf_op jit(solution)/shard_map/all_to_all | solution.py:298
  42.1 0.1 broadcast_in_dim.7.gain
  42.2 3.7 %mix.1 = bf16[64,16,512]{2,1,0:T(8,128)(2,1)} custom-call(f32[64,512]{1,0:T(8,128)S(1)} %broadcast_in_dim.7.gain, bf16[192,256]{1,0:T(8,128)(2,1)S(1)} %concatenate.8.weights, bf16[64,16,512]{2,1,0:T(8,128)(2,1)S(1)} %bitcast.6), custom_call_target="tpu_custom_call" | custom-call | tf_op jit(solution)/shard_map/mix/pallas_call | solution.py:362
  45.9 0.0 copy-start.1
  45.9 2.8 %all-to-all-start.1 = ((bf16[32,2,16,512]{3,2,1,0:T(8,128)(2,1)}), bf16[32,2,16,512]{3,2,1,0:T(8,128)(2,1)S(1)}, u32[]{:S(2)}, u32[]{:S(2)}) async-start(bf16[32,2,16,512]{3,2,1,0:T(8,128)(2,1)} %bitcast.3), calls=%async_computation.1 | async-start | bytes 2097152 | tf_op jit(solution)/shard_map/all_to_all | solution.py:298
  48.7 0.0 copy-done
  48.7 0.1 constant_dynamic-slice_fusion
  48.8 27.0 %all-to-all-done.1 = bf16[32,2,16,512]{3,2,1,0:T(8,128)(2,1)S(1)} async-done(((bf16[32,2,16,512]{3,2,1,0:T(8,128)(2,1)}), bf16[32,2,16,512]{3,2,1,0:T(8,128)(2,1)S(1)}, u32[]{:S(2)}, u32[]{:S(2)}) %all-to-all-start.1) | async-done | bytes 1048608 | tf_op jit(solution)/shard_map/all_to_all | solution.py:298
  75.8 0.1 broadcast_in_dim.6.taps
  75.9 0.0 copy-done.1
  75.9 3.0 %spread.1 = bf16[2,512,512]{2,1,0:T(8,128)(2,1)} custom-call(f32[3,3,2,128]{3,2,1,0:T(2,128)S(1)} %broadcast_in_dim.6.taps, bf16[32,1,2,16,512]{4,3,2,1,0:T(8,128)(2,1)S(1)} %copy-done.1, bf16[32,1,2,16,512]{4,3,2,1,0:T(8,128)(2,1)S(1)} %bitcast.7), custom_call_target="tpu_custom_call" | custom-call | tf_op jit(solution)/shard_map/spread/pallas_call | solution.py:390
  (9 shorter events, 0.1 us)
Async XLA Ops:
  0.0 48.7 %copy-start = (f32[3,3,64]{2,1,0:T(4,128)S(1)}, f32[3,3,64]{2,1,0:T(4,128)}, u32[]{:S(2)}) copy-start(f32[3,3,64]{2,1,0:T(4,128)} %param.19) | copy-start | bytes 6916
  7.6 7.3 %copy-start.5 = (f32[256]{0:T(256)S(1)}, f32[256]{0:T(256)}, u32[]{:S(2)}) copy-start(f32[256]{0:T(256)} %param.17) | copy-start | bytes 3076
  7.6 34.4 %all-to-all-start = ((bf16[32,2,16,512]{3,2,1,0:T(8,128)(2,1)}), bf16[32,2,16,512]{3,2,1,0:T(8,128)(2,1)S(1)}, u32[]{:S(2)}, u32[]{:S(2)}) async-start(bf16[32,2,16,512]{3,2,1,0:T(8,128)(2,1)} %bitcast.5), calls=%async_computation | async-start | bytes 2097152 | tf_op jit(solution)/shard_map/all_to_all | solution.py:298
  15.0 0.7 copy-start.2
  15.8 0.8 copy-start.3
  15.8 0.8 copy-start.4
  45.9 30.0 %copy-start.1 = (bf16[32,1,2,16,512]{4,3,2,1,0:T(8,128)(2,1)S(1)}, bf16[32,1,2,16,512]{4,3,2,1,0:T(8,128)(2,1)}, u32[]{:S(2)}) copy-start(bf16[32,1,2,16,512]{4,3,2,1,0:T(8,128)(2,1)} %conv.1.stepped) | copy-start | bytes 3145732
  45.9 29.9 %all-to-all-start.1 = ((bf16[32,2,16,512]{3,2,1,0:T(8,128)(2,1)}), bf16[32,2,16,512]{3,2,1,0:T(8,128)(2,1)S(1)}, u32[]{:S(2)}, u32[]{:S(2)}) async-start(bf16[32,2,16,512]{3,2,1,0:T(8,128)(2,1)} %bitcast.3), calls=%async_computation.1 | async-start | bytes 2097152 | tf_op jit(solution)/shard_map/all_to_all | solution.py:298

commit v14 on v13

--- a/solution.py
+++ b/solution.py
@@ -168,15 +168,15 @@
         send.wait()
 
 
-def mix_kernel(gain, weights, tiles, out_h, w_in_t, swap, normed, hidden, mixed, out, sems):
+def mix_kernel(place_of, gain, weights, tiles, out_h, w_in_t, swap, normed, hidden, mixed, out, sems):
     channels, band, part = tiles.shape
     groups = channels // band
 
     depth = channels + band
     w_in_t[...] = weights[: w_in_t.shape[1], :].astype(F32).T.astype(BF16)
     w_out_t = weights[w_in_t.shape[1] :, :]
-    place = [lax.broadcasted_iota(jnp.int32, swap.shape, axis) for axis in range(2)]
-    swap[...] = jnp.where(place[0] % band * band + place[0] // band == place[1], 1.0, 0.0).astype(BF16)
+    index = [lax.broadcasted_iota(jnp.int32, swap.shape, axis) for axis in range(2)]
+    swap[...] = jnp.where(index[0] % band * band + index[0] // band == index[1], 1.0, 0.0).astype(BF16)
     normed[:, channels:, :] = jnp.ones((band, band, part), BF16)
     power = jnp.zeros((band, part), F32)
     for c in range(channels):
@@ -208,23 +208,25 @@
     for g in range(groups):
         block = mixed[:, g * band : (g + 1) * band, :].reshape(band * band, part)
         swapped = dot(swap[...], block).astype(BF16)
-        where = pl.ds(g * band, band)
-        out[where] = swapped.reshape(band, band, part)
-        sends.append(pltpu.make_async_copy(out.at[where], out_h.at[where], sems.at[g]))
-        sends[-1].start()
+        swapped = swapped.reshape(band, band, part)
+        for k in range(0, band, 2):
+            at = 2 * place_of[(g * band + k) // 2]
+            out[at : at + 2] = swapped[k : k + 2]
+            where = pl.ds(at, 2)
+            sends.append(pltpu.make_async_copy(out.at[where], out_h.at[where], sems.at[len(sends)]))
+            sends[-1].start()
     for send in sends:
         send.wait()
 
 
-def spread_kernel(taps, stepped, mixed, out, above, middle, below, result, sems):
+def spread_kernel(place_of, taps, stepped, mixed, out, above, middle, below, result, sems):
     bands, parts, ch_dev, band, part = stepped.shape
     img = parts * part
     group = 4
     size = group * band
 
-    def rows_of(source, start, ch):
-        pieces = [source[start : start + group, p, ch].reshape(size, part) for p in range(parts)]
-        return jnp.concatenate(pieces, axis=1).astype(F32)
+    def rows_of(block):
+        return jnp.concatenate([jnp.concatenate([block(p, b) for b in range(group)]) for p in range(parts)], axis=1).astype(F32)
 
     zero = jnp.zeros((img // 128, 8, 128), F32)
     above[:, 0:8, :] = zero
@@ -235,7 +237,7 @@
         k = [[taps[i, j, ch : ch + 1, :] for j in range(3)] for i in range(3)]
 
         def across(start):
-            x = rows_of(mixed, start, ch)
+            x = rows_of(lambda p, b: mixed[place_of[(start + b) * parts + p], ch])
             low, high = pltpu.roll(x, 1, 1), pltpu.roll(x, img - 1, 1)
             at = start * band
             for n in range(img // 128):
@@ -251,7 +253,7 @@
 
         def down(start):
             at = start * band
-            base = rows_of(stepped, start, ch)
+            base = rows_of(lambda p, b: stepped[start + b, p, ch])
             for n in range(img // 128):
                 total = above[n, at + 7 : at + 7 + size, :] + below[n, at + 1 : at + 1 + size, :]
                 total = total + middle[n, at : at + size, :]
@@ -283,10 +285,10 @@
     return pltpu.CompilerParams(vmem_limit_bytes=mib * MIB)
 
 
-def partner_order(n_rows, n_cols):
+def partner_order(n_rows, n_cols, back):
     y, x = n_rows // 2 * n_cols, n_rows // 4 * n_cols
     half, near, core = n_cols // 2, n_cols // 4, 1
-    steps = [y | x | half | near, core, y | half, y, x]
+    steps = [half | near, core, near, x, y] if back else [half, near, core, x, y]
     steps += [bit for bit in (1 << k for k in range(1, 16)) if bit < n_rows * n_cols and bit not in (y, x, half, near)]
     order = [half]
     for step in steps:
@@ -314,7 +316,7 @@
     psf_len = psf.shape[1]
     assert ch_dev == 2
     n_dev = n_rows * n_cols
-    order = partner_order(n_rows, n_cols)
+    forth, back = (partner_order(n_rows, n_cols, way) for way in (False, True))
     channels = gain.shape[0]
     hidden = b_in.shape[0]
     part = img * img // (n_dev * BAND)
@@ -355,12 +357,12 @@
     )
 
     def ordered(values):
-        return jnp.concatenate([values[d * ch_dev : (d + 1) * ch_dev] for d in order], axis=0)
-
-    tiles = exchange(stepped.reshape(n_dev, ch_dev, BAND, part), order).reshape(channels, BAND, part)
+        return jnp.concatenate([values[d * ch_dev : (d + 1) * ch_dev] for d in forth], axis=0)
+
+    tiles = exchange(stepped.reshape(n_dev, ch_dev, BAND, part), forth).reshape(channels, BAND, part)
 
     mixed = pl.pallas_call(
-        mix_kernel,
+        functools.partial(mix_kernel, [back.index(device) for device in forth]),
         out_shape=jax.ShapeDtypeStruct((channels, BAND, part), BF16),
         in_specs=[VMEM] * 3,
         out_specs=HBM,
@@ -371,7 +373,7 @@
             pltpu.VMEM((BAND, hidden, part), BF16),
             pltpu.VMEM((BAND, channels, part), BF16),
             pltpu.VMEM((channels, BAND, part), BF16),
-            pltpu.SemaphoreType.DMA((channels // BAND,)),
+            pltpu.SemaphoreType.DMA((n_dev,)),
         ],
         compiler_params=params(24),
         name="mix",
@@ -381,14 +383,14 @@
         tiles,
     )
 
-    returned = exchange(mixed.reshape(n_dev, ch_dev, BAND, part), order).reshape(blocks)
+    returned = exchange(mixed.reshape(n_dev, ch_dev, BAND, part), back)
     position = lax.axis_index("all").astype(jnp.int32) * ch_dev
     taps = lax.dynamic_slice_in_dim(kernel, position, ch_dev, axis=2)
     taps = jnp.broadcast_to(taps[..., None], (3, 3, ch_dev, 128))
     plane = pltpu.VMEM((img // 128, img + 8, 128), F32)
 
     return pl.pallas_call(
-        spread_kernel,
+        functools.partial(spread_kernel, [back.index(device) for device in forth]),
         out_shape=jax.ShapeDtypeStruct((ch_dev, img, img), BF16),
         in_specs=[VMEM] * 3,
         out_specs=HBM,

time: 79.3 us -> 79.3 us (level)
  starting transfers between devices: 10.1 us -> 11.2 us
  waiting for transfers between devices: 51.8 us -> 50.7 us
    all_to_all x2, waiting for transfers between devices: 51.8 us -> 50.7 us  [exchange(): lax.all_to_all(blocks, 'all', split_axis=0, concat_axis=0, axis_index_gro...]
    all_to_all x2, starting transfers between devices: 10.1 us -> 11.2 us  [exchange(): lax.all_to_all(blocks, 'all', split_axis=0, concat_axis=0, axis_index_gro...]
where the time goes in v14:
time: 79.3 us; the launch traced here: 79 us
  waiting for transfers between devices  50.7 us (64%)
  Pallas kernels  14.5 us (18%)
  starting transfers between devices  11.2 us (14%)
  local copies, waits for them, and re-layouts  2.44 us (3%)
    all_to_all x2, waiting for transfers between devices, exchange(): lax.all_to_all(blocks, 'all', split_axis=0, concat_axis=0, axis_index_gro...  50.7 us
    all_to_all x2, starting transfers between devices, exchange(): lax.all_to_all(blocks, 'all', split_axis=0, concat_axis=0, axis_index_gro...  11.2 us
    pallas_call x1, Pallas kernels, local(): pl.pallas_call(conv_kernel, out_shape=jax.ShapeDtypeStruct(blocks, BF16),...  7.61 us
    pallas_call x1, Pallas kernels, local(): pl.pallas_call(functools.partial(mix_kernel, [back.index(device) for devi...  3.9 us
    pallas_call x1, Pallas kernels, local(): pl.pallas_call(functools.partial(spread_kernel, [back.index(device) for d...  3 us
  transfers between devices with their start and end apart: 2, of which 2 were waited for; matrix products, arithmetic and copies ran while one was open for 1% of the time, Pallas kernels for 0%

profile of v14, /device:TPU:0, one launch (start us, length us, event | category | flops | bytes accessed | tf_op | source)
XLA Modules:
  0.0 79.0 jit_solution(15573864204418905897)
XLA Ops:
  0.0 0.0 copy-start
  0.0 7.6 %conv.1.stepped = bf16[32,1,2,16,512]{4,3,2,1,0:T(8,128)(2,1)} custom-call(f32[2]{0:T(128)} %rate_h.1, bf16[2,512,512]{2,1,0:T(8,128)(2,1)} %model_h.1, bf16[2,512,512]{2,1,0:T(8,128)(2,1)} %dirty_h.1, bf16[2,256,256]{2,1,0:T(8,128)(2,1)} %psf_h.1, bf16[640,640]{1,0:T(8,128)(2,1)} %constant.16.clone.table_h, bf16[640,640]{1,0:T(8,128)(2,1)} %constant.17.clone.turned_h), custom_call_target="tpu_custom_call" | custom-call | tf_op jit(solution)/shard_map/conv/pallas_call | solution.py:330
  7.6 0.0 copy-start.5
  7.6 7.3 %all-to-all-start = ((bf16[32,2,16,512]{3,2,1,0:T(8,128)(2,1)}), bf16[32,2,16,512]{3,2,1,0:T(8,128)(2,1)S(1)}, u32[]{:S(2)}, u32[]{:S(2)}) async-start(bf16[32,2,16,512]{3,2,1,0:T(8,128)(2,1)} %bitcast.4), calls=%async_computation | async-start | bytes 2097152 | tf_op jit(solution)/shard_map/all_to_all | solution.py:300
  14.9 0.0 copy-done.5
  15.0 0.0 copy-start.2
  15.0 0.6 copy-done.2
  15.7 0.1 fusion.7
  15.7 0.1 fusion.6
  15.8 0.0 copy-start.3
  15.8 0.0 copy-start.4
  15.8 0.1 concatenate.7
  15.9 0.6 copy-done.3
  16.6 0.0 copy-done.4
  16.7 0.6 concatenate.8.weights
  17.3 23.6 %all-to-all-done = bf16[32,2,16,512]{3,2,1,0:T(8,128)(2,1)S(1)} async-done(((bf16[32,2,16,512]{3,2,1,0:T(8,128)(2,1)}), bf16[32,2,16,512]{3,2,1,0:T(8,128)(2,1)S(1)}, u32[]{:S(2)}, u32[]{:S(2)}) %all-to-all-start) | async-done | bytes 1048608 | tf_op jit(solution)/shard_map/all_to_all | solution.py:300
  40.9 0.1 broadcast_in_dim.7.gain
  41.0 3.9 %mix.1 = bf16[64,16,512]{2,1,0:T(8,128)(2,1)} custom-call(f32[64,512]{1,0:T(8,128)S(1)} %broadcast_in_dim.7.gain, bf16[192,256]{1,0:T(8,128)(2,1)S(1)} %concatenate.8.weights, bf16[64,16,512]{2,1,0:T(8,128)(2,1)S(1)} %bitcast.5), custom_call_target="tpu_custom_call" | custom-call | tf_op jit(solution)/shard_map/mix/pallas_call | solution.py:364
  44.9 0.0 copy-start.1
  44.9 3.9 %all-to-all-start.1 = ((bf16[32,2,16,512]{3,2,1,0:T(8,128)(2,1)}), bf16[32,2,16,512]{3,2,1,0:T(8,128)(2,1)S(1)}, u32[]{:S(2)}, u32[]{:S(2)}) async-start(bf16[32,2,16,512]{3,2,1,0:T(8,128)(2,1)} %bitcast.3), calls=%async_computation.1 | async-start | bytes 2097152 | tf_op jit(solution)/shard_map/all_to_all | solution.py:300
  48.8 0.0 copy-done
  48.8 0.1 constant_dynamic-slice_fusion
  48.9 27.0 %all-to-all-done.1.mixed = bf16[32,2,16,512]{3,2,1,0:T(8,128)(2,1)S(1)} async-done(((bf16[32,2,16,512]{3,2,1,0:T(8,128)(2,1)}), bf16[32,2,16,512]{3,2,1,0:T(8,128)(2,1)S(1)}, u32[]{:S(2)}, u32[]{:S(2)}) %all-to-all-start.1) | async-done | bytes 1048608 | tf_op jit(solution)/shard_map/all_to_all | solution.py:300
  75.9 0.1 broadcast_in_dim.6.taps
  76.0 0.0 copy-done.1
  76.0 3.0 %spread.1 = bf16[2,512,512]{2,1,0:T(8,128)(2,1)} custom-call(f32[3,3,2,128]{3,2,1,0:T(2,128)S(1)} %broadcast_in_dim.6.taps, bf16[32,1,2,16,512]{4,3,2,1,0:T(8,128)(2,1)S(1)} %copy-done.1, bf16[32,2,16,512]{3,2,1,0:T(8,128)(2,1)S(1)} %all-to-all-done.1.mixed), custom_call_target="tpu_custom_call" | custom-call | tf_op jit(solution)/shard_map/spread/pallas_call | solution.py:392
  (9 shorter events, 0.1 us)
Async XLA Ops:
  0.0 48.8 %copy-start = (f32[3,3,64]{2,1,0:T(4,128)S(1)}, f32[3,3,64]{2,1,0:T(4,128)}, u32[]{:S(2)}) copy-start(f32[3,3,64]{2,1,0:T(4,128)} %param.19) | copy-start | bytes 6916
  7.6 7.3 %copy-start.5 = (f32[256]{0:T(256)S(1)}, f32[256]{0:T(256)}, u32[]{:S(2)}) copy-start(f32[256]{0:T(256)} %param.17) | copy-start | bytes 3076
  7.6 33.3 %all-to-all-start = ((bf16[32,2,16,512]{3,2,1,0:T(8,128)(2,1)}), bf16[32,2,16,512]{3,2,1,0:T(8,128)(2,1)S(1)}, u32[]{:S(2)}, u32[]{:S(2)}) async-start(bf16[32,2,16,512]{3,2,1,0:T(8,128)(2,1)} %bitcast.4), calls=%async_computation | async-start | bytes 2097152 | tf_op jit(solution)/shard_map/all_to_all | solution.py:300
  15.0 0.7 copy-start.2
  15.8 0.8 copy-start.3
  15.8 0.8 copy-start.4
  44.9 31.1 %copy-start.1 = (bf16[32,1,2,16,512]{4,3,2,1,0:T(8,128)(2,1)S(1)}, bf16[32,1,2,16,512]{4,3,2,1,0:T(8,128)(2,1)}, u32[]{:S(2)}) copy-start(bf16[32,1,2,16,512]{4,3,2,1,0:T(8,128)(2,1)} %conv.1.stepped) | copy-start | bytes 3145732
  44.9 31.0 %all-to-all-start.1 = ((bf16[32,2,16,512]{3,2,1,0:T(8,128)(2,1)}), bf16[32,2,16,512]{3,2,1,0:T(8,128)(2,1)S(1)}, u32[]{:S(2)}, u32[]{:S(2)}) async-start(bf16[32,2,16,512]{3,2,1,0:T(8,128)(2,1)} %bitcast.3), calls=%async_computation.1 | async-start | bytes 2097152 | tf_op jit(solution)/shard_map/all_to_all | solution.py:300

commit v15 on v13

--- a/solution.py
+++ b/solution.py
@@ -284,11 +284,10 @@
 
 
 def partner_order(n_rows, n_cols):
-    y, x = n_rows // 2 * n_cols, n_rows // 4 * n_cols
     half, near, core = n_cols // 2, n_cols // 4, 1
-    steps = [y | x | half | near, core, y | half, y, x]
-    steps += [bit for bit in (1 << k for k in range(1, 16)) if bit < n_rows * n_cols and bit not in (y, x, half, near)]
-    order = [half]
+    steps = [half, core]
+    steps += [bit for bit in (1 << k for k in range(1, 16)) if bit < n_rows * n_cols and bit != half]
+    order = [near]
     for step in steps:
         order += [device ^ step for device in order]
     return order

time: 79.3 us -> 77.5 us (0.977)
  waiting for transfers between devices: 51.8 us -> 49.5 us
    all_to_all x2, waiting for transfers between devices: 51.8 us -> 49.5 us  [exchange(): lax.all_to_all(blocks, 'all', split_axis=0, concat_axis=0, axis_index_gro...]
where the time goes in v15:
time: 77.5 us; the launch traced here: 77.1 us
  waiting for transfers between devices  49.5 us (64%)
  Pallas kernels  14.4 us (19%)
  starting transfers between devices  10.6 us (14%)
  local copies, waits for them, and re-layouts  2.44 us (3%)
    all_to_all x2, waiting for transfers between devices, exchange(): lax.all_to_all(blocks, 'all', split_axis=0, concat_axis=0, axis_index_gro...  49.5 us
    all_to_all x2, starting transfers between devices, exchange(): lax.all_to_all(blocks, 'all', split_axis=0, concat_axis=0, axis_index_gro...  10.6 us
    pallas_call x1, Pallas kernels, local(): pl.pallas_call(conv_kernel, out_shape=jax.ShapeDtypeStruct(blocks, BF16),...  7.61 us
    pallas_call x1, Pallas kernels, local(): pl.pallas_call(mix_kernel, out_shape=jax.ShapeDtypeStruct((channels, BAND...  3.7 us
    pallas_call x1, Pallas kernels, local(): pl.pallas_call(spread_kernel, out_shape=jax.ShapeDtypeStruct((ch_dev, img...  3.04 us
  transfers between devices with their start and end apart: 2, of which 2 were waited for; matrix products, arithmetic and copies ran while one was open for 1% of the time, Pallas kernels for 0%

profile of v15, /device:TPU:0, one launch (start us, length us, event | category | flops | bytes accessed | tf_op | source)
XLA Modules:
  0.0 77.1 jit_solution(16798672264467670907)
XLA Ops:
  0.0 0.0 copy-start
  0.0 7.6 %conv.1.stepped = bf16[32,1,2,16,512]{4,3,2,1,0:T(8,128)(2,1)} custom-call(f32[2]{0:T(128)} %rate_h.1, bf16[2,512,512]{2,1,0:T(8,128)(2,1)} %model_h.1, bf16[2,512,512]{2,1,0:T(8,128)(2,1)} %dirty_h.1, bf16[2,256,256]{2,1,0:T(8,128)(2,1)} %psf_h.1, bf16[640,640]{1,0:T(8,128)(2,1)} %constant.16.clone.table_h, bf16[640,640]{1,0:T(8,128)(2,1)} %constant.17.clone.turned_h), custom_call_target="tpu_custom_call" | custom-call | tf_op jit(solution)/shard_map/conv/pallas_call | solution.py:327
  7.6 0.0 copy-start.5
  7.6 7.3 %all-to-all-start = ((bf16[32,2,16,512]{3,2,1,0:T(8,128)(2,1)}), bf16[32,2,16,512]{3,2,1,0:T(8,128)(2,1)S(1)}, u32[]{:S(2)}, u32[]{:S(2)}) async-start(bf16[32,2,16,512]{3,2,1,0:T(8,128)(2,1)} %bitcast.5), calls=%async_computation | async-start | bytes 2097152 | tf_op jit(solution)/shard_map/all_to_all | solution.py:297
  14.9 0.0 copy-done.5
  15.0 0.0 copy-start.2
  15.0 0.6 copy-done.2
  15.7 0.1 fusion.7
  15.7 0.1 fusion.6
  15.8 0.0 copy-start.3
  15.8 0.0 copy-start.4
  15.8 0.1 concatenate.7
  15.9 0.6 copy-done.3
  16.6 0.0 copy-done.4
  16.7 0.6 concatenate.8.weights
  17.3 23.6 %all-to-all-done = bf16[32,2,16,512]{3,2,1,0:T(8,128)(2,1)S(1)} async-done(((bf16[32,2,16,512]{3,2,1,0:T(8,128)(2,1)}), bf16[32,2,16,512]{3,2,1,0:T(8,128)(2,1)S(1)}, u32[]{:S(2)}, u32[]{:S(2)}) %all-to-all-start) | async-done | bytes 1048608 | tf_op jit(solution)/shard_map/all_to_all | solution.py:297
  40.9 0.1 broadcast_in_dim.7.gain
  41.0 3.7 %mix.1 = bf16[64,16,512]{2,1,0:T(8,128)(2,1)} custom-call(f32[64,512]{1,0:T(8,128)S(1)} %broadcast_in_dim.7.gain, bf16[192,256]{1,0:T(8,128)(2,1)S(1)} %concatenate.8.weights, bf16[64,16,512]{2,1,0:T(8,128)(2,1)S(1)} %bitcast.6), custom_call_target="tpu_custom_call" | custom-call | tf_op jit(solution)/shard_map/mix/pallas_call | solution.py:361
  44.7 0.0 copy-start.1
  44.7 3.3 %all-to-all-start.1 = ((bf16[32,2,16,512]{3,2,1,0:T(8,128)(2,1)}), bf16[32,2,16,512]{3,2,1,0:T(8,128)(2,1)S(1)}, u32[]{:S(2)}, u32[]{:S(2)}) async-start(bf16[32,2,16,512]{3,2,1,0:T(8,128)(2,1)} %bitcast.3), calls=%async_computation.1 | async-start | bytes 2097152 | tf_op jit(solution)/shard_map/all_to_all | solution.py:297
  48.0 0.0 copy-done
  48.1 0.1 constant_dynamic-slice_fusion
  48.1 25.9 %all-to-all-done.1 = bf16[32,2,16,512]{3,2,1,0:T(8,128)(2,1)S(1)} async-done(((bf16[32,2,16,512]{3,2,1,0:T(8,128)(2,1)}), bf16[32,2,16,512]{3,2,1,0:T(8,128)(2,1)S(1)}, u32[]{:S(2)}, u32[]{:S(2)}) %all-to-all-start.1) | async-done | bytes 1048608 | tf_op jit(solution)/shard_map/all_to_all | solution.py:297
  74.0 0.1 broadcast_in_dim.6.taps
  74.1 0.0 copy-done.1
  74.1 3.0 %spread.1 = bf16[2,512,512]{2,1,0:T(8,128)(2,1)} custom-call(f32[3,3,2,128]{3,2,1,0:T(2,128)S(1)} %broadcast_in_dim.6.taps, bf16[32,1,2,16,512]{4,3,2,1,0:T(8,128)(2,1)S(1)} %copy-done.1, bf16[32,1,2,16,512]{4,3,2,1,0:T(8,128)(2,1)S(1)} %bitcast.7), custom_call_target="tpu_custom_call" | custom-call | tf_op jit(solution)/shard_map/spread/pallas_call | solution.py:389
  (9 shorter events, 0.1 us)
Async XLA Ops:
  0.0 48.0 %copy-start = (f32[3,3,64]{2,1,0:T(4,128)S(1)}, f32[3,3,64]{2,1,0:T(4,128)}, u32[]{:S(2)}) copy-start(f32[3,3,64]{2,1,0:T(4,128)} %param.19) | copy-start | bytes 6916
  7.6 7.3 %copy-start.5 = (f32[256]{0:T(256)S(1)}, f32[256]{0:T(256)}, u32[]{:S(2)}) copy-start(f32[256]{0:T(256)} %param.17) | copy-start | bytes 3076
  7.6 33.3 %all-to-all-start = ((bf16[32,2,16,512]{3,2,1,0:T(8,128)(2,1)}), bf16[32,2,16,512]{3,2,1,0:T(8,128)(2,1)S(1)}, u32[]{:S(2)}, u32[]{:S(2)}) async-start(bf16[32,2,16,512]{3,2,1,0:T(8,128)(2,1)} %bitcast.5), calls=%async_computation | async-start | bytes 2097152 | tf_op jit(solution)/shard_map/all_to_all | solution.py:297
  15.0 0.7 copy-start.2
  15.8 0.8 copy-start.3
  15.8 0.8 %copy-start.4 = (bf16[64,256]{1,0:T(8,128)(2,1)S(1)}, bf16[64,256]{1,0:T(8,128)(2,1)}, u32[]{:S(2)}) copy-start(bf16[64,256]{1,0:T(8,128)(2,1)} %param.16) | copy-start | bytes 98308
  44.7 29.4 %copy-start.1 = (bf16[32,1,2,16,512]{4,3,2,1,0:T(8,128)(2,1)S(1)}, bf16[32,1,2,16,512]{4,3,2,1,0:T(8,128)(2,1)}, u32[]{:S(2)}) copy-start(bf16[32,1,2,16,512]{4,3,2,1,0:T(8,128)(2,1)} %conv.1.stepped) | copy-start | bytes 3145732
  44.7 29.3 %all-to-all-start.1 = ((bf16[32,2,16,512]{3,2,1,0:T(8,128)(2,1)}), bf16[32,2,16,512]{3,2,1,0:T(8,128)(2,1)S(1)}, u32[]{:S(2)}, u32[]{:S(2)}) async-start(bf16[32,2,16,512]{3,2,1,0:T(8,128)(2,1)} %bitcast.3), calls=%async_computation.1 | async-start | bytes 2097152 | tf_op jit(solution)/shard_map/all_to_all | solution.py:297

commit v16 on v15

--- a/solution.py
+++ b/solution.py
@@ -70,8 +70,6 @@
     load("turned_1", turned_h, turned, taps, img - taps, 2)
     load("model_1", model_h.at[1], model.at[1], 0, img, 2)
     load("table", table_h, table, 0, length, 4)
-    load("rest", turned_h, turned, img, length - img, 1)
-    load("dirty", dirty_h, dirty, 0, 2, 2)
     loads["rate"] = [pltpu.make_async_copy(rate_h, rate, sems.at[sum(map(len, loads.values()))])]
     loads["rate"][0].start()
 
@@ -87,6 +85,8 @@
                     target[rows, to] = dot(source[ch, rows, :], turned[:depth, lanes]).astype(BF16)
 
     columns(psf, taps, cols_q, (("psf", "turned_0"), ()))
+    load("rest", turned_h, turned, img, length - img, 1)
+    load("dirty", dirty_h, dirty, 0, 2, 2)
     columns(model, img, cols_x, (("model_0", "turned_1"), ("model_1",)))
 
     def spectra(lanes):
@@ -285,9 +285,9 @@
 
 def partner_order(n_rows, n_cols):
     half, near, core = n_cols // 2, n_cols // 4, 1
-    steps = [half, core]
+    steps = [half | near, core]
     steps += [bit for bit in (1 << k for k in range(1, 16)) if bit < n_rows * n_cols and bit != half]
-    order = [near]
+    order = [half | near]
     for step in steps:
         order += [device ^ step for device in order]
     return order

time: 77.5 us -> 80.2 us (1.035)
  waiting for transfers between devices: 49.5 us -> 52.8 us
    all_to_all x2, waiting for transfers between devices: 49.5 us -> 52.8 us  [exchange(): lax.all_to_all(blocks, 'all', split_axis=0, concat_axis=0, axis_index_gro...]
where the time goes in v16:
time: 80.2 us; the launch traced here: 79.8 us
  waiting for transfers between devices  52.8 us (66%)
  Pallas kernels  14.4 us (18%)
  starting transfers between devices  10.1 us (13%)
  local copies, waits for them, and re-layouts  2.44 us (3%)
    all_to_all x2, waiting for transfers between devices, exchange(): lax.all_to_all(blocks, 'all', split_axis=0, concat_axis=0, axis_index_gro...  52.8 us
    all_to_all x2, starting transfers between devices, exchange(): lax.all_to_all(blocks, 'all', split_axis=0, concat_axis=0, axis_index_gro...  10.1 us
    pallas_call x1, Pallas kernels, local(): pl.pallas_call(conv_kernel, out_shape=jax.ShapeDtypeStruct(blocks, BF16),...  7.61 us
    pallas_call x1, Pallas kernels, local(): pl.pallas_call(mix_kernel, out_shape=jax.ShapeDtypeStruct((channels, BAND...  3.71 us
    pallas_call x1, Pallas kernels, local(): pl.pallas_call(spread_kernel, out_shape=jax.ShapeDtypeStruct((ch_dev, img...  3.04 us
  transfers between devices with their start and end apart: 2, of which 2 were waited for; matrix products, arithmetic and copies ran while one was open for 1% of the time, Pallas kernels for 0%

profile of v16, /device:TPU:0, one launch (start us, length us, event | category | flops | bytes accessed | tf_op | source)
XLA Modules:
  0.0 79.8 jit_solution(3336879993051609526)
XLA Ops:
  0.0 0.0 copy-start
  0.0 7.6 %conv.1.stepped = bf16[32,1,2,16,512]{4,3,2,1,0:T(8,128)(2,1)} custom-call(f32[2]{0:T(128)} %rate_h.1, bf16[2,512,512]{2,1,0:T(8,128)(2,1)} %model_h.1, bf16[2,512,512]{2,1,0:T(8,128)(2,1)} %dirty_h.1, bf16[2,256,256]{2,1,0:T(8,128)(2,1)} %psf_h.1, bf16[640,640]{1,0:T(8,128)(2,1)} %constant.16.clone.table_h, bf16[640,640]{1,0:T(8,128)(2,1)} %constant.17.clone.turned_h), custom_call_target="tpu_custom_call" | custom-call | tf_op jit(solution)/shard_map/conv/pallas_call | solution.py:327
  7.6 0.0 copy-start.5
  7.6 7.3 %all-to-all-start = ((bf16[32,2,16,512]{3,2,1,0:T(8,128)(2,1)}), bf16[32,2,16,512]{3,2,1,0:T(8,128)(2,1)S(1)}, u32[]{:S(2)}, u32[]{:S(2)}) async-start(bf16[32,2,16,512]{3,2,1,0:T(8,128)(2,1)} %bitcast.5), calls=%async_computation | async-start | bytes 2097152 | tf_op jit(solution)/shard_map/all_to_all | solution.py:297
  14.9 0.0 copy-done.5
  15.0 0.0 copy-start.2
  15.0 0.6 copy-done.2
  15.7 0.1 fusion.7
  15.7 0.1 fusion.6
  15.8 0.0 copy-start.3
  15.8 0.0 copy-start.4
  15.8 0.1 concatenate.7
  15.9 0.6 copy-done.3
  16.6 0.0 copy-done.4
  16.7 0.6 concatenate.8.weights
  17.3 25.3 %all-to-all-done = bf16[32,2,16,512]{3,2,1,0:T(8,128)(2,1)S(1)} async-done(((bf16[32,2,16,512]{3,2,1,0:T(8,128)(2,1)}), bf16[32,2,16,512]{3,2,1,0:T(8,128)(2,1)S(1)}, u32[]{:S(2)}, u32[]{:S(2)}) %all-to-all-start) | async-done | bytes 1048608 | tf_op jit(solution)/shard_map/all_to_all | solution.py:297
  42.5 0.1 broadcast_in_dim.7.gain
  42.6 3.7 %mix.1 = bf16[64,16,512]{2,1,0:T(8,128)(2,1)} custom-call(f32[64,512]{1,0:T(8,128)S(1)} %broadcast_in_dim.7.gain, bf16[192,256]{1,0:T(8,128)(2,1)S(1)} %concatenate.8.weights, bf16[64,16,512]{2,1,0:T(8,128)(2,1)S(1)} %bitcast.6), custom_call_target="tpu_custom_call" | custom-call | tf_op jit(solution)/shard_map/mix/pallas_call | solution.py:361
  46.3 0.0 copy-start.1
  46.3 2.8 %all-to-all-start.1 = ((bf16[32,2,16,512]{3,2,1,0:T(8,128)(2,1)}), bf16[32,2,16,512]{3,2,1,0:T(8,128)(2,1)S(1)}, u32[]{:S(2)}, u32[]{:S(2)}) async-start(bf16[32,2,16,512]{3,2,1,0:T(8,128)(2,1)} %bitcast.3), calls=%async_computation.1 | async-start | bytes 2097152 | tf_op jit(solution)/shard_map/all_to_all | solution.py:297
  49.1 0.0 copy-done
  49.1 0.1 constant_dynamic-slice_fusion
  49.2 27.5 %all-to-all-done.1 = bf16[32,2,16,512]{3,2,1,0:T(8,128)(2,1)S(1)} async-done(((bf16[32,2,16,512]{3,2,1,0:T(8,128)(2,1)}), bf16[32,2,16,512]{3,2,1,0:T(8,128)(2,1)S(1)}, u32[]{:S(2)}, u32[]{:S(2)}) %all-to-all-start.1) | async-done | bytes 1048608 | tf_op jit(solution)/shard_map/all_to_all | solution.py:297
  76.7 0.1 broadcast_in_dim.6.taps
  76.8 0.0 copy-done.1
  76.8 3.0 %spread.1 = bf16[2,512,512]{2,1,0:T(8,128)(2,1)} custom-call(f32[3,3,2,128]{3,2,1,0:T(2,128)S(1)} %broadcast_in_dim.6.taps, bf16[32,1,2,16,512]{4,3,2,1,0:T(8,128)(2,1)S(1)} %copy-done.1, bf16[32,1,2,16,512]{4,3,2,1,0:T(8,128)(2,1)S(1)} %bitcast.7), custom_call_target="tpu_custom_call" | custom-call | tf_op jit(solution)/shard_map/spread/pallas_call | solution.py:389
  (9 shorter events, 0.1 us)
Async XLA Ops:
  0.0 49.1 %copy-start = (f32[3,3,64]{2,1,0:T(4,128)S(1)}, f32[3,3,64]{2,1,0:T(4,128)}, u32[]{:S(2)}) copy-start(f32[3,3,64]{2,1,0:T(4,128)} %param.19) | copy-start | bytes 6916
  7.6 7.3 %copy-start.5 = (f32[256]{0:T(256)S(1)}, f32[256]{0:T(256)}, u32[]{:S(2)}) copy-start(f32[256]{0:T(256)} %param.17) | copy-start | bytes 3076
  7.6 34.9 %all-to-all-start = ((bf16[32,2,16,512]{3,2,1,0:T(8,128)(2,1)}), bf16[32,2,16,512]{3,2,1,0:T(8,128)(2,1)S(1)}, u32[]{:S(2)}, u32[]{:S(2)}) async-start(bf16[32,2,16,512]{3,2,1,0:T(8,128)(2,1)} %bitcast.5), calls=%async_computation | async-start | bytes 2097152 | tf_op jit(solution)/shard_map/all_to_all | solution.py:297
  15.0 0.7 copy-start.2
  15.8 0.8 copy-start.3
  15.8 0.8 copy-start.4
  46.3 30.5 %copy-start.1 = (bf16[32,1,2,16,512]{4,3,2,1,0:T(8,128)(2,1)S(1)}, bf16[32,1,2,16,512]{4,3,2,1,0:T(8,128)(2,1)}, u32[]{:S(2)}) copy-start(bf16[32,1,2,16,512]{4,3,2,1,0:T(8,128)(2,1)} %conv.1.stepped) | copy-start | bytes 3145732
  46.3 30.4 %all-to-all-start.1 = ((bf16[32,2,16,512]{3,2,1,0:T(8,128)(2,1)}), bf16[32,2,16,512]{3,2,1,0:T(8,128)(2,1)S(1)}, u32[]{:S(2)}, u32[]{:S(2)}) async-start(bf16[32,2,16,512]{3,2,1,0:T(8,128)(2,1)} %bitcast.3), calls=%async_computation.1 | async-start | bytes 2097152 | tf_op jit(solution)/shard_map/all_to_all | solution.py:297

commit v17 on v16

--- a/solution.py
+++ b/solution.py
@@ -284,12 +284,12 @@
 
 
 def partner_order(n_rows, n_cols):
-    half, near, core = n_cols // 2, n_cols // 4, 1
-    steps = [half | near, core]
-    steps += [bit for bit in (1 << k for k in range(1, 16)) if bit < n_rows * n_cols and bit != half]
-    order = [half | near]
-    for step in steps:
-        order += [device ^ step for device in order]
+    side = n_cols // 2
+    up = [half * side + k for k in range(side) for half in (0, 1)]
+    order = []
+    for i in range(n_rows):
+        row = i ^ (i >> 1)
+        order += [row * n_cols + c for c in (reversed(up) if i % 2 else up)]
     return order
 
 

time: 80.2 us -> 77 us (0.960)
  waiting for transfers between devices: 52.8 us -> 48.6 us
  starting transfers between devices: 10.1 us -> 11.1 us
    all_to_all x2, waiting for transfers between devices: 52.8 us -> 48.6 us  [exchange(): lax.all_to_all(blocks, 'all', split_axis=0, concat_axis=0, axis_index_gro...]
    all_to_all x2, starting transfers between devices: 10.1 us -> 11.1 us  [exchange(): lax.all_to_all(blocks, 'all', split_axis=0, concat_axis=0, axis_index_gro...]
where the time goes in v17:
time: 77 us; the launch traced here: 76.7 us
  waiting for transfers between devices  48.6 us (63%)
  Pallas kernels  14.3 us (19%)
  starting transfers between devices  11.1 us (14%)
  local copies, waits for them, and re-layouts  2.44 us (3%)
    all_to_all x2, waiting for transfers between devices, exchange(): lax.all_to_all(blocks, 'all', split_axis=0, concat_axis=0, axis_index_gro...  48.6 us
    all_to_all x2, starting transfers between devices, exchange(): lax.all_to_all(blocks, 'all', split_axis=0, concat_axis=0, axis_index_gro...  11.1 us
    pallas_call x1, Pallas kernels, local(): pl.pallas_call(conv_kernel, out_shape=jax.ShapeDtypeStruct(blocks, BF16),...  7.61 us
    pallas_call x1, Pallas kernels, local(): pl.pallas_call(mix_kernel, out_shape=jax.ShapeDtypeStruct((channels, BAND...  3.7 us
    pallas_call x1, Pallas kernels, local(): pl.pallas_call(spread_kernel, out_shape=jax.ShapeDtypeStruct((ch_dev, img...  3.04 us
  transfers between devices with their start and end apart: 2, of which 2 were waited for; matrix products, arithmetic and copies ran while one was open for 1% of the time, Pallas kernels for 0%

profile of v17, /device:TPU:0, one launch (start us, length us, event | category | flops | bytes accessed | tf_op | source)
XLA Modules:
  0.0 76.7 jit_solution(4095653012852520883)
XLA Ops:
  0.0 0.0 copy-start
  0.0 7.6 %conv.1.stepped = bf16[32,1,2,16,512]{4,3,2,1,0:T(8,128)(2,1)} custom-call(f32[2]{0:T(128)} %rate_h.1, bf16[2,512,512]{2,1,0:T(8,128)(2,1)} %model_h.1, bf16[2,512,512]{2,1,0:T(8,128)(2,1)} %dirty_h.1, bf16[2,256,256]{2,1,0:T(8,128)(2,1)} %psf_h.1, bf16[640,640]{1,0:T(8,128)(2,1)} %constant.16.clone.table_h, bf16[640,640]{1,0:T(8,128)(2,1)} %constant.17.clone.turned_h), custom_call_target="tpu_custom_call" | custom-call | tf_op jit(solution)/shard_map/conv/pallas_call | solution.py:327
  7.6 0.0 copy-start.5
  7.6 7.3 %all-to-all-start = ((bf16[32,2,16,512]{3,2,1,0:T(8,128)(2,1)}), bf16[32,2,16,512]{3,2,1,0:T(8,128)(2,1)S(1)}, u32[]{:S(2)}, u32[]{:S(2)}) async-start(bf16[32,2,16,512]{3,2,1,0:T(8,128)(2,1)} %bitcast.5), calls=%async_computation | async-start | bytes 2097152 | tf_op jit(solution)/shard_map/all_to_all | solution.py:297
  14.9 0.0 copy-done.5
  15.0 0.0 copy-start.2
  15.0 0.6 copy-done.2
  15.7 0.1 fusion.7
  15.7 0.1 fusion.6
  15.8 0.0 copy-start.3
  15.8 0.0 copy-start.4
  15.8 0.1 concatenate.7
  15.9 0.6 copy-done.3
  16.6 0.0 copy-done.4
  16.7 0.6 concatenate.8.weights
  17.3 23.2 %all-to-all-done = bf16[32,2,16,512]{3,2,1,0:T(8,128)(2,1)S(1)} async-done(((bf16[32,2,16,512]{3,2,1,0:T(8,128)(2,1)}), bf16[32,2,16,512]{3,2,1,0:T(8,128)(2,1)S(1)}, u32[]{:S(2)}, u32[]{:S(2)}) %all-to-all-start) | async-done | bytes 1048608 | tf_op jit(solution)/shard_map/all_to_all | solution.py:297
  40.4 0.1 broadcast_in_dim.7.gain
  40.5 3.7 %mix.1 = bf16[64,16,512]{2,1,0:T(8,128)(2,1)} custom-call(f32[64,512]{1,0:T(8,128)S(1)} %broadcast_in_dim.7.gain, bf16[192,256]{1,0:T(8,128)(2,1)S(1)} %concatenate.8.weights, bf16[64,16,512]{2,1,0:T(8,128)(2,1)S(1)} %bitcast.6), custom_call_target="tpu_custom_call" | custom-call | tf_op jit(solution)/shard_map/mix/pallas_call | solution.py:361
  44.2 0.0 copy-start.1
  44.2 3.8 %all-to-all-start.1 = ((bf16[32,2,16,512]{3,2,1,0:T(8,128)(2,1)}), bf16[32,2,16,512]{3,2,1,0:T(8,128)(2,1)S(1)}, u32[]{:S(2)}, u32[]{:S(2)}) async-start(bf16[32,2,16,512]{3,2,1,0:T(8,128)(2,1)} %bitcast.3), calls=%async_computation.1 | async-start | bytes 2097152 | tf_op jit(solution)/shard_map/all_to_all | solution.py:297
  48.0 0.0 copy-done
  48.1 0.1 constant_dynamic-slice_fusion
  48.1 25.4 %all-to-all-done.1 = bf16[32,2,16,512]{3,2,1,0:T(8,128)(2,1)S(1)} async-done(((bf16[32,2,16,512]{3,2,1,0:T(8,128)(2,1)}), bf16[32,2,16,512]{3,2,1,0:T(8,128)(2,1)S(1)}, u32[]{:S(2)}, u32[]{:S(2)}) %all-to-all-start.1) | async-done | bytes 1048608 | tf_op jit(solution)/shard_map/all_to_all | solution.py:297
  73.5 0.1 broadcast_in_dim.6.taps
  73.6 0.0 copy-done.1
  73.6 3.0 %spread.1 = bf16[2,512,512]{2,1,0:T(8,128)(2,1)} custom-call(f32[3,3,2,128]{3,2,1,0:T(2,128)S(1)} %broadcast_in_dim.6.taps, bf16[32,1,2,16,512]{4,3,2,1,0:T(8,128)(2,1)S(1)} %copy-done.1, bf16[32,1,2,16,512]{4,3,2,1,0:T(8,128)(2,1)S(1)} %bitcast.7), custom_call_target="tpu_custom_call" | custom-call | tf_op jit(solution)/shard_map/spread/pallas_call | solution.py:389
  (9 shorter events, 0.1 us)
Async XLA Ops:
  0.0 48.0 %copy-start = (f32[3,3,64]{2,1,0:T(4,128)S(1)}, f32[3,3,64]{2,1,0:T(4,128)}, u32[]{:S(2)}) copy-start(f32[3,3,64]{2,1,0:T(4,128)} %param.19) | copy-start | bytes 6916
  7.6 7.3 %copy-start.5 = (f32[256]{0:T(256)S(1)}, f32[256]{0:T(256)}, u32[]{:S(2)}) copy-start(f32[256]{0:T(256)} %param.17) | copy-start | bytes 3076
  7.6 32.8 %all-to-all-start = ((bf16[32,2,16,512]{3,2,1,0:T(8,128)(2,1)}), bf16[32,2,16,512]{3,2,1,0:T(8,128)(2,1)S(1)}, u32[]{:S(2)}, u32[]{:S(2)}) async-start(bf16[32,2,16,512]{3,2,1,0:T(8,128)(2,1)} %bitcast.5), calls=%async_computation | async-start | bytes 2097152 | tf_op jit(solution)/shard_map/all_to_all | solution.py:297
  15.0 0.7 copy-start.2
  15.8 0.8 copy-start.3
  15.8 0.8 %copy-start.4 = (bf16[64,256]{1,0:T(8,128)(2,1)S(1)}, bf16[64,256]{1,0:T(8,128)(2,1)}, u32[]{:S(2)}) copy-start(bf16[64,256]{1,0:T(8,128)(2,1)} %param.16) | copy-start | bytes 98308
  44.2 29.4 %copy-start.1 = (bf16[32,1,2,16,512]{4,3,2,1,0:T(8,128)(2,1)S(1)}, bf16[32,1,2,16,512]{4,3,2,1,0:T(8,128)(2,1)}, u32[]{:S(2)}) copy-start(bf16[32,1,2,16,512]{4,3,2,1,0:T(8,128)(2,1)} %conv.1.stepped) | copy-start | bytes 3145732
  44.2 29.3 %all-to-all-start.1 = ((bf16[32,2,16,512]{3,2,1,0:T(8,128)(2,1)}), bf16[32,2,16,512]{3,2,1,0:T(8,128)(2,1)S(1)}, u32[]{:S(2)}, u32[]{:S(2)}) async-start(bf16[32,2,16,512]{3,2,1,0:T(8,128)(2,1)} %bitcast.3), calls=%async_computation.1 | async-start | bytes 2097152 | tf_op jit(solution)/shard_map/all_to_all | solution.py:297

commit v18 on v17

--- a/solution.py
+++ b/solution.py
@@ -216,60 +216,58 @@
         send.wait()
 
 
-def spread_kernel(taps, stepped, mixed, out, above, middle, below, result, sems):
+def spread_kernel(taps, stepped, mixed, out, rows_0, rows_1, result, sems):
     bands, parts, ch_dev, band, part = stepped.shape
     img = parts * part
-    group = 4
+    group = 2
     size = group * band
+    strips = [slice(n, n + 128) for n in range(0, img, 128)]
+    lane = lax.broadcasted_iota(jnp.int32, (size, 128), 1)
+    zero = jnp.zeros((len(strips), 8, 128), F32)
+    sends = []
 
     def rows_of(source, start, ch):
         pieces = [source[start : start + group, p, ch].reshape(size, part) for p in range(parts)]
         return jnp.concatenate(pieces, axis=1).astype(F32)
 
-    zero = jnp.zeros((img // 128, 8, 128), F32)
-    above[:, 0:8, :] = zero
-    below[:, img : img + 8, :] = zero
-    lane = lax.broadcasted_iota(jnp.int32, (size, 128), 1)
-    sends = []
-    for ch in range(ch_dev):
+    for ch, padded in ((0, rows_0), (1, rows_1)):
         k = [[taps[i, j, ch : ch + 1, :] for j in range(3)] for i in range(3)]
-
-        def across(start):
+        padded[:, 0:8, :] = zero
+        padded[:, img + 8 : img + 16, :] = zero
+
+        def fill(start):
             x = rows_of(mixed, start, ch)
-            low, high = pltpu.roll(x, 1, 1), pltpu.roll(x, img - 1, 1)
+            for n, lanes in enumerate(strips):
+                padded[n, start * band + 8 : start * band + 8 + size, :] = x[:, lanes]
+
+        def finish(start):
             at = start * band
-            for n in range(img // 128):
-                lanes = slice(n * 128, (n + 1) * 128)
-                left, here, right = low[:, lanes], x[:, lanes], high[:, lanes]
+            sums = [[], [], []]
+            for n in range(len(strips)):
+                x = [padded[n, at + 7 + i : at + 7 + i + size, :] for i in range(3)]
+                for j in range(3):
+                    sums[j].append(k[0][j] * x[0] + k[1][j] * x[1] + k[2][j] * x[2])
+            left = pltpu.roll(jnp.concatenate(sums[0], axis=1), 1, 1)
+            right = pltpu.roll(jnp.concatenate(sums[2], axis=1), img - 1, 1)
+            base = rows_of(stepped, start, ch)
+            for n, lanes in enumerate(strips):
+                low, high = left[:, lanes], right[:, lanes]
                 if n == 0:
-                    left = jnp.where(lane == 0, 0.0, left)
-                if n == img // 128 - 1:
-                    right = jnp.where(lane == 127, 0.0, right)
-                for target, row, off in ((above, 0, 8), (middle, 1, 0), (below, 2, 0)):
-                    value = k[row][0] * left + k[row][1] * here + k[row][2] * right
-                    target[n, at + off : at + off + size, :] = value
-
-        def down(start):
-            at = start * band
-            base = rows_of(stepped, start, ch)
-            for n in range(img // 128):
-                total = above[n, at + 7 : at + 7 + size, :] + below[n, at + 1 : at + 1 + size, :]
-                total = total + middle[n, at : at + size, :]
-                total = base[:, n * 128 : (n + 1) * 128] + total
-                result[ch, at : at + size, n * 128 : (n + 1) * 128] = total.astype(BF16)
-
-        def leave(start):
-            down(start)
-            rows = pl.ds(start * band, size)
-            at = sems.at[ch * (bands // group) + start // group]
-            sends.append(pltpu.make_async_copy(result.at[ch, rows], out.at[ch, rows], at))
-            sends[-1].start()
-
+                    low = jnp.where(lane == 0, 0.0, low)
+                if n == len(strips) - 1:
+                    high = jnp.where(lane == 127, 0.0, high)
+                total = base[:, lanes] + (sums[1][n] + (low + high))
+                result[ch, at : at + size, lanes] = total.astype(BF16)
+            if (at + size) % 64 == 0:
+                rows = pl.ds(at + size - 64, 64)
+                sends.append(pltpu.make_async_copy(result.at[ch, rows], out.at[ch, rows], sems.at[len(sends)]))
+                sends[-1].start()
+
+        fill(0)
         for start in range(0, bands, group):
-            across(start)
-            if start:
-                leave(start - group)
-        leave(bands - group)
+            if start + group < bands:
+                fill(start + group)
+            finish(start)
     for send in sends:
         send.wait()
 
@@ -384,7 +382,7 @@
     position = lax.axis_index("all").astype(jnp.int32) * ch_dev
     taps = lax.dynamic_slice_in_dim(kernel, position, ch_dev, axis=2)
     taps = jnp.broadcast_to(taps[..., None], (3, 3, ch_dev, 128))
-    plane = pltpu.VMEM((img // 128, img + 8, 128), F32)
+    plane = pltpu.VMEM((img // 128, img + 16, 128), F32)
 
     return pl.pallas_call(
         spread_kernel,
@@ -392,8 +390,8 @@
         in_specs=[VMEM] * 3,
         out_specs=HBM,
         scratch_shapes=[
-            plane, plane, plane, pltpu.VMEM((ch_dev, img, img), BF16),
-            pltpu.SemaphoreType.DMA((ch_dev * bands // 4,)),
+            plane, plane, pltpu.VMEM((ch_dev, img, img), BF16),
+            pltpu.SemaphoreType.DMA((ch_dev * img // 64,)),
         ],
         compiler_params=params(24),
         name="spread",

time: 77 us -> 76.8 us (level)
  no operation moved by 1% of the time
where the time goes in v18:
time: 76.8 us; the launch traced here: 76.5 us
  waiting for transfers between devices  48.6 us (63%)
  Pallas kernels  14.2 us (18%)
  starting transfers between devices  11.1 us (14%)
  local copies, waits for them, and re-layouts  2.44 us (3%)
    all_to_all x2, waiting for transfers between devices, exchange(): lax.all_to_all(blocks, 'all', split_axis=0, concat_axis=0, axis_index_gro...  48.6 us
    all_to_all x2, starting transfers between devices, exchange(): lax.all_to_all(blocks, 'all', split_axis=0, concat_axis=0, axis_index_gro...  11.1 us
    pallas_call x1, Pallas kernels, local(): pl.pallas_call(conv_kernel, out_shape=jax.ShapeDtypeStruct(blocks, BF16),...  7.61 us
    pallas_call x1, Pallas kernels, local(): pl.pallas_call(mix_kernel, out_shape=jax.ShapeDtypeStruct((channels, BAND...  3.7 us
    pallas_call x1, Pallas kernels, local(): pl.pallas_call(spread_kernel, out_shape=jax.ShapeDtypeStruct((ch_dev, img...  2.84 us
  transfers between devices with their start and end apart: 2, of which 2 were waited for; matrix products, arithmetic and copies ran while one was open for 1% of the time, Pallas kernels for 0%

profile of v18, /device:TPU:0, one launch (start us, length us, event | category | flops | bytes accessed | tf_op | source)
XLA Modules:
  0.0 76.5 jit_solution(14369219295678829881)
XLA Ops:
  0.0 0.0 copy-start
  0.0 7.6 %conv.1.stepped = bf16[32,1,2,16,512]{4,3,2,1,0:T(8,128)(2,1)} custom-call(f32[2]{0:T(128)} %rate_h.1, bf16[2,512,512]{2,1,0:T(8,128)(2,1)} %model_h.1, bf16[2,512,512]{2,1,0:T(8,128)(2,1)} %dirty_h.1, bf16[2,256,256]{2,1,0:T(8,128)(2,1)} %psf_h.1, bf16[640,640]{1,0:T(8,128)(2,1)} %constant.16.clone.table_h, bf16[640,640]{1,0:T(8,128)(2,1)} %constant.17.clone.turned_h), custom_call_target="tpu_custom_call" | custom-call | tf_op jit(solution)/shard_map/conv/pallas_call | solution.py:325
  7.6 0.0 copy-start.5
  7.6 7.3 %all-to-all-start = ((bf16[32,2,16,512]{3,2,1,0:T(8,128)(2,1)}), bf16[32,2,16,512]{3,2,1,0:T(8,128)(2,1)S(1)}, u32[]{:S(2)}, u32[]{:S(2)}) async-start(bf16[32,2,16,512]{3,2,1,0:T(8,128)(2,1)} %bitcast.5), calls=%async_computation | async-start | bytes 2097152 | tf_op jit(solution)/shard_map/all_to_all | solution.py:295
  14.9 0.0 copy-done.5
  15.0 0.0 copy-start.2
  15.0 0.6 copy-done.2
  15.7 0.1 fusion.7
  15.7 0.1 fusion.6
  15.8 0.0 copy-start.3
  15.8 0.0 copy-start.4
  15.8 0.1 concatenate.7
  15.9 0.6 copy-done.3
  16.6 0.0 copy-done.4
  16.7 0.6 concatenate.8.weights
  17.3 23.2 %all-to-all-done = bf16[32,2,16,512]{3,2,1,0:T(8,128)(2,1)S(1)} async-done(((bf16[32,2,16,512]{3,2,1,0:T(8,128)(2,1)}), bf16[32,2,16,512]{3,2,1,0:T(8,128)(2,1)S(1)}, u32[]{:S(2)}, u32[]{:S(2)}) %all-to-all-start) | async-done | bytes 1048608 | tf_op jit(solution)/shard_map/all_to_all | solution.py:295
  40.4 0.1 broadcast_in_dim.7.gain
  40.5 3.7 %mix.1 = bf16[64,16,512]{2,1,0:T(8,128)(2,1)} custom-call(f32[64,512]{1,0:T(8,128)S(1)} %broadcast_in_dim.7.gain, bf16[192,256]{1,0:T(8,128)(2,1)S(1)} %concatenate.8.weights, bf16[64,16,512]{2,1,0:T(8,128)(2,1)S(1)} %bitcast.6), custom_call_target="tpu_custom_call" | custom-call | tf_op jit(solution)/shard_map/mix/pallas_call | solution.py:359
  44.2 0.0 copy-start.1
  44.2 3.8 %all-to-all-start.1 = ((bf16[32,2,16,512]{3,2,1,0:T(8,128)(2,1)}), bf16[32,2,16,512]{3,2,1,0:T(8,128)(2,1)S(1)}, u32[]{:S(2)}, u32[]{:S(2)}) async-start(bf16[32,2,16,512]{3,2,1,0:T(8,128)(2,1)} %bitcast.3), calls=%async_computation.1 | async-start | bytes 2097152 | tf_op jit(solution)/shard_map/all_to_all | solution.py:295
  48.0 0.0 copy-done
  48.1 0.1 constant_dynamic-slice_fusion
  48.1 25.4 %all-to-all-done.1 = bf16[32,2,16,512]{3,2,1,0:T(8,128)(2,1)S(1)} async-done(((bf16[32,2,16,512]{3,2,1,0:T(8,128)(2,1)}), bf16[32,2,16,512]{3,2,1,0:T(8,128)(2,1)S(1)}, u32[]{:S(2)}, u32[]{:S(2)}) %all-to-all-start.1) | async-done | bytes 1048608 | tf_op jit(solution)/shard_map/all_to_all | solution.py:295
  73.5 0.1 broadcast_in_dim.6.taps
  73.6 0.0 copy-done.1
  73.6 2.8 %spread.1 = bf16[2,512,512]{2,1,0:T(8,128)(2,1)} custom-call(f32[3,3,2,128]{3,2,1,0:T(2,128)S(1)} %broadcast_in_dim.6.taps, bf16[32,1,2,16,512]{4,3,2,1,0:T(8,128)(2,1)S(1)} %copy-done.1, bf16[32,1,2,16,512]{4,3,2,1,0:T(8,128)(2,1)S(1)} %bitcast.7), custom_call_target="tpu_custom_call" | custom-call | tf_op jit(solution)/shard_map/spread/pallas_call | solution.py:387
  (9 shorter events, 0.1 us)
Async XLA Ops:
  0.0 48.0 %copy-start = (f32[3,3,64]{2,1,0:T(4,128)S(1)}, f32[3,3,64]{2,1,0:T(4,128)}, u32[]{:S(2)}) copy-start(f32[3,3,64]{2,1,0:T(4,128)} %param.19) | copy-start | bytes 6916
  7.6 7.3 %copy-start.5 = (f32[256]{0:T(256)S(1)}, f32[256]{0:T(256)}, u32[]{:S(2)}) copy-start(f32[256]{0:T(256)} %param.17) | copy-start | bytes 3076
  7.6 32.8 %all-to-all-start = ((bf16[32,2,16,512]{3,2,1,0:T(8,128)(2,1)}), bf16[32,2,16,512]{3,2,1,0:T(8,128)(2,1)S(1)}, u32[]{:S(2)}, u32[]{:S(2)}) async-start(bf16[32,2,16,512]{3,2,1,0:T(8,128)(2,1)} %bitcast.5), calls=%async_computation | async-start | bytes 2097152 | tf_op jit(solution)/shard_map/all_to_all | solution.py:295
  15.0 0.7 copy-start.2
  15.8 0.8 %copy-start.3 = (bf16[256,64]{0,1:T(8,128)(2,1)S(1)}, bf16[256,64]{0,1:T(8,128)(2,1)}, u32[]{:S(2)}) copy-start(bf16[256,64]{0,1:T(8,128)(2,1)} %param.18) | copy-start | bytes 98308
  15.8 0.8 %copy-start.4 = (bf16[64,256]{1,0:T(8,128)(2,1)S(1)}, bf16[64,256]{1,0:T(8,128)(2,1)}, u32[]{:S(2)}) copy-start(bf16[64,256]{1,0:T(8,128)(2,1)} %param.16) | copy-start | bytes 98308
  44.2 29.4 %copy-start.1 = (bf16[32,1,2,16,512]{4,3,2,1,0:T(8,128)(2,1)S(1)}, bf16[32,1,2,16,512]{4,3,2,1,0:T(8,128)(2,1)}, u32[]{:S(2)}) copy-start(bf16[32,1,2,16,512]{4,3,2,1,0:T(8,128)(2,1)} %conv.1.stepped) | copy-start | bytes 3145732
  44.2 29.3 %all-to-all-start.1 = ((bf16[32,2,16,512]{3,2,1,0:T(8,128)(2,1)}), bf16[32,2,16,512]{3,2,1,0:T(8,128)(2,1)S(1)}, u32[]{:S(2)}, u32[]{:S(2)}) async-start(bf16[32,2,16,512]{3,2,1,0:T(8,128)(2,1)} %bitcast.3), calls=%async_computation.1 | async-start | bytes 2097152 | tf_op jit(solution)/shard_map/all_to_all | solution.py:295

commit v19 on v18

--- a/solution.py
+++ b/solution.py
@@ -173,6 +173,7 @@
     groups = channels // band
 
     depth = channels + band
+    blocks = [slice(n, min(n + 256, part)) for n in range(0, part, 256)]
     w_in_t[...] = weights[: w_in_t.shape[1], :].astype(F32).T.astype(BF16)
     w_out_t = weights[w_in_t.shape[1] :, :]
     place = [lax.broadcasted_iota(jnp.int32, swap.shape, axis) for axis in range(2)]
@@ -188,11 +189,13 @@
             (tiles[c].astype(F32) * inverse * gain[c : c + 1, :]).astype(BF16)
             for c in range(g * band, (g + 1) * band)
         ]
-        swapped = dot(swap[...], jnp.concatenate(rows, axis=0)).astype(BF16)
-        normed[:, g * band : (g + 1) * band, :] = swapped.reshape(band, band, part)
+        block = jnp.concatenate(rows, axis=0)
+        for lanes in blocks:
+            for h in range(0, band, 8):
+                swapped = dot(swap[h * band : (h + 8) * band, :], block[:, lanes]).astype(BF16)
+                normed[h : h + 8, g * band : (g + 1) * band, lanes] = swapped.reshape(8, band, -1)
 
     a = math.sqrt(2.0 / math.pi)
-    blocks = [slice(n, min(n + 256, part)) for n in range(0, part, 256)]
     for r in range(band):
         for lanes in blocks:
             for h in range(0, hidden.shape[1], 128):
@@ -207,9 +210,11 @@
     sends = []
     for g in range(groups):
         block = mixed[:, g * band : (g + 1) * band, :].reshape(band * band, part)
-        swapped = dot(swap[...], block).astype(BF16)
+        for lanes in blocks:
+            for h in range(0, band, 8):
+                swapped = dot(swap[h * band : (h + 8) * band, :], block[:, lanes]).astype(BF16)
+                out[g * band + h : g * band + h + 8, :, lanes] = swapped.reshape(8, band, -1)
         where = pl.ds(g * band, band)
-        out[where] = swapped.reshape(band, band, part)
         sends.append(pltpu.make_async_copy(out.at[where], out_h.at[where], sems.at[g]))
         sends[-1].start()
     for send in sends:
@@ -283,12 +288,8 @@
 
 def partner_order(n_rows, n_cols):
     side = n_cols // 2
-    up = [half * side + k for k in range(side) for half in (0, 1)]
-    order = []
-    for i in range(n_rows):
-        row = i ^ (i >> 1)
-        order += [row * n_cols + c for c in (reversed(up) if i % 2 else up)]
-    return order
+    up = [half * side + k + c for k in range(0, side, 2) for half, c in ((1, 0), (0, 0), (0, 1), (1, 1))]
+    return [row * n_cols + c for row in range(n_rows) for c in up]
 
 
 def exchange(blocks, order):

time: 76.8 us -> 77.2 us (level)
  the two profiles are of different devices: /device:TPU:0 before, /device:TPU:1 now
where the time goes in v19:
time: 77.2 us; the launch traced here: 76.8 us
  waiting for transfers between devices  49.8 us (65%)
  Pallas kernels  14.2 us (18%)
  starting transfers between devices  9.74 us (13%)
  local copies, waits for them, and re-layouts  3.02 us (4%)
    all_to_all x2, waiting for transfers between devices, exchange(): lax.all_to_all(blocks, 'all', split_axis=0, concat_axis=0, axis_index_gro...  49.8 us
    all_to_all x2, starting transfers between devices, exchange(): lax.all_to_all(blocks, 'all', split_axis=0, concat_axis=0, axis_index_gro...  9.74 us
    pallas_call x1, Pallas kernels, local(): pl.pallas_call(conv_kernel, out_shape=jax.ShapeDtypeStruct(blocks, BF16),...  7.62 us
    pallas_call x1, Pallas kernels, local(): pl.pallas_call(mix_kernel, out_shape=jax.ShapeDtypeStruct((channels, BAND...  3.72 us
    pallas_call x1, Pallas kernels, local(): pl.pallas_call(spread_kernel, out_shape=jax.ShapeDtypeStruct((ch_dev, img...  2.84 us
  transfers between devices with their start and end apart: 2, of which 2 were waited for; matrix products, arithmetic and copies ran while one was open for 2% of the time, Pallas kernels for 0%

profile of v19, /device:TPU:1, one launch (start us, length us, event | category | flops | bytes accessed | tf_op | source)
XLA Modules:
  0.0 76.8 jit_solution(4979914576688084767)
XLA Ops:
  0.0 0.0 copy-start
  0.0 7.6 %conv.1.stepped = bf16[32,1,2,16,512]{4,3,2,1,0:T(8,128)(2,1)} custom-call(f32[2]{0:T(128)} %rate_h.1, bf16[2,512,512]{2,1,0:T(8,128)(2,1)} %model_h.1, bf16[2,512,512]{2,1,0:T(8,128)(2,1)} %dirty_h.1, bf16[2,256,256]{2,1,0:T(8,128)(2,1)} %psf_h.1, bf16[640,640]{1,0:T(8,128)(2,1)} %constant.16.clone.table_h, bf16[640,640]{1,0:T(8,128)(2,1)} %constant.17.clone.turned_h), custom_call_target="tpu_custom_call" | custom-call | tf_op jit(solution)/shard_map/conv/pallas_call | solution.py:326
  7.6 0.0 copy-start.5
  7.6 7.1 %all-to-all-start = ((bf16[32,2,16,512]{3,2,1,0:T(8,128)(2,1)}), bf16[32,2,16,512]{3,2,1,0:T(8,128)(2,1)S(1)}, u32[]{:S(2)}, u32[]{:S(2)}) async-start(bf16[32,2,16,512]{3,2,1,0:T(8,128)(2,1)} %bitcast.5), calls=%async_computation | async-start | bytes 2097152 | tf_op jit(solution)/shard_map/all_to_all | solution.py:296
  14.7 0.0 copy-done.5
  14.8 0.0 copy-start.2
  14.8 0.6 copy-done.2
  15.5 0.1 fusion.6
  15.5 0.0 copy-start.3
  15.5 0.1 fusion.7
  15.6 0.0 copy-start.4
  15.6 0.1 concatenate.8
  15.7 0.6 copy-done.3
  16.3 0.1 copy-done.4
  16.5 1.2 %concatenate.9.weights = bf16[192,256]{1,0:T(8,128)(2,1)S(1)} concatenate(bf16[2,256]{1,0:T(2,128)(2,1)S(1)} %get-tuple-element.44, bf16[4,256]{1,0:T(4,128)(2,1)S(1)} %get-tuple-element.56, bf16[4,256]{1,0:T(4,128)(2,1)S(1)} %get-tuple-element.55, bf16[4,256]{1,0:T(4,128)(2,1)S(1)} %get-tuple-element.54, bf16[2,256]{1,0:T(2,128)(2,1)S(1)} %get-tuple-element.43, ...), dimensions={0} | concatenate | bytes 196608 | tf_op jit(solution)/shard_map/concatenate | solution.py:307
  17.6 23.5 %all-to-all-done = bf16[32,2,16,512]{3,2,1,0:T(8,128)(2,1)S(1)} async-done(((bf16[32,2,16,512]{3,2,1,0:T(8,128)(2,1)}), bf16[32,2,16,512]{3,2,1,0:T(8,128)(2,1)S(1)}, u32[]{:S(2)}, u32[]{:S(2)}) %all-to-all-start) | async-done | bytes 1048608 | tf_op jit(solution)/shard_map/all_to_all | solution.py:296
  41.1 0.1 broadcast_in_dim.7.gain
  41.2 3.7 %mix.1 = bf16[64,16,512]{2,1,0:T(8,128)(2,1)} custom-call(f32[64,512]{1,0:T(8,128)S(1)} %broadcast_in_dim.7.gain, bf16[192,256]{1,0:T(8,128)(2,1)S(1)} %concatenate.9.weights, bf16[64,16,512]{2,1,0:T(8,128)(2,1)S(1)} %bitcast.6), custom_call_target="tpu_custom_call" | custom-call | tf_op jit(solution)/shard_map/mix/pallas_call | solution.py:360
  44.9 0.0 copy-start.1
  44.9 2.6 %all-to-all-start.1 = ((bf16[32,2,16,512]{3,2,1,0:T(8,128)(2,1)}), bf16[32,2,16,512]{3,2,1,0:T(8,128)(2,1)S(1)}, u32[]{:S(2)}, u32[]{:S(2)}) async-start(bf16[32,2,16,512]{3,2,1,0:T(8,128)(2,1)} %bitcast.3), calls=%async_computation.1 | async-start | bytes 2097152 | tf_op jit(solution)/shard_map/all_to_all | solution.py:296
  47.6 0.0 copy-done
  47.6 0.1 constant_dynamic-slice_fusion
  47.7 26.3 %all-to-all-done.1 = bf16[32,2,16,512]{3,2,1,0:T(8,128)(2,1)S(1)} async-done(((bf16[32,2,16,512]{3,2,1,0:T(8,128)(2,1)}), bf16[32,2,16,512]{3,2,1,0:T(8,128)(2,1)S(1)}, u32[]{:S(2)}, u32[]{:S(2)}) %all-to-all-start.1) | async-done | bytes 1048608 | tf_op jit(solution)/shard_map/all_to_all | solution.py:296
  73.9 0.1 broadcast_in_dim.6.taps
  74.0 0.0 copy-done.1
  74.0 2.8 %spread.1 = bf16[2,512,512]{2,1,0:T(8,128)(2,1)} custom-call(f32[3,3,2,128]{3,2,1,0:T(2,128)S(1)} %broadcast_in_dim.6.taps, bf16[32,1,2,16,512]{4,3,2,1,0:T(8,128)(2,1)S(1)} %copy-done.1, bf16[32,1,2,16,512]{4,3,2,1,0:T(8,128)(2,1)S(1)} %bitcast.7), custom_call_target="tpu_custom_call" | custom-call | tf_op jit(solution)/shard_map/spread/pallas_call | solution.py:388
  (9 shorter events, 0.1 us)
Async XLA Ops:
  0.0 47.6 %copy-start = (f32[3,3,64]{2,1,0:T(4,128)S(1)}, f32[3,3,64]{2,1,0:T(4,128)}, u32[]{:S(2)}) copy-start(f32[3,3,64]{2,1,0:T(4,128)} %param.19) | copy-start | bytes 6916
  7.6 7.1 %copy-start.5 = (f32[256]{0:T(256)S(1)}, f32[256]{0:T(256)}, u32[]{:S(2)}) copy-start(f32[256]{0:T(256)} %param.17) | copy-start | bytes 3076
  7.6 33.5 %all-to-all-start = ((bf16[32,2,16,512]{3,2,1,0:T(8,128)(2,1)}), bf16[32,2,16,512]{3,2,1,0:T(8,128)(2,1)S(1)}, u32[]{:S(2)}, u32[]{:S(2)}) async-start(bf16[32,2,16,512]{3,2,1,0:T(8,128)(2,1)} %bitcast.5), calls=%async_computation | async-start | bytes 2097152 | tf_op jit(solution)/shard_map/all_to_all | solution.py:296
  14.8 0.7 copy-start.2
  15.5 0.8 copy-start.3
  15.6 0.8 %copy-start.4 = (bf16[64,256]{1,0:T(8,128)(2,1)S(1)}, bf16[64,256]{1,0:T(8,128)(2,1)}, u32[]{:S(2)}) copy-start(bf16[64,256]{1,0:T(8,128)(2,1)} %param.16) | copy-start | bytes 98308
  44.9 29.1 %copy-start.1 = (bf16[32,1,2,16,512]{4,3,2,1,0:T(8,128)(2,1)S(1)}, bf16[32,1,2,16,512]{4,3,2,1,0:T(8,128)(2,1)}, u32[]{:S(2)}) copy-start(bf16[32,1,2,16,512]{4,3,2,1,0:T(8,128)(2,1)} %conv.1.stepped) | copy-start | bytes 3145732
  44.9 29.0 %all-to-all-start.1 = ((bf16[32,2,16,512]{3,2,1,0:T(8,128)(2,1)}), bf16[32,2,16,512]{3,2,1,0:T(8,128)(2,1)S(1)}, u32[]{:S(2)}, u32[]{:S(2)}) async-start(bf16[32,2,16,512]{3,2,1,0:T(8,128)(2,1)} %bitcast.3), calls=%async_computation.1 | async-start | bytes 2097152 | tf_op jit(solution)/shard_map/all_to_all | solution.py:296

commit v20 on v19

--- a/solution.py
+++ b/solution.py
@@ -288,8 +288,13 @@
 
 def partner_order(n_rows, n_cols):
     side = n_cols // 2
-    up = [half * side + k + c for k in range(0, side, 2) for half, c in ((1, 0), (0, 0), (0, 1), (1, 1))]
-    return [row * n_cols + c for row in range(n_rows) for c in up]
+    up = [half * side + k for k in range(0, side, 2) for half in (0, 1)]
+    order = []
+    for core in range(2):
+        for i in range(n_rows):
+            row = i ^ (i >> 1)
+            order += [row * n_cols + c + core for c in (reversed(up) if i % 2 else up)]
+    return order
 
 
 def exchange(blocks, order):

time: 77.2 us -> 80.3 us (1.040)
  the two profiles are of different devices: /device:TPU:1 before, /device:TPU:0 now
where the time goes in v20:
time: 80.3 us; the launch traced here: 79.9 us
  waiting for transfers between devices  53 us (66%)
  Pallas kernels  14.2 us (18%)
  starting transfers between devices  10.1 us (13%)
  local copies, waits for them, and re-layouts  2.45 us (3%)
    all_to_all x2, waiting for transfers between devices, exchange(): lax.all_to_all(blocks, 'all', split_axis=0, concat_axis=0, axis_index_gro...  53 us
    all_to_all x2, starting transfers between devices, exchange(): lax.all_to_all(blocks, 'all', split_axis=0, concat_axis=0, axis_index_gro...  10.1 us
    pallas_call x1, Pallas kernels, local(): pl.pallas_call(conv_kernel, out_shape=jax.ShapeDtypeStruct(blocks, BF16),...  7.61 us
    pallas_call x1, Pallas kernels, local(): pl.pallas_call(mix_kernel, out_shape=jax.ShapeDtypeStruct((channels, BAND...  3.72 us
    pallas_call x1, Pallas kernels, local(): pl.pallas_call(spread_kernel, out_shape=jax.ShapeDtypeStruct((ch_dev, img...  2.84 us
  transfers between devices with their start and end apart: 2, of which 2 were waited for; matrix products, arithmetic and copies ran while one was open for 1% of the time, Pallas kernels for 0%

profile of v20, /device:TPU:0, one launch (start us, length us, event | category | flops | bytes accessed | tf_op | source)
XLA Modules:
  0.0 79.9 jit_solution(1779833817624367627)
XLA Ops:
  0.0 0.0 copy-start
  0.0 7.6 %conv.1.stepped = bf16[32,1,2,16,512]{4,3,2,1,0:T(8,128)(2,1)} custom-call(f32[2]{0:T(128)} %rate_h.1, bf16[2,512,512]{2,1,0:T(8,128)(2,1)} %model_h.1, bf16[2,512,512]{2,1,0:T(8,128)(2,1)} %dirty_h.1, bf16[2,256,256]{2,1,0:T(8,128)(2,1)} %psf_h.1, bf16[640,640]{1,0:T(8,128)(2,1)} %constant.16.clone.table_h, bf16[640,640]{1,0:T(8,128)(2,1)} %constant.17.clone.turned_h), custom_call_target="tpu_custom_call" | custom-call | tf_op jit(solution)/shard_map/conv/pallas_call | solution.py:331
  7.6 0.0 copy-start.5
  7.6 7.3 %all-to-all-start = ((bf16[32,2,16,512]{3,2,1,0:T(8,128)(2,1)}), bf16[32,2,16,512]{3,2,1,0:T(8,128)(2,1)S(1)}, u32[]{:S(2)}, u32[]{:S(2)}) async-start(bf16[32,2,16,512]{3,2,1,0:T(8,128)(2,1)} %bitcast.5), calls=%async_computation | async-start | bytes 2097152 | tf_op jit(solution)/shard_map/all_to_all | solution.py:301
  14.9 0.0 copy-done.5
  15.0 0.0 copy-start.2
  15.0 0.6 copy-done.2
  15.7 0.1 fusion.7
  15.7 0.1 fusion.6
  15.8 0.0 copy-start.3
  15.8 0.0 copy-start.4
  15.8 0.1 concatenate.7
  15.9 0.6 copy-done.3
  16.6 0.0 copy-done.4
  16.7 0.6 concatenate.8.weights
  17.3 25.4 %all-to-all-done = bf16[32,2,16,512]{3,2,1,0:T(8,128)(2,1)S(1)} async-done(((bf16[32,2,16,512]{3,2,1,0:T(8,128)(2,1)}), bf16[32,2,16,512]{3,2,1,0:T(8,128)(2,1)S(1)}, u32[]{:S(2)}, u32[]{:S(2)}) %all-to-all-start) | async-done | bytes 1048608 | tf_op jit(solution)/shard_map/all_to_all | solution.py:301
  42.7 0.1 broadcast_in_dim.7.gain
  42.7 3.7 %mix.1 = bf16[64,16,512]{2,1,0:T(8,128)(2,1)} custom-call(f32[64,512]{1,0:T(8,128)S(1)} %broadcast_in_dim.7.gain, bf16[192,256]{1,0:T(8,128)(2,1)S(1)} %concatenate.8.weights, bf16[64,16,512]{2,1,0:T(8,128)(2,1)S(1)} %bitcast.6), custom_call_target="tpu_custom_call" | custom-call | tf_op jit(solution)/shard_map/mix/pallas_call | solution.py:365
  46.5 0.0 copy-start.1
  46.5 2.8 %all-to-all-start.1 = ((bf16[32,2,16,512]{3,2,1,0:T(8,128)(2,1)}), bf16[32,2,16,512]{3,2,1,0:T(8,128)(2,1)S(1)}, u32[]{:S(2)}, u32[]{:S(2)}) async-start(bf16[32,2,16,512]{3,2,1,0:T(8,128)(2,1)} %bitcast.3), calls=%async_computation.1 | async-start | bytes 2097152 | tf_op jit(solution)/shard_map/all_to_all | solution.py:301
  49.3 0.0 copy-done
  49.3 0.1 constant_dynamic-slice_fusion
  49.4 27.6 %all-to-all-done.1 = bf16[32,2,16,512]{3,2,1,0:T(8,128)(2,1)S(1)} async-done(((bf16[32,2,16,512]{3,2,1,0:T(8,128)(2,1)}), bf16[32,2,16,512]{3,2,1,0:T(8,128)(2,1)S(1)}, u32[]{:S(2)}, u32[]{:S(2)}) %all-to-all-start.1) | async-done | bytes 1048608 | tf_op jit(solution)/shard_map/all_to_all | solution.py:301
  77.0 0.1 broadcast_in_dim.6.taps
  77.1 0.0 copy-done.1
  77.1 2.8 %spread.1 = bf16[2,512,512]{2,1,0:T(8,128)(2,1)} custom-call(f32[3,3,2,128]{3,2,1,0:T(2,128)S(1)} %broadcast_in_dim.6.taps, bf16[32,1,2,16,512]{4,3,2,1,0:T(8,128)(2,1)S(1)} %copy-done.1, bf16[32,1,2,16,512]{4,3,2,1,0:T(8,128)(2,1)S(1)} %bitcast.7), custom_call_target="tpu_custom_call" | custom-call | tf_op jit(solution)/shard_map/spread/pallas_call | solution.py:393
  (9 shorter events, 0.1 us)
Async XLA Ops:
  0.0 49.3 %copy-start = (f32[3,3,64]{2,1,0:T(4,128)S(1)}, f32[3,3,64]{2,1,0:T(4,128)}, u32[]{:S(2)}) copy-start(f32[3,3,64]{2,1,0:T(4,128)} %param.19) | copy-start | bytes 6916
  7.6 7.3 %copy-start.5 = (f32[256]{0:T(256)S(1)}, f32[256]{0:T(256)}, u32[]{:S(2)}) copy-start(f32[256]{0:T(256)} %param.17) | copy-start | bytes 3076
  7.6 35.0 %all-to-all-start = ((bf16[32,2,16,512]{3,2,1,0:T(8,128)(2,1)}), bf16[32,2,16,512]{3,2,1,0:T(8,128)(2,1)S(1)}, u32[]{:S(2)}, u32[]{:S(2)}) async-start(bf16[32,2,16,512]{3,2,1,0:T(8,128)(2,1)} %bitcast.5), calls=%async_computation | async-start | bytes 2097152 | tf_op jit(solution)/shard_map/all_to_all | solution.py:301
  15.0 0.7 copy-start.2
  15.8 0.8 copy-start.3
  15.8 0.8 copy-start.4
  46.5 30.6 %copy-start.1 = (bf16[32,1,2,16,512]{4,3,2,1,0:T(8,128)(2,1)S(1)}, bf16[32,1,2,16,512]{4,3,2,1,0:T(8,128)(2,1)}, u32[]{:S(2)}) copy-start(bf16[32,1,2,16,512]{4,3,2,1,0:T(8,128)(2,1)} %conv.1.stepped) | copy-start | bytes 3145732
  46.5 30.5 %all-to-all-start.1 = ((bf16[32,2,16,512]{3,2,1,0:T(8,128)(2,1)}), bf16[32,2,16,512]{3,2,1,0:T(8,128)(2,1)S(1)}, u32[]{:S(2)}, u32[]{:S(2)}) async-start(bf16[32,2,16,512]{3,2,1,0:T(8,128)(2,1)} %bitcast.3), calls=%async_computation.1 | async-start | bytes 2097152 | tf_op jit(solution)/shard_map/all_to_all | solution.py:301

commit v21 on v19

--- a/solution.py
+++ b/solution.py
@@ -288,8 +288,8 @@
 
 def partner_order(n_rows, n_cols):
     side = n_cols // 2
-    up = [half * side + k + c for k in range(0, side, 2) for half, c in ((1, 0), (0, 0), (0, 1), (1, 1))]
-    return [row * n_cols + c for row in range(n_rows) for c in up]
+    down = [half * side + k for k in reversed(range(0, side, 2)) for half in (1, 0)]
+    return [(i ^ (i >> 1)) * n_cols + c + core for core in range(2) for i in range(n_rows) for c in down]
 
 
 def exchange(blocks, order):

time: 77.2 us -> 78.7 us (1.019)
  the two profiles are of different devices: /device:TPU:1 before, /device:TPU:0 now
where the time goes in v21:
time: 78.7 us; the launch traced here: 78.3 us
  waiting for transfers between devices  51.2 us (65%)
  Pallas kernels  14.2 us (18%)
  starting transfers between devices  10.4 us (13%)
  local copies, waits for them, and re-layouts  2.45 us (3%)
    all_to_all x2, waiting for transfers between devices, exchange(): lax.all_to_all(blocks, 'all', split_axis=0, concat_axis=0, axis_index_gro...  51.2 us
    all_to_all x2, starting transfers between devices, exchange(): lax.all_to_all(blocks, 'all', split_axis=0, concat_axis=0, axis_index_gro...  10.4 us
    pallas_call x1, Pallas kernels, local(): pl.pallas_call(conv_kernel, out_shape=jax.ShapeDtypeStruct(blocks, BF16),...  7.61 us
    pallas_call x1, Pallas kernels, local(): pl.pallas_call(mix_kernel, out_shape=jax.ShapeDtypeStruct((channels, BAND...  3.73 us
    pallas_call x1, Pallas kernels, local(): pl.pallas_call(spread_kernel, out_shape=jax.ShapeDtypeStruct((ch_dev, img...  2.84 us
  transfers between devices with their start and end apart: 2, of which 2 were waited for; matrix products, arithmetic and copies ran while one was open for 1% of the time, Pallas kernels for 0%

profile of v21, /device:TPU:0, one launch (start us, length us, event | category | flops | bytes accessed | tf_op | source)
XLA Modules:
  0.0 78.3 jit_solution(37492792733524177)
XLA Ops:
  0.0 0.0 copy-start
  0.0 7.6 %conv.1.stepped = bf16[32,1,2,16,512]{4,3,2,1,0:T(8,128)(2,1)} custom-call(f32[2]{0:T(128)} %rate_h.1, bf16[2,512,512]{2,1,0:T(8,128)(2,1)} %model_h.1, bf16[2,512,512]{2,1,0:T(8,128)(2,1)} %dirty_h.1, bf16[2,256,256]{2,1,0:T(8,128)(2,1)} %psf_h.1, bf16[640,640]{1,0:T(8,128)(2,1)} %constant.16.clone.table_h, bf16[640,640]{1,0:T(8,128)(2,1)} %constant.17.clone.turned_h), custom_call_target="tpu_custom_call" | custom-call | tf_op jit(solution)/shard_map/conv/pallas_call | solution.py:326
  7.6 0.0 copy-start.5
  7.6 7.3 %all-to-all-start = ((bf16[32,2,16,512]{3,2,1,0:T(8,128)(2,1)}), bf16[32,2,16,512]{3,2,1,0:T(8,128)(2,1)S(1)}, u32[]{:S(2)}, u32[]{:S(2)}) async-start(bf16[32,2,16,512]{3,2,1,0:T(8,128)(2,1)} %bitcast.5), calls=%async_computation | async-start | bytes 2097152 | tf_op jit(solution)/shard_map/all_to_all | solution.py:296
  14.9 0.0 copy-done.5
  15.0 0.0 copy-start.2
  15.0 0.6 copy-done.2
  15.7 0.1 fusion.7
  15.7 0.1 fusion.6
  15.8 0.0 copy-start.3
  15.8 0.0 copy-start.4
  15.8 0.1 concatenate.7
  15.9 0.6 copy-done.3
  16.6 0.0 copy-done.4
  16.7 0.6 concatenate.8.weights
  17.3 24.5 %all-to-all-done = bf16[32,2,16,512]{3,2,1,0:T(8,128)(2,1)S(1)} async-done(((bf16[32,2,16,512]{3,2,1,0:T(8,128)(2,1)}), bf16[32,2,16,512]{3,2,1,0:T(8,128)(2,1)S(1)}, u32[]{:S(2)}, u32[]{:S(2)}) %all-to-all-start) | async-done | bytes 1048608 | tf_op jit(solution)/shard_map/all_to_all | solution.py:296
  41.7 0.1 broadcast_in_dim.7.gain
  41.8 3.7 %mix.1 = bf16[64,16,512]{2,1,0:T(8,128)(2,1)} custom-call(f32[64,512]{1,0:T(8,128)S(1)} %broadcast_in_dim.7.gain, bf16[192,256]{1,0:T(8,128)(2,1)S(1)} %concatenate.8.weights, bf16[64,16,512]{2,1,0:T(8,128)(2,1)S(1)} %bitcast.6), custom_call_target="tpu_custom_call" | custom-call | tf_op jit(solution)/shard_map/mix/pallas_call | solution.py:360
  45.6 0.0 copy-start.1
  45.6 3.1 %all-to-all-start.1 = ((bf16[32,2,16,512]{3,2,1,0:T(8,128)(2,1)}), bf16[32,2,16,512]{3,2,1,0:T(8,128)(2,1)S(1)}, u32[]{:S(2)}, u32[]{:S(2)}) async-start(bf16[32,2,16,512]{3,2,1,0:T(8,128)(2,1)} %bitcast.3), calls=%async_computation.1 | async-start | bytes 2097152 | tf_op jit(solution)/shard_map/all_to_all | solution.py:296
  48.6 0.0 copy-done
  48.6 0.1 constant_dynamic-slice_fusion
  48.7 26.7 %all-to-all-done.1 = bf16[32,2,16,512]{3,2,1,0:T(8,128)(2,1)S(1)} async-done(((bf16[32,2,16,512]{3,2,1,0:T(8,128)(2,1)}), bf16[32,2,16,512]{3,2,1,0:T(8,128)(2,1)S(1)}, u32[]{:S(2)}, u32[]{:S(2)}) %all-to-all-start.1) | async-done | bytes 1048608 | tf_op jit(solution)/shard_map/all_to_all | solution.py:296
  75.4 0.1 broadcast_in_dim.6.taps
  75.5 0.0 copy-done.1
  75.5 2.8 %spread.1 = bf16[2,512,512]{2,1,0:T(8,128)(2,1)} custom-call(f32[3,3,2,128]{3,2,1,0:T(2,128)S(1)} %broadcast_in_dim.6.taps, bf16[32,1,2,16,512]{4,3,2,1,0:T(8,128)(2,1)S(1)} %copy-done.1, bf16[32,1,2,16,512]{4,3,2,1,0:T(8,128)(2,1)S(1)} %bitcast.7), custom_call_target="tpu_custom_call" | custom-call | tf_op jit(solution)/shard_map/spread/pallas_call | solution.py:388
  (9 shorter events, 0.1 us)
Async XLA Ops:
  0.0 48.6 %copy-start = (f32[3,3,64]{2,1,0:T(4,128)S(1)}, f32[3,3,64]{2,1,0:T(4,128)}, u32[]{:S(2)}) copy-start(f32[3,3,64]{2,1,0:T(4,128)} %param.19) | copy-start | bytes 6916
  7.6 7.3 %copy-start.5 = (f32[256]{0:T(256)S(1)}, f32[256]{0:T(256)}, u32[]{:S(2)}) copy-start(f32[256]{0:T(256)} %param.17) | copy-start | bytes 3076
  7.6 34.1 %all-to-all-start = ((bf16[32,2,16,512]{3,2,1,0:T(8,128)(2,1)}), bf16[32,2,16,512]{3,2,1,0:T(8,128)(2,1)S(1)}, u32[]{:S(2)}, u32[]{:S(2)}) async-start(bf16[32,2,16,512]{3,2,1,0:T(8,128)(2,1)} %bitcast.5), calls=%async_computation | async-start | bytes 2097152 | tf_op jit(solution)/shard_map/all_to_all | solution.py:296
  15.0 0.7 copy-start.2
  15.8 0.8 copy-start.3
  15.8 0.8 copy-start.4
  45.6 30.0 %copy-start.1 = (bf16[32,1,2,16,512]{4,3,2,1,0:T(8,128)(2,1)S(1)}, bf16[32,1,2,16,512]{4,3,2,1,0:T(8,128)(2,1)}, u32[]{:S(2)}) copy-start(bf16[32,1,2,16,512]{4,3,2,1,0:T(8,128)(2,1)} %conv.1.stepped) | copy-start | bytes 3145732
  45.6 29.9 %all-to-all-start.1 = ((bf16[32,2,16,512]{3,2,1,0:T(8,128)(2,1)}), bf16[32,2,16,512]{3,2,1,0:T(8,128)(2,1)S(1)}, u32[]{:S(2)}, u32[]{:S(2)}) async-start(bf16[32,2,16,512]{3,2,1,0:T(8,128)(2,1)} %bitcast.3), calls=%async_computation.1 | async-start | bytes 2097152 | tf_op jit(solution)/shard_map/all_to_all | solution.py:296

commit v22 on v19

--- a/solution.py
+++ b/solution.py
@@ -221,7 +221,7 @@
         send.wait()
 
 
-def spread_kernel(taps, stepped, mixed, out, rows_0, rows_1, result, sems):
+def spread_kernel(place_of, taps, stepped, mixed, out, rows_0, rows_1, result, sems):
     bands, parts, ch_dev, band, part = stepped.shape
     img = parts * part
     group = 2
@@ -231,9 +231,9 @@
     zero = jnp.zeros((len(strips), 8, 128), F32)
     sends = []
 
-    def rows_of(source, start, ch):
-        pieces = [source[start : start + group, p, ch].reshape(size, part) for p in range(parts)]
-        return jnp.concatenate(pieces, axis=1).astype(F32)
+    def rows_of(block):
+        columns = [jnp.concatenate([block(b, p) for b in range(group)], axis=0) for p in range(parts)]
+        return jnp.concatenate(columns, axis=1).astype(F32)
 
     for ch, padded in ((0, rows_0), (1, rows_1)):
         k = [[taps[i, j, ch : ch + 1, :] for j in range(3)] for i in range(3)]
@@ -241,7 +241,7 @@
         padded[:, img + 8 : img + 16, :] = zero
 
         def fill(start):
-            x = rows_of(mixed, start, ch)
+            x = rows_of(lambda b, p: mixed[place_of[(start + b) * parts + p], ch])
             for n, lanes in enumerate(strips):
                 padded[n, start * band + 8 : start * band + 8 + size, :] = x[:, lanes]
 
@@ -254,7 +254,7 @@
                     sums[j].append(k[0][j] * x[0] + k[1][j] * x[1] + k[2][j] * x[2])
             left = pltpu.roll(jnp.concatenate(sums[0], axis=1), 1, 1)
             right = pltpu.roll(jnp.concatenate(sums[2], axis=1), img - 1, 1)
-            base = rows_of(stepped, start, ch)
+            base = rows_of(lambda b, p: stepped[start + b, p, ch])
             for n, lanes in enumerate(strips):
                 low, high = left[:, lanes], right[:, lanes]
                 if n == 0:
@@ -286,10 +286,19 @@
     return pltpu.CompilerParams(vmem_limit_bytes=mib * MIB)
 
 
-def partner_order(n_rows, n_cols):
+def forth_order(n_rows, n_cols):
     side = n_cols // 2
     up = [half * side + k + c for k in range(0, side, 2) for half, c in ((1, 0), (0, 0), (0, 1), (1, 1))]
     return [row * n_cols + c for row in range(n_rows) for c in up]
+
+
+def back_order(n_rows, n_cols):
+    side = n_cols // 2
+    up = [half * side + k for k in range(side) for half in (0, 1)]
+    order = []
+    for i in range(n_rows):
+        order += [(i ^ (i >> 1)) * n_cols + c for c in (reversed(up) if i % 2 else up)]
+    return order
 
 
 def exchange(blocks, order):
@@ -312,7 +321,7 @@
     psf_len = psf.shape[1]
     assert ch_dev == 2
     n_dev = n_rows * n_cols
-    order = partner_order(n_rows, n_cols)
+    forth, back = forth_order(n_rows, n_cols), back_order(n_rows, n_cols)
     channels = gain.shape[0]
     hidden = b_in.shape[0]
     part = img * img // (n_dev * BAND)
@@ -352,10 +361,10 @@
         (stepped, gain, w_in, b_in, w_out, kernel)
     )
 
-    def ordered(values):
+    def ordered(values, order):
         return jnp.concatenate([values[d * ch_dev : (d + 1) * ch_dev] for d in order], axis=0)
 
-    tiles = exchange(stepped.reshape(n_dev, ch_dev, BAND, part), order).reshape(channels, BAND, part)
+    tiles = exchange(stepped.reshape(n_dev, ch_dev, BAND, part), forth).reshape(channels, BAND, part)
 
     mixed = pl.pallas_call(
         mix_kernel,
@@ -374,19 +383,19 @@
         compiler_params=params(24),
         name="mix",
     )(
-        jnp.broadcast_to(ordered(gain)[:, None], (channels, part)),
-        layers(ordered(w_in), b_in, ordered(w_out.T), wide),
+        jnp.broadcast_to(ordered(gain, forth)[:, None], (channels, part)),
+        layers(ordered(w_in, forth), b_in, ordered(w_out.T, back), wide),
         tiles,
     )
 
-    returned = exchange(mixed.reshape(n_dev, ch_dev, BAND, part), order).reshape(blocks)
+    returned = exchange(mixed.reshape(n_dev, ch_dev, BAND, part), back)
     position = lax.axis_index("all").astype(jnp.int32) * ch_dev
     taps = lax.dynamic_slice_in_dim(kernel, position, ch_dev, axis=2)
     taps = jnp.broadcast_to(taps[..., None], (3, 3, ch_dev, 128))
     plane = pltpu.VMEM((img // 128, img + 16, 128), F32)
 
     return pl.pallas_call(
-        spread_kernel,
+        functools.partial(spread_kernel, [back.index(device) for device in forth]),
         out_shape=jax.ShapeDtypeStruct((ch_dev, img, img), BF16),
         in_specs=[VMEM] * 3,
         out_specs=HBM,

time: 77.2 us -> 76.5 us (level)
  the two profiles are of different devices: /device:TPU:1 before, /device:TPU:0 now
where the time goes in v22:
time: 76.5 us; the launch traced here: 76.1 us
  waiting for transfers between devices  45.5 us (59%)
  Pallas kernels  14.1 us (18%)
  starting transfers between devices  13.6 us (18%)
  local copies, waits for them, and re-layouts  2.73 us (4%)
    all_to_all x2, waiting for transfers between devices, exchange(): lax.all_to_all(blocks, 'all', split_axis=0, concat_axis=0, axis_index_gro...  45.5 us
    all_to_all x2, starting transfers between devices, exchange(): lax.all_to_all(blocks, 'all', split_axis=0, concat_axis=0, axis_index_gro...  13.6 us
    pallas_call x1, Pallas kernels, local(): pl.pallas_call(conv_kernel, out_shape=jax.ShapeDtypeStruct(blocks, BF16),...  7.61 us
    pallas_call x1, Pallas kernels, local(): pl.pallas_call(mix_kernel, out_shape=jax.ShapeDtypeStruct((channels, BAND...  3.73 us
    pallas_call x1, Pallas kernels, local(): pl.pallas_call(functools.partial(spread_kernel, [back.index(device) for d...  2.74 us
  transfers between devices with their start and end apart: 2, of which 2 were waited for; matrix products, arithmetic and copies ran while one was open for 2% of the time, Pallas kernels for 0%

profile of v22, /device:TPU:0, one launch (start us, length us, event | category | flops | bytes accessed | tf_op | source)
XLA Modules:
  0.0 76.1 jit_solution(15632926437311863966)
XLA Ops:
  0.0 0.0 copy-start
  0.0 7.6 %conv.1.stepped = bf16[32,1,2,16,512]{4,3,2,1,0:T(8,128)(2,1)} custom-call(f32[2]{0:T(128)} %rate_h.1, bf16[2,512,512]{2,1,0:T(8,128)(2,1)} %model_h.1, bf16[2,512,512]{2,1,0:T(8,128)(2,1)} %dirty_h.1, bf16[2,256,256]{2,1,0:T(8,128)(2,1)} %psf_h.1, bf16[640,640]{1,0:T(8,128)(2,1)} %constant.16.clone.table_h, bf16[640,640]{1,0:T(8,128)(2,1)} %constant.17.clone.turned_h), custom_call_target="tpu_custom_call" | custom-call | tf_op jit(solution)/shard_map/conv/pallas_call | solution.py:335
  7.6 0.0 copy-start.5
  7.6 7.3 %all-to-all-start = ((bf16[32,2,16,512]{3,2,1,0:T(8,128)(2,1)}), bf16[32,2,16,512]{3,2,1,0:T(8,128)(2,1)S(1)}, u32[]{:S(2)}, u32[]{:S(2)}) async-start(bf16[32,2,16,512]{3,2,1,0:T(8,128)(2,1)} %bitcast.4), calls=%async_computation | async-start | bytes 2097152 | tf_op jit(solution)/shard_map/all_to_all | solution.py:305
  14.9 0.0 copy-done.5
  15.0 0.0 copy-start.2
  15.0 0.6 copy-done.2
  15.7 0.1 fusion.6
  15.7 0.0 copy-start.3
  15.7 0.1 fusion.7
  15.8 0.0 copy-start.4
  15.8 0.1 concatenate.8
  15.9 0.6 copy-done.3
  16.5 0.1 copy-done.4
  16.7 0.9 %concatenate.9.weights = bf16[192,256]{1,0:T(8,128)(2,1)S(1)} concatenate(bf16[2,256]{1,0:T(2,128)(2,1)S(1)} %get-tuple-element.56, bf16[4,256]{1,0:T(4,128)(2,1)S(1)} %get-tuple-element.68, bf16[4,256]{1,0:T(4,128)(2,1)S(1)} %get-tuple-element.67, bf16[4,256]{1,0:T(4,128)(2,1)S(1)} %get-tuple-element.66, bf16[2,256]{1,0:T(2,128)(2,1)S(1)} %get-tuple-element.55, ...), dimensions={0} | concatenate | bytes 196608 | tf_op jit(solution)/shard_map/concatenate | solution.py:316
  17.5 20.1 %all-to-all-done = bf16[32,2,16,512]{3,2,1,0:T(8,128)(2,1)S(1)} async-done(((bf16[32,2,16,512]{3,2,1,0:T(8,128)(2,1)}), bf16[32,2,16,512]{3,2,1,0:T(8,128)(2,1)S(1)}, u32[]{:S(2)}, u32[]{:S(2)}) %all-to-all-start) | async-done | bytes 1048608 | tf_op jit(solution)/shard_map/all_to_all | solution.py:305
  37.6 0.1 broadcast_in_dim.7.gain
  37.7 3.7 %mix.1 = bf16[64,16,512]{2,1,0:T(8,128)(2,1)} custom-call(f32[64,512]{1,0:T(8,128)S(1)} %broadcast_in_dim.7.gain, bf16[192,256]{1,0:T(8,128)(2,1)S(1)} %concatenate.9.weights, bf16[64,16,512]{2,1,0:T(8,128)(2,1)S(1)} %bitcast.5), custom_call_target="tpu_custom_call" | custom-call | tf_op jit(solution)/shard_map/mix/pallas_call | solution.py:369
  41.5 0.0 copy-start.1
  41.5 6.3 %all-to-all-start.1 = ((bf16[32,2,16,512]{3,2,1,0:T(8,128)(2,1)}), bf16[32,2,16,512]{3,2,1,0:T(8,128)(2,1)S(1)}, u32[]{:S(2)}, u32[]{:S(2)}) async-start(bf16[32,2,16,512]{3,2,1,0:T(8,128)(2,1)} %bitcast.3), calls=%async_computation.1 | async-start | bytes 2097152 | tf_op jit(solution)/shard_map/all_to_all | solution.py:305
  47.8 0.0 copy-done
  47.8 0.1 constant_dynamic-slice_fusion
  47.9 25.4 %all-to-all-done.1.mixed = bf16[32,2,16,512]{3,2,1,0:T(8,128)(2,1)S(1)} async-done(((bf16[32,2,16,512]{3,2,1,0:T(8,128)(2,1)}), bf16[32,2,16,512]{3,2,1,0:T(8,128)(2,1)S(1)}, u32[]{:S(2)}, u32[]{:S(2)}) %all-to-all-start.1) | async-done | bytes 1048608 | tf_op jit(solution)/shard_map/all_to_all | solution.py:305
  73.3 0.1 broadcast_in_dim.6.taps
  73.3 0.0 copy-done.1
  73.3 2.7 %spread.1 = bf16[2,512,512]{2,1,0:T(8,128)(2,1)} custom-call(f32[3,3,2,128]{3,2,1,0:T(2,128)S(1)} %broadcast_in_dim.6.taps, bf16[32,1,2,16,512]{4,3,2,1,0:T(8,128)(2,1)S(1)} %copy-done.1, bf16[32,2,16,512]{3,2,1,0:T(8,128)(2,1)S(1)} %all-to-all-done.1.mixed), custom_call_target="tpu_custom_call" | custom-call | tf_op jit(solution)/shard_map/spread/pallas_call | solution.py:397
  (9 shorter events, 0.1 us)
Async XLA Ops:
  0.0 47.8 %copy-start = (f32[3,3,64]{2,1,0:T(4,128)S(1)}, f32[3,3,64]{2,1,0:T(4,128)}, u32[]{:S(2)}) copy-start(f32[3,3,64]{2,1,0:T(4,128)} %param.19) | copy-start | bytes 6916
  7.6 7.3 %copy-start.5 = (f32[256]{0:T(256)S(1)}, f32[256]{0:T(256)}, u32[]{:S(2)}) copy-start(f32[256]{0:T(256)} %param.17) | copy-start | bytes 3076
  7.6 30.0 %all-to-all-start = ((bf16[32,2,16,512]{3,2,1,0:T(8,128)(2,1)}), bf16[32,2,16,512]{3,2,1,0:T(8,128)(2,1)S(1)}, u32[]{:S(2)}, u32[]{:S(2)}) async-start(bf16[32,2,16,512]{3,2,1,0:T(8,128)(2,1)} %bitcast.4), calls=%async_computation | async-start | bytes 2097152 | tf_op jit(solution)/shard_map/all_to_all | solution.py:305
  15.0 0.7 copy-start.2
  15.7 0.8 %copy-start.3 = (bf16[64,256]{1,0:T(8,128)(2,1)S(1)}, bf16[64,256]{1,0:T(8,128)(2,1)}, u32[]{:S(2)}) copy-start(bf16[64,256]{1,0:T(8,128)(2,1)} %param.16) | copy-start | bytes 98308
  15.8 0.8 %copy-start.4 = (bf16[256,64]{0,1:T(8,128)(2,1)S(1)}, bf16[256,64]{0,1:T(8,128)(2,1)}, u32[]{:S(2)}) copy-start(bf16[256,64]{0,1:T(8,128)(2,1)} %param.18) | copy-start | bytes 98308
  41.5 31.9 %copy-start.1 = (bf16[32,1,2,16,512]{4,3,2,1,0:T(8,128)(2,1)S(1)}, bf16[32,1,2,16,512]{4,3,2,1,0:T(8,128)(2,1)}, u32[]{:S(2)}) copy-start(bf16[32,1,2,16,512]{4,3,2,1,0:T(8,128)(2,1)} %conv.1.stepped) | copy-start | bytes 3145732
  41.5 31.8 %all-to-all-start.1 = ((bf16[32,2,16,512]{3,2,1,0:T(8,128)(2,1)}), bf16[32,2,16,512]{3,2,1,0:T(8,128)(2,1)S(1)}, u32[]{:S(2)}, u32[]{:S(2)}) async-start(bf16[32,2,16,512]{3,2,1,0:T(8,128)(2,1)} %bitcast.3), calls=%async_computation.1 | async-start | bytes 2097152 | tf_op jit(solution)/shard_map/all_to_all | solution.py:305

commit v23 on v22

--- a/solution.py
+++ b/solution.py
@@ -200,9 +200,9 @@
         for lanes in blocks:
             for h in range(0, hidden.shape[1], 128):
                 rows = slice(h, h + 128)
-                inner = dot(w_in_t[rows, :depth], normed[r, :, lanes]).astype(BF16)
-                bent = inner * (BF16(a) + BF16(a * 0.044715) * (inner * inner))
-                hidden[r, rows, lanes] = inner + inner * jnp.tanh(bent)
+                inner = dot(w_in_t[rows, :depth], normed[r, :, lanes])
+                bent = inner * (a + (a * 0.044715) * (inner * inner))
+                hidden[r, rows, lanes] = (inner + inner * jnp.tanh(bent)).astype(BF16)
     for r in range(band):
         for lanes in blocks:
             mixed[r, :, lanes] = (0.5 * dot(w_out_t, hidden[r, :, lanes])).astype(BF16)

time: 76.5 us -> 77.1 us (level)
  no operation moved by 1% of the time
where the time goes in v23:
time: 77.1 us; the launch traced here: 76.7 us
  waiting for transfers between devices  45.5 us (59%)
  Pallas kernels  14.7 us (19%)
  starting transfers between devices  13.6 us (18%)
  local copies, waits for them, and re-layouts  2.73 us (4%)
    all_to_all x2, waiting for transfers between devices, exchange(): lax.all_to_all(blocks, 'all', split_axis=0, concat_axis=0, axis_index_gro...  45.5 us
    all_to_all x2, starting transfers between devices, exchange(): lax.all_to_all(blocks, 'all', split_axis=0, concat_axis=0, axis_index_gro...  13.6 us
    pallas_call x1, Pallas kernels, local(): pl.pallas_call(conv_kernel, out_shape=jax.ShapeDtypeStruct(blocks, BF16),...  7.61 us
    pallas_call x1, Pallas kernels, local(): pl.pallas_call(mix_kernel, out_shape=jax.ShapeDtypeStruct((channels, BAND...  4.37 us
    pallas_call x1, Pallas kernels, local(): pl.pallas_call(functools.partial(spread_kernel, [back.index(device) for d...  2.74 us
  transfers between devices with their start and end apart: 2, of which 2 were waited for; matrix products, arithmetic and copies ran while one was open for 2% of the time, Pallas kernels for 0%

profile of v23, /device:TPU:0, one launch (start us, length us, event | category | flops | bytes accessed | tf_op | source)
XLA Modules:
  0.0 76.7 jit_solution(233592589289113434)
XLA Ops:
  0.0 0.0 copy-start
  0.0 7.6 %conv.1.stepped = bf16[32,1,2,16,512]{4,3,2,1,0:T(8,128)(2,1)} custom-call(f32[2]{0:T(128)} %rate_h.1, bf16[2,512,512]{2,1,0:T(8,128)(2,1)} %model_h.1, bf16[2,512,512]{2,1,0:T(8,128)(2,1)} %dirty_h.1, bf16[2,256,256]{2,1,0:T(8,128)(2,1)} %psf_h.1, bf16[640,640]{1,0:T(8,128)(2,1)} %constant.16.clone.table_h, bf16[640,640]{1,0:T(8,128)(2,1)} %constant.17.clone.turned_h), custom_call_target="tpu_custom_call" | custom-call | tf_op jit(solution)/shard_map/conv/pallas_call | solution.py:335
  7.6 0.0 copy-start.5
  7.6 7.3 %all-to-all-start = ((bf16[32,2,16,512]{3,2,1,0:T(8,128)(2,1)}), bf16[32,2,16,512]{3,2,1,0:T(8,128)(2,1)S(1)}, u32[]{:S(2)}, u32[]{:S(2)}) async-start(bf16[32,2,16,512]{3,2,1,0:T(8,128)(2,1)} %bitcast.4), calls=%async_computation | async-start | bytes 2097152 | tf_op jit(solution)/shard_map/all_to_all | solution.py:305
  14.9 0.0 copy-done.5
  15.0 0.0 copy-start.2
  15.0 0.6 copy-done.2
  15.7 0.1 fusion.6
  15.7 0.0 copy-start.3
  15.7 0.1 fusion.7
  15.8 0.0 copy-start.4
  15.8 0.1 concatenate.8
  15.9 0.6 copy-done.3
  16.5 0.1 copy-done.4
  16.7 0.9 %concatenate.9.weights = bf16[192,256]{1,0:T(8,128)(2,1)S(1)} concatenate(bf16[2,256]{1,0:T(2,128)(2,1)S(1)} %get-tuple-element.56, bf16[4,256]{1,0:T(4,128)(2,1)S(1)} %get-tuple-element.68, bf16[4,256]{1,0:T(4,128)(2,1)S(1)} %get-tuple-element.67, bf16[4,256]{1,0:T(4,128)(2,1)S(1)} %get-tuple-element.66, bf16[2,256]{1,0:T(2,128)(2,1)S(1)} %get-tuple-element.55, ...), dimensions={0} | concatenate | bytes 196608 | tf_op jit(solution)/shard_map/concatenate | solution.py:316
  17.5 20.1 %all-to-all-done = bf16[32,2,16,512]{3,2,1,0:T(8,128)(2,1)S(1)} async-done(((bf16[32,2,16,512]{3,2,1,0:T(8,128)(2,1)}), bf16[32,2,16,512]{3,2,1,0:T(8,128)(2,1)S(1)}, u32[]{:S(2)}, u32[]{:S(2)}) %all-to-all-start) | async-done | bytes 1048608 | tf_op jit(solution)/shard_map/all_to_all | solution.py:305
  37.6 0.1 broadcast_in_dim.7.gain
  37.7 4.4 %mix.1 = bf16[64,16,512]{2,1,0:T(8,128)(2,1)} custom-call(f32[64,512]{1,0:T(8,128)S(1)} %broadcast_in_dim.7.gain, bf16[192,256]{1,0:T(8,128)(2,1)S(1)} %concatenate.9.weights, bf16[64,16,512]{2,1,0:T(8,128)(2,1)S(1)} %bitcast.5), custom_call_target="tpu_custom_call" | custom-call | tf_op jit(solution)/shard_map/mix/pallas_call | solution.py:369
  42.1 0.0 copy-start.1
  42.1 6.3 %all-to-all-start.1 = ((bf16[32,2,16,512]{3,2,1,0:T(8,128)(2,1)}), bf16[32,2,16,512]{3,2,1,0:T(8,128)(2,1)S(1)}, u32[]{:S(2)}, u32[]{:S(2)}) async-start(bf16[32,2,16,512]{3,2,1,0:T(8,128)(2,1)} %bitcast.3), calls=%async_computation.1 | async-start | bytes 2097152 | tf_op jit(solution)/shard_map/all_to_all | solution.py:305
  48.4 0.0 copy-done
  48.4 0.1 constant_dynamic-slice_fusion
  48.5 25.4 %all-to-all-done.1.mixed = bf16[32,2,16,512]{3,2,1,0:T(8,128)(2,1)S(1)} async-done(((bf16[32,2,16,512]{3,2,1,0:T(8,128)(2,1)}), bf16[32,2,16,512]{3,2,1,0:T(8,128)(2,1)S(1)}, u32[]{:S(2)}, u32[]{:S(2)}) %all-to-all-start.1) | async-done | bytes 1048608 | tf_op jit(solution)/shard_map/all_to_all | solution.py:305
  73.9 0.1 broadcast_in_dim.6.taps
  74.0 0.0 copy-done.1
  74.0 2.7 %spread.1 = bf16[2,512,512]{2,1,0:T(8,128)(2,1)} custom-call(f32[3,3,2,128]{3,2,1,0:T(2,128)S(1)} %broadcast_in_dim.6.taps, bf16[32,1,2,16,512]{4,3,2,1,0:T(8,128)(2,1)S(1)} %copy-done.1, bf16[32,2,16,512]{3,2,1,0:T(8,128)(2,1)S(1)} %all-to-all-done.1.mixed), custom_call_target="tpu_custom_call" | custom-call | tf_op jit(solution)/shard_map/spread/pallas_call | solution.py:397
  (9 shorter events, 0.1 us)
Async XLA Ops:
  0.0 48.4 %copy-start = (f32[3,3,64]{2,1,0:T(4,128)S(1)}, f32[3,3,64]{2,1,0:T(4,128)}, u32[]{:S(2)}) copy-start(f32[3,3,64]{2,1,0:T(4,128)} %param.19) | copy-start | bytes 6916
  7.6 7.3 %copy-start.5 = (f32[256]{0:T(256)S(1)}, f32[256]{0:T(256)}, u32[]{:S(2)}) copy-start(f32[256]{0:T(256)} %param.17) | copy-start | bytes 3076
  7.6 30.0 %all-to-all-start = ((bf16[32,2,16,512]{3,2,1,0:T(8,128)(2,1)}), bf16[32,2,16,512]{3,2,1,0:T(8,128)(2,1)S(1)}, u32[]{:S(2)}, u32[]{:S(2)}) async-start(bf16[32,2,16,512]{3,2,1,0:T(8,128)(2,1)} %bitcast.4), calls=%async_computation | async-start | bytes 2097152 | tf_op jit(solution)/shard_map/all_to_all | solution.py:305
  15.0 0.7 copy-start.2
  15.7 0.8 copy-start.3
  15.8 0.8 %copy-start.4 = (bf16[256,64]{0,1:T(8,128)(2,1)S(1)}, bf16[256,64]{0,1:T(8,128)(2,1)}, u32[]{:S(2)}) copy-start(bf16[256,64]{0,1:T(8,128)(2,1)} %param.18) | copy-start | bytes 98308
  42.1 31.9 %copy-start.1 = (bf16[32,1,2,16,512]{4,3,2,1,0:T(8,128)(2,1)S(1)}, bf16[32,1,2,16,512]{4,3,2,1,0:T(8,128)(2,1)}, u32[]{:S(2)}) copy-start(bf16[32,1,2,16,512]{4,3,2,1,0:T(8,128)(2,1)} %conv.1.stepped) | copy-start | bytes 3145732
  42.1 31.8 %all-to-all-start.1 = ((bf16[32,2,16,512]{3,2,1,0:T(8,128)(2,1)}), bf16[32,2,16,512]{3,2,1,0:T(8,128)(2,1)S(1)}, u32[]{:S(2)}, u32[]{:S(2)}) async-start(bf16[32,2,16,512]{3,2,1,0:T(8,128)(2,1)} %bitcast.3), calls=%async_computation.1 | async-start | bytes 2097152 | tf_op jit(solution)/shard_map/all_to_all | solution.py:305

commit v24 on v23

--- a/solution.py
+++ b/solution.py
@@ -196,16 +196,16 @@
                 normed[h : h + 8, g * band : (g + 1) * band, lanes] = swapped.reshape(8, band, -1)
 
     a = math.sqrt(2.0 / math.pi)
-    for r in range(band):
+    lag = 2
+    for r in range(band + lag):
         for lanes in blocks:
-            for h in range(0, hidden.shape[1], 128):
+            for h in range(0, hidden.shape[1], 128) if r < band else ():
                 rows = slice(h, h + 128)
                 inner = dot(w_in_t[rows, :depth], normed[r, :, lanes])
                 bent = inner * (a + (a * 0.044715) * (inner * inner))
                 hidden[r, rows, lanes] = (inner + inner * jnp.tanh(bent)).astype(BF16)
-    for r in range(band):
-        for lanes in blocks:
-            mixed[r, :, lanes] = (0.5 * dot(w_out_t, hidden[r, :, lanes])).astype(BF16)
+            if r >= lag:
+                mixed[r - lag, :, lanes] = (0.5 * dot(w_out_t, hidden[r - lag, :, lanes])).astype(BF16)
 
     sends = []
     for g in range(groups):

time: 77.1 us -> 77 us (level)
  no operation moved by 1% of the time
where the time goes in v24:
time: 77 us; the launch traced here: 76.6 us
  waiting for transfers between devices  45.5 us (59%)
  Pallas kernels  14.6 us (19%)
  starting transfers between devices  13.6 us (18%)
  local copies, waits for them, and re-layouts  2.73 us (4%)
    all_to_all x2, waiting for transfers between devices, exchange(): lax.all_to_all(blocks, 'all', split_axis=0, concat_axis=0, axis_index_gro...  45.5 us
    all_to_all x2, starting transfers between devices, exchange(): lax.all_to_all(blocks, 'all', split_axis=0, concat_axis=0, axis_index_gro...  13.6 us
    pallas_call x1, Pallas kernels, local(): pl.pallas_call(conv_kernel, out_shape=jax.ShapeDtypeStruct(blocks, BF16),...  7.61 us
    pallas_call x1, Pallas kernels, local(): pl.pallas_call(mix_kernel, out_shape=jax.ShapeDtypeStruct((channels, BAND...  4.28 us
    pallas_call x1, Pallas kernels, local(): pl.pallas_call(functools.partial(spread_kernel, [back.index(device) for d...  2.74 us
  transfers between devices with their start and end apart: 2, of which 2 were waited for; matrix products, arithmetic and copies ran while one was open for 2% of the time, Pallas kernels for 0%

profile of v24, /device:TPU:0, one launch (start us, length us, event | category | flops | bytes accessed | tf_op | source)
XLA Modules:
  0.0 76.6 jit_solution(8522520561333719388)
XLA Ops:
  0.0 0.0 copy-start
  0.0 7.6 %conv.1.stepped = bf16[32,1,2,16,512]{4,3,2,1,0:T(8,128)(2,1)} custom-call(f32[2]{0:T(128)} %rate_h.1, bf16[2,512,512]{2,1,0:T(8,128)(2,1)} %model_h.1, bf16[2,512,512]{2,1,0:T(8,128)(2,1)} %dirty_h.1, bf16[2,256,256]{2,1,0:T(8,128)(2,1)} %psf_h.1, bf16[640,640]{1,0:T(8,128)(2,1)} %constant.16.clone.table_h, bf16[640,640]{1,0:T(8,128)(2,1)} %constant.17.clone.turned_h), custom_call_target="tpu_custom_call" | custom-call | tf_op jit(solution)/shard_map/conv/pallas_call | solution.py:335
  7.6 0.0 copy-start.5
  7.6 7.3 %all-to-all-start = ((bf16[32,2,16,512]{3,2,1,0:T(8,128)(2,1)}), bf16[32,2,16,512]{3,2,1,0:T(8,128)(2,1)S(1)}, u32[]{:S(2)}, u32[]{:S(2)}) async-start(bf16[32,2,16,512]{3,2,1,0:T(8,128)(2,1)} %bitcast.4), calls=%async_computation | async-start | bytes 2097152 | tf_op jit(solution)/shard_map/all_to_all | solution.py:305
  14.9 0.0 copy-done.5
  15.0 0.0 copy-start.2
  15.0 0.6 copy-done.2
  15.7 0.1 fusion.6
  15.7 0.0 copy-start.3
  15.7 0.1 fusion.7
  15.8 0.0 copy-start.4
  15.8 0.1 concatenate.8
  15.9 0.6 copy-done.3
  16.5 0.1 copy-done.4
  16.7 0.9 %concatenate.9.weights = bf16[192,256]{1,0:T(8,128)(2,1)S(1)} concatenate(bf16[2,256]{1,0:T(2,128)(2,1)S(1)} %get-tuple-element.56, bf16[4,256]{1,0:T(4,128)(2,1)S(1)} %get-tuple-element.68, bf16[4,256]{1,0:T(4,128)(2,1)S(1)} %get-tuple-element.67, bf16[4,256]{1,0:T(4,128)(2,1)S(1)} %get-tuple-element.66, bf16[2,256]{1,0:T(2,128)(2,1)S(1)} %get-tuple-element.55, ...), dimensions={0} | concatenate | bytes 196608 | tf_op jit(solution)/shard_map/concatenate | solution.py:316
  17.5 20.1 %all-to-all-done = bf16[32,2,16,512]{3,2,1,0:T(8,128)(2,1)S(1)} async-done(((bf16[32,2,16,512]{3,2,1,0:T(8,128)(2,1)}), bf16[32,2,16,512]{3,2,1,0:T(8,128)(2,1)S(1)}, u32[]{:S(2)}, u32[]{:S(2)}) %all-to-all-start) | async-done | bytes 1048608 | tf_op jit(solution)/shard_map/all_to_all | solution.py:305
  37.6 0.1 broadcast_in_dim.7.gain
  37.7 4.3 %mix.1 = bf16[64,16,512]{2,1,0:T(8,128)(2,1)} custom-call(f32[64,512]{1,0:T(8,128)S(1)} %broadcast_in_dim.7.gain, bf16[192,256]{1,0:T(8,128)(2,1)S(1)} %concatenate.9.weights, bf16[64,16,512]{2,1,0:T(8,128)(2,1)S(1)} %bitcast.5), custom_call_target="tpu_custom_call" | custom-call | tf_op jit(solution)/shard_map/mix/pallas_call | solution.py:369
  42.0 0.0 copy-start.1
  42.0 6.3 %all-to-all-start.1 = ((bf16[32,2,16,512]{3,2,1,0:T(8,128)(2,1)}), bf16[32,2,16,512]{3,2,1,0:T(8,128)(2,1)S(1)}, u32[]{:S(2)}, u32[]{:S(2)}) async-start(bf16[32,2,16,512]{3,2,1,0:T(8,128)(2,1)} %bitcast.3), calls=%async_computation.1 | async-start | bytes 2097152 | tf_op jit(solution)/shard_map/all_to_all | solution.py:305
  48.3 0.0 copy-done
  48.3 0.1 constant_dynamic-slice_fusion
  48.4 25.4 %all-to-all-done.1.mixed = bf16[32,2,16,512]{3,2,1,0:T(8,128)(2,1)S(1)} async-done(((bf16[32,2,16,512]{3,2,1,0:T(8,128)(2,1)}), bf16[32,2,16,512]{3,2,1,0:T(8,128)(2,1)S(1)}, u32[]{:S(2)}, u32[]{:S(2)}) %all-to-all-start.1) | async-done | bytes 1048608 | tf_op jit(solution)/shard_map/all_to_all | solution.py:305
  73.8 0.1 broadcast_in_dim.6.taps
  73.9 0.0 copy-done.1
  73.9 2.7 %spread.1 = bf16[2,512,512]{2,1,0:T(8,128)(2,1)} custom-call(f32[3,3,2,128]{3,2,1,0:T(2,128)S(1)} %broadcast_in_dim.6.taps, bf16[32,1,2,16,512]{4,3,2,1,0:T(8,128)(2,1)S(1)} %copy-done.1, bf16[32,2,16,512]{3,2,1,0:T(8,128)(2,1)S(1)} %all-to-all-done.1.mixed), custom_call_target="tpu_custom_call" | custom-call | tf_op jit(solution)/shard_map/spread/pallas_call | solution.py:397
  (9 shorter events, 0.1 us)
Async XLA Ops:
  0.0 48.3 %copy-start = (f32[3,3,64]{2,1,0:T(4,128)S(1)}, f32[3,3,64]{2,1,0:T(4,128)}, u32[]{:S(2)}) copy-start(f32[3,3,64]{2,1,0:T(4,128)} %param.19) | copy-start | bytes 6916
  7.6 7.3 %copy-start.5 = (f32[256]{0:T(256)S(1)}, f32[256]{0:T(256)}, u32[]{:S(2)}) copy-start(f32[256]{0:T(256)} %param.17) | copy-start | bytes 3076
  7.6 30.0 %all-to-all-start = ((bf16[32,2,16,512]{3,2,1,0:T(8,128)(2,1)}), bf16[32,2,16,512]{3,2,1,0:T(8,128)(2,1)S(1)}, u32[]{:S(2)}, u32[]{:S(2)}) async-start(bf16[32,2,16,512]{3,2,1,0:T(8,128)(2,1)} %bitcast.4), calls=%async_computation | async-start | bytes 2097152 | tf_op jit(solution)/shard_map/all_to_all | solution.py:305
  15.0 0.7 copy-start.2
  15.7 0.8 copy-start.3
  15.8 0.8 %copy-start.4 = (bf16[256,64]{0,1:T(8,128)(2,1)S(1)}, bf16[256,64]{0,1:T(8,128)(2,1)}, u32[]{:S(2)}) copy-start(bf16[256,64]{0,1:T(8,128)(2,1)} %param.18) | copy-start | bytes 98308
  42.0 31.9 %copy-start.1 = (bf16[32,1,2,16,512]{4,3,2,1,0:T(8,128)(2,1)S(1)}, bf16[32,1,2,16,512]{4,3,2,1,0:T(8,128)(2,1)}, u32[]{:S(2)}) copy-start(bf16[32,1,2,16,512]{4,3,2,1,0:T(8,128)(2,1)} %conv.1.stepped) | copy-start | bytes 3145732
  42.0 31.8 %all-to-all-start.1 = ((bf16[32,2,16,512]{3,2,1,0:T(8,128)(2,1)}), bf16[32,2,16,512]{3,2,1,0:T(8,128)(2,1)S(1)}, u32[]{:S(2)}, u32[]{:S(2)}) async-start(bf16[32,2,16,512]{3,2,1,0:T(8,128)(2,1)} %bitcast.3), calls=%async_computation.1 | async-start | bytes 2097152 | tf_op jit(solution)/shard_map/all_to_all | solution.py:305

commit v25 on v24

--- a/solution.py
+++ b/solution.py
@@ -294,10 +294,11 @@
 
 def back_order(n_rows, n_cols):
     side = n_cols // 2
-    up = [half * side + k for k in range(side) for half in (0, 1)]
     order = []
-    for i in range(n_rows):
-        order += [(i ^ (i >> 1)) * n_cols + c for c in (reversed(up) if i % 2 else up)]
+    for row in range(n_rows):
+        shift = 0 if row % 2 else side // 2
+        places = [(k + shift) % side for k in range(side)]
+        order += [row * n_cols + half * side + k for k in places for half in (1, 0)]
     return order
 
 

time: 77 us -> 78.8 us (1.023)
  waiting for transfers between devices: 45.5 us -> 47.1 us
    all_to_all x2, waiting for transfers between devices: 45.5 us -> 47.1 us  [exchange(): lax.all_to_all(blocks, 'all', split_axis=0, concat_axis=0, axis_index_gro...]
where the time goes in v25:
time: 78.8 us; the launch traced here: 78.4 us
  waiting for transfers between devices  47.1 us (60%)
  Pallas kernels  14.6 us (19%)
  starting transfers between devices  13.6 us (17%)
  local copies, waits for them, and re-layouts  2.91 us (4%)
    all_to_all x2, waiting for transfers between devices, exchange(): lax.all_to_all(blocks, 'all', split_axis=0, concat_axis=0, axis_index_gro...  47.1 us
    all_to_all x2, starting transfers between devices, exchange(): lax.all_to_all(blocks, 'all', split_axis=0, concat_axis=0, axis_index_gro...  13.6 us
    pallas_call x1, Pallas kernels, local(): pl.pallas_call(conv_kernel, out_shape=jax.ShapeDtypeStruct(blocks, BF16),...  7.61 us
    pallas_call x1, Pallas kernels, local(): pl.pallas_call(mix_kernel, out_shape=jax.ShapeDtypeStruct((channels, BAND...  4.29 us
    pallas_call x1, Pallas kernels, local(): pl.pallas_call(functools.partial(spread_kernel, [back.index(device) for d...  2.74 us
  transfers between devices with their start and end apart: 2, of which 2 were waited for; matrix products, arithmetic and copies ran while one was open for 2% of the time, Pallas kernels for 0%

profile of v25, /device:TPU:0, one launch (start us, length us, event | category | flops | bytes accessed | tf_op | source)
XLA Modules:
  0.0 78.4 jit_solution(9941718767241302408)
XLA Ops:
  0.0 0.0 copy-start
  0.0 7.6 %conv.1.stepped = bf16[32,1,2,16,512]{4,3,2,1,0:T(8,128)(2,1)} custom-call(f32[2]{0:T(128)} %rate_h.1, bf16[2,512,512]{2,1,0:T(8,128)(2,1)} %model_h.1, bf16[2,512,512]{2,1,0:T(8,128)(2,1)} %dirty_h.1, bf16[2,256,256]{2,1,0:T(8,128)(2,1)} %psf_h.1, bf16[640,640]{1,0:T(8,128)(2,1)} %constant.16.clone.table_h, bf16[640,640]{1,0:T(8,128)(2,1)} %constant.17.clone.turned_h), custom_call_target="tpu_custom_call" | custom-call | tf_op jit(solution)/shard_map/conv/pallas_call | solution.py:336
  7.6 0.0 copy-start.5
  7.6 7.3 %all-to-all-start = ((bf16[32,2,16,512]{3,2,1,0:T(8,128)(2,1)}), bf16[32,2,16,512]{3,2,1,0:T(8,128)(2,1)S(1)}, u32[]{:S(2)}, u32[]{:S(2)}) async-start(bf16[32,2,16,512]{3,2,1,0:T(8,128)(2,1)} %bitcast.4), calls=%async_computation | async-start | bytes 2097152 | tf_op jit(solution)/shard_map/all_to_all | solution.py:306
  14.9 0.0 copy-done.5
  15.0 0.0 copy-start.2
  15.0 0.6 copy-done.2
  15.7 0.1 fusion.7
  15.7 0.0 copy-start.4
  15.7 0.1 fusion.8
  15.8 0.0 copy-start.3
  15.8 0.1 concatenate.8
  15.9 0.6 copy-done.4
  16.5 0.1 copy-done.3
  16.7 1.0 %concatenate.9.weights = bf16[192,256]{1,0:T(8,128)(2,1)S(1)} concatenate(bf16[2,256]{1,0:T(2,128)(2,1)S(1)} %get-tuple-element.54, bf16[4,256]{1,0:T(4,128)(2,1)S(1)} %get-tuple-element.66, bf16[4,256]{1,0:T(4,128)(2,1)S(1)} %get-tuple-element.65, bf16[4,256]{1,0:T(4,128)(2,1)S(1)} %get-tuple-element.64, bf16[2,256]{1,0:T(2,128)(2,1)S(1)} %get-tuple-element.53, ...), dimensions={0} | concatenate | bytes 196608 | tf_op jit(solution)/shard_map/concatenate | solution.py:317
  17.7 19.9 %all-to-all-done = bf16[32,2,16,512]{3,2,1,0:T(8,128)(2,1)S(1)} async-done(((bf16[32,2,16,512]{3,2,1,0:T(8,128)(2,1)}), bf16[32,2,16,512]{3,2,1,0:T(8,128)(2,1)S(1)}, u32[]{:S(2)}, u32[]{:S(2)}) %all-to-all-start) | async-done | bytes 1048608 | tf_op jit(solution)/shard_map/all_to_all | solution.py:306
  37.6 0.1 broadcast_in_dim.7.gain
  37.7 4.3 %mix.1 = bf16[64,16,512]{2,1,0:T(8,128)(2,1)} custom-call(f32[64,512]{1,0:T(8,128)S(1)} %broadcast_in_dim.7.gain, bf16[192,256]{1,0:T(8,128)(2,1)S(1)} %concatenate.9.weights, bf16[64,16,512]{2,1,0:T(8,128)(2,1)S(1)} %bitcast.5), custom_call_target="tpu_custom_call" | custom-call | tf_op jit(solution)/shard_map/mix/pallas_call | solution.py:370
  42.0 0.0 copy-start.1
  42.0 6.3 %all-to-all-start.1 = ((bf16[32,2,16,512]{3,2,1,0:T(8,128)(2,1)}), bf16[32,2,16,512]{3,2,1,0:T(8,128)(2,1)S(1)}, u32[]{:S(2)}, u32[]{:S(2)}) async-start(bf16[32,2,16,512]{3,2,1,0:T(8,128)(2,1)} %bitcast.3), calls=%async_computation.1 | async-start | bytes 2097152 | tf_op jit(solution)/shard_map/all_to_all | solution.py:306
  48.3 0.0 copy-done
  48.3 0.1 constant_dynamic-slice_fusion
  48.4 27.2 %all-to-all-done.1.mixed = bf16[32,2,16,512]{3,2,1,0:T(8,128)(2,1)S(1)} async-done(((bf16[32,2,16,512]{3,2,1,0:T(8,128)(2,1)}), bf16[32,2,16,512]{3,2,1,0:T(8,128)(2,1)S(1)}, u32[]{:S(2)}, u32[]{:S(2)}) %all-to-all-start.1) | async-done | bytes 1048608 | tf_op jit(solution)/shard_map/all_to_all | solution.py:306
  75.6 0.1 broadcast_in_dim.6.taps
  75.6 0.0 copy-done.1
  75.7 2.7 %spread.1 = bf16[2,512,512]{2,1,0:T(8,128)(2,1)} custom-call(f32[3,3,2,128]{3,2,1,0:T(2,128)S(1)} %broadcast_in_dim.6.taps, bf16[32,1,2,16,512]{4,3,2,1,0:T(8,128)(2,1)S(1)} %copy-done.1, bf16[32,2,16,512]{3,2,1,0:T(8,128)(2,1)S(1)} %all-to-all-done.1.mixed), custom_call_target="tpu_custom_call" | custom-call | tf_op jit(solution)/shard_map/spread/pallas_call | solution.py:398
  (10 shorter events, 0.1 us)
Async XLA Ops:
  0.0 48.3 %copy-start = (f32[3,3,64]{2,1,0:T(4,128)S(1)}, f32[3,3,64]{2,1,0:T(4,128)}, u32[]{:S(2)}) copy-start(f32[3,3,64]{2,1,0:T(4,128)} %param.19) | copy-start | bytes 6916
  7.6 7.3 %copy-start.5 = (f32[256]{0:T(256)S(1)}, f32[256]{0:T(256)}, u32[]{:S(2)}) copy-start(f32[256]{0:T(256)} %param.17) | copy-start | bytes 3076
  7.6 30.0 %all-to-all-start = ((bf16[32,2,16,512]{3,2,1,0:T(8,128)(2,1)}), bf16[32,2,16,512]{3,2,1,0:T(8,128)(2,1)S(1)}, u32[]{:S(2)}, u32[]{:S(2)}) async-start(bf16[32,2,16,512]{3,2,1,0:T(8,128)(2,1)} %bitcast.4), calls=%async_computation | async-start | bytes 2097152 | tf_op jit(solution)/shard_map/all_to_all | solution.py:306
  15.0 0.7 copy-start.2
  15.7 0.8 copy-start.4
  15.8 0.8 copy-start.3
  42.0 33.6 %copy-start.1 = (bf16[32,1,2,16,512]{4,3,2,1,0:T(8,128)(2,1)S(1)}, bf16[32,1,2,16,512]{4,3,2,1,0:T(8,128)(2,1)}, u32[]{:S(2)}) copy-start(bf16[32,1,2,16,512]{4,3,2,1,0:T(8,128)(2,1)} %conv.1.stepped) | copy-start | bytes 3145732
  42.0 33.5 %all-to-all-start.1 = ((bf16[32,2,16,512]{3,2,1,0:T(8,128)(2,1)}), bf16[32,2,16,512]{3,2,1,0:T(8,128)(2,1)S(1)}, u32[]{:S(2)}, u32[]{:S(2)}) async-start(bf16[32,2,16,512]{3,2,1,0:T(8,128)(2,1)} %bitcast.3), calls=%async_computation.1 | async-start | bytes 2097152 | tf_op jit(solution)/shard_map/all_to_all | solution.py:306

commit v26 on v24

--- a/solution.py
+++ b/solution.py
@@ -199,8 +199,8 @@
     lag = 2
     for r in range(band + lag):
         for lanes in blocks:
-            for h in range(0, hidden.shape[1], 128) if r < band else ():
-                rows = slice(h, h + 128)
+            for h in range(0, hidden.shape[1], 256) if r < band else ():
+                rows = slice(h, h + 256)
                 inner = dot(w_in_t[rows, :depth], normed[r, :, lanes])
                 bent = inner * (a + (a * 0.044715) * (inner * inner))
                 hidden[r, rows, lanes] = (inner + inner * jnp.tanh(bent)).astype(BF16)

time: 77 us -> 76.9 us (level)
  no operation moved by 1% of the time
where the time goes in v26:
time: 76.9 us; the launch traced here: 76.5 us
  waiting for transfers between devices  45.5 us (59%)
  Pallas kernels  14.5 us (19%)
  starting transfers between devices  13.6 us (18%)
  local copies, waits for them, and re-layouts  2.73 us (4%)
    all_to_all x2, waiting for transfers between devices, exchange(): lax.all_to_all(blocks, 'all', split_axis=0, concat_axis=0, axis_index_gro...  45.5 us
    all_to_all x2, starting transfers between devices, exchange(): lax.all_to_all(blocks, 'all', split_axis=0, concat_axis=0, axis_index_gro...  13.6 us
    pallas_call x1, Pallas kernels, local(): pl.pallas_call(conv_kernel, out_shape=jax.ShapeDtypeStruct(blocks, BF16),...  7.61 us
    pallas_call x1, Pallas kernels, local(): pl.pallas_call(mix_kernel, out_shape=jax.ShapeDtypeStruct((channels, BAND...  4.14 us
    pallas_call x1, Pallas kernels, local(): pl.pallas_call(functools.partial(spread_kernel, [back.index(device) for d...  2.74 us
  transfers between devices with their start and end apart: 2, of which 2 were waited for; matrix products, arithmetic and copies ran while one was open for 2% of the time, Pallas kernels for 0%

profile of v26, /device:TPU:0, one launch (start us, length us, event | category | flops | bytes accessed | tf_op | source)
XLA Modules:
  0.0 76.5 jit_solution(14194632069480081466)
XLA Ops:
  0.0 0.0 copy-start
  0.0 7.6 %conv.1.stepped = bf16[32,1,2,16,512]{4,3,2,1,0:T(8,128)(2,1)} custom-call(f32[2]{0:T(128)} %rate_h.1, bf16[2,512,512]{2,1,0:T(8,128)(2,1)} %model_h.1, bf16[2,512,512]{2,1,0:T(8,128)(2,1)} %dirty_h.1, bf16[2,256,256]{2,1,0:T(8,128)(2,1)} %psf_h.1, bf16[640,640]{1,0:T(8,128)(2,1)} %constant.16.clone.table_h, bf16[640,640]{1,0:T(8,128)(2,1)} %constant.17.clone.turned_h), custom_call_target="tpu_custom_call" | custom-call | tf_op jit(solution)/shard_map/conv/pallas_call | solution.py:335
  7.6 0.0 copy-start.5
  7.6 7.3 %all-to-all-start = ((bf16[32,2,16,512]{3,2,1,0:T(8,128)(2,1)}), bf16[32,2,16,512]{3,2,1,0:T(8,128)(2,1)S(1)}, u32[]{:S(2)}, u32[]{:S(2)}) async-start(bf16[32,2,16,512]{3,2,1,0:T(8,128)(2,1)} %bitcast.4), calls=%async_computation | async-start | bytes 2097152 | tf_op jit(solution)/shard_map/all_to_all | solution.py:305
  14.9 0.0 copy-done.5
  15.0 0.0 copy-start.2
  15.0 0.6 copy-done.2
  15.7 0.1 fusion.6
  15.7 0.0 copy-start.3
  15.7 0.1 fusion.7
  15.8 0.0 copy-start.4
  15.8 0.1 concatenate.8
  15.9 0.6 copy-done.3
  16.5 0.1 copy-done.4
  16.7 0.9 %concatenate.9.weights = bf16[192,256]{1,0:T(8,128)(2,1)S(1)} concatenate(bf16[2,256]{1,0:T(2,128)(2,1)S(1)} %get-tuple-element.56, bf16[4,256]{1,0:T(4,128)(2,1)S(1)} %get-tuple-element.68, bf16[4,256]{1,0:T(4,128)(2,1)S(1)} %get-tuple-element.67, bf16[4,256]{1,0:T(4,128)(2,1)S(1)} %get-tuple-element.66, bf16[2,256]{1,0:T(2,128)(2,1)S(1)} %get-tuple-element.55, ...), dimensions={0} | concatenate | bytes 196608 | tf_op jit(solution)/shard_map/concatenate | solution.py:316
  17.5 20.1 %all-to-all-done = bf16[32,2,16,512]{3,2,1,0:T(8,128)(2,1)S(1)} async-done(((bf16[32,2,16,512]{3,2,1,0:T(8,128)(2,1)}), bf16[32,2,16,512]{3,2,1,0:T(8,128)(2,1)S(1)}, u32[]{:S(2)}, u32[]{:S(2)}) %all-to-all-start) | async-done | bytes 1048608 | tf_op jit(solution)/shard_map/all_to_all | solution.py:305
  37.6 0.1 broadcast_in_dim.7.gain
  37.7 4.1 %mix.1 = bf16[64,16,512]{2,1,0:T(8,128)(2,1)} custom-call(f32[64,512]{1,0:T(8,128)S(1)} %broadcast_in_dim.7.gain, bf16[192,256]{1,0:T(8,128)(2,1)S(1)} %concatenate.9.weights, bf16[64,16,512]{2,1,0:T(8,128)(2,1)S(1)} %bitcast.5), custom_call_target="tpu_custom_call" | custom-call | tf_op jit(solution)/shard_map/mix/pallas_call | solution.py:369
  41.9 0.0 copy-start.1
  41.9 6.3 %all-to-all-start.1 = ((bf16[32,2,16,512]{3,2,1,0:T(8,128)(2,1)}), bf16[32,2,16,512]{3,2,1,0:T(8,128)(2,1)S(1)}, u32[]{:S(2)}, u32[]{:S(2)}) async-start(bf16[32,2,16,512]{3,2,1,0:T(8,128)(2,1)} %bitcast.3), calls=%async_computation.1 | async-start | bytes 2097152 | tf_op jit(solution)/shard_map/all_to_all | solution.py:305
  48.2 0.0 copy-done
  48.2 0.1 constant_dynamic-slice_fusion
  48.3 25.4 %all-to-all-done.1.mixed = bf16[32,2,16,512]{3,2,1,0:T(8,128)(2,1)S(1)} async-done(((bf16[32,2,16,512]{3,2,1,0:T(8,128)(2,1)}), bf16[32,2,16,512]{3,2,1,0:T(8,128)(2,1)S(1)}, u32[]{:S(2)}, u32[]{:S(2)}) %all-to-all-start.1) | async-done | bytes 1048608 | tf_op jit(solution)/shard_map/all_to_all | solution.py:305
  73.7 0.1 broadcast_in_dim.6.taps
  73.8 0.0 copy-done.1
  73.8 2.7 %spread.1 = bf16[2,512,512]{2,1,0:T(8,128)(2,1)} custom-call(f32[3,3,2,128]{3,2,1,0:T(2,128)S(1)} %broadcast_in_dim.6.taps, bf16[32,1,2,16,512]{4,3,2,1,0:T(8,128)(2,1)S(1)} %copy-done.1, bf16[32,2,16,512]{3,2,1,0:T(8,128)(2,1)S(1)} %all-to-all-done.1.mixed), custom_call_target="tpu_custom_call" | custom-call | tf_op jit(solution)/shard_map/spread/pallas_call | solution.py:397
  (9 shorter events, 0.1 us)
Async XLA Ops:
  0.0 48.2 %copy-start = (f32[3,3,64]{2,1,0:T(4,128)S(1)}, f32[3,3,64]{2,1,0:T(4,128)}, u32[]{:S(2)}) copy-start(f32[3,3,64]{2,1,0:T(4,128)} %param.19) | copy-start | bytes 6916
  7.6 7.3 %copy-start.5 = (f32[256]{0:T(256)S(1)}, f32[256]{0:T(256)}, u32[]{:S(2)}) copy-start(f32[256]{0:T(256)} %param.17) | copy-start | bytes 3076
  7.6 30.0 %all-to-all-start = ((bf16[32,2,16,512]{3,2,1,0:T(8,128)(2,1)}), bf16[32,2,16,512]{3,2,1,0:T(8,128)(2,1)S(1)}, u32[]{:S(2)}, u32[]{:S(2)}) async-start(bf16[32,2,16,512]{3,2,1,0:T(8,128)(2,1)} %bitcast.4), calls=%async_computation | async-start | bytes 2097152 | tf_op jit(solution)/shard_map/all_to_all | solution.py:305
  15.0 0.7 copy-start.2
  15.7 0.8 copy-start.3
  15.8 0.8 %copy-start.4 = (bf16[256,64]{0,1:T(8,128)(2,1)S(1)}, bf16[256,64]{0,1:T(8,128)(2,1)}, u32[]{:S(2)}) copy-start(bf16[256,64]{0,1:T(8,128)(2,1)} %param.18) | copy-start | bytes 98308
  41.9 31.9 %copy-start.1 = (bf16[32,1,2,16,512]{4,3,2,1,0:T(8,128)(2,1)S(1)}, bf16[32,1,2,16,512]{4,3,2,1,0:T(8,128)(2,1)}, u32[]{:S(2)}) copy-start(bf16[32,1,2,16,512]{4,3,2,1,0:T(8,128)(2,1)} %conv.1.stepped) | copy-start | bytes 3145732
  41.9 31.8 %all-to-all-start.1 = ((bf16[32,2,16,512]{3,2,1,0:T(8,128)(2,1)}), bf16[32,2,16,512]{3,2,1,0:T(8,128)(2,1)S(1)}, u32[]{:S(2)}, u32[]{:S(2)}) async-start(bf16[32,2,16,512]{3,2,1,0:T(8,128)(2,1)} %bitcast.3), calls=%async_computation.1 | async-start | bytes 2097152 | tf_op jit(solution)/shard_map/all_to_all | solution.py:305
